TPU v7x, 32 devices: a whole 2x2x4 slice. The times are simulated.
32 devices in a mesh: probe: 4 (over z), sx: 4 (over x, core), sy: 2 (over y).
Axes of the slice: x: 2, y: 2, z: 4, core: 2. Of those that a mesh axis runs over, the one named last changes fastest.
Arguments:
- probes: float32 [8, 128, 64, 256], P('probe', 'sx', 'sy'), may hold values from -6 to 6
- velocity: float32 [3, 128, 64, 256], P(None, 'sx', 'sy'), may hold values from -0.15 to 0.15
- diffusivity: float32 [128, 64, 256], P('sx', 'sy'), may hold values from 0.02 to 0.15
- obs_weight: float32 [128, 64, 256], P('sx', 'sy'), may hold values from 0.05 to 1
Outputs:
- basis_fields: float32 [8, 128, 64, 256], P('probe', 'sx', 'sy')
- projected_hessian: float32 [8, 8], replicated
All inputs are finite; a program needn't handle non-finite values.
Results may differ from a plain program's by a relative error of at most 0.00013.
Values sent between devices are 32-bit elements; how exact they have to be, the bound alone decides.
No kernel may reach another device: no remote copies, remote signals or barrier semaphores. Data moves between devices by JAX's collectives and lax.ppermute only.
A program may use at most 128 MiB of HBM per device.

v0:
```python
import functools

import jax
import jax.numpy as jnp
from jax import lax
from jax.experimental import pallas as pl
from jax.experimental.pallas import tpu as pltpu
from jax.sharding import PartitionSpec as P

STEPS = 4
SUB = 8
LANES = 128
ROWS = 2
VMEM_LIMIT = 58 * 1024 * 1024
FLOPS_PER_MICRO = 1.15e9
BYTES_PER_MICRO = 3.6e6


def kernel_call(body, outs, scratch, ins, micros, anywhere=(), outs_anywhere=()):
    spec = lambda n, names: pl.BlockSpec(memory_space=pl.ANY if n in names else pltpu.VMEM)
    specs = [spec(n, anywhere) for n in range(len(ins))]
    specs[0] = pl.BlockSpec(memory_space=pltpu.SMEM)
    return pl.pallas_call(
        body,
        out_shape=outs,
        in_specs=specs,
        out_specs=[spec(n, outs_anywhere) for n in range(len(outs))],
        scratch_shapes=scratch,
        compiler_params=pltpu.CompilerParams(vmem_limit_bytes=VMEM_LIMIT),
        cost_estimate=pl.CostEstimate(
            flops=int(micros * FLOPS_PER_MICRO),
            bytes_accessed=int(micros * BYTES_PER_MICRO),
            transcendentals=0,
        ),
    )(*ins)


def f32(*shape):
    return jax.ShapeDtypeStruct(shape, jnp.float32)


def strip_shapes(fields, x, y, z, both):
    packs = [f32(fields, x // 2, SUB, z), f32(fields, 2, SUB, z), f32(fields, 2, SUB, z)]
    return [f32(fields, STEPS, y, z)] * 2 + packs * (2 if both else 1)


def pack_starts(packs, y, side):
    if packs == 2:
        return [(0, False), (y - SUB, True)]
    return [(pl.multiple_of(jnp.where(side == 0, y - SUB, 0), SUB), side == 0)]


def packed_pair(row, first, second, last):
    hi = lambda: jnp.where(row < STEPS, pltpu.roll(first, STEPS, 0), second)
    lo = lambda: jnp.where(row < STEPS, first, pltpu.roll(second, STEPS, 0))
    if isinstance(last, bool):
        return hi() if last else lo()
    return jnp.where(last, hi(), lo())


def write_packs(field, n, rows, last, outs):
    pack, corner_lo, corner_hi = outs[2 + 3 * n : 5 + 3 * n]
    half, z = pack.shape[1], pack.shape[3]
    row = lax.broadcasted_iota(jnp.int32, (SUB, z), 0)

    def step(i, carry):
        pack[field, i] = packed_pair(row, rows(2 * i), rows(2 * i + 1), last)
        return carry

    lax.fori_loop(0, half, step, None, unroll=4)
    for i in range(2):
        corner_lo[field, i] = pack[field, i]
        corner_hi[field, i] = pack[field, half - 2 + i]


def write_strips(tile, outs, side):
    fields, x, y, _ = tile.shape
    for p in range(fields):
        for i in range(STEPS):
            outs[0][p, i] = tile[p, i]
            outs[1][p, i] = tile[p, x - STEPS + i]
        for n, (start, last) in enumerate(pack_starts((len(outs) - 2) // 3, y, side)):
            write_packs(p, n, lambda i: tile[p, i, pl.ds(start, SUB)], last, outs)


def exchange(strips):
    nx, ny = lax.axis_size("sx"), lax.axis_size("sy")
    up = [(i, i + 1) for i in range(nx - 1)]
    down = [(j, i) for i, j in up]

    def moved(value, dx, dys):
        pairs = []
        for i in range(nx):
            for j in range(ny):
                for dy in dys(j):
                    if 0 <= i + dx < nx and 0 <= j + dy < ny:
                        pairs.append((i * ny + j, (i + dx) * ny + j + dy))
        return lax.ppermute(value, ("sx", "sy"), pairs)

    below = lax.ppermute(strips[1], "sx", up)
    above = lax.ppermute(strips[0], "sx", down)
    received = [below, above]
    if len(strips) == 5:
        flip = lambda j: (1 - 2 * j,)
        pack, corner_lo, corner_hi = strips[2:]
        received += [moved(pack, 0, flip), moved(corner_hi, 1, flip), moved(corner_lo, -1, flip)]
    else:
        for n, dy in ((0, -1), (1, 1)):
            pack, corner_lo, corner_hi = strips[2 + 3 * n : 5 + 3 * n]
            one = lambda j, dy=dy: (dy,)
            received += [moved(pack, 0, one), moved(corner_hi, 1, one), moved(corner_lo, -1, one)]
    return received


class Copies:
    def __init__(self, sems):
        self.sems, self.open, self.used = sems, [], 0

    def start(self, src, dst):
        copy = pltpu.make_async_copy(src, dst, self.sems.at[self.used])
        self.used += 1
        copy.start()
        self.open.append(copy)
        return copy

    def wait(self):
        for copy in self.open:
            copy.wait()
        self.open = []


def start_widening(copies, dst, tile, field, received):
    x, y = tile.shape[0], tile.shape[1]
    copies.start(tile, dst.at[pl.ds(0, x), pl.ds(0, y)])
    copies.start(received[1].at[field], dst.at[pl.ds(x, STEPS), pl.ds(0, y)])
    copies.start(received[0].at[field], dst.at[pl.ds(x + STEPS, STEPS), pl.ds(0, y)])


def widen_rows(dst, field, received, side):
    half, z = received[2].shape[1], received[2].shape[3]
    x, y = 2 * half, dst.shape[1] - SUB
    row = lax.broadcasted_iota(jnp.int32, (SUB, z), 0)
    both = len(received) > 5

    def put(at, packs):
        if both:
            hi, lo = packs
        else:
            hi = jnp.where(side == 0, packs[0], 0.0)
            lo = jnp.where(side == 0, 0.0, packs[0])
        dst[at, y : y + SUB] = jnp.where(row < STEPS, hi, pltpu.roll(lo, STEPS, 0))
        dst[at + 1, y : y + SUB] = jnp.where(row < STEPS, pltpu.roll(hi, STEPS, 0), lo)

    groups = [received[2:5]] + ([received[5:8]] if both else [])

    def main(i, carry):
        put(2 * i, [g[0][field, i] for g in groups])
        return carry

    lax.fori_loop(0, half, main, None, unroll=4)
    for i in range(2):
        put(x + 2 * i, [g[2][field, i] for g in groups])
        put(x + STEPS + 2 * i, [g[1][field, i] for g in groups])


def coefficient_rows(coef):
    _, wide, rows, z = coef.shape
    lane = lax.broadcasted_iota(jnp.int32, (SUB, z), 1)

    def row(i, carry):
        for c in range(rows // SUB):
            at = pl.ds(SUB * c, SUB)
            spread = coef[0, i, at]
            values = [1.0 - 6.0 * spread]
            for d in range(3):
                half = 0.5 * coef[1 + 2 * d, i, at]
                plus, minus = spread - half, spread + half
                if d == 2:
                    plus = jnp.where(lane == z - 1, 0.0, plus)
                    minus = jnp.where(lane == 0, 0.0, minus)
                values += [plus, minus]
            for s, value in enumerate(values):
                coef[s, i, at] = value
        return carry

    lax.fori_loop(0, wide, row, None)


def sweep(coef, src, first, stop, adjoint, done, write):
    fields, wide, rows, z = src.shape
    chunks, cols = rows // SUB, z // LANES
    sub = lax.broadcasted_iota(jnp.int32, (SUB, LANES), 0)
    lane = lax.broadcasted_iota(jnp.int32, (SUB, LANES), 1)
    first_row, last_row = sub == 0, sub == SUB - 1
    first_lane, last_lane = lane == 0, lane == LANES - 1

    def piece(ref, lead, xi, c, j):
        return ref[lead, xi, SUB * c : SUB * (c + 1), LANES * j : LANES * (j + 1)]

    def body(pair, carry):
        wrap = lambda a: jnp.where(a < 0, a + wide, a)
        base = first + ROWS * pair
        at = [wrap(base + d) for d in range(-1, ROWS + 1)]
        kept = {}

        def load(ref, lead, r, c, j):
            key = (ref is coef, lead, r, c % chunks, j)
            if key not in kept:
                kept[key] = piece(ref, lead, at[r + 1], c % chunks, j)
            return kept[key]

        def scaled(slot, p, r, c, j):
            u = load(src, p, r, c, j)
            return load(coef, slot, r, c, j) * u if adjoint else u

        def turned(slot, shift, p, r, c, j):
            key = ("turned", slot, p, r, c % chunks, j)
            if key not in kept:
                kept[key] = pltpu.roll(scaled(slot, p, r, c, j), shift, 0)
            return kept[key]

        for c in range(done):
            results = []
            for r in range(ROWS):
                plus, minus = {}, {}
                for j in range(cols):
                    for p in range(fields):
                        plus[p, j] = pltpu.roll(scaled(6, p, r, c, j), LANES - 1, 1)
                        minus[p, j] = pltpu.roll(scaled(5, p, r, c, j), 1, 1)
                for j in range(cols):
                    for p in range(fields):
                        u, xp, xm = (load(src, p, r + d, c, j) for d in (0, 1, -1))
                        yp = jnp.where(last_row, turned(4, SUB - 1, p, r, c + 1, j), turned(4, SUB - 1, p, r, c, j))
                        ym = jnp.where(first_row, turned(3, 1, p, r, c - 1, j), turned(3, 1, p, r, c, j))
                        zp = jnp.where(last_lane, plus[p, (j + 1) % cols], plus[p, j])
                        zm = jnp.where(first_lane, minus[p, (j - 1) % cols], minus[p, j])
                        if adjoint:
                            xs = load(coef, 2, r + 1, c, j) * xp + load(coef, 1, r - 1, c, j) * xm
                            ys, zs = yp + ym, zp + zm
                        else:
                            xs = load(coef, 1, r, c, j) * xp + load(coef, 2, r, c, j) * xm
                            ys = load(coef, 3, r, c, j) * yp + load(coef, 4, r, c, j) * ym
                            zs = load(coef, 5, r, c, j) * zp + load(coef, 6, r, c, j) * zm
                        value = (load(coef, 0, r, c, j) * u + xs) + (ys + zs)
                        results.append((p, at[r + 1], c, j, value))
            for result in results:
                write(*result)
        return carry

    lax.fori_loop(0, (stop - first) // ROWS, body, None)


def run_steps(coef, states, out, adjoint, weight=None, parts=None):
    x, tile_rows = out.shape[1], out.shape[2]
    for step in range(STEPS):
        src, dst = states[step % 2], states[(step + 1) % 2]
        last = step == STEPS - 1

        def write(p, i, c, j, value):
            at = (pl.ds(SUB * c, SUB), pl.ds(LANES * j, LANES))
            if last:
                out[p, i, *at] = value if weight is None else weight[i, *at] * value
            else:
                dst[p, i, *at] = value

        done = (tile_rows if last else src.shape[2]) // SUB
        reach = STEPS - 1 - step
        bounds = [-reach, x + reach]
        if step == 0 and parts is not None:
            bounds[1:1] = [SUB * (n + 1) - 1 for n in range(len(parts) - 1)]
        for n in range(len(bounds) - 1):
            if step == 0 and parts is not None:
                parts[n]()
            sweep(coef, src, bounds[n], bounds[n + 1], adjoint, done, write)


def pack_kernel(fields_in, scalars, *refs):
    sources, outs, (buffers, sems) = refs[:fields_in], refs[fields_in:-2], refs[-2:]
    side = scalars[0]
    tiles = [ref.at[n] for ref in sources for n in range(ref.shape[0])]
    x, y, _ = tiles[0].shape
    starts = pack_starts((len(outs) - 2) // 3, y, side)
    copies = Copies(sems)
    for f, tile in enumerate(tiles):
        for n, (start, _) in enumerate(starts):
            copies.start(tile.at[:, pl.ds(start, SUB)], buffers.at[n, f])
    loads, copies.open = copies.open, []
    for f, tile in enumerate(tiles):
        copies.start(tile.at[pl.ds(0, STEPS)], outs[0].at[f])
        copies.start(tile.at[pl.ds(x - STEPS, STEPS)], outs[1].at[f])
    for f in range(len(tiles)):
        for n, (_, last) in enumerate(starts):
            loads[f * len(starts) + n].wait()
            write_packs(f, n, lambda i: buffers[n, f, i], last, outs)
    copies.wait()


def first_kernel(count, scalars, diffusivity, velocity, probes, weight, *refs):
    side = scalars[0]
    received, coef_out, out = refs[:count], refs[count], refs[count + 1]
    strips, (coef, state, other, sems) = refs[count + 2 : -4], refs[-4:]
    copies = Copies(sems)
    tiles = [diffusivity.at[0]] + [velocity.at[d] for d in range(3)]
    slots = [coef.at[s] for s in (0, 1, 3, 5)]
    for p in range(probes.shape[0]):
        tiles.append(probes.at[p])
        slots.append(state.at[p])
    for f, (tile, slot) in enumerate(zip(tiles, slots)):
        start_widening(copies, slot, tile, f, received)
    for f, slot in enumerate(slots):
        widen_rows(slot, f, received, side)
    copies.wait()
    coefficient_rows(coef)
    copies.start(coef, coef_out)
    run_steps(coef, (state, other), out, False, weight)
    write_strips(out, strips, side)
    copies.wait()


def next_kernel(count, adjoint, scalars, coef_in, tile, *refs):
    side = scalars[0]
    weight = None if adjoint else refs[0]
    refs = refs if adjoint else refs[1:]
    received, out = refs[:count], refs[count]
    strips, (coef, state, other, sems) = refs[count + 1 : -4], refs[-4:]
    fields, x = tile.shape[0], tile.shape[1]
    copies = Copies(sems)
    for p in range(fields):
        start_widening(copies, state.at[p], tile.at[p], p, received)
    ends = Copies(sems.at[pl.ds(3 * fields, x // SUB + 1)])
    rows = [(x, 2 * STEPS)] + [(n, SUB) for n in range(0, x, SUB)]
    waits = []
    for at, size in rows:
        part = (slice(None), pl.ds(at, size))
        waits.append(ends.start(coef_in.at[part], coef.at[part]).wait)
    for p in range(fields):
        widen_rows(state.at[p], p, received, side)
    copies.wait()
    waits[0]()
    run_steps(coef, (state, other), out, adjoint, weight, waits[1:])
    if strips:
        write_strips(out, strips, side)


def dots_kernel(own_group, scalars, images, second, others, out):
    group, x, y, z = images.shape
    chunks, cols = y // SUB, z // LANES
    pairs = [(a, b) for a in range(group) for b in range(group) if not own_group or b <= a]

    def body(i, sums):
        sums = list(sums)
        for c in range(chunks):
            for j in range(cols):
                at = (pl.ds(SUB * c, SUB), pl.ds(LANES * j, LANES))
                other = [others[b, i, *at] for b in range(group)]
                mine = [images[a, i, *at] for a in range(group)]
                then = [second[a, i, *at] for a in range(group)]
                for n, (a, b) in enumerate(pairs):
                    sums[2 * n] = sums[2 * n] + mine[a] * other[b]
                    sums[2 * n + 1] = sums[2 * n + 1] + then[a] * other[b]
        return tuple(sums)

    zero = jnp.zeros((SUB, LANES), jnp.float32)
    sums = lax.fori_loop(0, x, body, (zero,) * (2 * len(pairs)))
    row0, col0 = scalars[1] * group, scalars[2] * group
    count = out.shape[0]
    row = lax.broadcasted_iota(jnp.int32, out.shape, 0)
    lane = lax.broadcasted_iota(jnp.int32, out.shape, 1)
    total = jnp.zeros(out.shape, jnp.float32)
    for n, (a, b) in enumerate(pairs):
        for k in range(2):
            value = jnp.sum(jnp.sum(sums[2 * n + k], axis=0, keepdims=True), axis=1, keepdims=True)
            here = (row == row0 + a) & (lane == col0 + b + k * count) & (scalars[2] >= 0)
            total = total + jnp.where(here, value, 0.0)
    out[...] = total


def basis_kernel(inverse, *refs):
    images, out = refs[:-1], refs[-1]
    group, x, y, z = out.shape
    chunks, cols = y // SUB, z // LANES

    def body(i, carry):
        for c in range(chunks):
            for j in range(cols):
                at = (pl.ds(SUB * c, SUB), pl.ds(LANES * j, LANES))
                sums = [None] * group
                for s, image in enumerate(images):
                    for b in range(group):
                        value = image[b, i, *at]
                        for a in range(group):
                            term = inverse[a, s * group + b] * value
                            sums[a] = term if sums[a] is None else sums[a] + term
                for a in range(group):
                    out[a, i, *at] = sums[a]
        return carry

    lax.fori_loop(0, x, body, None)


def all_sum(value):
    for axis in ("sx", "sy", "probe"):
        devices = lax.axis_size(axis)
        if devices & (devices - 1):
            value = lax.psum(value, axis)
            continue
        bit = 1
        while bit < devices:
            value = value + lax.ppermute(value, axis, [(i, i ^ bit) for i in range(devices)])
            bit *= 2
    return value


def shards(probes, velocity, diffusivity, obs_weight):
    group, x, y, z = probes.shape
    groups = lax.axis_size("probe")
    count = group * groups
    ncells = x * y * z * lax.axis_size("sx") * lax.axis_size("sy")
    both = lax.axis_size("sy") != 2
    side, mine = lax.axis_index("sy"), lax.axis_index("probe")

    def scalars(other):
        return jnp.stack([side, mine, mine - other]).astype(jnp.int32)

    where = scalars(0)
    wide = (x + 2 * STEPS, y + 2 * STEPS, z)
    tile = f32(group, x, y, z)
    strips2 = strip_shapes(group, x, y, z, both)
    fields = [diffusivity[None], velocity, probes]
    total = 4 + group

    def scratch(copies):
        return [
            pltpu.VMEM((7,) + wide, jnp.float32),
            pltpu.VMEM((group,) + wide, jnp.float32),
            pltpu.VMEM((group,) + wide, jnp.float32),
            pltpu.SemaphoreType.DMA((copies,)),
        ]

    packs = 2 if both else 1
    strips = kernel_call(
        functools.partial(pack_kernel, len(fields)),
        strip_shapes(total, x, y, z, both),
        [pltpu.VMEM((packs, total, x, SUB, z), jnp.float32), pltpu.SemaphoreType.DMA((total * (packs + 2),))],
        [where] + fields,
        3.0,
        anywhere=(1, 2, 3),
    )
    received = exchange(strips)
    coef, halfway, *strips = kernel_call(
        functools.partial(first_kernel, len(received)),
        [f32(7, *wide), tile] + strips2,
        scratch(3 * total + 1),
        [where] + fields + [obs_weight] + received,
        14.0,
        anywhere=(1, 2, 3, 5, 6),
        outs_anywhere=(0,),
    )

    def model(field, strips, adjoint, last=False):
        received = exchange(strips)
        ins = [where, coef, field] + ([] if adjoint else [obs_weight])
        return kernel_call(
            functools.partial(next_kernel, len(received), adjoint),
            [tile] + ([] if last else strips2),
            scratch(3 * group + x // SUB + 1),
            ins + received,
            12.0,
            anywhere=(1, 2, len(ins), len(ins) + 1),
        )

    images, *strips = model(halfway, strips, True)

    right = [(i, i + 1) for i in range(groups - 1)]
    passed = [images]
    for _ in range(groups - 1):
        passed.append(lax.ppermute(passed[-1], "probe", right))

    halfway, *strips = model(images, strips, False)
    (second,) = model(halfway, strips, True, True)

    partial = None
    for n, others in enumerate(passed):
        (part,) = kernel_call(
            functools.partial(dots_kernel, n == 0),
            [f32(count, LANES)],
            [],
            [scalars(n), images, second, others],
            4.0,
        )
        partial = part if partial is None else partial + part
    inner = all_sum(partial) / ncells
    strict = jnp.tril(jnp.ones((count, count), jnp.float32), -1)
    gram, ritz = inner[:, :count], inner[:, count : 2 * count]
    gram = gram + (gram * strict).T
    ritz = ritz + (ritz * strict).T
    lower = jnp.linalg.cholesky(gram)
    inverse = jax.scipy.linalg.solve_triangular(lower, jnp.eye(count, dtype=jnp.float32), lower=True)
    highest = lax.Precision.HIGHEST
    projected = jnp.dot(jnp.dot(inverse, ritz, precision=highest), inverse.T, precision=highest)

    rows = lax.dynamic_slice_in_dim(inverse, mine * group, group, 0)
    parts = []
    for n in range(groups):
        part = lax.dynamic_slice_in_dim(rows, jnp.maximum(mine - n, 0) * group, group, 1)
        parts.append(jnp.where(mine >= n, part, 0.0))
    (basis,) = kernel_call(basis_kernel, [tile], [], [jnp.concatenate(parts, 1)] + passed, 6.0)
    return (basis, projected)


def solution(mesh):
    return jax.shard_map(
        shards,
        mesh=mesh,
        in_specs=(
            P("probe", "sx", "sy", None),
            P(None, "sx", "sy", None),
            P("sx", "sy", None),
            P("sx", "sy", None),
        ),
        out_specs=(P("probe", "sx", "sy", None), P()),
        check_vma=False,
    )
```

profile of v0, /device:TPU:0, one launch (start us, length us, event | category | flops | bytes accessed | tf_op | source)
XLA Modules:
  0.0 281.0 jit_solution(718591035260310458)
XLA Ops:
  0.6 0.6 pad_add_fusion.scalars
  1.3 4.1 %shard_map.59 = (f32[6,4,32,256]{3,2,1,0:T(8,128)}, f32[6,4,32,256]{3,2,1,0:T(8,128)}, f32[6,16,8,256]{3,2,1,0:T(8,128)}, f32[6,2,8,256]{3,2,1,0:T(8,128)}, f32[6,2,8,256]{3,2,1,0:T(8,128)}) custom-call(s32[3]{0:T(128)} %pad_add_fusion.scalars, f32[1,32,32,256]{3,2,1,0:T(8,128)} %bitcast.28, f32[3,32,32,256]{3,2,1,0:T(8,128)} %velocity.1, ...), custom_call_target="tpu_custom_call" | custom-call | flops 3449999872 | bytes 10800000 | tf_op jit(solution)/shard_map/pallas_call | solution.py:23
  5.4 2.4 collective-permute-start
  7.8 1.3 collective-permute-start.1
  9.1 2.4 collective-permute-start.2
  11.5 4.1 %collective-permute-start.3 = (f32[6,2,8,256]{3,2,1,0:T(8,128)}, f32[6,2,8,256]{3,2,1,0:T(8,128)S(1)}, u32[]{:S(2)}, u32[]{:S(2)}) collective-permute-start(f32[6,2,8,256]{3,2,1,0:T(8,128)} %get-tuple-element.29), channel_id=1, source_target_pairs={{0,3},{1,2},{2,5},{3,4},{4,7},{5,6},{8,11},{9,10},{10,13},{11,12},... | collective-permute-start | bytes 294920 | tf_op jit(solution)/shard_map/ppermute | solution.py:98
  15.6 1.3 collective-permute-start.4
  16.9 14.6 %collective-permute-done.3.refs_3_ = f32[6,2,8,256]{3,2,1,0:T(8,128)S(1)} collective-permute-done((f32[6,2,8,256]{3,2,1,0:T(8,128)}, f32[6,2,8,256]{3,2,1,0:T(8,128)S(1)}, u32[]{:S(2)}, u32[]{:S(2)}) %collective-permute-start.3) | collective-permute-done | bytes 98336 | tf_op jit(solution)/shard_map/ppermute | solution.py:98
  31.5 1.8 collective-permute-done.4.refs_4_
  34.5 0.9 copy-done.5
  35.4 18.4 %shard_map.60 = (f32[7,40,40,256]{3,2,1,0:T(8,128)}, f32[2,32,32,256]{3,2,1,0:T(8,128)}, f32[2,4,32,256]{3,2,1,0:T(8,128)}, f32[2,4,32,256]{3,2,1,0:T(8,128)}, f...) custom-call(s32[3]{0:T(128)} %pad_add_fusion.scalars, f32[1,32,32,256]{3,2,1,0:T(8,128)} %bitcast.29, ...), custom_call_target="tpu_custom_call" | custom-call | flops 16099999744 | bytes 50400000 | tf_op jit(solution)/shard_map/pallas_call | solution.py:23
  53.8 1.7 collective-permute-start.5
  55.5 1.3 collective-permute-start.6
  56.8 1.7 collective-permute-start.7
  58.5 4.1 %collective-permute-start.8 = (f32[2,2,8,256]{3,2,1,0:T(8,128)}, f32[2,2,8,256]{3,2,1,0:T(8,128)S(1)}, u32[]{:S(2)}, u32[]{:S(2)}) collective-permute-start(f32[2,2,8,256]{3,2,1,0:T(8,128)} %get-tuple-element.36), channel_id=1, source_target_pairs={{0,3},{1,2},{2,5},{3,4},{4,7},{5,6},{8,11},{9,10},{10,13},{11,12},... | collective-permute-start | bytes 98312 | tf_op jit(solution)/shard_map/ppermute | solution.py:98
  62.6 1.3 collective-permute-start.9
  63.9 2.0 collective-permute-done.8.refs_3_
  65.9 2.4 collective-permute-done.9.refs_4_
  69.2 17.6 %shard_map.61 = (f32[2,32,32,256]{3,2,1,0:T(8,128)}, f32[2,4,32,256]{3,2,1,0:T(8,128)}, f32[2,4,32,256]{3,2,1,0:T(8,128)}, f32[2,16,8,256]{3,2,1,0:T(8,128)}, f3...) custom-call(s32[3]{0:T(128)} %pad_add_fusion.scalars, f32[7,40,40,256]{3,2,1,0:T(8,128)} %get-tuple-element.31.coef_in, ...), custom_call_target="tpu_custom_call" | custom-call | flops 13799999488 | bytes 43200000 | tf_op jit(solution)/shard_map/pallas_call | solution.py:23
  86.8 3.6 %collective-permute-start.20 = (f32[2,32,32,256]{3,2,1,0:T(8,128)}, f32[2,32,32,256]{3,2,1,0:T(8,128)S(1)}, u32[]{:S(2)}, u32[]{:S(2)}) collective-permute-start(f32[2,32,32,256]{3,2,1,0:T(8,128)} %get-tuple-element.38.tile.images.others.refs_0_), channel_id=1, source_target_pairs={{0,8},{8,16},{16,24},{1,9},{9,17},{17,25},{2,10},{10,18},{18,26},{... | collective-permute-start | bytes 6291464 | tf_op jit(solution)/shard_map/ppermute | solution.py:477
  90.5 44.6 %collective-permute-done.20.others.refs_1_ = f32[2,32,32,256]{3,2,1,0:T(8,128)S(1)} collective-permute-done((f32[2,32,32,256]{3,2,1,0:T(8,128)}, f32[2,32,32,256]{3,2,1,0:T(8,128)S(1)}, u32[]{:S(2)}, u32[]{:S(2)}) %collective-permute-start.20) | collective-permute-done | bytes 2097184 | tf_op jit(solution)/shard_map/ppermute | solution.py:477
  135.0 5.6 %collective-permute-start.21 = (f32[2,32,32,256]{3,2,1,0:T(8,128)S(1)}, f32[2,32,32,256]{3,2,1,0:T(8,128)}, u32[]{:S(2)}, u32[]{:S(2)}) collective-permute-start(f32[2,32,32,256]{3,2,1,0:T(8,128)S(1)} %collective-permute-done.20.others.refs_1_), channel_id=1, source_target_pairs={{0,8},{8,16},{16,24},{1,9},{9,17},{17,25},{2,10},{10,18},{18,26},{... | collective-permute-start | bytes 6291464 | tf_op jit(solution)/shard_map/ppermute | solution.py:477
  140.6 3.1 %collective-permute-start.10 = (f32[2,4,32,256]{3,2,1,0:T(8,128)}, f32[2,4,32,256]{3,2,1,0:T(8,128)S(1)}, u32[]{:S(2)}, u32[]{:S(2)}) collective-permute-start(f32[2,4,32,256]{3,2,1,0:T(8,128)} %get-tuple-element.39), channel_id=1, source_target_pairs={{0,2},{2,4},{4,6},{1,3},{3,5},{5,7},{8,10},{10,12},{12,14},{9,11},... | collective-permute-start | bytes 786440 | tf_op jit(solution)/shard_map/ppermute | solution.py:100
  143.7 1.3 collective-permute-start.11
  145.0 1.6 collective-permute-start.12
  146.6 3.4 %collective-permute-start.13 = (f32[2,2,8,256]{3,2,1,0:T(8,128)}, f32[2,2,8,256]{3,2,1,0:T(8,128)S(1)}, u32[]{:S(2)}, u32[]{:S(2)}) collective-permute-start(f32[2,2,8,256]{3,2,1,0:T(8,128)} %get-tuple-element.42), channel_id=1, source_target_pairs={{0,3},{1,2},{2,5},{3,4},{4,7},{5,6},{8,11},{9,10},{10,13},{11,12},... | collective-permute-start | bytes 98312 | tf_op jit(solution)/shard_map/ppermute | solution.py:98
  150.0 3.6 %collective-permute-done.13.refs_4_ = f32[2,2,8,256]{3,2,1,0:T(8,128)S(1)} collective-permute-done((f32[2,2,8,256]{3,2,1,0:T(8,128)}, f32[2,2,8,256]{3,2,1,0:T(8,128)S(1)}, u32[]{:S(2)}, u32[]{:S(2)}) %collective-permute-start.13) | collective-permute-done | bytes 32800 | tf_op jit(solution)/shard_map/ppermute | solution.py:98
  153.6 1.3 collective-permute-start.14
  154.9 4.2 %collective-permute-done.14.refs_5_ = f32[2,2,8,256]{3,2,1,0:T(8,128)S(1)} collective-permute-done((f32[2,2,8,256]{3,2,1,0:T(8,128)}, f32[2,2,8,256]{3,2,1,0:T(8,128)S(1)}, u32[]{:S(2)}, u32[]{:S(2)}) %collective-permute-start.14) | collective-permute-done | bytes 32800 | tf_op jit(solution)/shard_map/ppermute | solution.py:98
  160.0 0.7 copy-done.13
  160.7 17.2 %shard_map.62 = (f32[2,32,32,256]{3,2,1,0:T(8,128)}, f32[2,4,32,256]{3,2,1,0:T(8,128)}, f32[2,4,32,256]{3,2,1,0:T(8,128)}, f32[2,16,8,256]{3,2,1,0:T(8,128)}, f3...) custom-call(s32[3]{0:T(128)} %pad_add_fusion.scalars, f32[7,40,40,256]{3,2,1,0:T(8,128)} %get-tuple-element.31.coef_in, ...), custom_call_target="tpu_custom_call" | custom-call | flops 13799999488 | bytes 43200000 | tf_op jit(solution)/shard_map/pallas_call | solution.py:23
  177.9 3.4 %collective-permute-start.15 = (f32[2,4,32,256]{3,2,1,0:T(8,128)}, f32[2,4,32,256]{3,2,1,0:T(8,128)S(1)}, u32[]{:S(2)}, u32[]{:S(2)}) collective-permute-start(f32[2,4,32,256]{3,2,1,0:T(8,128)} %get-tuple-element.45), channel_id=1, source_target_pairs={{0,2},{2,4},{4,6},{1,3},{3,5},{5,7},{8,10},{10,12},{12,14},{9,11},... | collective-permute-start | bytes 786440 | tf_op jit(solution)/shard_map/ppermute | solution.py:100
  181.3 1.3 collective-permute-start.16
  182.6 1.6 collective-permute-start.17
  184.8 3.5 %collective-permute-start.18 = (f32[2,2,8,256]{3,2,1,0:T(8,128)}, f32[2,2,8,256]{3,2,1,0:T(8,128)S(1)}, u32[]{:S(2)}, u32[]{:S(2)}) collective-permute-start(f32[2,2,8,256]{3,2,1,0:T(8,128)} %get-tuple-element.48), channel_id=1, source_target_pairs={{0,3},{1,2},{2,5},{3,4},{4,7},{5,6},{8,11},{9,10},{10,13},{11,12},... | collective-permute-start | bytes 98312 | tf_op jit(solution)/shard_map/ppermute | solution.py:98
  188.4 0.7 pad_add_fusion.2.scalars
  189.0 2.6 collective-permute-done.18.refs_3_
  191.6 1.3 collective-permute-start.19
  193.4 2.7 collective-permute-start.22
  196.1 0.9 collective-permute-done.19.refs_4_
  198.0 17.2 %shard_map.63.second = f32[2,32,32,256]{3,2,1,0:T(8,128)} custom-call(s32[3]{0:T(128)} %pad_add_fusion.scalars, f32[7,40,40,256]{3,2,1,0:T(8,128)} %get-tuple-element.31.coef_in, f32[2,32,32,256]{3,2,1,0:T(8,128)} %get-tuple-element.44.tile, f32[2,4,32,256]{3,2,1,0:T(8,128)} %copy-done.6, f32[2,4,32,256]{3,2,1,0:T(8,128)} %copy-done.7, ...), custom_call_target="tpu_custom_call" | custom-call | flops 13799999488 | bytes 43200000 | tf_op jit(solution)/shard_map/pallas_call | solution.py:23
  215.2 4.1 %shard_map.64 = f32[8,128]{1,0:T(8,128)} custom-call(s32[3]{0:T(128)} %pad_add_fusion.scalars, f32[2,32,32,256]{3,2,1,0:T(8,128)} %get-tuple-element.38.tile.images.others.refs_0_, f32[2,32,32,256]{3,2,1,0:T(8,128)} %shard_map.63.second, f32[2,32,32,256]{3,2,1,0:T(8,128)} %get-tuple-element.38.tile.images.others.refs_0_), custom_call_target="tpu_custom_call" | custom-call | flops 4600000000 | bytes 14400000 | tf_op jit(solution)/shard_map/pallas_call | solution.py:23
  219.3 4.3 %shard_map.65 = f32[8,128]{1,0:T(8,128)} custom-call(s32[3]{0:T(128)} %pad_add_fusion.2.scalars, f32[2,32,32,256]{3,2,1,0:T(8,128)} %get-tuple-element.38.tile.images.others.refs_0_, f32[2,32,32,256]{3,2,1,0:T(8,128)} %shard_map.63.second, f32[2,32,32,256]{3,2,1,0:T(8,128)} %copy-done.1), custom_call_target="tpu_custom_call" | custom-call | flops 4600000000 | bytes 14400000 | tf_op jit(solution)/shard_map/pallas_call | solution.py:23
  223.6 0.7 add.79
  224.4 4.2 %shard_map.66 = f32[8,128]{1,0:T(8,128)} custom-call(s32[3]{0:T(128)} %pad_add_fusion.3.scalars, f32[2,32,32,256]{3,2,1,0:T(8,128)} %get-tuple-element.38.tile.images.others.refs_0_, f32[2,32,32,256]{3,2,1,0:T(8,128)} %shard_map.63.second, f32[2,32,32,256]{3,2,1,0:T(8,128)} %collective-permute-done.21.others.refs_2_), custom_call_target="tpu_custom_call" | custom-call | flops 4600000000 | bytes 14400000 | tf_op jit(solution)/shard_map/pallas_call | solution.py:23
  228.6 0.8 copy.17
  229.4 12.6 %collective-permute-done.22.others.refs_3_ = f32[2,32,32,256]{3,2,1,0:T(8,128)S(1)} collective-permute-done((f32[2,32,32,256]{3,2,1,0:T(8,128)}, f32[2,32,32,256]{3,2,1,0:T(8,128)S(1)}, u32[]{:S(2)}, u32[]{:S(2)}) %collective-permute-start.22) | collective-permute-done | bytes 2097184 | tf_op jit(solution)/shard_map/ppermute | solution.py:477
  242.0 1.3 copy-done.2
  243.3 4.2 %shard_map.67 = f32[8,128]{1,0:T(8,128)} custom-call(s32[3]{0:T(128)} %pad_add_fusion.4.scalars, f32[2,32,32,256]{3,2,1,0:T(8,128)} %get-tuple-element.38.tile.images.others.refs_0_, f32[2,32,32,256]{3,2,1,0:T(8,128)} %shard_map.63.second, f32[2,32,32,256]{3,2,1,0:T(8,128)} %copy-done.2), custom_call_target="tpu_custom_call" | custom-call | flops 4600000000 | bytes 14400000 | tf_op jit(solution)/shard_map/pallas_call | solution.py:23
  247.6 0.8 copy.18
  248.9 0.9 collective-permute-done.23
  249.8 3.2 %collective-permute-start.24 = (f32[8,128]{0,1:T(8,128)S(1)}, f32[8,128]{0,1:T(8,128)S(1)}, u32[]{:S(2)}, u32[]{:S(2)}) collective-permute-start(f32[8,128]{0,1:T(8,128)S(1)} %add.82), channel_id=1, source_target_pairs={{0,4},{2,6},{4,0},{6,2},{1,5},{3,7},{5,1},{7,3},{8,12},{10,14},{12... | collective-permute-start | bytes 12296 | tf_op jit(solution)/shard_map/ppermute | solution.py:409
  253.0 2.4 collective-permute-done.24
  255.4 0.9 collective-permute-start.25
  256.3 3.4 %collective-permute-done.25 = f32[8,128]{0,1:T(8,128)S(1)} collective-permute-done((f32[8,128]{0,1:T(8,128)S(1)}, f32[8,128]{0,1:T(8,128)S(1)}, u32[]{:S(2)}, u32[]{:S(2)}) %collective-permute-start.25) | collective-permute-done | bytes 4128 | tf_op jit(solution)/shard_map/ppermute | solution.py:409
  259.7 2.4 collective-permute-start.26
  262.2 2.2 collective-permute-done.26
  264.4 3.3 %collective-permute-start.27 = (f32[8,128]{0,1:T(8,128)S(1)}, f32[8,128]{0,1:T(8,128)S(1)}, u32[]{:S(2)}, u32[]{:S(2)}) collective-permute-start(f32[8,128]{0,1:T(8,128)S(1)} %add.85), channel_id=1, source_target_pairs={{0,16},{8,24},{16,0},{24,8},{1,17},{9,25},{17,1},{25,9},{2,18},{10... | collective-permute-start | bytes 12296 | tf_op jit(solution)/shard_map/ppermute | solution.py:409
  267.7 2.2 collective-permute-done.27
  270.3 0.7 cholesky.16
  271.1 0.6 compare_reduce_fusion
  271.7 0.6 fusion
  273.5 0.7 fusion.17
  274.9 6.1 %shard_map.68 = f32[2,32,32,256]{3,2,1,0:T(8,128)} custom-call(f32[2,8]{1,0:T(2,128)} %pad_maximum_fusion.inverse, f32[2,32,32,256]{3,2,1,0:T(8,128)} %get-tuple-element.38.tile.images.others.refs_0_, f32[2,32,32,256]{3,2,1,0:T(8,128)} %copy-done.1, f32[2,32,32,256]{3,2,1,0:T(8,128)} %collective-permute-done.21.others.refs_2_, f32[2,32,32,256]{3,2,1,0:T(8,128)} %copy-done.2), custom_call_target="tpu_custom_call" | custom-call | flops 6899999744 | bytes 21600000 | tf_op jit(solution)/shard_map/pallas_call | solution.py:23
  (81 shorter events, 7.8 us)
Async XLA Ops:
  5.4 27.9 %collective-permute-start = (f32[6,4,32,256]{3,2,1,0:T(8,128)}, f32[6,4,32,256]{3,2,1,0:T(8,128)S(1)}, u32[]{:S(2)}, u32[]{:S(2)}) collective-permute-start(f32[6,4,32,256]{3,2,1,0:T(8,128)} %get-tuple-element.26), channel_id=1, source_target_pairs={{0,2},{2,4},{4,6},{1,3},{3,5},{5,7},{8,10},{10,12},{12,14},{9,11},... | collective-permute-start | bytes 2359304 | tf_op jit(solution)/shard_map/ppermute | solution.py:100
  7.8 25.5 %collective-permute-start.1 = (f32[6,4,32,256]{3,2,1,0:T(8,128)}, f32[6,4,32,256]{3,2,1,0:T(8,128)S(1)}, u32[]{:S(2)}, u32[]{:S(2)}) collective-permute-start(f32[6,4,32,256]{3,2,1,0:T(8,128)} %get-tuple-element.27), channel_id=1, source_target_pairs={{2,0},{4,2},{6,4},{3,1},{5,3},{7,5},{10,8},{12,10},{14,12},{11,9},... | collective-permute-start | bytes 2359304 | tf_op jit(solution)/shard_map/ppermute | solution.py:101
  9.1 24.2 %collective-permute-start.2 = (f32[6,16,8,256]{3,2,1,0:T(8,128)}, f32[6,16,8,256]{3,2,1,0:T(8,128)S(1)}, u32[]{:S(2)}, u32[]{:S(2)}) collective-permute-start(f32[6,16,8,256]{3,2,1,0:T(8,128)} %get-tuple-element.28), channel_id=1, source_target_pairs={{0,1},{1,0},{2,3},{3,2},{4,5},{5,4},{6,7},{7,6},{8,9},{9,8},{10,11... | collective-permute-start | bytes 2359304 | tf_op jit(solution)/shard_map/ppermute | solution.py:98
  11.5 20.0 %collective-permute-start.3 = (f32[6,2,8,256]{3,2,1,0:T(8,128)}, f32[6,2,8,256]{3,2,1,0:T(8,128)S(1)}, u32[]{:S(2)}, u32[]{:S(2)}) collective-permute-start(f32[6,2,8,256]{3,2,1,0:T(8,128)} %get-tuple-element.29), channel_id=1, source_target_pairs={{0,3},{1,2},{2,5},{3,4},{4,7},{5,6},{8,11},{9,10},{10,13},{11,12},... | collective-permute-start | bytes 294920 | tf_op jit(solution)/shard_map/ppermute | solution.py:98
  15.6 17.7 %collective-permute-start.4 = (f32[6,2,8,256]{3,2,1,0:T(8,128)}, f32[6,2,8,256]{3,2,1,0:T(8,128)S(1)}, u32[]{:S(2)}, u32[]{:S(2)}) collective-permute-start(f32[6,2,8,256]{3,2,1,0:T(8,128)} %get-tuple-element.30), channel_id=1, source_target_pairs={{2,1},{3,0},{4,3},{5,2},{6,5},{7,4},{10,9},{11,8},{12,11},{13,10},... | collective-permute-start | bytes 294920 | tf_op jit(solution)/shard_map/ppermute | solution.py:98
  31.5 1.8 copy-start.15
  33.3 0.6 copy-start.16
  33.3 1.0 copy-start.3
  33.3 1.3 copy-start.4
  34.5 0.9 copy-start.5
  53.8 14.5 %collective-permute-start.5 = (f32[2,4,32,256]{3,2,1,0:T(8,128)}, f32[2,4,32,256]{3,2,1,0:T(8,128)S(1)}, u32[]{:S(2)}, u32[]{:S(2)}) collective-permute-start(f32[2,4,32,256]{3,2,1,0:T(8,128)} %get-tuple-element.33), channel_id=1, source_target_pairs={{0,2},{2,4},{4,6},{1,3},{3,5},{5,7},{8,10},{10,12},{12,14},{9,11},... | collective-permute-start | bytes 786440 | tf_op jit(solution)/shard_map/ppermute | solution.py:100
  55.5 12.8 %collective-permute-start.6 = (f32[2,4,32,256]{3,2,1,0:T(8,128)}, f32[2,4,32,256]{3,2,1,0:T(8,128)S(1)}, u32[]{:S(2)}, u32[]{:S(2)}) collective-permute-start(f32[2,4,32,256]{3,2,1,0:T(8,128)} %get-tuple-element.34), channel_id=1, source_target_pairs={{2,0},{4,2},{6,4},{3,1},{5,3},{7,5},{10,8},{12,10},{14,12},{11,9},... | collective-permute-start | bytes 786440 | tf_op jit(solution)/shard_map/ppermute | solution.py:101
  56.8 11.5 %collective-permute-start.7 = (f32[2,16,8,256]{3,2,1,0:T(8,128)}, f32[2,16,8,256]{3,2,1,0:T(8,128)S(1)}, u32[]{:S(2)}, u32[]{:S(2)}) collective-permute-start(f32[2,16,8,256]{3,2,1,0:T(8,128)} %get-tuple-element.35), channel_id=1, source_target_pairs={{0,1},{1,0},{2,3},{3,2},{4,5},{5,4},{6,7},{7,6},{8,9},{9,8},{10,11... | collective-permute-start | bytes 786440 | tf_op jit(solution)/shard_map/ppermute | solution.py:98
  58.5 7.4 %collective-permute-start.8 = (f32[2,2,8,256]{3,2,1,0:T(8,128)}, f32[2,2,8,256]{3,2,1,0:T(8,128)S(1)}, u32[]{:S(2)}, u32[]{:S(2)}) collective-permute-start(f32[2,2,8,256]{3,2,1,0:T(8,128)} %get-tuple-element.36), channel_id=1, source_target_pairs={{0,3},{1,2},{2,5},{3,4},{4,7},{5,6},{8,11},{9,10},{10,13},{11,12},... | collective-permute-start | bytes 98312 | tf_op jit(solution)/shard_map/ppermute | solution.py:98
  62.6 5.7 %collective-permute-start.9 = (f32[2,2,8,256]{3,2,1,0:T(8,128)}, f32[2,2,8,256]{3,2,1,0:T(8,128)S(1)}, u32[]{:S(2)}, u32[]{:S(2)}) collective-permute-start(f32[2,2,8,256]{3,2,1,0:T(8,128)} %get-tuple-element.37), channel_id=1, source_target_pairs={{2,1},{3,0},{4,3},{5,2},{6,5},{7,4},{10,9},{11,8},{12,11},{13,10},... | collective-permute-start | bytes 98312 | tf_op jit(solution)/shard_map/ppermute | solution.py:98
  65.9 2.4 copy-start.19
  68.3 0.6 copy-start.20
  68.3 0.7 copy-start.10
  68.3 0.8 copy-start.12
  68.3 0.9 copy-start.14
  86.8 48.2 %collective-permute-start.20 = (f32[2,32,32,256]{3,2,1,0:T(8,128)}, f32[2,32,32,256]{3,2,1,0:T(8,128)S(1)}, u32[]{:S(2)}, u32[]{:S(2)}) collective-permute-start(f32[2,32,32,256]{3,2,1,0:T(8,128)} %get-tuple-element.38.tile.images.others.refs_0_), channel_id=1, source_target_pairs={{0,8},{8,16},{16,24},{1,9},{9,17},{17,25},{2,10},{10,18},{18,26},{... | collective-permute-start | bytes 6291464 | tf_op jit(solution)/shard_map/ppermute | solution.py:477
  135.0 42.8 %copy-start.1 = (f32[2,32,32,256]{3,2,1,0:T(8,128)}, f32[2,32,32,256]{3,2,1,0:T(8,128)S(1)}, u32[]{:S(2)}) copy-start(f32[2,32,32,256]{3,2,1,0:T(8,128)S(1)} %collective-permute-done.20.others.refs_1_) | copy-start | bytes 6291460
  135.0 58.4 %collective-permute-start.21 = (f32[2,32,32,256]{3,2,1,0:T(8,128)S(1)}, f32[2,32,32,256]{3,2,1,0:T(8,128)}, u32[]{:S(2)}, u32[]{:S(2)}) collective-permute-start(f32[2,32,32,256]{3,2,1,0:T(8,128)S(1)} %collective-permute-done.20.others.refs_1_), channel_id=1, source_target_pairs={{0,8},{8,16},{16,24},{1,9},{9,17},{17,25},{2,10},{10,18},{18,26},{... | collective-permute-start | bytes 6291464 | tf_op jit(solution)/shard_map/ppermute | solution.py:477
  140.6 18.5 %collective-permute-start.10 = (f32[2,4,32,256]{3,2,1,0:T(8,128)}, f32[2,4,32,256]{3,2,1,0:T(8,128)S(1)}, u32[]{:S(2)}, u32[]{:S(2)}) collective-permute-start(f32[2,4,32,256]{3,2,1,0:T(8,128)} %get-tuple-element.39), channel_id=1, source_target_pairs={{0,2},{2,4},{4,6},{1,3},{3,5},{5,7},{8,10},{10,12},{12,14},{9,11},... | collective-permute-start | bytes 786440 | tf_op jit(solution)/shard_map/ppermute | solution.py:100
  143.7 15.5 %collective-permute-start.11 = (f32[2,4,32,256]{3,2,1,0:T(8,128)}, f32[2,4,32,256]{3,2,1,0:T(8,128)S(1)}, u32[]{:S(2)}, u32[]{:S(2)}) collective-permute-start(f32[2,4,32,256]{3,2,1,0:T(8,128)} %get-tuple-element.40), channel_id=1, source_target_pairs={{2,0},{4,2},{6,4},{3,1},{5,3},{7,5},{10,8},{12,10},{14,12},{11,9},... | collective-permute-start | bytes 786440 | tf_op jit(solution)/shard_map/ppermute | solution.py:101
  145.0 14.2 %collective-permute-start.12 = (f32[2,16,8,256]{3,2,1,0:T(8,128)}, f32[2,16,8,256]{3,2,1,0:T(8,128)S(1)}, u32[]{:S(2)}, u32[]{:S(2)}) collective-permute-start(f32[2,16,8,256]{3,2,1,0:T(8,128)} %get-tuple-element.41), channel_id=1, source_target_pairs={{0,1},{1,0},{2,3},{3,2},{4,5},{5,4},{6,7},{7,6},{8,9},{9,8},{10,11... | collective-permute-start | bytes 786440 | tf_op jit(solution)/shard_map/ppermute | solution.py:98
  146.6 7.1 %collective-permute-start.13 = (f32[2,2,8,256]{3,2,1,0:T(8,128)}, f32[2,2,8,256]{3,2,1,0:T(8,128)S(1)}, u32[]{:S(2)}, u32[]{:S(2)}) collective-permute-start(f32[2,2,8,256]{3,2,1,0:T(8,128)} %get-tuple-element.42), channel_id=1, source_target_pairs={{0,3},{1,2},{2,5},{3,4},{4,7},{5,6},{8,11},{9,10},{10,13},{11,12},... | collective-permute-start | bytes 98312 | tf_op jit(solution)/shard_map/ppermute | solution.py:98
  153.6 5.5 %copy-start.18 = (f32[2,2,8,256]{3,2,1,0:T(8,128)}, f32[2,2,8,256]{3,2,1,0:T(8,128)S(1)}, u32[]{:S(2)}) copy-start(f32[2,2,8,256]{3,2,1,0:T(8,128)S(1)} %collective-permute-done.13.refs_4_) | copy-start | bytes 98308
  153.6 5.5 %collective-permute-start.14 = (f32[2,2,8,256]{3,2,1,0:T(8,128)}, f32[2,2,8,256]{3,2,1,0:T(8,128)S(1)}, u32[]{:S(2)}, u32[]{:S(2)}) collective-permute-start(f32[2,2,8,256]{3,2,1,0:T(8,128)} %get-tuple-element.43), channel_id=1, source_target_pairs={{2,1},{3,0},{4,3},{5,2},{6,5},{7,4},{10,9},{11,8},{12,11},{13,10},... | collective-permute-start | bytes 98312 | tf_op jit(solution)/shard_map/ppermute | solution.py:98
  159.1 0.6 copy-start.22
  159.1 0.7 copy-start.9
  159.2 0.8 copy-start.11
  160.0 0.7 copy-start.13
  177.9 19.2 %collective-permute-start.15 = (f32[2,4,32,256]{3,2,1,0:T(8,128)}, f32[2,4,32,256]{3,2,1,0:T(8,128)S(1)}, u32[]{:S(2)}, u32[]{:S(2)}) collective-permute-start(f32[2,4,32,256]{3,2,1,0:T(8,128)} %get-tuple-element.45), channel_id=1, source_target_pairs={{0,2},{2,4},{4,6},{1,3},{3,5},{5,7},{8,10},{10,12},{12,14},{9,11},... | collective-permute-start | bytes 786440 | tf_op jit(solution)/shard_map/ppermute | solution.py:100
  181.3 15.8 %collective-permute-start.16 = (f32[2,4,32,256]{3,2,1,0:T(8,128)}, f32[2,4,32,256]{3,2,1,0:T(8,128)S(1)}, u32[]{:S(2)}, u32[]{:S(2)}) collective-permute-start(f32[2,4,32,256]{3,2,1,0:T(8,128)} %get-tuple-element.46), channel_id=1, source_target_pairs={{2,0},{4,2},{6,4},{3,1},{5,3},{7,5},{10,8},{12,10},{14,12},{11,9},... | collective-permute-start | bytes 786440 | tf_op jit(solution)/shard_map/ppermute | solution.py:101
  182.6 14.5 %collective-permute-start.17 = (f32[2,16,8,256]{3,2,1,0:T(8,128)}, f32[2,16,8,256]{3,2,1,0:T(8,128)S(1)}, u32[]{:S(2)}, u32[]{:S(2)}) collective-permute-start(f32[2,16,8,256]{3,2,1,0:T(8,128)} %get-tuple-element.47), channel_id=1, source_target_pairs={{0,1},{1,0},{2,3},{3,2},{4,5},{5,4},{6,7},{7,6},{8,9},{9,8},{10,11... | collective-permute-start | bytes 786440 | tf_op jit(solution)/shard_map/ppermute | solution.py:98
  184.8 6.7 %collective-permute-start.18 = (f32[2,2,8,256]{3,2,1,0:T(8,128)}, f32[2,2,8,256]{3,2,1,0:T(8,128)S(1)}, u32[]{:S(2)}, u32[]{:S(2)}) collective-permute-start(f32[2,2,8,256]{3,2,1,0:T(8,128)} %get-tuple-element.48), channel_id=1, source_target_pairs={{0,3},{1,2},{2,5},{3,4},{4,7},{5,6},{8,11},{9,10},{10,13},{11,12},... | collective-permute-start | bytes 98312 | tf_op jit(solution)/shard_map/ppermute | solution.py:98
  191.6 5.5 %copy-start.17 = (f32[2,2,8,256]{3,2,1,0:T(8,128)}, f32[2,2,8,256]{3,2,1,0:T(8,128)S(1)}, u32[]{:S(2)}) copy-start(f32[2,2,8,256]{3,2,1,0:T(8,128)S(1)} %collective-permute-done.18.refs_3_) | copy-start | bytes 98308
  191.6 5.5 %collective-permute-start.19 = (f32[2,2,8,256]{3,2,1,0:T(8,128)}, f32[2,2,8,256]{3,2,1,0:T(8,128)S(1)}, u32[]{:S(2)}, u32[]{:S(2)}) collective-permute-start(f32[2,2,8,256]{3,2,1,0:T(8,128)} %get-tuple-element.49), channel_id=1, source_target_pairs={{2,1},{3,0},{4,3},{5,2},{6,5},{7,4},{10,9},{11,8},{12,11},{13,10},... | collective-permute-start | bytes 98312 | tf_op jit(solution)/shard_map/ppermute | solution.py:98
  193.4 48.6 %collective-permute-start.22 = (f32[2,32,32,256]{3,2,1,0:T(8,128)}, f32[2,32,32,256]{3,2,1,0:T(8,128)S(1)}, u32[]{:S(2)}, u32[]{:S(2)}) collective-permute-start(f32[2,32,32,256]{3,2,1,0:T(8,128)} %collective-permute-done.21.others.refs_2_), channel_id=1, source_target_pairs={{0,8},{8,16},{16,24},{1,9},{9,17},{17,25},{2,10},{10,18},{18,26},{... | collective-permute-start | bytes 6291464 | tf_op jit(solution)/shard_map/ppermute | solution.py:477
  197.1 0.6 copy-start.21
  197.1 0.7 copy-start.6
  197.1 0.8 copy-start.7
  197.1 0.9 copy-start.8
  219.3 4.3 %copy-start = (f32[8,128]{1,0:T(8,128)S(1)}, f32[8,128]{1,0:T(8,128)}, u32[]{:S(2)}) copy-start(f32[8,128]{1,0:T(8,128)} %shard_map.64) | copy-start | bytes 12292
  242.0 1.3 copy-start.2
  248.4 1.4 collective-permute-start.23
  249.8 5.6 %collective-permute-start.24 = (f32[8,128]{0,1:T(8,128)S(1)}, f32[8,128]{0,1:T(8,128)S(1)}, u32[]{:S(2)}, u32[]{:S(2)}) collective-permute-start(f32[8,128]{0,1:T(8,128)S(1)} %add.82), channel_id=1, source_target_pairs={{0,4},{2,6},{4,0},{6,2},{1,5},{3,7},{5,1},{7,3},{8,12},{10,14},{12... | collective-permute-start | bytes 12296 | tf_op jit(solution)/shard_map/ppermute | solution.py:409
  255.4 4.3 %collective-permute-start.25 = (f32[8,128]{0,1:T(8,128)S(1)}, f32[8,128]{0,1:T(8,128)S(1)}, u32[]{:S(2)}, u32[]{:S(2)}) collective-permute-start(f32[8,128]{0,1:T(8,128)S(1)} %add.83), channel_id=1, source_target_pairs={{0,1},{1,0},{2,3},{3,2},{4,5},{5,4},{6,7},{7,6},{8,9},{9,8},{10,11... | collective-permute-start | bytes 12296 | tf_op jit(solution)/shard_map/ppermute | solution.py:409
  259.7 4.7 %collective-permute-start.26 = (f32[8,128]{0,1:T(8,128)S(1)}, f32[8,128]{0,1:T(8,128)S(1)}, u32[]{:S(2)}, u32[]{:S(2)}) collective-permute-start(f32[8,128]{0,1:T(8,128)S(1)} %add.84), channel_id=1, source_target_pairs={{0,8},{8,0},{16,24},{24,16},{1,9},{9,1},{17,25},{25,17},{2,10},{10... | collective-permute-start | bytes 12296 | tf_op jit(solution)/shard_map/ppermute | solution.py:409
  264.4 5.5 %collective-permute-start.27 = (f32[8,128]{0,1:T(8,128)S(1)}, f32[8,128]{0,1:T(8,128)S(1)}, u32[]{:S(2)}, u32[]{:S(2)}) collective-permute-start(f32[8,128]{0,1:T(8,128)S(1)} %add.85), channel_id=1, source_target_pairs={{0,16},{8,24},{16,0},{24,8},{1,17},{9,25},{17,1},{25,9},{2,18},{10... | collective-permute-start | bytes 12296 | tf_op jit(solution)/shard_map/ppermute | solution.py:409
where the time goes:
time: 282 us; the launch traced here: 281 us
  waiting for transfers between devices  100 us (35%)
  Pallas kernels  97.5 us (35%)
  starting transfers between devices  65.5 us (23%)
  local copies, waits for them, and re-layouts  8.7 us (3%)
  other arithmetic  6.69 us (2%)
    pallas_call x10, Pallas kernels, kernel_call(): pl.pallas_call(body, out_shape=outs, in_specs=specs, out_specs=[spec(n, o...  97.5 us
    ppermute x3, waiting for transfers between devices, shards(): passed.append(lax.ppermute(passed[-1], 'probe', right))  57.1 us
    ppermute x12, waiting for transfers between devices, moved(): return lax.ppermute(value, ('sx', 'sy'), pairs)  32.1 us
    ppermute x12, starting transfers between devices, moved(): return lax.ppermute(value, ('sx', 'sy'), pairs)  27.5 us
    ppermute x3, starting transfers between devices, shards(): passed.append(lax.ppermute(passed[-1], 'probe', right))  11.9 us
    ppermute x5, waiting for transfers between devices, all_sum(): lax.ppermute(value, axis, [(i, i ^ bit) for i in range(devices)])  11.2 us
    ppermute x4, starting transfers between devices, exchange(): below = lax.ppermute(strips[1], 'sx', up)  10.6 us
    ppermute x5, starting transfers between devices, all_sum(): lax.ppermute(value, axis, [(i, i ^ bit) for i in range(devices)])  10.3 us
  transfers between devices with their start and end apart: 28, of which 15 were waited for; matrix products, arithmetic and copies ran while one was open for 1% of the time, Pallas kernels for 17%

commit v1 on v0

--- a/solution.py
+++ b/solution.py
@@ -404,10 +404,15 @@
         if devices & (devices - 1):
             value = lax.psum(value, axis)
             continue
+        move = lambda bits: lax.ppermute(value, axis, [(i, i ^ bits) for i in range(devices)])
         bit = 1
         while bit < devices:
-            value = value + lax.ppermute(value, axis, [(i, i ^ bit) for i in range(devices)])
-            bit *= 2
+            if 4 * bit <= devices:
+                value = (value + move(bit)) + (move(2 * bit) + move(3 * bit))
+                bit *= 4
+            else:
+                value = value + move(bit)
+                bit *= 2
     return value
 
 
@@ -438,14 +443,23 @@
         ]
 
     packs = 2 if both else 1
-    strips = kernel_call(
-        functools.partial(pack_kernel, len(fields)),
-        strip_shapes(total, x, y, z, both),
-        [pltpu.VMEM((packs, total, x, SUB, z), jnp.float32), pltpu.SemaphoreType.DMA((total * (packs + 2),))],
-        [where] + fields,
-        3.0,
-        anywhere=(1, 2, 3),
-    )
+
+    def pack(sources):
+        number = sum(a.shape[0] for a in sources)
+        return kernel_call(
+            functools.partial(pack_kernel, len(sources)),
+            strip_shapes(number, x, y, z, both),
+            [pltpu.VMEM((packs, number, x, SUB, z), jnp.float32), pltpu.SemaphoreType.DMA((number * (packs + 2),))],
+            [where] + sources,
+            3.0,
+            anywhere=range(1, len(sources) + 1),
+        )
+
+    def right(value, hops):
+        return lax.ppermute(value, "probe", [(i, i + hops) for i in range(groups - hops)])
+
+    next_probes = right(probes, 1)
+    strips = pack(fields)
     received = exchange(strips)
     coef, halfway, *strips = kernel_call(
         functools.partial(first_kernel, len(received)),
@@ -470,13 +484,13 @@
         )
 
     images, *strips = model(halfway, strips, True)
-
-    right = [(i, i + 1) for i in range(groups - 1)]
-    passed = [images]
-    for _ in range(groups - 1):
-        passed.append(lax.ppermute(passed[-1], "probe", right))
-
+    far = [right(images, hops) for hops in range(3, groups)]
+
+    half_next, *strips_next = model(next_probes, pack([next_probes]), False)
     halfway, *strips = model(images, strips, False)
+    (images_next,) = model(half_next, strips_next, True, True)
+    images_next, far = lax.optimization_barrier((images_next, far))
+    passed = [images, images_next, right(images_next, 1)] + far
     (second,) = model(halfway, strips, True, True)
 
     partial = None

time: 282 us -> 286 us (1.014)
  waiting for transfers between devices: 100 us -> 41.6 us
  Pallas kernels: 97.5 us -> 135 us
  starting transfers between devices: 65.5 us -> 93.6 us
    ppermute x8 -> x10, waiting for transfers between devices: 68.3 us -> 23.1 us  [the longest x7 11.6 us: all_sum(): lax.ppermute(value, axis, [(i, i ^ bits) for i in range(devices)])]
    pallas_call x10 -> x13, Pallas kernels: 97.5 us -> 135 us  [kernel_call(): pl.pallas_call(body, out_shape=outs, in_specs=specs, out_specs=[spec(n, o...]
    ppermute x12 -> x18, starting transfers between devices: 27.5 us -> 42.8 us  [moved(): return lax.ppermute(value, ('sx', 'sy'), pairs)]
    ppermute x12 -> x18, waiting for transfers between devices: 32.1 us -> 18.4 us  [moved(): return lax.ppermute(value, ('sx', 'sy'), pairs)]
    ppermute x4 -> x6, starting transfers between devices: 10.6 us -> 22.1 us  [exchange(): below = lax.ppermute(strips[1], 'sx', up)]
    ppermute x4 -> x6, starting transfers between devices: 5.17 us -> 7.75 us  [exchange(): above = lax.ppermute(strips[0], 'sx', down)]
    unnamed x46 -> x72, local copies, waits for them, and re-layouts: 6.69 us -> 4.15 us
    ppermute x8 -> x10, starting transfers between devices: 22.2 us -> 21 us  [the longest x3 10.8 us: right(): lax.ppermute(value, 'probe', [(i, i + hops) for i in range(groups - hops)])]
  transfers between devices with their start and end apart: 28 -> 40, of which waited for: 15 -> 8; matrix products, arithmetic and copies ran while one was open for 1% -> 1% of each run, Pallas kernels for 17% -> 42%
where the time goes in v1:
time: 286 us; the launch traced here: 285 us
  Pallas kernels  135 us (47%)
  starting transfers between devices  93.6 us (33%)
  waiting for transfers between devices  41.6 us (15%)
  local copies, waits for them, and re-layouts  6.21 us (2%)
  other arithmetic  6.12 us (2%)
    pallas_call x13, Pallas kernels, kernel_call(): pl.pallas_call(body, out_shape=outs, in_specs=specs, out_specs=[spec(n, o...  135 us
    ppermute x18, starting transfers between devices, moved(): return lax.ppermute(value, ('sx', 'sy'), pairs)  42.8 us
    ppermute x6, starting transfers between devices, exchange(): below = lax.ppermute(strips[1], 'sx', up)  22.1 us
    ppermute x18, waiting for transfers between devices, moved(): return lax.ppermute(value, ('sx', 'sy'), pairs)  18.4 us
    ppermute x7, waiting for transfers between devices, all_sum(): lax.ppermute(value, axis, [(i, i ^ bits) for i in range(devices)])  11.6 us
    ppermute x3, waiting for transfers between devices, right(): lax.ppermute(value, 'probe', [(i, i + hops) for i in range(groups - hops)])  11.5 us
    ppermute x3, starting transfers between devices, right(): lax.ppermute(value, 'probe', [(i, i + hops) for i in range(groups - hops)])  10.8 us
    ppermute x7, starting transfers between devices, all_sum(): lax.ppermute(value, axis, [(i, i ^ bits) for i in range(devices)])  10.2 us
  transfers between devices with their start and end apart: 40, of which 8 were waited for; matrix products, arithmetic and copies ran while one was open for 1% of the time, Pallas kernels for 42%

profile of v1, /device:TPU:0, one launch (start us, length us, event | category | flops | bytes accessed | tf_op | source)
XLA Modules:
  0.0 285.0 jit_solution(289929731078353633)
XLA Ops:
  1.2 4.3 %shard_map.59 = (f32[6,4,32,256]{3,2,1,0:T(8,128)}, f32[6,4,32,256]{3,2,1,0:T(8,128)}, f32[6,16,8,256]{3,2,1,0:T(8,128)}, f32[6,2,8,256]{3,2,1,0:T(8,128)}, f32[6,2,8,256]{3,2,1,0:T(8,128)}) custom-call(s32[3]{0:T(128)} %pad_add_fusion.scalars, f32[1,32,32,256]{3,2,1,0:T(8,128)} %bitcast.28, f32[3,32,32,256]{3,2,1,0:T(8,128)} %velocity.1, ...), custom_call_target="tpu_custom_call" | custom-call | flops 3449999872 | bytes 10800000 | tf_op jit(solution)/shard_map/pallas_call | solution.py:23
  5.5 2.4 collective-permute-start
  7.9 1.3 collective-permute-start.1
  9.2 2.5 collective-permute-start.2
  11.7 3.6 %collective-permute-start.20 = (f32[2,32,32,256]{3,2,1,0:T(8,128)S(1)}, f32[2,32,32,256]{3,2,1,0:T(8,128)S(1)}, u32[]{:S(2)}, u32[]{:S(2)}) collective-permute-start(f32[2,32,32,256]{3,2,1,0:T(8,128)S(1)} %copy-done.1), channel_id=1, source_target_pairs={{0,8},{8,16},{16,24},{1,9},{9,17},{17,25},{2,10},{10,18},{18,26},{... | collective-permute-start | bytes 6291464 | tf_op jit(solution)/shard_map/ppermute | solution.py:459
  15.3 3.8 %collective-permute-start.3 = (f32[6,2,8,256]{3,2,1,0:T(8,128)}, f32[6,2,8,256]{3,2,1,0:T(8,128)S(1)}, u32[]{:S(2)}, u32[]{:S(2)}) collective-permute-start(f32[6,2,8,256]{3,2,1,0:T(8,128)} %get-tuple-element.42), channel_id=1, source_target_pairs={{0,3},{1,2},{2,5},{3,4},{4,7},{5,6},{8,11},{9,10},{10,13},{11,12},... | collective-permute-start | bytes 294920 | tf_op jit(solution)/shard_map/ppermute | solution.py:98
  19.1 11.5 %collective-permute-done.3.refs_3_ = f32[6,2,8,256]{3,2,1,0:T(8,128)S(1)} collective-permute-done((f32[6,2,8,256]{3,2,1,0:T(8,128)}, f32[6,2,8,256]{3,2,1,0:T(8,128)S(1)}, u32[]{:S(2)}, u32[]{:S(2)}) %collective-permute-start.3) | collective-permute-done | bytes 98336 | tf_op jit(solution)/shard_map/ppermute | solution.py:98
  30.6 1.3 collective-permute-start.4
  31.9 4.9 %collective-permute-done.4.refs_4_ = f32[6,2,8,256]{3,2,1,0:T(8,128)S(1)} collective-permute-done((f32[6,2,8,256]{3,2,1,0:T(8,128)}, f32[6,2,8,256]{3,2,1,0:T(8,128)S(1)}, u32[]{:S(2)}, u32[]{:S(2)}) %collective-permute-start.4) | collective-permute-done | bytes 98336 | tf_op jit(solution)/shard_map/ppermute | solution.py:98
  38.0 18.4 %shard_map.60 = (f32[7,40,40,256]{3,2,1,0:T(8,128)}, f32[2,32,32,256]{3,2,1,0:T(8,128)}, f32[2,4,32,256]{3,2,1,0:T(8,128)}, f32[2,4,32,256]{3,2,1,0:T(8,128)}, f...) custom-call(s32[3]{0:T(128)} %pad_add_fusion.scalars, f32[1,32,32,256]{3,2,1,0:T(8,128)} %bitcast.29, ...), custom_call_target="tpu_custom_call" | custom-call | flops 16099999744 | bytes 50400000 | tf_op jit(solution)/shard_map/pallas_call | solution.py:23
  56.4 4.5 %collective-permute-start.8 = (f32[2,2,8,256]{3,2,1,0:T(8,128)}, f32[2,2,8,256]{3,2,1,0:T(8,128)S(1)}, u32[]{:S(2)}, u32[]{:S(2)}) collective-permute-start(f32[2,2,8,256]{3,2,1,0:T(8,128)} %get-tuple-element.49), channel_id=1, source_target_pairs={{0,3},{1,2},{2,5},{3,4},{4,7},{5,6},{8,11},{9,10},{10,13},{11,12},... | collective-permute-start | bytes 98312 | tf_op jit(solution)/shard_map/ppermute | solution.py:98
  60.9 1.3 collective-permute-start.9
  62.2 3.1 %collective-permute-start.5 = (f32[2,4,32,256]{3,2,1,0:T(8,128)}, f32[2,4,32,256]{3,2,1,0:T(8,128)S(1)}, u32[]{:S(2)}, u32[]{:S(2)}) collective-permute-start(f32[2,4,32,256]{3,2,1,0:T(8,128)} %get-tuple-element.46), channel_id=1, source_target_pairs={{0,2},{2,4},{4,6},{1,3},{3,5},{5,7},{8,10},{10,12},{12,14},{9,11},... | collective-permute-start | bytes 786440 | tf_op jit(solution)/shard_map/ppermute | solution.py:100
  65.3 1.3 collective-permute-start.6
  66.7 1.6 collective-permute-start.7
  68.3 2.8 shard_map.65
  71.1 4.9 %collective-permute-start.21 = (f32[2,4,32,256]{3,2,1,0:T(8,128)}, f32[2,4,32,256]{3,2,1,0:T(8,128)S(1)}, u32[]{:S(2)}, u32[]{:S(2)}) collective-permute-start(f32[2,4,32,256]{3,2,1,0:T(8,128)} %get-tuple-element.63), channel_id=1, source_target_pairs={{0,2},{2,4},{4,6},{1,3},{3,5},{5,7},{8,10},{10,12},{12,14},{9,11},... | collective-permute-start | bytes 786440 | tf_op jit(solution)/shard_map/ppermute | solution.py:100
  76.1 1.3 collective-permute-start.22
  78.8 17.6 %shard_map.61 = (f32[2,32,32,256]{3,2,1,0:T(8,128)}, f32[2,4,32,256]{3,2,1,0:T(8,128)}, f32[2,4,32,256]{3,2,1,0:T(8,128)}, f32[2,16,8,256]{3,2,1,0:T(8,128)}, f3...) custom-call(s32[3]{0:T(128)} %pad_add_fusion.scalars, f32[7,40,40,256]{3,2,1,0:T(8,128)} %get-tuple-element.44.coef_in, ...), custom_call_target="tpu_custom_call" | custom-call | flops 13799999488 | bytes 43200000 | tf_op jit(solution)/shard_map/pallas_call | solution.py:23
  96.4 5.1 %collective-permute-start.13 = (f32[2,2,8,256]{3,2,1,0:T(8,128)}, f32[2,2,8,256]{3,2,1,0:T(8,128)S(1)}, u32[]{:S(2)}, u32[]{:S(2)}) collective-permute-start(f32[2,2,8,256]{3,2,1,0:T(8,128)} %get-tuple-element.55), channel_id=1, source_target_pairs={{0,3},{1,2},{2,5},{3,4},{4,7},{5,6},{8,11},{9,10},{10,13},{11,12},... | collective-permute-start | bytes 98312 | tf_op jit(solution)/shard_map/ppermute | solution.py:98
  101.5 4.2 %collective-permute-start.24 = (f32[2,2,8,256]{3,2,1,0:T(8,128)S(1)}, f32[2,2,8,256]{3,2,1,0:T(8,128)S(1)}, u32[]{:S(2)}, u32[]{:S(2)}) collective-permute-start(f32[2,2,8,256]{3,2,1,0:T(8,128)S(1)} %copy-done.29), channel_id=1, source_target_pairs={{0,3},{1,2},{2,5},{3,4},{4,7},{5,6},{8,11},{9,10},{10,13},{11,12},... | collective-permute-start | bytes 98312 | tf_op jit(solution)/shard_map/ppermute | solution.py:98
  105.7 1.3 collective-permute-start.25
  107.7 1.3 collective-permute-start.14
  109.0 2.0 collective-permute-done.25.refs_5_
  111.0 2.6 collective-permute-start.10
  113.5 1.3 collective-permute-start.11
  114.9 0.9 collective-permute-start.12
  115.7 5.6 %collective-permute-start.31 = (f32[2,32,32,256]{3,2,1,0:T(8,128)}, f32[2,32,32,256]{3,2,1,0:T(8,128)S(1)}, u32[]{:S(2)}, u32[]{:S(2)}) collective-permute-start(f32[2,32,32,256]{3,2,1,0:T(8,128)} %get-tuple-element.51.tile.images.others.refs_0_), channel_id=1, source_target_pairs={{0,24},{1,25},{2,26},{3,27},{4,28},{5,29},{6,30},{7,31}} | collective-permute-start | bytes 6291464 | tf_op jit(solution)/shard_map/ppermute | solution.py:459
  121.4 17.2 %shard_map.66 = (f32[2,32,32,256]{3,2,1,0:T(8,128)}, f32[2,4,32,256]{3,2,1,0:T(8,128)}, f32[2,4,32,256]{3,2,1,0:T(8,128)}, f32[2,16,8,256]{3,2,1,0:T(8,128)}, f3...) custom-call(s32[3]{0:T(128)} %pad_add_fusion.scalars, f32[7,40,40,256]{3,2,1,0:T(8,128)} %get-tuple-element.44.coef_in, ...), custom_call_target="tpu_custom_call" | custom-call | flops 13799999488 | bytes 43200000 | tf_op jit(solution)/shard_map/pallas_call | solution.py:23
  138.6 4.8 %collective-permute-start.29 = (f32[2,2,8,256]{3,2,1,0:T(8,128)}, f32[2,2,8,256]{3,2,1,0:T(8,128)S(1)}, u32[]{:S(2)}, u32[]{:S(2)}) collective-permute-start(f32[2,2,8,256]{3,2,1,0:T(8,128)} %get-tuple-element.72), channel_id=1, source_target_pairs={{0,3},{1,2},{2,5},{3,4},{4,7},{5,6},{8,11},{9,10},{10,13},{11,12},... | collective-permute-start | bytes 98312 | tf_op jit(solution)/shard_map/ppermute | solution.py:98
  144.0 1.3 collective-permute-start.30
  145.3 4.7 %collective-permute-start.26 = (f32[2,4,32,256]{3,2,1,0:T(8,128)}, f32[2,4,32,256]{3,2,1,0:T(8,128)S(1)}, u32[]{:S(2)}, u32[]{:S(2)}) collective-permute-start(f32[2,4,32,256]{3,2,1,0:T(8,128)} %get-tuple-element.69), channel_id=1, source_target_pairs={{0,2},{2,4},{4,6},{1,3},{3,5},{5,7},{8,10},{10,12},{12,14},{9,11},... | collective-permute-start | bytes 786440 | tf_op jit(solution)/shard_map/ppermute | solution.py:100
  150.0 1.3 collective-permute-start.27
  151.3 1.3 collective-permute-start.28
  152.6 17.2 %shard_map.62 = (f32[2,32,32,256]{3,2,1,0:T(8,128)}, f32[2,4,32,256]{3,2,1,0:T(8,128)}, f32[2,4,32,256]{3,2,1,0:T(8,128)}, f32[2,16,8,256]{3,2,1,0:T(8,128)}, f3...) custom-call(s32[3]{0:T(128)} %pad_add_fusion.scalars, f32[7,40,40,256]{3,2,1,0:T(8,128)} %get-tuple-element.44.coef_in, ...), custom_call_target="tpu_custom_call" | custom-call | flops 13799999488 | bytes 43200000 | tf_op jit(solution)/shard_map/pallas_call | solution.py:23
  169.8 5.0 %collective-permute-start.18 = (f32[2,2,8,256]{3,2,1,0:T(8,128)}, f32[2,2,8,256]{3,2,1,0:T(8,128)S(1)}, u32[]{:S(2)}, u32[]{:S(2)}) collective-permute-start(f32[2,2,8,256]{3,2,1,0:T(8,128)} %get-tuple-element.61), channel_id=1, source_target_pairs={{0,3},{1,2},{2,5},{3,4},{4,7},{5,6},{8,11},{9,10},{10,13},{11,12},... | collective-permute-start | bytes 98312 | tf_op jit(solution)/shard_map/ppermute | solution.py:98
  174.9 1.3 collective-permute-start.19
  176.2 4.4 %collective-permute-start.15 = (f32[2,4,32,256]{3,2,1,0:T(8,128)}, f32[2,4,32,256]{3,2,1,0:T(8,128)S(1)}, u32[]{:S(2)}, u32[]{:S(2)}) collective-permute-start(f32[2,4,32,256]{3,2,1,0:T(8,128)} %get-tuple-element.58), channel_id=1, source_target_pairs={{0,2},{2,4},{4,6},{1,3},{3,5},{5,7},{8,10},{10,12},{12,14},{9,11},... | collective-permute-start | bytes 786440 | tf_op jit(solution)/shard_map/ppermute | solution.py:100
  180.6 1.3 collective-permute-start.16
  181.9 0.9 collective-permute-start.17
  182.8 17.2 %shard_map.67.others.refs_1_ = f32[2,32,32,256]{3,2,1,0:T(8,128)} custom-call(s32[3]{0:T(128)} %pad_add_fusion.scalars, f32[7,40,40,256]{3,2,1,0:T(8,128)} %get-tuple-element.44.coef_in, f32[2,32,32,256]{3,2,1,0:T(8,128)} %get-tuple-element.68.tile, f32[2,4,32,256]{3,2,1,0:T(8,128)} %copy-done.13, f32[2,4,32,256]{3,2,1,0:T(8,128)} %copy-done.14, ...), custom_call_target="tpu_custom_call" | custom-call | flops 13799999488 | bytes 43200000 | tf_op jit(solution)/shard_map/pallas_call | solution.py:23
  200.1 1.6 collective-permute-start.32
  202.6 17.2 %shard_map.63.second = f32[2,32,32,256]{3,2,1,0:T(8,128)} custom-call(s32[3]{0:T(128)} %pad_add_fusion.scalars, f32[7,40,40,256]{3,2,1,0:T(8,128)} %get-tuple-element.44.coef_in, f32[2,32,32,256]{3,2,1,0:T(8,128)} %get-tuple-element.57.tile, f32[2,4,32,256]{3,2,1,0:T(8,128)} %copy-done.18, f32[2,4,32,256]{3,2,1,0:T(8,128)} %copy-done.20, ...), custom_call_target="tpu_custom_call" | custom-call | flops 13799999488 | bytes 43200000 | tf_op jit(solution)/shard_map/pallas_call | solution.py:23
  219.9 4.1 %shard_map.64 = f32[8,128]{1,0:T(8,128)} custom-call(s32[3]{0:T(128)} %pad_add_fusion.scalars, f32[2,32,32,256]{3,2,1,0:T(8,128)} %get-tuple-element.51.tile.images.others.refs_0_, f32[2,32,32,256]{3,2,1,0:T(8,128)} %shard_map.63.second, f32[2,32,32,256]{3,2,1,0:T(8,128)} %get-tuple-element.51.tile.images.others.refs_0_), custom_call_target="tpu_custom_call" | custom-call | flops 4600000000 | bytes 14400000 | tf_op jit(solution)/shard_map/pallas_call | solution.py:23
  224.0 4.3 %shard_map.68 = f32[8,128]{1,0:T(8,128)} custom-call(s32[3]{0:T(128)} %get-tuple-element.82.scalars, f32[2,32,32,256]{3,2,1,0:T(8,128)} %get-tuple-element.51.tile.images.others.refs_0_, f32[2,32,32,256]{3,2,1,0:T(8,128)} %shard_map.63.second, f32[2,32,32,256]{3,2,1,0:T(8,128)} %shard_map.67.others.refs_1_), custom_call_target="tpu_custom_call" | custom-call | flops 4600000000 | bytes 14400000 | tf_op jit(solution)/shard_map/pallas_call | solution.py:23
  228.2 0.7 add.85
  229.0 4.2 %shard_map.70 = f32[8,128]{1,0:T(8,128)} custom-call(s32[3]{0:T(128)} %get-tuple-element.83.scalars, f32[2,32,32,256]{3,2,1,0:T(8,128)} %get-tuple-element.51.tile.images.others.refs_0_, f32[2,32,32,256]{3,2,1,0:T(8,128)} %shard_map.63.second, f32[2,32,32,256]{3,2,1,0:T(8,128)} %copy-done.2), custom_call_target="tpu_custom_call" | custom-call | flops 4600000000 | bytes 14400000 | tf_op jit(solution)/shard_map/pallas_call | solution.py:23
  233.3 0.8 copy.19
  234.1 11.5 %collective-permute-done.32.others.refs_2_ = f32[2,32,32,256]{3,2,1,0:T(8,128)S(1)} collective-permute-done((f32[2,32,32,256]{3,2,1,0:T(8,128)}, f32[2,32,32,256]{3,2,1,0:T(8,128)S(1)}, u32[]{:S(2)}, u32[]{:S(2)}) %collective-permute-start.32) | collective-permute-done | bytes 2097184 | tf_op jit(solution)/shard_map/ppermute | solution.py:459
  245.6 1.3 copy-done.3
  246.9 4.2 %shard_map.69 = f32[8,128]{1,0:T(8,128)} custom-call(s32[3]{0:T(128)} %pad_add_fusion.3.scalars, f32[2,32,32,256]{3,2,1,0:T(8,128)} %get-tuple-element.51.tile.images.others.refs_0_, f32[2,32,32,256]{3,2,1,0:T(8,128)} %shard_map.63.second, f32[2,32,32,256]{3,2,1,0:T(8,128)} %copy-done.3), custom_call_target="tpu_custom_call" | custom-call | flops 4600000000 | bytes 14400000 | tf_op jit(solution)/shard_map/pallas_call | solution.py:23
  251.2 0.8 copy.18
  252.0 2.1 collective-permute-start.35
  254.0 2.6 collective-permute-start.34
  256.7 3.0 %collective-permute-done.34 = f32[8,128]{0,1:T(8,128)S(1)} collective-permute-done((f32[8,128]{0,1:T(8,128)S(1)}, f32[8,128]{0,1:T(8,128)S(1)}, u32[]{:S(2)}, u32[]{:S(2)}) %collective-permute-start.34) | collective-permute-done | bytes 4128 | tf_op jit(solution)/shard_map/ppermute | solution.py:407
  259.8 1.0 collective-permute-start.36
  260.7 3.4 %collective-permute-done.36 = f32[8,128]{0,1:T(8,128)S(1)} collective-permute-done((f32[8,128]{0,1:T(8,128)S(1)}, f32[8,128]{0,1:T(8,128)S(1)}, u32[]{:S(2)}, u32[]{:S(2)}) %collective-permute-start.36) | collective-permute-done | bytes 4128 | tf_op jit(solution)/shard_map/ppermute | solution.py:407
  264.1 2.0 collective-permute-start.39
  266.2 1.9 collective-permute-start.38
  268.6 2.3 collective-permute-done.39
  270.9 2.8 collective-permute-done.38
  274.2 0.7 cholesky.16
  277.3 0.7 fusion.17
  278.8 6.1 %shard_map.71 = f32[2,32,32,256]{3,2,1,0:T(8,128)} custom-call(f32[2,8]{1,0:T(2,128)} %pad_maximum_fusion.inverse, f32[2,32,32,256]{3,2,1,0:T(8,128)} %get-tuple-element.51.tile.images.others.refs_0_, f32[2,32,32,256]{3,2,1,0:T(8,128)} %shard_map.67.others.refs_1_, f32[2,32,32,256]{3,2,1,0:T(8,128)} %copy-done.3, f32[2,32,32,256]{3,2,1,0:T(8,128)} %copy-done.2), custom_call_target="tpu_custom_call" | custom-call | flops 6899999744 | bytes 21600000 | tf_op jit(solution)/shard_map/pallas_call | solution.py:23
  (133 shorter events, 9.7 us)
Async XLA Ops:
  1.2 10.4 %copy-start.1 = (f32[2,32,32,256]{3,2,1,0:T(8,128)S(1)}, f32[2,32,32,256]{3,2,1,0:T(8,128)}, u32[]{:S(2)}) copy-start(f32[2,32,32,256]{3,2,1,0:T(8,128)} %probes.1) | copy-start | bytes 6291460
  5.5 31.3 %collective-permute-start = (f32[6,4,32,256]{3,2,1,0:T(8,128)}, f32[6,4,32,256]{3,2,1,0:T(8,128)S(1)}, u32[]{:S(2)}, u32[]{:S(2)}) collective-permute-start(f32[6,4,32,256]{3,2,1,0:T(8,128)} %get-tuple-element.39), channel_id=1, source_target_pairs={{0,2},{2,4},{4,6},{1,3},{3,5},{5,7},{8,10},{10,12},{12,14},{9,11},... | collective-permute-start | bytes 2359304 | tf_op jit(solution)/shard_map/ppermute | solution.py:100
  7.9 28.9 %collective-permute-start.1 = (f32[6,4,32,256]{3,2,1,0:T(8,128)}, f32[6,4,32,256]{3,2,1,0:T(8,128)S(1)}, u32[]{:S(2)}, u32[]{:S(2)}) collective-permute-start(f32[6,4,32,256]{3,2,1,0:T(8,128)} %get-tuple-element.40), channel_id=1, source_target_pairs={{2,0},{4,2},{6,4},{3,1},{5,3},{7,5},{10,8},{12,10},{14,12},{11,9},... | collective-permute-start | bytes 2359304 | tf_op jit(solution)/shard_map/ppermute | solution.py:101
  9.2 27.6 %collective-permute-start.2 = (f32[6,16,8,256]{3,2,1,0:T(8,128)}, f32[6,16,8,256]{3,2,1,0:T(8,128)}, u32[]{:S(2)}, u32[]{:S(2)}) collective-permute-start(f32[6,16,8,256]{3,2,1,0:T(8,128)} %get-tuple-element.41), channel_id=1, source_target_pairs={{0,1},{1,0},{2,3},{3,2},{4,5},{5,4},{6,7},{7,6},{8,9},{9,8},{10,11... | collective-permute-start | bytes 2359304 | tf_op jit(solution)/shard_map/ppermute | solution.py:98
  11.7 55.0 %collective-permute-start.20 = (f32[2,32,32,256]{3,2,1,0:T(8,128)S(1)}, f32[2,32,32,256]{3,2,1,0:T(8,128)S(1)}, u32[]{:S(2)}, u32[]{:S(2)}) collective-permute-start(f32[2,32,32,256]{3,2,1,0:T(8,128)S(1)} %copy-done.1), channel_id=1, source_target_pairs={{0,8},{8,16},{16,24},{1,9},{9,17},{17,25},{2,10},{10,18},{18,26},{... | collective-permute-start | bytes 6291464 | tf_op jit(solution)/shard_map/ppermute | solution.py:459
  15.3 15.3 %collective-permute-start.3 = (f32[6,2,8,256]{3,2,1,0:T(8,128)}, f32[6,2,8,256]{3,2,1,0:T(8,128)S(1)}, u32[]{:S(2)}, u32[]{:S(2)}) collective-permute-start(f32[6,2,8,256]{3,2,1,0:T(8,128)} %get-tuple-element.42), channel_id=1, source_target_pairs={{0,3},{1,2},{2,5},{3,4},{4,7},{5,6},{8,11},{9,10},{10,13},{11,12},... | collective-permute-start | bytes 294920 | tf_op jit(solution)/shard_map/ppermute | solution.py:98
  30.6 6.2 %copy-start.22 = (f32[6,2,8,256]{3,2,1,0:T(8,128)}, f32[6,2,8,256]{3,2,1,0:T(8,128)S(1)}, u32[]{:S(2)}) copy-start(f32[6,2,8,256]{3,2,1,0:T(8,128)S(1)} %collective-permute-done.3.refs_3_) | copy-start | bytes 294916
  30.6 6.2 %collective-permute-start.4 = (f32[6,2,8,256]{3,2,1,0:T(8,128)}, f32[6,2,8,256]{3,2,1,0:T(8,128)S(1)}, u32[]{:S(2)}, u32[]{:S(2)}) collective-permute-start(f32[6,2,8,256]{3,2,1,0:T(8,128)} %get-tuple-element.43), channel_id=1, source_target_pairs={{2,1},{3,0},{4,3},{5,2},{6,5},{7,4},{10,9},{11,8},{12,11},{13,10},... | collective-permute-start | bytes 294920 | tf_op jit(solution)/shard_map/ppermute | solution.py:98
  56.4 14.7 %collective-permute-start.8 = (f32[2,2,8,256]{3,2,1,0:T(8,128)}, f32[2,2,8,256]{3,2,1,0:T(8,128)S(1)}, u32[]{:S(2)}, u32[]{:S(2)}) collective-permute-start(f32[2,2,8,256]{3,2,1,0:T(8,128)} %get-tuple-element.49), channel_id=1, source_target_pairs={{0,3},{1,2},{2,5},{3,4},{4,7},{5,6},{8,11},{9,10},{10,13},{11,12},... | collective-permute-start | bytes 98312 | tf_op jit(solution)/shard_map/ppermute | solution.py:98
  60.9 15.1 %collective-permute-start.9 = (f32[2,2,8,256]{3,2,1,0:T(8,128)}, f32[2,2,8,256]{3,2,1,0:T(8,128)S(1)}, u32[]{:S(2)}, u32[]{:S(2)}) collective-permute-start(f32[2,2,8,256]{3,2,1,0:T(8,128)} %get-tuple-element.50), channel_id=1, source_target_pairs={{2,1},{3,0},{4,3},{5,2},{6,5},{7,4},{10,9},{11,8},{12,11},{13,10},... | collective-permute-start | bytes 98312 | tf_op jit(solution)/shard_map/ppermute | solution.py:98
  62.2 15.2 %collective-permute-start.5 = (f32[2,4,32,256]{3,2,1,0:T(8,128)}, f32[2,4,32,256]{3,2,1,0:T(8,128)S(1)}, u32[]{:S(2)}, u32[]{:S(2)}) collective-permute-start(f32[2,4,32,256]{3,2,1,0:T(8,128)} %get-tuple-element.46), channel_id=1, source_target_pairs={{0,2},{2,4},{4,6},{1,3},{3,5},{5,7},{8,10},{10,12},{12,14},{9,11},... | collective-permute-start | bytes 786440 | tf_op jit(solution)/shard_map/ppermute | solution.py:100
  65.3 12.6 %collective-permute-start.6 = (f32[2,4,32,256]{3,2,1,0:T(8,128)}, f32[2,4,32,256]{3,2,1,0:T(8,128)S(1)}, u32[]{:S(2)}, u32[]{:S(2)}) collective-permute-start(f32[2,4,32,256]{3,2,1,0:T(8,128)} %get-tuple-element.47), channel_id=1, source_target_pairs={{2,0},{4,2},{6,4},{3,1},{5,3},{7,5},{10,8},{12,10},{14,12},{11,9},... | collective-permute-start | bytes 786440 | tf_op jit(solution)/shard_map/ppermute | solution.py:101
  66.7 11.3 %collective-permute-start.7 = (f32[2,16,8,256]{3,2,1,0:T(8,128)}, f32[2,16,8,256]{3,2,1,0:T(8,128)S(1)}, u32[]{:S(2)}, u32[]{:S(2)}) collective-permute-start(f32[2,16,8,256]{3,2,1,0:T(8,128)} %get-tuple-element.48), channel_id=1, source_target_pairs={{0,1},{1,0},{2,3},{3,2},{4,5},{5,4},{6,7},{7,6},{8,9},{9,8},{10,11... | collective-permute-start | bytes 786440 | tf_op jit(solution)/shard_map/ppermute | solution.py:98
  71.1 6.9 %copy-start.31 = (f32[2,2,8,256]{3,2,1,0:T(8,128)}, f32[2,2,8,256]{3,2,1,0:T(8,128)S(1)}, u32[]{:S(2)}) copy-start(f32[2,2,8,256]{3,2,1,0:T(8,128)S(1)} %collective-permute-done.8.refs_3_) | copy-start | bytes 98308
  71.1 42.4 %collective-permute-start.21 = (f32[2,4,32,256]{3,2,1,0:T(8,128)}, f32[2,4,32,256]{3,2,1,0:T(8,128)S(1)}, u32[]{:S(2)}, u32[]{:S(2)}) collective-permute-start(f32[2,4,32,256]{3,2,1,0:T(8,128)} %get-tuple-element.63), channel_id=1, source_target_pairs={{0,2},{2,4},{4,6},{1,3},{3,5},{5,7},{8,10},{10,12},{12,14},{9,11},... | collective-permute-start | bytes 786440 | tf_op jit(solution)/shard_map/ppermute | solution.py:100
  76.1 2.0 copy-start.33
  76.1 38.8 %collective-permute-start.22 = (f32[2,4,32,256]{3,2,1,0:T(8,128)}, f32[2,4,32,256]{3,2,1,0:T(8,128)S(1)}, u32[]{:S(2)}, u32[]{:S(2)}) collective-permute-start(f32[2,4,32,256]{3,2,1,0:T(8,128)} %get-tuple-element.64), channel_id=1, source_target_pairs={{2,0},{4,2},{6,4},{3,1},{5,3},{7,5},{10,8},{12,10},{14,12},{11,9},... | collective-permute-start | bytes 786440 | tf_op jit(solution)/shard_map/ppermute | solution.py:101
  77.4 38.3 %collective-permute-start.23 = (f32[2,16,8,256]{3,2,1,0:T(8,128)}, f32[2,16,8,256]{3,2,1,0:T(8,128)S(1)}, u32[]{:S(2)}, u32[]{:S(2)}) collective-permute-start(f32[2,16,8,256]{3,2,1,0:T(8,128)} %get-tuple-element.65), channel_id=1, source_target_pairs={{0,1},{1,0},{2,3},{3,2},{4,5},{5,4},{6,7},{7,6},{8,9},{9,8},{10,11... | collective-permute-start | bytes 786440 | tf_op jit(solution)/shard_map/ppermute | solution.py:98
  78.8 22.7 %copy-start.29 = (f32[2,2,8,256]{3,2,1,0:T(8,128)S(1)}, f32[2,2,8,256]{3,2,1,0:T(8,128)}, u32[]{:S(2)}) copy-start(f32[2,2,8,256]{3,2,1,0:T(8,128)} %get-tuple-element.66) | copy-start | bytes 98308
  78.8 26.9 %copy-start.27 = (f32[2,2,8,256]{3,2,1,0:T(8,128)S(1)}, f32[2,2,8,256]{3,2,1,0:T(8,128)}, u32[]{:S(2)}) copy-start(f32[2,2,8,256]{3,2,1,0:T(8,128)} %get-tuple-element.67) | copy-start | bytes 98308
  96.4 9.3 %collective-permute-start.13 = (f32[2,2,8,256]{3,2,1,0:T(8,128)}, f32[2,2,8,256]{3,2,1,0:T(8,128)S(1)}, u32[]{:S(2)}, u32[]{:S(2)}) collective-permute-start(f32[2,2,8,256]{3,2,1,0:T(8,128)} %get-tuple-element.55), channel_id=1, source_target_pairs={{0,3},{1,2},{2,5},{3,4},{4,7},{5,6},{8,11},{9,10},{10,13},{11,12},... | collective-permute-start | bytes 98312 | tf_op jit(solution)/shard_map/ppermute | solution.py:98
  101.5 6.2 %collective-permute-start.24 = (f32[2,2,8,256]{3,2,1,0:T(8,128)S(1)}, f32[2,2,8,256]{3,2,1,0:T(8,128)S(1)}, u32[]{:S(2)}, u32[]{:S(2)}) collective-permute-start(f32[2,2,8,256]{3,2,1,0:T(8,128)S(1)} %copy-done.29), channel_id=1, source_target_pairs={{0,3},{1,2},{2,5},{3,4},{4,7},{5,6},{8,11},{9,10},{10,13},{11,12},... | collective-permute-start | bytes 98312 | tf_op jit(solution)/shard_map/ppermute | solution.py:98
  105.7 32.9 %copy-start.24 = (f32[2,2,8,256]{3,2,1,0:T(8,128)}, f32[2,2,8,256]{3,2,1,0:T(8,128)S(1)}, u32[]{:S(2)}) copy-start(f32[2,2,8,256]{3,2,1,0:T(8,128)S(1)} %collective-permute-done.13.refs_4_) | copy-start | bytes 98308
  105.7 5.2 %collective-permute-start.25 = (f32[2,2,8,256]{3,2,1,0:T(8,128)S(1)}, f32[2,2,8,256]{3,2,1,0:T(8,128)S(1)}, u32[]{:S(2)}, u32[]{:S(2)}) collective-permute-start(f32[2,2,8,256]{3,2,1,0:T(8,128)S(1)} %copy-done.27), channel_id=1, source_target_pairs={{2,1},{3,0},{4,3},{5,2},{6,5},{7,4},{10,9},{11,8},{12,11},{13,10},... | collective-permute-start | bytes 98312 | tf_op jit(solution)/shard_map/ppermute | solution.py:98
  107.7 13.7 %copy-start.32 = (f32[2,2,8,256]{3,2,1,0:T(8,128)}, f32[2,2,8,256]{3,2,1,0:T(8,128)S(1)}, u32[]{:S(2)}) copy-start(f32[2,2,8,256]{3,2,1,0:T(8,128)S(1)} %collective-permute-done.24.refs_4_) | copy-start | bytes 98308
  107.7 30.9 %collective-permute-start.14 = (f32[2,2,8,256]{3,2,1,0:T(8,128)}, f32[2,2,8,256]{3,2,1,0:T(8,128)S(1)}, u32[]{:S(2)}, u32[]{:S(2)}) collective-permute-start(f32[2,2,8,256]{3,2,1,0:T(8,128)} %get-tuple-element.56), channel_id=1, source_target_pairs={{2,1},{3,0},{4,3},{5,2},{6,5},{7,4},{10,9},{11,8},{12,11},{13,10},... | collective-permute-start | bytes 98312 | tf_op jit(solution)/shard_map/ppermute | solution.py:98
  111.0 10.4 %copy-start.35 = (f32[2,2,8,256]{3,2,1,0:T(8,128)}, f32[2,2,8,256]{3,2,1,0:T(8,128)S(1)}, u32[]{:S(2)}) copy-start(f32[2,2,8,256]{3,2,1,0:T(8,128)S(1)} %collective-permute-done.25.refs_5_) | copy-start | bytes 98308
  111.0 33.0 %collective-permute-start.10 = (f32[2,4,32,256]{3,2,1,0:T(8,128)}, f32[2,4,32,256]{3,2,1,0:T(8,128)S(1)}, u32[]{:S(2)}, u32[]{:S(2)}) collective-permute-start(f32[2,4,32,256]{3,2,1,0:T(8,128)} %get-tuple-element.52), channel_id=1, source_target_pairs={{0,2},{2,4},{4,6},{1,3},{3,5},{5,7},{8,10},{10,12},{12,14},{9,11},... | collective-permute-start | bytes 786440 | tf_op jit(solution)/shard_map/ppermute | solution.py:100
  113.5 7.9 %copy-start.7 = (f32[2,4,32,256]{3,2,1,0:T(8,128)}, f32[2,4,32,256]{3,2,1,0:T(8,128)S(1)}, u32[]{:S(2)}) copy-start(f32[2,4,32,256]{3,2,1,0:T(8,128)S(1)} %collective-permute-done.21.refs_1_) | copy-start | bytes 786436
  113.5 31.7 %collective-permute-start.11 = (f32[2,4,32,256]{3,2,1,0:T(8,128)}, f32[2,4,32,256]{3,2,1,0:T(8,128)S(1)}, u32[]{:S(2)}, u32[]{:S(2)}) collective-permute-start(f32[2,4,32,256]{3,2,1,0:T(8,128)} %get-tuple-element.53), channel_id=1, source_target_pairs={{2,0},{4,2},{6,4},{3,1},{5,3},{7,5},{10,8},{12,10},{14,12},{11,9},... | collective-permute-start | bytes 786440 | tf_op jit(solution)/shard_map/ppermute | solution.py:101
  114.8 6.6 %copy-start.8 = (f32[2,4,32,256]{3,2,1,0:T(8,128)}, f32[2,4,32,256]{3,2,1,0:T(8,128)S(1)}, u32[]{:S(2)}) copy-start(f32[2,4,32,256]{3,2,1,0:T(8,128)S(1)} %collective-permute-done.22.refs_2_) | copy-start | bytes 786436
  114.9 35.1 %collective-permute-start.12 = (f32[2,16,8,256]{3,2,1,0:T(8,128)}, f32[2,16,8,256]{3,2,1,0:T(8,128)S(1)}, u32[]{:S(2)}, u32[]{:S(2)}) collective-permute-start(f32[2,16,8,256]{3,2,1,0:T(8,128)} %get-tuple-element.54), channel_id=1, source_target_pairs={{0,1},{1,0},{2,3},{3,2},{4,5},{5,4},{6,7},{7,6},{8,9},{9,8},{10,11... | collective-permute-start | bytes 786440 | tf_op jit(solution)/shard_map/ppermute | solution.py:98
  115.7 5.7 %copy-start.9 = (f32[2,16,8,256]{3,2,1,0:T(8,128)}, f32[2,16,8,256]{3,2,1,0:T(8,128)S(1)}, u32[]{:S(2)}) copy-start(f32[2,16,8,256]{3,2,1,0:T(8,128)S(1)} %collective-permute-done.23.refs_3_) | copy-start | bytes 786436
  115.7 66.2 %collective-permute-start.31 = (f32[2,32,32,256]{3,2,1,0:T(8,128)}, f32[2,32,32,256]{3,2,1,0:T(8,128)S(1)}, u32[]{:S(2)}, u32[]{:S(2)}) collective-permute-start(f32[2,32,32,256]{3,2,1,0:T(8,128)} %get-tuple-element.51.tile.images.others.refs_0_), channel_id=1, source_target_pairs={{0,24},{1,25},{2,26},{3,27},{4,28},{5,29},{6,30},{7,31}} | collective-permute-start | bytes 6291464 | tf_op jit(solution)/shard_map/ppermute | solution.py:459
  138.6 14.0 %copy-start.25 = (f32[2,2,8,256]{3,2,1,0:T(8,128)}, f32[2,2,8,256]{3,2,1,0:T(8,128)S(1)}, u32[]{:S(2)}) copy-start(f32[2,2,8,256]{3,2,1,0:T(8,128)S(1)} %collective-permute-done.14.refs_5_) | copy-start | bytes 98308
  138.6 12.7 %collective-permute-start.29 = (f32[2,2,8,256]{3,2,1,0:T(8,128)}, f32[2,2,8,256]{3,2,1,0:T(8,128)S(1)}, u32[]{:S(2)}, u32[]{:S(2)}) collective-permute-start(f32[2,2,8,256]{3,2,1,0:T(8,128)} %get-tuple-element.72), channel_id=1, source_target_pairs={{0,3},{1,2},{2,5},{3,4},{4,7},{5,6},{8,11},{9,10},{10,13},{11,12},... | collective-permute-start | bytes 98312 | tf_op jit(solution)/shard_map/ppermute | solution.py:98
  144.0 8.6 %copy-start.10 = (f32[2,4,32,256]{3,2,1,0:T(8,128)}, f32[2,4,32,256]{3,2,1,0:T(8,128)S(1)}, u32[]{:S(2)}) copy-start(f32[2,4,32,256]{3,2,1,0:T(8,128)S(1)} %collective-permute-done.10.refs_1_) | copy-start | bytes 786436
  144.0 25.8 %collective-permute-start.30 = (f32[2,2,8,256]{3,2,1,0:T(8,128)}, f32[2,2,8,256]{3,2,1,0:T(8,128)S(1)}, u32[]{:S(2)}, u32[]{:S(2)}) collective-permute-start(f32[2,2,8,256]{3,2,1,0:T(8,128)} %get-tuple-element.73), channel_id=1, source_target_pairs={{2,1},{3,0},{4,3},{5,2},{6,5},{7,4},{10,9},{11,8},{12,11},{13,10},... | collective-permute-start | bytes 98312 | tf_op jit(solution)/shard_map/ppermute | solution.py:98
  145.3 7.3 %copy-start.11 = (f32[2,4,32,256]{3,2,1,0:T(8,128)}, f32[2,4,32,256]{3,2,1,0:T(8,128)S(1)}, u32[]{:S(2)}) copy-start(f32[2,4,32,256]{3,2,1,0:T(8,128)S(1)} %collective-permute-done.11.refs_2_) | copy-start | bytes 786436
  145.3 29.6 %collective-permute-start.26 = (f32[2,4,32,256]{3,2,1,0:T(8,128)}, f32[2,4,32,256]{3,2,1,0:T(8,128)S(1)}, u32[]{:S(2)}, u32[]{:S(2)}) collective-permute-start(f32[2,4,32,256]{3,2,1,0:T(8,128)} %get-tuple-element.69), channel_id=1, source_target_pairs={{0,2},{2,4},{4,6},{1,3},{3,5},{5,7},{8,10},{10,12},{12,14},{9,11},... | collective-permute-start | bytes 786440 | tf_op jit(solution)/shard_map/ppermute | solution.py:100
  150.0 2.6 copy-start.12
  150.0 26.2 %collective-permute-start.27 = (f32[2,4,32,256]{3,2,1,0:T(8,128)}, f32[2,4,32,256]{3,2,1,0:T(8,128)S(1)}, u32[]{:S(2)}, u32[]{:S(2)}) collective-permute-start(f32[2,4,32,256]{3,2,1,0:T(8,128)} %get-tuple-element.70), channel_id=1, source_target_pairs={{2,0},{4,2},{6,4},{3,1},{5,3},{7,5},{10,8},{12,10},{14,12},{11,9},... | collective-permute-start | bytes 786440 | tf_op jit(solution)/shard_map/ppermute | solution.py:101
  151.3 18.5 %copy-start.26 = (f32[2,2,8,256]{3,2,1,0:T(8,128)}, f32[2,2,8,256]{3,2,1,0:T(8,128)S(1)}, u32[]{:S(2)}) copy-start(f32[2,2,8,256]{3,2,1,0:T(8,128)S(1)} %collective-permute-done.29.refs_3_) | copy-start | bytes 98308
  151.3 29.3 %collective-permute-start.28 = (f32[2,16,8,256]{3,2,1,0:T(8,128)}, f32[2,16,8,256]{3,2,1,0:T(8,128)S(1)}, u32[]{:S(2)}, u32[]{:S(2)}) collective-permute-start(f32[2,16,8,256]{3,2,1,0:T(8,128)} %get-tuple-element.71), channel_id=1, source_target_pairs={{0,1},{1,0},{2,3},{3,2},{4,5},{5,4},{6,7},{7,6},{8,9},{9,8},{10,11... | collective-permute-start | bytes 786440 | tf_op jit(solution)/shard_map/ppermute | solution.py:98
  169.8 13.0 %copy-start.28 = (f32[2,2,8,256]{3,2,1,0:T(8,128)}, f32[2,2,8,256]{3,2,1,0:T(8,128)S(1)}, u32[]{:S(2)}) copy-start(f32[2,2,8,256]{3,2,1,0:T(8,128)S(1)} %collective-permute-done.30.refs_4_) | copy-start | bytes 98308
  169.8 30.3 %collective-permute-start.18 = (f32[2,2,8,256]{3,2,1,0:T(8,128)}, f32[2,2,8,256]{3,2,1,0:T(8,128)S(1)}, u32[]{:S(2)}, u32[]{:S(2)}) collective-permute-start(f32[2,2,8,256]{3,2,1,0:T(8,128)} %get-tuple-element.61), channel_id=1, source_target_pairs={{0,3},{1,2},{2,5},{3,4},{4,7},{5,6},{8,11},{9,10},{10,13},{11,12},... | collective-permute-start | bytes 98312 | tf_op jit(solution)/shard_map/ppermute | solution.py:98
  174.9 8.0 %copy-start.13 = (f32[2,4,32,256]{3,2,1,0:T(8,128)}, f32[2,4,32,256]{3,2,1,0:T(8,128)S(1)}, u32[]{:S(2)}) copy-start(f32[2,4,32,256]{3,2,1,0:T(8,128)S(1)} %collective-permute-done.26.refs_0_) | copy-start | bytes 786436
  174.9 26.8 %collective-permute-start.19 = (f32[2,2,8,256]{3,2,1,0:T(8,128)}, f32[2,2,8,256]{3,2,1,0:T(8,128)S(1)}, u32[]{:S(2)}, u32[]{:S(2)}) collective-permute-start(f32[2,2,8,256]{3,2,1,0:T(8,128)} %get-tuple-element.62), channel_id=1, source_target_pairs={{2,1},{3,0},{4,3},{5,2},{6,5},{7,4},{10,9},{11,8},{12,11},{13,10},... | collective-permute-start | bytes 98312 | tf_op jit(solution)/shard_map/ppermute | solution.py:98
  176.2 6.6 %copy-start.14 = (f32[2,4,32,256]{3,2,1,0:T(8,128)}, f32[2,4,32,256]{3,2,1,0:T(8,128)S(1)}, u32[]{:S(2)}) copy-start(f32[2,4,32,256]{3,2,1,0:T(8,128)S(1)} %collective-permute-done.27.refs_1_) | copy-start | bytes 786436
  176.2 25.5 %collective-permute-start.15 = (f32[2,4,32,256]{3,2,1,0:T(8,128)}, f32[2,4,32,256]{3,2,1,0:T(8,128)S(1)}, u32[]{:S(2)}, u32[]{:S(2)}) collective-permute-start(f32[2,4,32,256]{3,2,1,0:T(8,128)} %get-tuple-element.58), channel_id=1, source_target_pairs={{0,2},{2,4},{4,6},{1,3},{3,5},{5,7},{8,10},{10,12},{12,14},{9,11},... | collective-permute-start | bytes 786440 | tf_op jit(solution)/shard_map/ppermute | solution.py:100
  180.6 2.2 copy-start.16
  180.6 21.1 %collective-permute-start.16 = (f32[2,4,32,256]{3,2,1,0:T(8,128)}, f32[2,4,32,256]{3,2,1,0:T(8,128)S(1)}, u32[]{:S(2)}, u32[]{:S(2)}) collective-permute-start(f32[2,4,32,256]{3,2,1,0:T(8,128)} %get-tuple-element.59), channel_id=1, source_target_pairs={{2,0},{4,2},{6,4},{3,1},{5,3},{7,5},{10,8},{12,10},{14,12},{11,9},... | collective-permute-start | bytes 786440 | tf_op jit(solution)/shard_map/ppermute | solution.py:101
  181.9 18.1 %copy-start.2 = (f32[2,32,32,256]{3,2,1,0:T(8,128)}, f32[2,32,32,256]{3,2,1,0:T(8,128)S(1)}, u32[]{:S(2)}) copy-start(f32[2,32,32,256]{3,2,1,0:T(8,128)S(1)} %collective-permute-done.31.others.refs_3_) | copy-start | bytes 6291460
  181.9 19.8 %collective-permute-start.17 = (f32[2,16,8,256]{3,2,1,0:T(8,128)}, f32[2,16,8,256]{3,2,1,0:T(8,128)S(1)}, u32[]{:S(2)}, u32[]{:S(2)}) collective-permute-start(f32[2,16,8,256]{3,2,1,0:T(8,128)} %get-tuple-element.60), channel_id=1, source_target_pairs={{0,1},{1,0},{2,3},{3,2},{4,5},{5,4},{6,7},{7,6},{8,9},{9,8},{10,11... | collective-permute-start | bytes 786440 | tf_op jit(solution)/shard_map/ppermute | solution.py:98
  200.1 1.7 copy-start.30
  200.1 45.5 %collective-permute-start.32 = (f32[2,32,32,256]{3,2,1,0:T(8,128)}, f32[2,32,32,256]{3,2,1,0:T(8,128)S(1)}, u32[]{:S(2)}, u32[]{:S(2)}) collective-permute-start(f32[2,32,32,256]{3,2,1,0:T(8,128)} %shard_map.67.others.refs_1_), channel_id=1, source_target_pairs={{0,8},{8,16},{16,24},{1,9},{9,17},{17,25},{2,10},{10,18},{18,26},{... | collective-permute-start | bytes 6291464 | tf_op jit(solution)/shard_map/ppermute | solution.py:459
  224.0 4.3 %copy-start = (f32[8,128]{1,0:T(8,128)S(1)}, f32[8,128]{1,0:T(8,128)}, u32[]{:S(2)}) copy-start(f32[8,128]{1,0:T(8,128)} %shard_map.64) | copy-start | bytes 12292
  252.0 4.7 %collective-permute-start.35 = (f32[8,128]{0,1:T(8,128)S(1)}, f32[8,128]{0,1:T(8,128)S(1)}, u32[]{:S(2)}, u32[]{:S(2)}) collective-permute-start(f32[8,128]{0,1:T(8,128)S(1)} %add_add_fusion.1), channel_id=1, source_target_pairs={{0,6},{2,4},{4,2},{6,0},{1,7},{3,5},{5,3},{7,1},{8,14},{10,12},{12... | collective-permute-start | bytes 12296 | tf_op jit(solution)/shard_map/ppermute | solution.py:407
  254.0 5.7 %collective-permute-start.34 = (f32[8,128]{0,1:T(8,128)S(1)}, f32[8,128]{0,1:T(8,128)S(1)}, u32[]{:S(2)}, u32[]{:S(2)}) collective-permute-start(f32[8,128]{0,1:T(8,128)S(1)} %add_add_fusion.1), channel_id=1, source_target_pairs={{0,4},{2,6},{4,0},{6,2},{1,5},{3,7},{5,1},{7,3},{8,12},{10,14},{12... | collective-permute-start | bytes 12296 | tf_op jit(solution)/shard_map/ppermute | solution.py:407
  256.7 3.1 %collective-permute-start.33 = (f32[8,128]{0,1:T(8,128)S(1)}, f32[8,128]{0,1:T(8,128)S(1)}, u32[]{:S(2)}, u32[]{:S(2)}) collective-permute-start(f32[8,128]{0,1:T(8,128)S(1)} %add_add_fusion.1), channel_id=1, source_target_pairs={{0,2},{2,0},{4,6},{6,4},{1,3},{3,1},{5,7},{7,5},{8,10},{10,8},{12,... | collective-permute-start | bytes 12296 | tf_op jit(solution)/shard_map/ppermute | solution.py:407
  259.8 4.4 %collective-permute-start.36 = (f32[8,128]{0,1:T(8,128)S(1)}, f32[8,128]{0,1:T(8,128)S(1)}, u32[]{:S(2)}, u32[]{:S(2)}) collective-permute-start(f32[8,128]{0,1:T(8,128)S(1)} %add_add_fusion), channel_id=1, source_target_pairs={{0,1},{1,0},{2,3},{3,2},{4,5},{5,4},{6,7},{7,6},{8,9},{9,8},{10,11... | collective-permute-start | bytes 12296 | tf_op jit(solution)/shard_map/ppermute | solution.py:407
  264.1 6.8 %collective-permute-start.39 = (f32[8,128]{0,1:T(8,128)S(1)}, f32[8,128]{0,1:T(8,128)S(1)}, u32[]{:S(2)}, u32[]{:S(2)}) collective-permute-start(f32[8,128]{0,1:T(8,128)S(1)} %add.91), channel_id=1, source_target_pairs={{0,24},{8,16},{16,8},{24,0},{1,25},{9,17},{17,9},{25,1},{2,26},{10... | collective-permute-start | bytes 12296 | tf_op jit(solution)/shard_map/ppermute | solution.py:407
  266.2 7.5 %collective-permute-start.38 = (f32[8,128]{0,1:T(8,128)S(1)}, f32[8,128]{0,1:T(8,128)S(1)}, u32[]{:S(2)}, u32[]{:S(2)}) collective-permute-start(f32[8,128]{0,1:T(8,128)S(1)} %add.91), channel_id=1, source_target_pairs={{0,16},{8,24},{16,0},{24,8},{1,17},{9,25},{17,1},{25,9},{2,18},{10... | collective-permute-start | bytes 12296 | tf_op jit(solution)/shard_map/ppermute | solution.py:407
  268.1 5.7 %collective-permute-start.37 = (f32[8,128]{0,1:T(8,128)S(1)}, f32[8,128]{0,1:T(8,128)S(1)}, u32[]{:S(2)}, u32[]{:S(2)}) collective-permute-start(f32[8,128]{0,1:T(8,128)S(1)} %add.91), channel_id=1, source_target_pairs={{0,8},{8,0},{16,24},{24,16},{1,9},{9,1},{17,25},{25,17},{2,10},{10... | collective-permute-start | bytes 12296 | tf_op jit(solution)/shard_map/ppermute | solution.py:407
  (12 other events, 10.8 us)

commit v2 on v1

--- a/solution.py
+++ b/solution.py
@@ -11,6 +11,7 @@
 SUB = 8
 LANES = 128
 ROWS = 2
+BLOCK = 4
 VMEM_LIMIT = 58 * 1024 * 1024
 FLOPS_PER_MICRO = 1.15e9
 BYTES_PER_MICRO = 3.6e6
@@ -342,60 +343,93 @@
         write_strips(out, strips, side)
 
 
-def dots_kernel(own_group, scalars, images, second, others, out):
-    group, x, y, z = images.shape
+def blocked_call(body, out_shape, out_block, scratch, scalars, ins, micros):
+    group, x, y, z = ins[0].shape
+    block = pl.BlockSpec((group, BLOCK, y, z), lambda i: (0, i, 0, 0))
+    out = block if out_block else pl.BlockSpec(out_shape.shape, lambda i: (0, 0))
+    return pl.pallas_call(
+        body,
+        grid=(x // BLOCK,),
+        out_shape=out_shape,
+        in_specs=[pl.BlockSpec(memory_space=pltpu.SMEM)] + [block] * len(ins),
+        out_specs=out,
+        scratch_shapes=scratch,
+        compiler_params=pltpu.CompilerParams(vmem_limit_bytes=VMEM_LIMIT),
+        cost_estimate=pl.CostEstimate(
+            flops=int(micros * FLOPS_PER_MICRO),
+            bytes_accessed=int(micros * BYTES_PER_MICRO),
+            transcendentals=0,
+        ),
+    )(scalars, *ins)
+
+
+def dots_pairs(group, slots):
+    return [(s, a, b) for s in range(slots) for a in range(group) for b in range(group) if s or b <= a]
+
+
+def dots_kernel(scalars, second, *refs):
+    passed, (out, held) = refs[:-2], refs[-2:]
+    group, rows, y, z = second.shape
     chunks, cols = y // SUB, z // LANES
-    pairs = [(a, b) for a in range(group) for b in range(group) if not own_group or b <= a]
+    pairs = dots_pairs(group, len(passed))
+    at_step = pl.program_id(0)
+
+    @pl.when(at_step == 0)
+    def _():
+        held[...] = jnp.zeros(held.shape, jnp.float32)
 
     def body(i, sums):
         sums = list(sums)
         for c in range(chunks):
             for j in range(cols):
                 at = (pl.ds(SUB * c, SUB), pl.ds(LANES * j, LANES))
-                other = [others[b, i, *at] for b in range(group)]
-                mine = [images[a, i, *at] for a in range(group)]
+                mine = [passed[0][a, i, *at] for a in range(group)]
                 then = [second[a, i, *at] for a in range(group)]
-                for n, (a, b) in enumerate(pairs):
-                    sums[2 * n] = sums[2 * n] + mine[a] * other[b]
-                    sums[2 * n + 1] = sums[2 * n + 1] + then[a] * other[b]
+                other = {(s, b): passed[s][b, i, *at] for s in range(1, len(passed)) for b in range(group)}
+                for n, (s, a, b) in enumerate(pairs):
+                    value = other[s, b] if s else mine[b]
+                    sums[2 * n] = sums[2 * n] + mine[a] * value
+                    sums[2 * n + 1] = sums[2 * n + 1] + then[a] * value
         return tuple(sums)
 
-    zero = jnp.zeros((SUB, LANES), jnp.float32)
-    sums = lax.fori_loop(0, x, body, (zero,) * (2 * len(pairs)))
-    row0, col0 = scalars[1] * group, scalars[2] * group
-    count = out.shape[0]
-    row = lax.broadcasted_iota(jnp.int32, out.shape, 0)
-    lane = lax.broadcasted_iota(jnp.int32, out.shape, 1)
-    total = jnp.zeros(out.shape, jnp.float32)
-    for n, (a, b) in enumerate(pairs):
-        for k in range(2):
-            value = jnp.sum(jnp.sum(sums[2 * n + k], axis=0, keepdims=True), axis=1, keepdims=True)
-            here = (row == row0 + a) & (lane == col0 + b + k * count) & (scalars[2] >= 0)
-            total = total + jnp.where(here, value, 0.0)
-    out[...] = total
+    sums = lax.fori_loop(0, rows, body, tuple(held[n] for n in range(2 * len(pairs))))
+    for n, value in enumerate(sums):
+        held[n] = value
+
+    @pl.when(at_step == pl.num_programs(0) - 1)
+    def _():
+        me = scalars[1]
+        count = out.shape[0]
+        row = lax.broadcasted_iota(jnp.int32, out.shape, 0)
+        lane = lax.broadcasted_iota(jnp.int32, out.shape, 1)
+        total = jnp.zeros(out.shape, jnp.float32)
+        for n, (s, a, b) in enumerate(pairs):
+            for k in range(2):
+                value = jnp.sum(jnp.sum(sums[2 * n + k], axis=0, keepdims=True), axis=1, keepdims=True)
+                column = (me - s) * group + b + k * count
+                here = (row == me * group + a) & (lane == column) & (me >= s)
+                total = total + jnp.where(here, value, 0.0)
+        out[...] = total
 
 
 def basis_kernel(inverse, *refs):
     images, out = refs[:-1], refs[-1]
-    group, x, y, z = out.shape
-    chunks, cols = y // SUB, z // LANES
+    group, rows, y, z = out.shape
+    factors = [[inverse[a, n] for n in range(group * len(images))] for a in range(group)]
 
     def body(i, carry):
-        for c in range(chunks):
-            for j in range(cols):
+        for c in range(y // SUB):
+            for j in range(z // LANES):
                 at = (pl.ds(SUB * c, SUB), pl.ds(LANES * j, LANES))
-                sums = [None] * group
-                for s, image in enumerate(images):
-                    for b in range(group):
-                        value = image[b, i, *at]
-                        for a in range(group):
-                            term = inverse[a, s * group + b] * value
-                            sums[a] = term if sums[a] is None else sums[a] + term
+                values = [image[b, i, *at] for image in images for b in range(group)]
                 for a in range(group):
-                    out[a, i, *at] = sums[a]
+                    terms = [factor * value for factor, value in zip(factors[a], values)]
+                    while len(terms) > 1:
+                        terms = [sum(terms[n : n + 2][1:], terms[n]) for n in range(0, len(terms), 2)]
+                    out[a, i, *at] = terms[0]
         return carry
 
-    lax.fori_loop(0, x, body, None)
+    lax.fori_loop(0, rows, body, None)
 
 
 def all_sum(value):
@@ -424,10 +458,7 @@
     both = lax.axis_size("sy") != 2
     side, mine = lax.axis_index("sy"), lax.axis_index("probe")
 
-    def scalars(other):
-        return jnp.stack([side, mine, mine - other]).astype(jnp.int32)
-
-    where = scalars(0)
+    where = jnp.stack([side, mine]).astype(jnp.int32)
     wide = (x + 2 * STEPS, y + 2 * STEPS, z)
     tile = f32(group, x, y, z)
     strips2 = strip_shapes(group, x, y, z, both)
@@ -471,8 +502,7 @@
         outs_anywhere=(0,),
     )
 
-    def model(field, strips, adjoint, last=False):
-        received = exchange(strips)
+    def model(field, received, adjoint, last=False):
         ins = [where, coef, field] + ([] if adjoint else [obs_weight])
         return kernel_call(
             functools.partial(next_kernel, len(received), adjoint),
@@ -483,26 +513,29 @@
             anywhere=(1, 2, len(ins), len(ins) + 1),
         )
 
-    images, *strips = model(halfway, strips, True)
+    images, *strips = model(halfway, exchange(strips), True)
     far = [right(images, hops) for hops in range(3, groups)]
 
-    half_next, *strips_next = model(next_probes, pack([next_probes]), False)
-    halfway, *strips = model(images, strips, False)
-    (images_next,) = model(half_next, strips_next, True, True)
-    images_next, far = lax.optimization_barrier((images_next, far))
-    passed = [images, images_next, right(images_next, 1)] + far
-    (second,) = model(halfway, strips, True, True)
-
-    partial = None
-    for n, others in enumerate(passed):
-        (part,) = kernel_call(
-            functools.partial(dots_kernel, n == 0),
-            [f32(count, LANES)],
-            [],
-            [scalars(n), images, second, others],
-            4.0,
-        )
-        partial = part if partial is None else partial + part
+    half_next, *strips_next = model(next_probes, exchange(pack([next_probes])), False)
+    strips, half_next = lax.optimization_barrier((strips, half_next))
+    (images_next,) = model(half_next, exchange(strips_next), True, True)
+    ready, (shifting, far) = images_next, lax.optimization_barrier((images_next, far))
+    passed = [images, images_next, right(shifting, 1)] + far
+
+    received, _ = lax.optimization_barrier((exchange(strips), ready))
+    halfway, *strips = model(images, received, False)
+    (second,) = model(halfway, exchange(strips), True, True)
+
+    slots = len(passed)
+    partial = blocked_call(
+        dots_kernel,
+        f32(count, LANES),
+        False,
+        [pltpu.VMEM((2 * len(dots_pairs(group, slots)), SUB, LANES), jnp.float32)],
+        where,
+        [second] + passed,
+        5.0,
+    )
     inner = all_sum(partial) / ncells
     strict = jnp.tril(jnp.ones((count, count), jnp.float32), -1)
     gram, ritz = inner[:, :count], inner[:, count : 2 * count]
@@ -518,7 +551,7 @@
     for n in range(groups):
         part = lax.dynamic_slice_in_dim(rows, jnp.maximum(mine - n, 0) * group, group, 1)
         parts.append(jnp.where(mine >= n, part, 0.0))
-    (basis,) = kernel_call(basis_kernel, [tile], [], [jnp.concatenate(parts, 1)] + passed, 6.0)
+    basis = blocked_call(basis_kernel, tile, True, [], jnp.concatenate(parts, 1), passed, 4.0)
     return (basis, projected)
 
 

time: 286 us -> 277 us (0.969)
  Pallas kernels: 135 us -> 127 us
    pallas_call x13 -> x8, Pallas kernels: 135 us -> 112 us  [kernel_call(): pl.pallas_call(body, out_shape=outs, in_specs=specs, out_specs=[spec(n, o...]
    pallas_call x0 -> x2, Pallas kernels: none -> 15.1 us  [blocked_call(): pl.pallas_call(body, grid=(x // BLOCK,), out_shape=out_shape, in_specs=[p...]
    ppermute x18, waiting for transfers between devices: 18.4 us -> 30.8 us  [moved(): return lax.ppermute(value, ('sx', 'sy'), pairs)]
    ppermute x3, waiting for transfers between devices: 11.5 us -> 0.01 us  [right(): lax.ppermute(value, 'probe', [(i, i + hops) for i in range(groups - hops)])]
  transfers between devices with their start and end apart: 40 -> 40, of which waited for: 8 -> 12; matrix products, arithmetic and copies ran while one was open for 1% -> 0% of each run, Pallas kernels for 42% -> 39%
where the time goes in v2:
time: 277 us; the launch traced here: 275 us
  Pallas kernels  127 us (46%)
  starting transfers between devices  94.8 us (34%)
  waiting for transfers between devices  40.8 us (15%)
  local copies, waits for them, and re-layouts  5.99 us (2%)
  other arithmetic  4.14 us (1%)
    pallas_call x8, Pallas kernels, kernel_call(): pl.pallas_call(body, out_shape=outs, in_specs=specs, out_specs=[spec(n, o...  112 us
    ppermute x18, starting transfers between devices, moved(): return lax.ppermute(value, ('sx', 'sy'), pairs)  42.6 us
    ppermute x18, waiting for transfers between devices, moved(): return lax.ppermute(value, ('sx', 'sy'), pairs)  30.8 us
    ppermute x6, starting transfers between devices, exchange(): below = lax.ppermute(strips[1], 'sx', up)  23.9 us
    pallas_call x2, Pallas kernels, blocked_call(): pl.pallas_call(body, grid=(x // BLOCK,), out_shape=out_shape, in_specs=[p...  15.1 us
    ppermute x3, starting transfers between devices, right(): lax.ppermute(value, 'probe', [(i, i + hops) for i in range(groups - hops)])  10.8 us
    ppermute x7, waiting for transfers between devices, all_sum(): lax.ppermute(value, axis, [(i, i ^ bits) for i in range(devices)])  9.96 us
    ppermute x7, starting transfers between devices, all_sum(): lax.ppermute(value, axis, [(i, i ^ bits) for i in range(devices)])  9.69 us
  transfers between devices with their start and end apart: 40, of which 12 were waited for; matrix products, arithmetic and copies ran while one was open for 0% of the time, Pallas kernels for 39%

profile of v2, /device:TPU:0, one launch (start us, length us, event | category | flops | bytes accessed | tf_op | source)
XLA Modules:
  0.0 275.4 jit_solution(10720607854798232510)
XLA Ops:
  1.2 4.3 %shard_map.59 = (f32[6,4,32,256]{3,2,1,0:T(8,128)}, f32[6,4,32,256]{3,2,1,0:T(8,128)}, f32[6,16,8,256]{3,2,1,0:T(8,128)}, f32[6,2,8,256]{3,2,1,0:T(8,128)}, f32[6,2,8,256]{3,2,1,0:T(8,128)}) custom-call(s32[2]{0:T(128)} %pad_add_fusion.scalars, f32[1,32,32,256]{3,2,1,0:T(8,128)} %bitcast.25, f32[3,32,32,256]{3,2,1,0:T(8,128)} %velocity.1, ...), custom_call_target="tpu_custom_call" | custom-call | flops 3449999872 | bytes 10800000 | tf_op jit(solution)/shard_map/pallas_call | solution.py:24
  5.5 2.4 collective-permute-start
  7.9 1.3 collective-permute-start.1
  9.2 2.5 collective-permute-start.2
  11.7 3.6 %collective-permute-start.10 = (f32[2,32,32,256]{3,2,1,0:T(8,128)S(1)}, f32[2,32,32,256]{3,2,1,0:T(8,128)S(1)}, u32[]{:S(2)}, u32[]{:S(2)}) collective-permute-start(f32[2,32,32,256]{3,2,1,0:T(8,128)S(1)} %copy-done), channel_id=1, source_target_pairs={{0,8},{8,16},{16,24},{1,9},{9,17},{17,25},{2,10},{10,18},{18,26},{... | collective-permute-start | bytes 6291464 | tf_op jit(solution)/shard_map/ppermute | solution.py:490
  15.3 3.8 %collective-permute-start.3 = (f32[6,2,8,256]{3,2,1,0:T(8,128)}, f32[6,2,8,256]{3,2,1,0:T(8,128)S(1)}, u32[]{:S(2)}, u32[]{:S(2)}) collective-permute-start(f32[6,2,8,256]{3,2,1,0:T(8,128)} %get-tuple-element.53), channel_id=1, source_target_pairs={{0,3},{1,2},{2,5},{3,4},{4,7},{5,6},{8,11},{9,10},{10,13},{11,12},... | collective-permute-start | bytes 294920 | tf_op jit(solution)/shard_map/ppermute | solution.py:99
  19.0 11.5 %collective-permute-done.3.refs_3_ = f32[6,2,8,256]{3,2,1,0:T(8,128)S(1)} collective-permute-done((f32[6,2,8,256]{3,2,1,0:T(8,128)}, f32[6,2,8,256]{3,2,1,0:T(8,128)S(1)}, u32[]{:S(2)}, u32[]{:S(2)}) %collective-permute-start.3) | collective-permute-done | bytes 98336 | tf_op jit(solution)/shard_map/ppermute | solution.py:99
  30.6 1.3 collective-permute-start.4
  31.9 4.9 %collective-permute-done.4.refs_4_ = f32[6,2,8,256]{3,2,1,0:T(8,128)S(1)} collective-permute-done((f32[6,2,8,256]{3,2,1,0:T(8,128)}, f32[6,2,8,256]{3,2,1,0:T(8,128)S(1)}, u32[]{:S(2)}, u32[]{:S(2)}) %collective-permute-start.4) | collective-permute-done | bytes 98336 | tf_op jit(solution)/shard_map/ppermute | solution.py:99
  37.9 18.4 %shard_map.60 = (f32[7,40,40,256]{3,2,1,0:T(8,128)}, f32[2,32,32,256]{3,2,1,0:T(8,128)}, f32[2,4,32,256]{3,2,1,0:T(8,128)}, f32[2,4,32,256]{3,2,1,0:T(8,128)}, f...) custom-call(s32[2]{0:T(128)} %pad_add_fusion.scalars, f32[1,32,32,256]{3,2,1,0:T(8,128)} %bitcast.26, ...), custom_call_target="tpu_custom_call" | custom-call | flops 16099999744 | bytes 50400000 | tf_op jit(solution)/shard_map/pallas_call | solution.py:24
  56.3 3.4 %collective-permute-start.5 = (f32[2,4,32,256]{3,2,1,0:T(8,128)}, f32[2,4,32,256]{3,2,1,0:T(8,128)S(1)}, u32[]{:S(2)}, u32[]{:S(2)}) collective-permute-start(f32[2,4,32,256]{3,2,1,0:T(8,128)} %get-tuple-element.57), channel_id=1, source_target_pairs={{0,2},{2,4},{4,6},{1,3},{3,5},{5,7},{8,10},{10,12},{12,14},{9,11},... | collective-permute-start | bytes 786440 | tf_op jit(solution)/shard_map/ppermute | solution.py:101
  59.7 1.3 collective-permute-start.6
  61.0 1.6 collective-permute-start.7
  62.7 4.1 %collective-permute-start.8 = (f32[2,2,8,256]{3,2,1,0:T(8,128)}, f32[2,2,8,256]{3,2,1,0:T(8,128)S(1)}, u32[]{:S(2)}, u32[]{:S(2)}) collective-permute-start(f32[2,2,8,256]{3,2,1,0:T(8,128)} %get-tuple-element.60), channel_id=1, source_target_pairs={{0,3},{1,2},{2,5},{3,4},{4,7},{5,6},{8,11},{9,10},{10,13},{11,12},... | collective-permute-start | bytes 98312 | tf_op jit(solution)/shard_map/ppermute | solution.py:99
  66.8 1.3 collective-permute-start.9
  68.1 2.8 %shard_map.62 = (f32[2,4,32,256]{3,2,1,0:T(8,128)}, f32[2,4,32,256]{3,2,1,0:T(8,128)}, f32[2,16,8,256]{3,2,1,0:T(8,128)}, f32[2,2,8,256]{3,2,1,0:T(8,128)}, f32[2,2,8,256]{3,2,1,0:T(8,128)}) custom-call(s32[2]{0:T(128)} %pad_add_fusion.scalars, f32[2,32,32,256]{3,2,1,0:T(8,128)} %copy-done.3), custom_call_target="tpu_custom_call" | custom-call | flops 3449999872 | bytes 10800000 | tf_op jit(solution)/shard_map/pallas_call | solution.py:24
  71.0 4.4 %collective-permute-start.11 = (f32[2,4,32,256]{3,2,1,0:T(8,128)}, f32[2,4,32,256]{3,2,1,0:T(8,128)S(1)}, u32[]{:S(2)}, u32[]{:S(2)}) collective-permute-start(f32[2,4,32,256]{3,2,1,0:T(8,128)} %get-tuple-element.68), channel_id=1, source_target_pairs={{0,2},{2,4},{4,6},{1,3},{3,5},{5,7},{8,10},{10,12},{12,14},{9,11},... | collective-permute-start | bytes 786440 | tf_op jit(solution)/shard_map/ppermute | solution.py:101
  75.4 1.3 collective-permute-start.12
  77.3 5.1 %collective-permute-start.14 = (f32[2,2,8,256]{3,2,1,0:T(8,128)}, f32[2,2,8,256]{3,2,1,0:T(8,128)S(1)}, u32[]{:S(2)}, u32[]{:S(2)}) collective-permute-start(f32[2,2,8,256]{3,2,1,0:T(8,128)} %get-tuple-element.71), channel_id=1, source_target_pairs={{0,3},{1,2},{2,5},{3,4},{4,7},{5,6},{8,11},{9,10},{10,13},{11,12},... | collective-permute-start | bytes 98312 | tf_op jit(solution)/shard_map/ppermute | solution.py:99
  82.4 1.3 collective-permute-start.15
  83.7 17.6 %shard_map.61 = (f32[2,32,32,256]{3,2,1,0:T(8,128)}, f32[2,4,32,256]{3,2,1,0:T(8,128)}, f32[2,4,32,256]{3,2,1,0:T(8,128)}, f32[2,16,8,256]{3,2,1,0:T(8,128)}, f3...) custom-call(s32[2]{0:T(128)} %pad_add_fusion.scalars, f32[7,40,40,256]{3,2,1,0:T(8,128)} %get-tuple-element.55.coef_in, ...), custom_call_target="tpu_custom_call" | custom-call | flops 13799999488 | bytes 43200000 | tf_op jit(solution)/shard_map/pallas_call | solution.py:24
  101.4 5.8 %collective-permute-start.31 = (f32[2,32,32,256]{3,2,1,0:T(8,128)}, f32[2,32,32,256]{3,2,1,0:T(8,128)S(1)}, u32[]{:S(2)}, u32[]{:S(2)}) collective-permute-start(f32[2,32,32,256]{3,2,1,0:T(8,128)} %get-tuple-element.62.tile.refs_0_), channel_id=1, source_target_pairs={{0,24},{1,25},{2,26},{3,27},{4,28},{5,29},{6,30},{7,31}} | collective-permute-start | bytes 6291464 | tf_op jit(solution)/shard_map/ppermute | solution.py:490
  108.0 0.7 copy-done.14
  108.7 17.2 %shard_map.63 = (f32[2,32,32,256]{3,2,1,0:T(8,128)}, f32[2,4,32,256]{3,2,1,0:T(8,128)}, f32[2,4,32,256]{3,2,1,0:T(8,128)}, f32[2,16,8,256]{3,2,1,0:T(8,128)}, f3...) custom-call(s32[2]{0:T(128)} %pad_add_fusion.scalars, f32[7,40,40,256]{3,2,1,0:T(8,128)} %get-tuple-element.55.coef_in, ...), custom_call_target="tpu_custom_call" | custom-call | flops 13799999488 | bytes 43200000 | tf_op jit(solution)/shard_map/pallas_call | solution.py:24
  125.9 4.1 %collective-permute-start.21 = (f32[2,4,32,256]{3,2,1,0:T(8,128)}, f32[2,4,32,256]{3,2,1,0:T(8,128)S(1)}, u32[]{:S(2)}, u32[]{:S(2)}) collective-permute-start(f32[2,4,32,256]{3,2,1,0:T(8,128)} %get-tuple-element.80), channel_id=1, source_target_pairs={{0,2},{2,4},{4,6},{1,3},{3,5},{5,7},{8,10},{10,12},{12,14},{9,11},... | collective-permute-start | bytes 786440 | tf_op jit(solution)/shard_map/ppermute | solution.py:101
  130.0 1.3 collective-permute-start.22
  131.3 1.6 collective-permute-start.23
  132.9 5.3 %collective-permute-start.19 = (f32[2,2,8,256]{3,2,1,0:T(8,128)S(1)}, f32[2,2,8,256]{3,2,1,0:T(8,128)S(1)}, u32[]{:S(2)}, u32[]{:S(2)}) collective-permute-start(f32[2,2,8,256]{3,2,1,0:T(8,128)S(1)} %copy-done.29), channel_id=1, source_target_pairs={{0,3},{1,2},{2,5},{3,4},{4,7},{5,6},{8,11},{9,10},{10,13},{11,12},... | collective-permute-start | bytes 98312 | tf_op jit(solution)/shard_map/ppermute | solution.py:99
  138.2 1.8 collective-permute-done.19.refs_4_
  140.0 3.8 %collective-permute-start.24 = (f32[2,2,8,256]{3,2,1,0:T(8,128)}, f32[2,2,8,256]{3,2,1,0:T(8,128)S(1)}, u32[]{:S(2)}, u32[]{:S(2)}) collective-permute-start(f32[2,2,8,256]{3,2,1,0:T(8,128)} %get-tuple-element.83), channel_id=1, source_target_pairs={{0,3},{1,2},{2,5},{3,4},{4,7},{5,6},{8,11},{9,10},{10,13},{11,12},... | collective-permute-start | bytes 98312 | tf_op jit(solution)/shard_map/ppermute | solution.py:99
  143.9 1.9 collective-permute-done.24.refs_3_
  145.8 1.3 collective-permute-start.25
  147.0 4.4 %collective-permute-done.25.refs_4_ = f32[2,2,8,256]{3,2,1,0:T(8,128)S(1)} collective-permute-done((f32[2,2,8,256]{3,2,1,0:T(8,128)}, f32[2,2,8,256]{3,2,1,0:T(8,128)S(1)}, u32[]{:S(2)}, u32[]{:S(2)}) %collective-permute-start.25) | collective-permute-done | bytes 32800 | tf_op jit(solution)/shard_map/ppermute | solution.py:99
  151.4 4.9 %collective-permute-start.16 = (f32[2,4,32,256]{3,2,1,0:T(8,128)S(1)}, f32[2,4,32,256]{3,2,1,0:T(8,128)S(1)}, u32[]{:S(2)}, u32[]{:S(2)}) collective-permute-start(f32[2,4,32,256]{3,2,1,0:T(8,128)S(1)} %copy-done.8), channel_id=1, source_target_pairs={{0,2},{2,4},{4,6},{1,3},{3,5},{5,7},{8,10},{10,12},{12,14},{9,11},... | collective-permute-start | bytes 786440 | tf_op jit(solution)/shard_map/ppermute | solution.py:101
  156.4 1.3 collective-permute-start.17
  158.3 1.3 collective-permute-start.20
  159.6 17.2 %shard_map.64.refs_1_ = f32[2,32,32,256]{3,2,1,0:T(8,128)} custom-call(s32[2]{0:T(128)} %pad_add_fusion.scalars, f32[7,40,40,256]{3,2,1,0:T(8,128)} %get-tuple-element.55.coef_in, f32[2,32,32,256]{3,2,1,0:T(8,128)} %get-tuple-element.79.tile, f32[2,4,32,256]{3,2,1,0:T(8,128)} %copy-done.15, f32[2,4,32,256]{3,2,1,0:T(8,128)} %copy-done.17, ...), custom_call_target="tpu_custom_call" | custom-call | flops 13799999488 | bytes 43200000 | tf_op jit(solution)/shard_map/pallas_call | solution.py:24
  176.9 1.4 collective-permute-start.32
  178.4 17.2 %shard_map.65 = (f32[2,32,32,256]{3,2,1,0:T(8,128)}, f32[2,4,32,256]{3,2,1,0:T(8,128)}, f32[2,4,32,256]{3,2,1,0:T(8,128)}, f32[2,16,8,256]{3,2,1,0:T(8,128)}, f3...) custom-call(s32[2]{0:T(128)} %pad_add_fusion.scalars, f32[7,40,40,256]{3,2,1,0:T(8,128)} %get-tuple-element.55.coef_in, ...), custom_call_target="tpu_custom_call" | custom-call | flops 13799999488 | bytes 43200000 | tf_op jit(solution)/shard_map/pallas_call | solution.py:24
  195.6 4.7 %collective-permute-start.26 = (f32[2,4,32,256]{3,2,1,0:T(8,128)}, f32[2,4,32,256]{3,2,1,0:T(8,128)S(1)}, u32[]{:S(2)}, u32[]{:S(2)}) collective-permute-start(f32[2,4,32,256]{3,2,1,0:T(8,128)} %get-tuple-element.91), channel_id=1, source_target_pairs={{0,2},{2,4},{4,6},{1,3},{3,5},{5,7},{8,10},{10,12},{12,14},{9,11},... | collective-permute-start | bytes 786440 | tf_op jit(solution)/shard_map/ppermute | solution.py:101
  200.3 1.3 collective-permute-start.27
  202.2 5.4 %collective-permute-start.29 = (f32[2,2,8,256]{3,2,1,0:T(8,128)}, f32[2,2,8,256]{3,2,1,0:T(8,128)S(1)}, u32[]{:S(2)}, u32[]{:S(2)}) collective-permute-start(f32[2,2,8,256]{3,2,1,0:T(8,128)} %get-tuple-element.94), channel_id=1, source_target_pairs={{0,3},{1,2},{2,5},{3,4},{4,7},{5,6},{8,11},{9,10},{10,13},{11,12},... | collective-permute-start | bytes 98312 | tf_op jit(solution)/shard_map/ppermute | solution.py:99
  207.5 2.0 collective-permute-done.29.refs_3_
  209.5 1.5 collective-permute-start.30
  211.0 4.2 %collective-permute-done.30.refs_4_ = f32[2,2,8,256]{3,2,1,0:T(8,128)S(1)} collective-permute-done((f32[2,2,8,256]{3,2,1,0:T(8,128)}, f32[2,2,8,256]{3,2,1,0:T(8,128)S(1)}, u32[]{:S(2)}, u32[]{:S(2)}) %collective-permute-start.30) | collective-permute-done | bytes 32800 | tf_op jit(solution)/shard_map/ppermute | solution.py:99
  216.1 17.2 %shard_map.66.second = f32[2,32,32,256]{3,2,1,0:T(8,128)} custom-call(s32[2]{0:T(128)} %pad_add_fusion.scalars, f32[7,40,40,256]{3,2,1,0:T(8,128)} %get-tuple-element.55.coef_in, f32[2,32,32,256]{3,2,1,0:T(8,128)} %get-tuple-element.90.tile, f32[2,4,32,256]{3,2,1,0:T(8,128)} %copy-done.21, f32[2,4,32,256]{3,2,1,0:T(8,128)} %copy-done.22, ...), custom_call_target="tpu_custom_call" | custom-call | flops 13799999488 | bytes 43200000 | tf_op jit(solution)/shard_map/pallas_call | solution.py:24
  233.3 1.3 copy-done.2
  234.6 7.8 %shard_map.67 = f32[8,128]{1,0:T(8,128)} custom-call(s32[2]{0:T(128)} %pad_add_fusion.scalars, f32[2,32,32,256]{3,2,1,0:T(8,128)} %shard_map.66.second, f32[2,32,32,256]{3,2,1,0:T(8,128)} %get-tuple-element.62.tile.refs_0_, f32[2,32,32,256]{3,2,1,0:T(8,128)} %shard_map.64.refs_1_, f32[2,32,32,256]{3,2,1,0:T(8,128)} %copy-done.2, f32[2,32,32,256]{3,2,1,0:T(8,128)} %copy-done.1), custom_call_target="tpu_custom_call" | custom-call | flops 5750000128 | bytes 18000000 | tf_op jit(solution)/shard_map/pallas_call | solution.py:350
  242.4 0.8 copy.18
  243.2 3.9 %collective-permute-start.34 = (f32[8,128]{0,1:T(8,128)S(1)}, f32[8,128]{0,1:T(8,128)S(1)}, u32[]{:S(2)}, u32[]{:S(2)}) collective-permute-start(f32[8,128]{0,1:T(8,128)S(1)} %copy.18), channel_id=1, source_target_pairs={{0,4},{2,6},{4,0},{6,2},{1,5},{3,7},{5,1},{7,3},{8,12},{10,14},{12... | collective-permute-start | bytes 12296 | tf_op jit(solution)/shard_map/ppermute | solution.py:441
  247.3 2.4 collective-permute-done.34
  249.7 1.4 collective-permute-done.35
  251.1 1.2 collective-permute-start.36
  252.3 3.1 %collective-permute-done.36 = f32[8,128]{0,1:T(8,128)S(1)} collective-permute-done((f32[8,128]{0,1:T(8,128)S(1)}, f32[8,128]{0,1:T(8,128)S(1)}, u32[]{:S(2)}, u32[]{:S(2)}) %collective-permute-start.36) | collective-permute-done | bytes 4128 | tf_op jit(solution)/shard_map/ppermute | solution.py:441
  255.9 4.0 %collective-permute-start.39 = (f32[8,128]{0,1:T(8,128)S(1)}, f32[8,128]{0,1:T(8,128)S(1)}, u32[]{:S(2)}, u32[]{:S(2)}) collective-permute-start(f32[8,128]{0,1:T(8,128)S(1)} %add.79), channel_id=1, source_target_pairs={{0,24},{8,16},{16,8},{24,0},{1,25},{9,17},{17,9},{25,1},{2,26},{10... | collective-permute-start | bytes 12296 | tf_op jit(solution)/shard_map/ppermute | solution.py:441
  260.0 1.5 collective-permute-done.38
  261.5 1.5 collective-permute-done.39
  263.3 0.7 cholesky.16
  264.1 0.6 compare_reduce_fusion
  264.8 0.6 fusion
  265.4 0.6 custom-call.7
  266.5 0.7 fusion.17
  267.3 0.7 pad_maximum_fusion.inverse
  268.0 7.4 %shard_map.68 = f32[2,32,32,256]{3,2,1,0:T(8,128)} custom-call(f32[2,8]{1,0:T(2,128)} %pad_maximum_fusion.inverse, f32[2,32,32,256]{3,2,1,0:T(8,128)} %get-tuple-element.62.tile.refs_0_, f32[2,32,32,256]{3,2,1,0:T(8,128)} %shard_map.64.refs_1_, f32[2,32,32,256]{3,2,1,0:T(8,128)} %copy-done.2, f32[2,32,32,256]{3,2,1,0:T(8,128)} %copy-done.1), custom_call_target="tpu_custom_call" | custom-call | flops 4600000000 | bytes 14400000 | tf_op jit(solution)/shard_map/pallas_call | solution.py:350
  (128 shorter events, 6.8 us)
Async XLA Ops:
  1.2 10.4 %copy-start = (f32[2,32,32,256]{3,2,1,0:T(8,128)S(1)}, f32[2,32,32,256]{3,2,1,0:T(8,128)}, u32[]{:S(2)}) copy-start(f32[2,32,32,256]{3,2,1,0:T(8,128)} %probes.1) | copy-start | bytes 6291460
  5.5 31.3 %collective-permute-start = (f32[6,4,32,256]{3,2,1,0:T(8,128)}, f32[6,4,32,256]{3,2,1,0:T(8,128)S(1)}, u32[]{:S(2)}, u32[]{:S(2)}) collective-permute-start(f32[6,4,32,256]{3,2,1,0:T(8,128)} %get-tuple-element.50), channel_id=1, source_target_pairs={{0,2},{2,4},{4,6},{1,3},{3,5},{5,7},{8,10},{10,12},{12,14},{9,11},... | collective-permute-start | bytes 2359304 | tf_op jit(solution)/shard_map/ppermute | solution.py:101
  7.9 28.9 %collective-permute-start.1 = (f32[6,4,32,256]{3,2,1,0:T(8,128)}, f32[6,4,32,256]{3,2,1,0:T(8,128)S(1)}, u32[]{:S(2)}, u32[]{:S(2)}) collective-permute-start(f32[6,4,32,256]{3,2,1,0:T(8,128)} %get-tuple-element.51), channel_id=1, source_target_pairs={{2,0},{4,2},{6,4},{3,1},{5,3},{7,5},{10,8},{12,10},{14,12},{11,9},... | collective-permute-start | bytes 2359304 | tf_op jit(solution)/shard_map/ppermute | solution.py:102
  9.2 27.6 %collective-permute-start.2 = (f32[6,16,8,256]{3,2,1,0:T(8,128)}, f32[6,16,8,256]{3,2,1,0:T(8,128)}, u32[]{:S(2)}, u32[]{:S(2)}) collective-permute-start(f32[6,16,8,256]{3,2,1,0:T(8,128)} %get-tuple-element.52), channel_id=1, source_target_pairs={{0,1},{1,0},{2,3},{3,2},{4,5},{5,4},{6,7},{7,6},{8,9},{9,8},{10,11... | collective-permute-start | bytes 2359304 | tf_op jit(solution)/shard_map/ppermute | solution.py:99
  11.7 55.2 %collective-permute-start.10 = (f32[2,32,32,256]{3,2,1,0:T(8,128)S(1)}, f32[2,32,32,256]{3,2,1,0:T(8,128)S(1)}, u32[]{:S(2)}, u32[]{:S(2)}) collective-permute-start(f32[2,32,32,256]{3,2,1,0:T(8,128)S(1)} %copy-done), channel_id=1, source_target_pairs={{0,8},{8,16},{16,24},{1,9},{9,17},{17,25},{2,10},{10,18},{18,26},{... | collective-permute-start | bytes 6291464 | tf_op jit(solution)/shard_map/ppermute | solution.py:490
  15.3 15.3 %collective-permute-start.3 = (f32[6,2,8,256]{3,2,1,0:T(8,128)}, f32[6,2,8,256]{3,2,1,0:T(8,128)S(1)}, u32[]{:S(2)}, u32[]{:S(2)}) collective-permute-start(f32[6,2,8,256]{3,2,1,0:T(8,128)} %get-tuple-element.53), channel_id=1, source_target_pairs={{0,3},{1,2},{2,5},{3,4},{4,7},{5,6},{8,11},{9,10},{10,13},{11,12},... | collective-permute-start | bytes 294920 | tf_op jit(solution)/shard_map/ppermute | solution.py:99
  30.6 6.2 %copy-start.24 = (f32[6,2,8,256]{3,2,1,0:T(8,128)}, f32[6,2,8,256]{3,2,1,0:T(8,128)S(1)}, u32[]{:S(2)}) copy-start(f32[6,2,8,256]{3,2,1,0:T(8,128)S(1)} %collective-permute-done.3.refs_3_) | copy-start | bytes 294916
  30.6 6.2 %collective-permute-start.4 = (f32[6,2,8,256]{3,2,1,0:T(8,128)}, f32[6,2,8,256]{3,2,1,0:T(8,128)S(1)}, u32[]{:S(2)}, u32[]{:S(2)}) collective-permute-start(f32[6,2,8,256]{3,2,1,0:T(8,128)} %get-tuple-element.54), channel_id=1, source_target_pairs={{2,1},{3,0},{4,3},{5,2},{6,5},{7,4},{10,9},{11,8},{12,11},{13,10},... | collective-permute-start | bytes 294920 | tf_op jit(solution)/shard_map/ppermute | solution.py:99
  56.3 20.4 %collective-permute-start.5 = (f32[2,4,32,256]{3,2,1,0:T(8,128)}, f32[2,4,32,256]{3,2,1,0:T(8,128)S(1)}, u32[]{:S(2)}, u32[]{:S(2)}) collective-permute-start(f32[2,4,32,256]{3,2,1,0:T(8,128)} %get-tuple-element.57), channel_id=1, source_target_pairs={{0,2},{2,4},{4,6},{1,3},{3,5},{5,7},{8,10},{10,12},{12,14},{9,11},... | collective-permute-start | bytes 786440 | tf_op jit(solution)/shard_map/ppermute | solution.py:101
  59.7 17.5 %collective-permute-start.6 = (f32[2,4,32,256]{3,2,1,0:T(8,128)}, f32[2,4,32,256]{3,2,1,0:T(8,128)S(1)}, u32[]{:S(2)}, u32[]{:S(2)}) collective-permute-start(f32[2,4,32,256]{3,2,1,0:T(8,128)} %get-tuple-element.58), channel_id=1, source_target_pairs={{2,0},{4,2},{6,4},{3,1},{5,3},{7,5},{10,8},{12,10},{14,12},{11,9},... | collective-permute-start | bytes 786440 | tf_op jit(solution)/shard_map/ppermute | solution.py:102
  61.0 21.3 %collective-permute-start.7 = (f32[2,16,8,256]{3,2,1,0:T(8,128)}, f32[2,16,8,256]{3,2,1,0:T(8,128)S(1)}, u32[]{:S(2)}, u32[]{:S(2)}) collective-permute-start(f32[2,16,8,256]{3,2,1,0:T(8,128)} %get-tuple-element.59), channel_id=1, source_target_pairs={{0,1},{1,0},{2,3},{3,2},{4,5},{5,4},{6,7},{7,6},{8,9},{9,8},{10,11... | collective-permute-start | bytes 786440 | tf_op jit(solution)/shard_map/ppermute | solution.py:99
  62.7 8.3 %collective-permute-start.8 = (f32[2,2,8,256]{3,2,1,0:T(8,128)}, f32[2,2,8,256]{3,2,1,0:T(8,128)S(1)}, u32[]{:S(2)}, u32[]{:S(2)}) collective-permute-start(f32[2,2,8,256]{3,2,1,0:T(8,128)} %get-tuple-element.60), channel_id=1, source_target_pairs={{0,3},{1,2},{2,5},{3,4},{4,7},{5,6},{8,11},{9,10},{10,13},{11,12},... | collective-permute-start | bytes 98312 | tf_op jit(solution)/shard_map/ppermute | solution.py:99
  66.8 8.6 %collective-permute-start.9 = (f32[2,2,8,256]{3,2,1,0:T(8,128)}, f32[2,2,8,256]{3,2,1,0:T(8,128)S(1)}, u32[]{:S(2)}, u32[]{:S(2)}) collective-permute-start(f32[2,2,8,256]{3,2,1,0:T(8,128)} %get-tuple-element.61), channel_id=1, source_target_pairs={{2,1},{3,0},{4,3},{5,2},{6,5},{7,4},{10,9},{11,8},{12,11},{13,10},... | collective-permute-start | bytes 98312 | tf_op jit(solution)/shard_map/ppermute | solution.py:99
  71.0 12.7 %copy-start.28 = (f32[2,2,8,256]{3,2,1,0:T(8,128)}, f32[2,2,8,256]{3,2,1,0:T(8,128)S(1)}, u32[]{:S(2)}) copy-start(f32[2,2,8,256]{3,2,1,0:T(8,128)S(1)} %collective-permute-done.8.refs_3_) | copy-start | bytes 98308
  71.0 36.2 %collective-permute-start.11 = (f32[2,4,32,256]{3,2,1,0:T(8,128)}, f32[2,4,32,256]{3,2,1,0:T(8,128)S(1)}, u32[]{:S(2)}, u32[]{:S(2)}) collective-permute-start(f32[2,4,32,256]{3,2,1,0:T(8,128)} %get-tuple-element.68), channel_id=1, source_target_pairs={{0,2},{2,4},{4,6},{1,3},{3,5},{5,7},{8,10},{10,12},{12,14},{9,11},... | collective-permute-start | bytes 786440 | tf_op jit(solution)/shard_map/ppermute | solution.py:101
  75.4 8.2 %copy-start.30 = (f32[2,2,8,256]{3,2,1,0:T(8,128)}, f32[2,2,8,256]{3,2,1,0:T(8,128)S(1)}, u32[]{:S(2)}) copy-start(f32[2,2,8,256]{3,2,1,0:T(8,128)S(1)} %collective-permute-done.9.refs_4_) | copy-start | bytes 98308
  75.4 31.8 %collective-permute-start.12 = (f32[2,4,32,256]{3,2,1,0:T(8,128)}, f32[2,4,32,256]{3,2,1,0:T(8,128)S(1)}, u32[]{:S(2)}, u32[]{:S(2)}) collective-permute-start(f32[2,4,32,256]{3,2,1,0:T(8,128)} %get-tuple-element.69), channel_id=1, source_target_pairs={{2,0},{4,2},{6,4},{3,1},{5,3},{7,5},{10,8},{12,10},{14,12},{11,9},... | collective-permute-start | bytes 786440 | tf_op jit(solution)/shard_map/ppermute | solution.py:102
  76.7 6.9 %copy-start.10 = (f32[2,4,32,256]{3,2,1,0:T(8,128)}, f32[2,4,32,256]{3,2,1,0:T(8,128)S(1)}, u32[]{:S(2)}) copy-start(f32[2,4,32,256]{3,2,1,0:T(8,128)S(1)} %collective-permute-done.5.refs_0_) | copy-start | bytes 786436
  76.8 30.5 %collective-permute-start.13 = (f32[2,16,8,256]{3,2,1,0:T(8,128)}, f32[2,16,8,256]{3,2,1,0:T(8,128)S(1)}, u32[]{:S(2)}, u32[]{:S(2)}) collective-permute-start(f32[2,16,8,256]{3,2,1,0:T(8,128)} %get-tuple-element.70), channel_id=1, source_target_pairs={{0,1},{1,0},{2,3},{3,2},{4,5},{5,4},{6,7},{7,6},{8,9},{9,8},{10,11... | collective-permute-start | bytes 786440 | tf_op jit(solution)/shard_map/ppermute | solution.py:99
  77.2 6.4 %copy-start.11 = (f32[2,4,32,256]{3,2,1,0:T(8,128)}, f32[2,4,32,256]{3,2,1,0:T(8,128)S(1)}, u32[]{:S(2)}) copy-start(f32[2,4,32,256]{3,2,1,0:T(8,128)S(1)} %collective-permute-done.6.refs_1_) | copy-start | bytes 786436
  77.3 24.1 %collective-permute-start.14 = (f32[2,2,8,256]{3,2,1,0:T(8,128)}, f32[2,2,8,256]{3,2,1,0:T(8,128)S(1)}, u32[]{:S(2)}, u32[]{:S(2)}) collective-permute-start(f32[2,2,8,256]{3,2,1,0:T(8,128)} %get-tuple-element.71), channel_id=1, source_target_pairs={{0,3},{1,2},{2,5},{3,4},{4,7},{5,6},{8,11},{9,10},{10,13},{11,12},... | collective-permute-start | bytes 98312 | tf_op jit(solution)/shard_map/ppermute | solution.py:99
  82.3 1.4 copy-start.13
  82.4 24.8 %collective-permute-start.15 = (f32[2,2,8,256]{3,2,1,0:T(8,128)}, f32[2,2,8,256]{3,2,1,0:T(8,128)S(1)}, u32[]{:S(2)}, u32[]{:S(2)}) collective-permute-start(f32[2,2,8,256]{3,2,1,0:T(8,128)} %get-tuple-element.72), channel_id=1, source_target_pairs={{2,1},{3,0},{4,3},{5,2},{6,5},{7,4},{10,9},{11,8},{12,11},{13,10},... | collective-permute-start | bytes 98312 | tf_op jit(solution)/shard_map/ppermute | solution.py:99
  101.3 5.9 %copy-start.31 = (f32[2,2,8,256]{3,2,1,0:T(8,128)}, f32[2,2,8,256]{3,2,1,0:T(8,128)S(1)}, u32[]{:S(2)}) copy-start(f32[2,2,8,256]{3,2,1,0:T(8,128)S(1)} %collective-permute-done.14.refs_4_) | copy-start | bytes 98308
  101.4 31.5 %copy-start.29 = (f32[2,2,8,256]{3,2,1,0:T(8,128)S(1)}, f32[2,2,8,256]{3,2,1,0:T(8,128)}, u32[]{:S(2)}) copy-start(f32[2,2,8,256]{3,2,1,0:T(8,128)} %get-tuple-element.77) | copy-start | bytes 98308
  101.4 50.1 %copy-start.8 = (f32[2,4,32,256]{3,2,1,0:T(8,128)S(1)}, f32[2,4,32,256]{3,2,1,0:T(8,128)}, u32[]{:S(2)}) copy-start(f32[2,4,32,256]{3,2,1,0:T(8,128)} %get-tuple-element.74) | copy-start | bytes 786436
  101.4 55.0 %copy-start.7 = (f32[2,4,32,256]{3,2,1,0:T(8,128)S(1)}, f32[2,4,32,256]{3,2,1,0:T(8,128)}, u32[]{:S(2)}) copy-start(f32[2,4,32,256]{3,2,1,0:T(8,128)} %get-tuple-element.75) | copy-start | bytes 786436
  101.4 56.3 %copy-start.6 = (f32[2,16,8,256]{3,2,1,0:T(8,128)S(1)}, f32[2,16,8,256]{3,2,1,0:T(8,128)}, u32[]{:S(2)}) copy-start(f32[2,16,8,256]{3,2,1,0:T(8,128)} %get-tuple-element.76) | copy-start | bytes 786436
  101.4 56.9 %copy-start.26 = (f32[2,2,8,256]{3,2,1,0:T(8,128)S(1)}, f32[2,2,8,256]{3,2,1,0:T(8,128)}, u32[]{:S(2)}) copy-start(f32[2,2,8,256]{3,2,1,0:T(8,128)} %get-tuple-element.78) | copy-start | bytes 98308
  101.4 75.5 %collective-permute-start.31 = (f32[2,32,32,256]{3,2,1,0:T(8,128)}, f32[2,32,32,256]{3,2,1,0:T(8,128)S(1)}, u32[]{:S(2)}, u32[]{:S(2)}) collective-permute-start(f32[2,32,32,256]{3,2,1,0:T(8,128)} %get-tuple-element.62.tile.refs_0_), channel_id=1, source_target_pairs={{0,24},{1,25},{2,26},{3,27},{4,28},{5,29},{6,30},{7,31}} | collective-permute-start | bytes 6291464 | tf_op jit(solution)/shard_map/ppermute | solution.py:490
  125.9 30.5 %collective-permute-start.21 = (f32[2,4,32,256]{3,2,1,0:T(8,128)}, f32[2,4,32,256]{3,2,1,0:T(8,128)S(1)}, u32[]{:S(2)}, u32[]{:S(2)}) collective-permute-start(f32[2,4,32,256]{3,2,1,0:T(8,128)} %get-tuple-element.80), channel_id=1, source_target_pairs={{0,2},{2,4},{4,6},{1,3},{3,5},{5,7},{8,10},{10,12},{12,14},{9,11},... | collective-permute-start | bytes 786440 | tf_op jit(solution)/shard_map/ppermute | solution.py:101
  130.0 27.7 %collective-permute-start.22 = (f32[2,4,32,256]{3,2,1,0:T(8,128)}, f32[2,4,32,256]{3,2,1,0:T(8,128)S(1)}, u32[]{:S(2)}, u32[]{:S(2)}) collective-permute-start(f32[2,4,32,256]{3,2,1,0:T(8,128)} %get-tuple-element.81), channel_id=1, source_target_pairs={{2,0},{4,2},{6,4},{3,1},{5,3},{7,5},{10,8},{12,10},{14,12},{11,9},... | collective-permute-start | bytes 786440 | tf_op jit(solution)/shard_map/ppermute | solution.py:102
  131.3 27.0 %collective-permute-start.23 = (f32[2,16,8,256]{3,2,1,0:T(8,128)}, f32[2,16,8,256]{3,2,1,0:T(8,128)S(1)}, u32[]{:S(2)}, u32[]{:S(2)}) collective-permute-start(f32[2,16,8,256]{3,2,1,0:T(8,128)} %get-tuple-element.82), channel_id=1, source_target_pairs={{0,1},{1,0},{2,3},{3,2},{4,5},{5,4},{6,7},{7,6},{8,9},{9,8},{10,11... | collective-permute-start | bytes 786440 | tf_op jit(solution)/shard_map/ppermute | solution.py:99
  132.9 7.1 %collective-permute-start.19 = (f32[2,2,8,256]{3,2,1,0:T(8,128)S(1)}, f32[2,2,8,256]{3,2,1,0:T(8,128)S(1)}, u32[]{:S(2)}, u32[]{:S(2)}) collective-permute-start(f32[2,2,8,256]{3,2,1,0:T(8,128)S(1)} %copy-done.29), channel_id=1, source_target_pairs={{0,3},{1,2},{2,5},{3,4},{4,7},{5,6},{8,11},{9,10},{10,13},{11,12},... | collective-permute-start | bytes 98312 | tf_op jit(solution)/shard_map/ppermute | solution.py:99
  140.0 36.8 %copy-start.27 = (f32[2,2,8,256]{3,2,1,0:T(8,128)}, f32[2,2,8,256]{3,2,1,0:T(8,128)S(1)}, u32[]{:S(2)}) copy-start(f32[2,2,8,256]{3,2,1,0:T(8,128)S(1)} %collective-permute-done.19.refs_4_) | copy-start | bytes 98308
  140.0 5.7 %collective-permute-start.24 = (f32[2,2,8,256]{3,2,1,0:T(8,128)}, f32[2,2,8,256]{3,2,1,0:T(8,128)S(1)}, u32[]{:S(2)}, u32[]{:S(2)}) collective-permute-start(f32[2,2,8,256]{3,2,1,0:T(8,128)} %get-tuple-element.83), channel_id=1, source_target_pairs={{0,3},{1,2},{2,5},{3,4},{4,7},{5,6},{8,11},{9,10},{10,13},{11,12},... | collective-permute-start | bytes 98312 | tf_op jit(solution)/shard_map/ppermute | solution.py:99
  145.7 13.8 %copy-start.33 = (f32[2,2,8,256]{3,2,1,0:T(8,128)}, f32[2,2,8,256]{3,2,1,0:T(8,128)S(1)}, u32[]{:S(2)}) copy-start(f32[2,2,8,256]{3,2,1,0:T(8,128)S(1)} %collective-permute-done.24.refs_3_) | copy-start | bytes 98308
  145.8 5.7 %collective-permute-start.25 = (f32[2,2,8,256]{3,2,1,0:T(8,128)}, f32[2,2,8,256]{3,2,1,0:T(8,128)S(1)}, u32[]{:S(2)}, u32[]{:S(2)}) collective-permute-start(f32[2,2,8,256]{3,2,1,0:T(8,128)} %get-tuple-element.84), channel_id=1, source_target_pairs={{2,1},{3,0},{4,3},{5,2},{6,5},{7,4},{10,9},{11,8},{12,11},{13,10},... | collective-permute-start | bytes 98312 | tf_op jit(solution)/shard_map/ppermute | solution.py:99
  151.4 8.2 %copy-start.35 = (f32[2,2,8,256]{3,2,1,0:T(8,128)}, f32[2,2,8,256]{3,2,1,0:T(8,128)S(1)}, u32[]{:S(2)}) copy-start(f32[2,2,8,256]{3,2,1,0:T(8,128)S(1)} %collective-permute-done.25.refs_4_) | copy-start | bytes 98308
  151.4 25.4 %collective-permute-start.16 = (f32[2,4,32,256]{3,2,1,0:T(8,128)S(1)}, f32[2,4,32,256]{3,2,1,0:T(8,128)S(1)}, u32[]{:S(2)}, u32[]{:S(2)}) collective-permute-start(f32[2,4,32,256]{3,2,1,0:T(8,128)S(1)} %copy-done.8), channel_id=1, source_target_pairs={{0,2},{2,4},{4,6},{1,3},{3,5},{5,7},{8,10},{10,12},{12,14},{9,11},... | collective-permute-start | bytes 786440 | tf_op jit(solution)/shard_map/ppermute | solution.py:101
  156.4 3.2 %copy-start.15 = (f32[2,4,32,256]{3,2,1,0:T(8,128)}, f32[2,4,32,256]{3,2,1,0:T(8,128)S(1)}, u32[]{:S(2)}) copy-start(f32[2,4,32,256]{3,2,1,0:T(8,128)S(1)} %collective-permute-done.21.refs_0_) | copy-start | bytes 786436
  156.4 20.5 %collective-permute-start.17 = (f32[2,4,32,256]{3,2,1,0:T(8,128)S(1)}, f32[2,4,32,256]{3,2,1,0:T(8,128)S(1)}, u32[]{:S(2)}, u32[]{:S(2)}) collective-permute-start(f32[2,4,32,256]{3,2,1,0:T(8,128)S(1)} %copy-done.7), channel_id=1, source_target_pairs={{2,0},{4,2},{6,4},{3,1},{5,3},{7,5},{10,8},{12,10},{14,12},{11,9},... | collective-permute-start | bytes 786440 | tf_op jit(solution)/shard_map/ppermute | solution.py:102
  157.7 1.9 copy-start.17
  157.7 19.2 %collective-permute-start.18 = (f32[2,16,8,256]{3,2,1,0:T(8,128)S(1)}, f32[2,16,8,256]{3,2,1,0:T(8,128)S(1)}, u32[]{:S(2)}, u32[]{:S(2)}) collective-permute-start(f32[2,16,8,256]{3,2,1,0:T(8,128)S(1)} %copy-done.6), channel_id=1, source_target_pairs={{0,1},{1,0},{2,3},{3,2},{4,5},{5,4},{6,7},{7,6},{8,9},{9,8},{10,11... | collective-permute-start | bytes 786440 | tf_op jit(solution)/shard_map/ppermute | solution.py:99
  158.3 18.6 %collective-permute-start.20 = (f32[2,2,8,256]{3,2,1,0:T(8,128)S(1)}, f32[2,2,8,256]{3,2,1,0:T(8,128)S(1)}, u32[]{:S(2)}, u32[]{:S(2)}) collective-permute-start(f32[2,2,8,256]{3,2,1,0:T(8,128)S(1)} %copy-done.26), channel_id=1, source_target_pairs={{2,1},{3,0},{4,3},{5,2},{6,5},{7,4},{10,9},{11,8},{12,11},{13,10},... | collective-permute-start | bytes 98312 | tf_op jit(solution)/shard_map/ppermute | solution.py:99
  176.9 1.5 copy-start.34
  176.9 1.5 copy-start.16
  176.9 1.5 copy-start.19
  176.9 1.5 copy-start.20
  176.9 18.7 %copy-start.1 = (f32[2,32,32,256]{3,2,1,0:T(8,128)}, f32[2,32,32,256]{3,2,1,0:T(8,128)S(1)}, u32[]{:S(2)}) copy-start(f32[2,32,32,256]{3,2,1,0:T(8,128)S(1)} %collective-permute-done.31.refs_3_) | copy-start | bytes 6291460
  176.9 56.4 %collective-permute-start.32 = (f32[2,32,32,256]{3,2,1,0:T(8,128)}, f32[2,32,32,256]{3,2,1,0:T(8,128)S(1)}, u32[]{:S(2)}, u32[]{:S(2)}) collective-permute-start(f32[2,32,32,256]{3,2,1,0:T(8,128)} %shard_map.64.refs_1_), channel_id=1, source_target_pairs={{0,8},{8,16},{16,24},{1,9},{9,17},{17,25},{2,10},{10,18},{18,26},{... | collective-permute-start | bytes 6291464 | tf_op jit(solution)/shard_map/ppermute | solution.py:490
  195.6 19.6 %collective-permute-start.26 = (f32[2,4,32,256]{3,2,1,0:T(8,128)}, f32[2,4,32,256]{3,2,1,0:T(8,128)S(1)}, u32[]{:S(2)}, u32[]{:S(2)}) collective-permute-start(f32[2,4,32,256]{3,2,1,0:T(8,128)} %get-tuple-element.91), channel_id=1, source_target_pairs={{0,2},{2,4},{4,6},{1,3},{3,5},{5,7},{8,10},{10,12},{12,14},{9,11},... | collective-permute-start | bytes 786440 | tf_op jit(solution)/shard_map/ppermute | solution.py:101
  200.3 14.9 %collective-permute-start.27 = (f32[2,4,32,256]{3,2,1,0:T(8,128)}, f32[2,4,32,256]{3,2,1,0:T(8,128)S(1)}, u32[]{:S(2)}, u32[]{:S(2)}) collective-permute-start(f32[2,4,32,256]{3,2,1,0:T(8,128)} %get-tuple-element.92), channel_id=1, source_target_pairs={{2,0},{4,2},{6,4},{3,1},{5,3},{7,5},{10,8},{12,10},{14,12},{11,9},... | collective-permute-start | bytes 786440 | tf_op jit(solution)/shard_map/ppermute | solution.py:102
  201.6 13.6 %collective-permute-start.28 = (f32[2,16,8,256]{3,2,1,0:T(8,128)}, f32[2,16,8,256]{3,2,1,0:T(8,128)S(1)}, u32[]{:S(2)}, u32[]{:S(2)}) collective-permute-start(f32[2,16,8,256]{3,2,1,0:T(8,128)} %get-tuple-element.93), channel_id=1, source_target_pairs={{0,1},{1,0},{2,3},{3,2},{4,5},{5,4},{6,7},{7,6},{8,9},{9,8},{10,11... | collective-permute-start | bytes 786440 | tf_op jit(solution)/shard_map/ppermute | solution.py:99
  202.2 7.4 %collective-permute-start.29 = (f32[2,2,8,256]{3,2,1,0:T(8,128)}, f32[2,2,8,256]{3,2,1,0:T(8,128)S(1)}, u32[]{:S(2)}, u32[]{:S(2)}) collective-permute-start(f32[2,2,8,256]{3,2,1,0:T(8,128)} %get-tuple-element.94), channel_id=1, source_target_pairs={{0,3},{1,2},{2,5},{3,4},{4,7},{5,6},{8,11},{9,10},{10,13},{11,12},... | collective-permute-start | bytes 98312 | tf_op jit(solution)/shard_map/ppermute | solution.py:99
  209.5 5.7 %copy-start.36 = (f32[2,2,8,256]{3,2,1,0:T(8,128)}, f32[2,2,8,256]{3,2,1,0:T(8,128)S(1)}, u32[]{:S(2)}) copy-start(f32[2,2,8,256]{3,2,1,0:T(8,128)S(1)} %collective-permute-done.29.refs_3_) | copy-start | bytes 98308
  209.5 5.7 %collective-permute-start.30 = (f32[2,2,8,256]{3,2,1,0:T(8,128)}, f32[2,2,8,256]{3,2,1,0:T(8,128)S(1)}, u32[]{:S(2)}, u32[]{:S(2)}) collective-permute-start(f32[2,2,8,256]{3,2,1,0:T(8,128)} %get-tuple-element.95), channel_id=1, source_target_pairs={{2,1},{3,0},{4,3},{5,2},{6,5},{7,4},{10,9},{11,8},{12,11},{13,10},... | collective-permute-start | bytes 98312 | tf_op jit(solution)/shard_map/ppermute | solution.py:99
  243.2 6.5 %collective-permute-start.34 = (f32[8,128]{0,1:T(8,128)S(1)}, f32[8,128]{0,1:T(8,128)S(1)}, u32[]{:S(2)}, u32[]{:S(2)}) collective-permute-start(f32[8,128]{0,1:T(8,128)S(1)} %copy.18), channel_id=1, source_target_pairs={{0,4},{2,6},{4,0},{6,2},{1,5},{3,7},{5,1},{7,3},{8,12},{10,14},{12... | collective-permute-start | bytes 12296 | tf_op jit(solution)/shard_map/ppermute | solution.py:441
  247.1 4.0 %collective-permute-start.35 = (f32[8,128]{0,1:T(8,128)S(1)}, f32[8,128]{0,1:T(8,128)S(1)}, u32[]{:S(2)}, u32[]{:S(2)}) collective-permute-start(f32[8,128]{0,1:T(8,128)S(1)} %copy.18), channel_id=1, source_target_pairs={{0,6},{2,4},{4,2},{6,0},{1,7},{3,5},{5,3},{7,1},{8,14},{10,12},{12... | collective-permute-start | bytes 12296 | tf_op jit(solution)/shard_map/ppermute | solution.py:441
  247.1 4.0 %collective-permute-start.33 = (f32[8,128]{0,1:T(8,128)S(1)}, f32[8,128]{0,1:T(8,128)S(1)}, u32[]{:S(2)}, u32[]{:S(2)}) collective-permute-start(f32[8,128]{0,1:T(8,128)S(1)} %copy.18), channel_id=1, source_target_pairs={{0,2},{2,0},{4,6},{6,4},{1,3},{3,1},{5,7},{7,5},{8,10},{10,8},{12,... | collective-permute-start | bytes 12296 | tf_op jit(solution)/shard_map/ppermute | solution.py:441
  251.1 4.3 %collective-permute-start.36 = (f32[8,128]{0,1:T(8,128)S(1)}, f32[8,128]{0,1:T(8,128)S(1)}, u32[]{:S(2)}, u32[]{:S(2)}) collective-permute-start(f32[8,128]{0,1:T(8,128)S(1)} %add_add_fusion), channel_id=1, source_target_pairs={{0,1},{1,0},{2,3},{3,2},{4,5},{5,4},{6,7},{7,6},{8,9},{9,8},{10,11... | collective-permute-start | bytes 12296 | tf_op jit(solution)/shard_map/ppermute | solution.py:441
  255.5 4.5 %collective-permute-start.37 = (f32[8,128]{0,1:T(8,128)S(1)}, f32[8,128]{0,1:T(8,128)S(1)}, u32[]{:S(2)}, u32[]{:S(2)}) collective-permute-start(f32[8,128]{0,1:T(8,128)S(1)} %add.79), channel_id=1, source_target_pairs={{0,8},{8,0},{16,24},{24,16},{1,9},{9,1},{17,25},{25,17},{2,10},{10... | collective-permute-start | bytes 12296 | tf_op jit(solution)/shard_map/ppermute | solution.py:441
  255.5 5.9 %collective-permute-start.38 = (f32[8,128]{0,1:T(8,128)S(1)}, f32[8,128]{0,1:T(8,128)S(1)}, u32[]{:S(2)}, u32[]{:S(2)}) collective-permute-start(f32[8,128]{0,1:T(8,128)S(1)} %add.79), channel_id=1, source_target_pairs={{0,16},{8,24},{16,0},{24,8},{1,17},{9,25},{17,1},{25,9},{2,18},{10... | collective-permute-start | bytes 12296 | tf_op jit(solution)/shard_map/ppermute | solution.py:441
  255.9 7.1 %collective-permute-start.39 = (f32[8,128]{0,1:T(8,128)S(1)}, f32[8,128]{0,1:T(8,128)S(1)}, u32[]{:S(2)}, u32[]{:S(2)}) collective-permute-start(f32[8,128]{0,1:T(8,128)S(1)} %add.79), channel_id=1, source_target_pairs={{0,24},{8,16},{16,8},{24,0},{1,25},{9,17},{17,9},{25,1},{2,26},{10... | collective-permute-start | bytes 12296 | tf_op jit(solution)/shard_map/ppermute | solution.py:441
  (14 other events, 12.5 us)

commit v3 on v2

--- a/solution.py
+++ b/solution.py
@@ -12,12 +12,12 @@
 LANES = 128
 ROWS = 2
 BLOCK = 4
-VMEM_LIMIT = 58 * 1024 * 1024
+MIB = 1024 * 1024
 FLOPS_PER_MICRO = 1.15e9
 BYTES_PER_MICRO = 3.6e6
 
 
-def kernel_call(body, outs, scratch, ins, micros, anywhere=(), outs_anywhere=()):
+def kernel_call(body, outs, scratch, ins, micros, mib, anywhere=(), outs_anywhere=()):
     spec = lambda n, names: pl.BlockSpec(memory_space=pl.ANY if n in names else pltpu.VMEM)
     specs = [spec(n, anywhere) for n in range(len(ins))]
     specs[0] = pl.BlockSpec(memory_space=pltpu.SMEM)
@@ -27,7 +27,7 @@
         in_specs=specs,
         out_specs=[spec(n, outs_anywhere) for n in range(len(outs))],
         scratch_shapes=scratch,
-        compiler_params=pltpu.CompilerParams(vmem_limit_bytes=VMEM_LIMIT),
+        compiler_params=pltpu.CompilerParams(vmem_limit_bytes=mib * MIB),
         cost_estimate=pl.CostEstimate(
             flops=int(micros * FLOPS_PER_MICRO),
             bytes_accessed=int(micros * BYTES_PER_MICRO),
@@ -251,7 +251,7 @@
     lax.fori_loop(0, (stop - first) // ROWS, body, None)
 
 
-def run_steps(coef, states, out, adjoint, weight=None, parts=None):
+def run_steps(coef, states, out, adjoint, weight=None):
     x, tile_rows = out.shape[1], out.shape[2]
     for step in range(STEPS):
         src, dst = states[step % 2], states[(step + 1) % 2]
@@ -266,13 +266,7 @@
 
         done = (tile_rows if last else src.shape[2]) // SUB
         reach = STEPS - 1 - step
-        bounds = [-reach, x + reach]
-        if step == 0 and parts is not None:
-            bounds[1:1] = [SUB * (n + 1) - 1 for n in range(len(parts) - 1)]
-        for n in range(len(bounds) - 1):
-            if step == 0 and parts is not None:
-                parts[n]()
-            sweep(coef, src, bounds[n], bounds[n + 1], adjoint, done, write)
+        sweep(coef, src, -reach, x + reach, adjoint, done, write)
 
 
 def pack_kernel(fields_in, scalars, *refs):
@@ -298,8 +292,8 @@
 
 def first_kernel(count, scalars, diffusivity, velocity, probes, weight, *refs):
     side = scalars[0]
-    received, coef_out, out = refs[:count], refs[count], refs[count + 1]
-    strips, (coef, state, other, sems) = refs[count + 2 : -4], refs[-4:]
+    received, coef, out = refs[:count], refs[count], refs[count + 1]
+    strips, (state, other, sems) = refs[count + 2 : -3], refs[-3:]
     copies = Copies(sems)
     tiles = [diffusivity.at[0]] + [velocity.at[d] for d in range(3)]
     slots = [coef.at[s] for s in (0, 1, 3, 5)]
@@ -312,33 +306,24 @@
         widen_rows(slot, f, received, side)
     copies.wait()
     coefficient_rows(coef)
-    copies.start(coef, coef_out)
     run_steps(coef, (state, other), out, False, weight)
     write_strips(out, strips, side)
-    copies.wait()
-
-
-def next_kernel(count, adjoint, scalars, coef_in, tile, *refs):
+
+
+def next_kernel(count, adjoint, scalars, coef, tile, *refs):
     side = scalars[0]
     weight = None if adjoint else refs[0]
     refs = refs if adjoint else refs[1:]
     received, out = refs[:count], refs[count]
-    strips, (coef, state, other, sems) = refs[count + 1 : -4], refs[-4:]
-    fields, x = tile.shape[0], tile.shape[1]
+    strips, (state, other, sems) = refs[count + 1 : -3], refs[-3:]
+    fields = tile.shape[0]
     copies = Copies(sems)
     for p in range(fields):
         start_widening(copies, state.at[p], tile.at[p], p, received)
-    ends = Copies(sems.at[pl.ds(3 * fields, x // SUB + 1)])
-    rows = [(x, 2 * STEPS)] + [(n, SUB) for n in range(0, x, SUB)]
-    waits = []
-    for at, size in rows:
-        part = (slice(None), pl.ds(at, size))
-        waits.append(ends.start(coef_in.at[part], coef.at[part]).wait)
     for p in range(fields):
         widen_rows(state.at[p], p, received, side)
     copies.wait()
-    waits[0]()
-    run_steps(coef, (state, other), out, adjoint, weight, waits[1:])
+    run_steps(coef, (state, other), out, adjoint, weight)
     if strips:
         write_strips(out, strips, side)
 
@@ -354,7 +339,7 @@
         in_specs=[pl.BlockSpec(memory_space=pltpu.SMEM)] + [block] * len(ins),
         out_specs=out,
         scratch_shapes=scratch,
-        compiler_params=pltpu.CompilerParams(vmem_limit_bytes=VMEM_LIMIT),
+        compiler_params=pltpu.CompilerParams(vmem_limit_bytes=12 * MIB),
         cost_estimate=pl.CostEstimate(
             flops=int(micros * FLOPS_PER_MICRO),
             bytes_accessed=int(micros * BYTES_PER_MICRO),
@@ -467,7 +452,6 @@
 
     def scratch(copies):
         return [
-            pltpu.VMEM((7,) + wide, jnp.float32),
             pltpu.VMEM((group,) + wide, jnp.float32),
             pltpu.VMEM((group,) + wide, jnp.float32),
             pltpu.SemaphoreType.DMA((copies,)),
@@ -483,6 +467,7 @@
             [pltpu.VMEM((packs, number, x, SUB, z), jnp.float32), pltpu.SemaphoreType.DMA((number * (packs + 2),))],
             [where] + sources,
             3.0,
+            12,
             anywhere=range(1, len(sources) + 1),
         )
 
@@ -495,11 +480,11 @@
     coef, halfway, *strips = kernel_call(
         functools.partial(first_kernel, len(received)),
         [f32(7, *wide), tile] + strips2,
-        scratch(3 * total + 1),
+        scratch(3 * total),
         [where] + fields + [obs_weight] + received,
         14.0,
+        14,
         anywhere=(1, 2, 3, 5, 6),
-        outs_anywhere=(0,),
     )
 
     def model(field, received, adjoint, last=False):
@@ -507,10 +492,11 @@
         return kernel_call(
             functools.partial(next_kernel, len(received), adjoint),
             [tile] + ([] if last else strips2),
-            scratch(3 * group + x // SUB + 1),
+            scratch(3 * group),
             ins + received,
             12.0,
-            anywhere=(1, 2, len(ins), len(ins) + 1),
+            14,
+            anywhere=(2, len(ins), len(ins) + 1),
         )
 
     images, *strips = model(halfway, exchange(strips), True)

time: 277 us -> 247 us (0.89)
  Pallas kernels: 127 us -> 90.2 us
  local copies, waits for them, and re-layouts: 5.99 us -> 11.3 us
    pallas_call x8, Pallas kernels: 112 us -> 81.7 us  [kernel_call(): pl.pallas_call(body, out_shape=outs, in_specs=specs, out_specs=[spec(n, o...]
    pallas_call x2, Pallas kernels: 15.1 us -> 8.56 us  [blocked_call(): pl.pallas_call(body, grid=(x // BLOCK,), out_shape=out_shape, in_specs=[p...]
    unnamed x76 -> x24, local copies, waits for them, and re-layouts: 4.83 us -> 10.8 us
  transfers between devices with their start and end apart: 40 -> 40, of which waited for: 12 -> 12; matrix products, arithmetic and copies ran while one was open for 0% -> 0% of each run, Pallas kernels for 39% -> 32%
where the time goes in v3:
time: 247 us; the launch traced here: 246 us
  starting transfers between devices  96.8 us (39%)
  Pallas kernels  90.2 us (37%)
  waiting for transfers between devices  41.9 us (17%)
  local copies, waits for them, and re-layouts  11.3 us (5%)
  other arithmetic  3.05 us (1%)
    pallas_call x8, Pallas kernels, kernel_call(): pl.pallas_call(body, out_shape=outs, in_specs=specs, out_specs=[spec(n, o...  81.7 us
    ppermute x18, starting transfers between devices, moved(): return lax.ppermute(value, ('sx', 'sy'), pairs)  42.5 us
    ppermute x18, waiting for transfers between devices, moved(): return lax.ppermute(value, ('sx', 'sy'), pairs)  29.7 us
    ppermute x6, starting transfers between devices, exchange(): below = lax.ppermute(strips[1], 'sx', up)  23.5 us
    ppermute x7, starting transfers between devices, all_sum(): lax.ppermute(value, axis, [(i, i ^ bits) for i in range(devices)])  12.3 us
    ppermute x7, waiting for transfers between devices, all_sum(): lax.ppermute(value, axis, [(i, i ^ bits) for i in range(devices)])  12.1 us
    unnamed x24, local copies, waits for them, and re-layouts  10.8 us
    ppermute x3, starting transfers between devices, right(): lax.ppermute(value, 'probe', [(i, i + hops) for i in range(groups - hops)])  10.7 us
  transfers between devices with their start and end apart: 40, of which 12 were waited for; matrix products, arithmetic and copies ran while one was open for 0% of the time, Pallas kernels for 32%

profile of v3, /device:TPU:0, one launch (start us, length us, event | category | flops | bytes accessed | tf_op | source)
XLA Modules:
  0.0 245.6 jit_solution(4290616188356099945)
XLA Ops:
  0.7 1.9 copy-done
  2.6 1.6 copy-done.2
  4.2 1.2 copy-done.9
  5.4 3.1 %shard_map.59 = (f32[6,4,32,256]{3,2,1,0:T(8,128)S(1)}, f32[6,4,32,256]{3,2,1,0:T(8,128)S(1)}, f32[6,16,8,256]{3,2,1,0:T(8,128)S(1)}, f32[6,2,8,256]{3,2,1,0:T(8,128)S(1)}, f32[6,2,8,256]{3,2,1,0:T(8,128)S(1)}) custom-call(s32[2]{0:T(128)S(1)} %pad_add_fusion.scalars, f32[1,32,32,256]{3,2,1,0:T(8,128)S(1)} %bitcast.25, f32[3,32,32,256]{3,2,1,0:T(8,128)S(1)} %copy-done, ...), custom_call_target="tpu_custom_call" | custom-call | flops 3449999872 | bytes 10800000 | tf_op jit(solution)/shard_map/pallas_call | solution.py:24
  8.5 2.4 collective-permute-start
  11.0 1.3 collective-permute-start.1
  12.3 2.4 collective-permute-start.2
  14.7 3.6 %collective-permute-start.10 = (f32[2,32,32,256]{3,2,1,0:T(8,128)S(1)}, f32[2,32,32,256]{3,2,1,0:T(8,128)S(1)}, u32[]{:S(2)}, u32[]{:S(2)}) collective-permute-start(f32[2,32,32,256]{3,2,1,0:T(8,128)S(1)} %copy-done.2), channel_id=1, source_target_pairs={{0,8},{8,16},{16,24},{1,9},{9,17},{17,25},{2,10},{10,18},{18,26},{... | collective-permute-start | bytes 6291464 | tf_op jit(solution)/shard_map/ppermute | solution.py:475
  18.3 3.8 %collective-permute-start.3 = (f32[6,2,8,256]{3,2,1,0:T(8,128)S(1)}, f32[6,2,8,256]{3,2,1,0:T(8,128)S(1)}, u32[]{:S(2)}, u32[]{:S(2)}) collective-permute-start(f32[6,2,8,256]{3,2,1,0:T(8,128)S(1)} %get-tuple-element.53), channel_id=1, source_target_pairs={{0,3},{1,2},{2,5},{3,4},{4,7},{5,6},{8,11},{9,10},{10,13},{11,12},... | collective-permute-start | bytes 294920 | tf_op jit(solution)/shard_map/ppermute | solution.py:99
  22.1 11.2 %collective-permute-done.3.refs_3_ = f32[6,2,8,256]{3,2,1,0:T(8,128)S(1)} collective-permute-done((f32[6,2,8,256]{3,2,1,0:T(8,128)S(1)}, f32[6,2,8,256]{3,2,1,0:T(8,128)S(1)}, u32[]{:S(2)}, u32[]{:S(2)}) %collective-permute-start.3) | collective-permute-done | bytes 98336 | tf_op jit(solution)/shard_map/ppermute | solution.py:99
  33.3 1.3 collective-permute-start.4
  34.6 4.8 %collective-permute-done.4.refs_4_ = f32[6,2,8,256]{3,2,1,0:T(8,128)S(1)} collective-permute-done((f32[6,2,8,256]{3,2,1,0:T(8,128)S(1)}, f32[6,2,8,256]{3,2,1,0:T(8,128)S(1)}, u32[]{:S(2)}, u32[]{:S(2)}) %collective-permute-start.4) | collective-permute-done | bytes 98336 | tf_op jit(solution)/shard_map/ppermute | solution.py:99
  39.4 14.3 %shard_map.60 = (f32[7,40,40,256]{3,2,1,0:T(8,128)S(1)}, f32[2,32,32,256]{3,2,1,0:T(8,128)S(1)}, f32[2,4,32,256]{3,2,1,0:T(8,128)S(1)}, f32[2,4,32,256]{3,2,1,0:...) custom-call(s32[2]{0:T(128)S(1)} %pad_add_fusion.scalars, ...), custom_call_target="tpu_custom_call" | custom-call | flops 16099999744 | bytes 50400000 | tf_op jit(solution)/shard_map/pallas_call | solution.py:24
  53.7 3.3 %collective-permute-start.5 = (f32[2,4,32,256]{3,2,1,0:T(8,128)S(1)}, f32[2,4,32,256]{3,2,1,0:T(8,128)S(1)}, u32[]{:S(2)}, u32[]{:S(2)}) collective-permute-start(f32[2,4,32,256]{3,2,1,0:T(8,128)S(1)} %get-tuple-element.57), channel_id=1, source_target_pairs={{0,2},{2,4},{4,6},{1,3},{3,5},{5,7},{8,10},{10,12},{12,14},{9,11},... | collective-permute-start | bytes 786440 | tf_op jit(solution)/shard_map/ppermute | solution.py:101
  57.1 1.3 collective-permute-start.6
  58.4 1.7 collective-permute-start.7
  60.1 4.0 %collective-permute-start.8 = (f32[2,2,8,256]{3,2,1,0:T(8,128)S(1)}, f32[2,2,8,256]{3,2,1,0:T(8,128)S(1)}, u32[]{:S(2)}, u32[]{:S(2)}) collective-permute-start(f32[2,2,8,256]{3,2,1,0:T(8,128)S(1)} %get-tuple-element.60), channel_id=1, source_target_pairs={{0,3},{1,2},{2,5},{3,4},{4,7},{5,6},{8,11},{9,10},{10,13},{11,12},... | collective-permute-start | bytes 98312 | tf_op jit(solution)/shard_map/ppermute | solution.py:99
  64.1 1.3 collective-permute-start.9
  65.4 1.4 shard_map.62
  67.1 4.1 %collective-permute-start.11 = (f32[2,4,32,256]{3,2,1,0:T(8,128)S(1)}, f32[2,4,32,256]{3,2,1,0:T(8,128)S(1)}, u32[]{:S(2)}, u32[]{:S(2)}) collective-permute-start(f32[2,4,32,256]{3,2,1,0:T(8,128)S(1)} %get-tuple-element.68), channel_id=1, source_target_pairs={{0,2},{2,4},{4,6},{1,3},{3,5},{5,7},{8,10},{10,12},{12,14},{9,11},... | collective-permute-start | bytes 786440 | tf_op jit(solution)/shard_map/ppermute | solution.py:101
  71.3 1.3 collective-permute-start.12
  73.1 5.0 %collective-permute-start.14 = (f32[2,2,8,256]{3,2,1,0:T(8,128)S(1)}, f32[2,2,8,256]{3,2,1,0:T(8,128)S(1)}, u32[]{:S(2)}, u32[]{:S(2)}) collective-permute-start(f32[2,2,8,256]{3,2,1,0:T(8,128)S(1)} %get-tuple-element.71), channel_id=1, source_target_pairs={{0,3},{1,2},{2,5},{3,4},{4,7},{5,6},{8,11},{9,10},{10,13},{11,12},... | collective-permute-start | bytes 98312 | tf_op jit(solution)/shard_map/ppermute | solution.py:99
  78.2 1.3 collective-permute-start.15
  79.5 12.8 %shard_map.61 = (f32[2,32,32,256]{3,2,1,0:T(8,128)S(1)}, f32[2,4,32,256]{3,2,1,0:T(8,128)S(1)}, f32[2,4,32,256]{3,2,1,0:T(8,128)S(1)}, f32[2,16,8,256]{3,2,1,0:T...) custom-call(s32[2]{0:T(128)S(1)} %pad_add_fusion.scalars, ...), custom_call_target="tpu_custom_call" | custom-call | flops 13799999488 | bytes 43200000 | tf_op jit(solution)/shard_map/pallas_call | solution.py:24
  92.3 5.6 %collective-permute-start.31 = (f32[2,32,32,256]{3,2,1,0:T(8,128)S(1)}, f32[2,32,32,256]{3,2,1,0:T(8,128)S(1)}, u32[]{:S(2)}, u32[]{:S(2)}) collective-permute-start(f32[2,32,32,256]{3,2,1,0:T(8,128)S(1)} %get-tuple-element.62.tile.refs_0_), channel_id=1, source_target_pairs={{0,24},{1,25},{2,26},{3,27},{4,28},{5,29},{6,30},{7,31}} | collective-permute-start | bytes 6291464 | tf_op jit(solution)/shard_map/ppermute | solution.py:475
  98.0 12.4 %shard_map.63 = (f32[2,32,32,256]{3,2,1,0:T(8,128)S(1)}, f32[2,4,32,256]{3,2,1,0:T(8,128)S(1)}, f32[2,4,32,256]{3,2,1,0:T(8,128)S(1)}, f32[2,16,8,256]{3,2,1,0:T...) custom-call(s32[2]{0:T(128)S(1)} %pad_add_fusion.scalars, ...), custom_call_target="tpu_custom_call" | custom-call | flops 13799999488 | bytes 43200000 | tf_op jit(solution)/shard_map/pallas_call | solution.py:24
  110.4 4.1 %collective-permute-start.21 = (f32[2,4,32,256]{3,2,1,0:T(8,128)S(1)}, f32[2,4,32,256]{3,2,1,0:T(8,128)S(1)}, u32[]{:S(2)}, u32[]{:S(2)}) collective-permute-start(f32[2,4,32,256]{3,2,1,0:T(8,128)S(1)} %get-tuple-element.80), channel_id=1, source_target_pairs={{0,2},{2,4},{4,6},{1,3},{3,5},{5,7},{8,10},{10,12},{12,14},{9,11},... | collective-permute-start | bytes 786440 | tf_op jit(solution)/shard_map/ppermute | solution.py:101
  114.5 1.3 collective-permute-start.22
  115.8 1.6 collective-permute-start.23
  117.4 5.3 %collective-permute-start.19 = (f32[2,2,8,256]{3,2,1,0:T(8,128)S(1)}, f32[2,2,8,256]{3,2,1,0:T(8,128)S(1)}, u32[]{:S(2)}, u32[]{:S(2)}) collective-permute-start(f32[2,2,8,256]{3,2,1,0:T(8,128)S(1)} %get-tuple-element.77), channel_id=1, source_target_pairs={{0,3},{1,2},{2,5},{3,4},{4,7},{5,6},{8,11},{9,10},{10,13},{11,12},... | collective-permute-start | bytes 98312 | tf_op jit(solution)/shard_map/ppermute | solution.py:99
  122.8 1.7 collective-permute-done.19.refs_4_
  124.5 3.8 %collective-permute-start.24 = (f32[2,2,8,256]{3,2,1,0:T(8,128)S(1)}, f32[2,2,8,256]{3,2,1,0:T(8,128)S(1)}, u32[]{:S(2)}, u32[]{:S(2)}) collective-permute-start(f32[2,2,8,256]{3,2,1,0:T(8,128)S(1)} %get-tuple-element.83), channel_id=1, source_target_pairs={{0,3},{1,2},{2,5},{3,4},{4,7},{5,6},{8,11},{9,10},{10,13},{11,12},... | collective-permute-start | bytes 98312 | tf_op jit(solution)/shard_map/ppermute | solution.py:99
  128.3 1.6 collective-permute-done.24.refs_3_
  129.9 1.3 collective-permute-start.25
  131.2 4.3 %collective-permute-done.25.refs_4_ = f32[2,2,8,256]{3,2,1,0:T(8,128)S(1)} collective-permute-done((f32[2,2,8,256]{3,2,1,0:T(8,128)S(1)}, f32[2,2,8,256]{3,2,1,0:T(8,128)S(1)}, u32[]{:S(2)}, u32[]{:S(2)}) %collective-permute-start.25) | collective-permute-done | bytes 32800 | tf_op jit(solution)/shard_map/ppermute | solution.py:99
  135.4 5.0 %collective-permute-start.16 = (f32[2,4,32,256]{3,2,1,0:T(8,128)S(1)}, f32[2,4,32,256]{3,2,1,0:T(8,128)S(1)}, u32[]{:S(2)}, u32[]{:S(2)}) collective-permute-start(f32[2,4,32,256]{3,2,1,0:T(8,128)S(1)} %get-tuple-element.74), channel_id=1, source_target_pairs={{0,2},{2,4},{4,6},{1,3},{3,5},{5,7},{8,10},{10,12},{12,14},{9,11},... | collective-permute-start | bytes 786440 | tf_op jit(solution)/shard_map/ppermute | solution.py:101
  140.4 1.3 collective-permute-start.17
  142.4 1.3 collective-permute-start.20
  143.7 12.6 %shard_map.64.refs_1_ = f32[2,32,32,256]{3,2,1,0:T(8,128)S(1)} custom-call(s32[2]{0:T(128)S(1)} %pad_add_fusion.scalars, f32[7,40,40,256]{3,2,1,0:T(8,128)S(1)} %get-tuple-element.55.coef, f32[2,32,32,256]{3,2,1,0:T(8,128)S(1)} %get-tuple-element.79.tile, f32[2,4,32,256]{3,2,1,0:T(8,128)S(1)} %collective-permute-done.21.refs_0_, ...), custom_call_target="tpu_custom_call" | custom-call | flops 13799999488 | bytes 43200000 | tf_op jit(solution)/shard_map/pallas_call | solution.py:24
  156.3 1.4 collective-permute-start.32
  157.8 12.4 %shard_map.65 = (f32[2,32,32,256]{3,2,1,0:T(8,128)S(1)}, f32[2,4,32,256]{3,2,1,0:T(8,128)S(1)}, f32[2,4,32,256]{3,2,1,0:T(8,128)S(1)}, f32[2,16,8,256]{3,2,1,0:T...) custom-call(s32[2]{0:T(128)S(1)} %pad_add_fusion.scalars, ...), custom_call_target="tpu_custom_call" | custom-call | flops 13799999488 | bytes 43200000 | tf_op jit(solution)/shard_map/pallas_call | solution.py:24
  170.2 4.6 %collective-permute-start.26 = (f32[2,4,32,256]{3,2,1,0:T(8,128)S(1)}, f32[2,4,32,256]{3,2,1,0:T(8,128)S(1)}, u32[]{:S(2)}, u32[]{:S(2)}) collective-permute-start(f32[2,4,32,256]{3,2,1,0:T(8,128)S(1)} %get-tuple-element.91), channel_id=1, source_target_pairs={{0,2},{2,4},{4,6},{1,3},{3,5},{5,7},{8,10},{10,12},{12,14},{9,11},... | collective-permute-start | bytes 786440 | tf_op jit(solution)/shard_map/ppermute | solution.py:101
  174.8 1.3 collective-permute-start.27
  176.8 5.3 %collective-permute-start.29 = (f32[2,2,8,256]{3,2,1,0:T(8,128)S(1)}, f32[2,2,8,256]{3,2,1,0:T(8,128)S(1)}, u32[]{:S(2)}, u32[]{:S(2)}) collective-permute-start(f32[2,2,8,256]{3,2,1,0:T(8,128)S(1)} %get-tuple-element.94), channel_id=1, source_target_pairs={{0,3},{1,2},{2,5},{3,4},{4,7},{5,6},{8,11},{9,10},{10,13},{11,12},... | collective-permute-start | bytes 98312 | tf_op jit(solution)/shard_map/ppermute | solution.py:99
  182.1 1.7 collective-permute-done.29.refs_3_
  183.8 1.3 collective-permute-start.30
  185.1 4.1 %collective-permute-done.30.refs_4_ = f32[2,2,8,256]{3,2,1,0:T(8,128)S(1)} collective-permute-done((f32[2,2,8,256]{3,2,1,0:T(8,128)S(1)}, f32[2,2,8,256]{3,2,1,0:T(8,128)S(1)}, u32[]{:S(2)}, u32[]{:S(2)}) %collective-permute-start.30) | collective-permute-done | bytes 32800 | tf_op jit(solution)/shard_map/ppermute | solution.py:99
  189.2 12.6 %shard_map.66.second = f32[2,32,32,256]{3,2,1,0:T(8,128)S(1)} custom-call(s32[2]{0:T(128)S(1)} %pad_add_fusion.scalars, f32[7,40,40,256]{3,2,1,0:T(8,128)S(1)} %get-tuple-element.55.coef, f32[2,32,32,256]{3,2,1,0:T(8,128)S(1)} %get-tuple-element.90.tile, f32[2,4,32,256]{3,2,1,0:T(8,128)S(1)} %collective-permute-done.26.refs_0_, ...), custom_call_target="tpu_custom_call" | custom-call | flops 13799999488 | bytes 43200000 | tf_op jit(solution)/shard_map/pallas_call | solution.py:24
  201.9 4.0 %shard_map.67 = f32[8,128]{1,0:T(8,128)S(1)} custom-call(s32[2]{0:T(128)S(1)} %pad_add_fusion.scalars, f32[2,32,32,256]{3,2,1,0:T(8,128)S(1)} %shard_map.66.second, f32[2,32,32,256]{3,2,1,0:T(8,128)S(1)} %get-tuple-element.62.tile.refs_0_, f32[2,32,32,256]{3,2,1,0:T(8,128)S(1)} %shard_map.64.refs_1_, f32[2,32,32,256]{3,2,1,0:T(8,128)S(1)} %collective-permute-done.32.refs_2_, ...), custom_call_target="tpu_custom_call" | custom-call | flops 5750000128 | bytes 18000000 | tf_op jit(solution)/shard_map/pallas_call | solution.py:335
  205.9 1.3 copy-done.7
  207.3 6.4 %collective-permute-start.34 = (f32[8,128]{0,1:T(8,128)S(1)}, f32[8,128]{0,1:T(8,128)S(1)}, u32[]{:S(2)}, u32[]{:S(2)}) collective-permute-start(f32[8,128]{0,1:T(8,128)S(1)} %copy.18), channel_id=1, source_target_pairs={{0,4},{2,6},{4,0},{6,2},{1,5},{3,7},{5,1},{7,3},{8,12},{10,14},{12... | collective-permute-start | bytes 12296 | tf_op jit(solution)/shard_map/ppermute | solution.py:426
  213.9 2.2 collective-permute-done.34
  216.1 2.0 collective-permute-done.35
  218.1 0.7 collective-permute-start.36
  218.9 3.6 %collective-permute-done.36 = f32[8,128]{0,1:T(8,128)S(1)} collective-permute-done((f32[8,128]{0,1:T(8,128)S(1)}, f32[8,128]{0,1:T(8,128)S(1)}, u32[]{:S(2)}, u32[]{:S(2)}) %collective-permute-start.36) | collective-permute-done | bytes 4128 | tf_op jit(solution)/shard_map/ppermute | solution.py:426
  222.5 2.5 %collective-permute-start.37 = (f32[8,128]{0,1:T(8,128)S(1)}, f32[8,128]{0,1:T(8,128)S(1)}, u32[]{:S(2)}, u32[]{:S(2)}) collective-permute-start(f32[8,128]{0,1:T(8,128)S(1)} %add.79), channel_id=1, source_target_pairs={{0,8},{8,0},{16,24},{24,16},{1,9},{9,1},{17,25},{25,17},{2,10},{10... | collective-permute-start | bytes 12296 | tf_op jit(solution)/shard_map/ppermute | solution.py:426
  225.0 2.4 collective-permute-start.39
  227.5 4.3 %collective-permute-done.38 = f32[8,128]{0,1:T(8,128)S(1)} collective-permute-done((f32[8,128]{0,1:T(8,128)S(1)}, f32[8,128]{0,1:T(8,128)S(1)}, u32[]{:S(2)}, u32[]{:S(2)}) %collective-permute-start.38) | collective-permute-done | bytes 4128 | tf_op jit(solution)/shard_map/ppermute | solution.py:426
  232.2 0.7 cholesky.16
  235.4 0.7 fusion.17
  236.3 1.6 copy-done.4
  237.9 1.6 copy-done.6
  239.5 1.6 copy-done.8
  241.1 4.6 %shard_map.68 = f32[2,32,32,256]{3,2,1,0:T(8,128)} custom-call(f32[2,8]{1,0:T(2,128)S(1)} %pad_maximum_fusion.inverse, f32[2,32,32,256]{3,2,1,0:T(8,128)S(1)} %get-tuple-element.62.tile.refs_0_, f32[2,32,32,256]{3,2,1,0:T(8,128)S(1)} %copy-done.6, f32[2,32,32,256]{3,2,1,0:T(8,128)S(1)} %copy-done.8, f32[2,32,32,256]{3,2,1,0:T(8,128)S(1)} %copy-done.4), custom_call_target="tpu_custom_call" | custom-call | flops 4600000000 | bytes 14400000 | tf_op jit(solution)/shard_map/pallas_call | solution.py:335
  (76 shorter events, 5.7 us)
Async XLA Ops:
  0.7 1.9 copy-start
  2.6 1.6 copy-start.2
  4.2 1.2 copy-start.9
  5.4 34.0 %copy-start.1 = (f32[3,32,32,256]{3,2,1,0:T(8,128)S(1)}, f32[3,32,32,256]{3,2,1,0:T(8,128)}, u32[]{:S(2)}) copy-start(f32[3,32,32,256]{3,2,1,0:T(8,128)} %velocity.1) | copy-start | bytes 9437188
  5.4 34.0 %copy-start.10 = (f32[32,32,256]{2,1,0:T(8,128)S(1)}, f32[32,32,256]{2,1,0:T(8,128)}, u32[]{:S(2)}) copy-start(f32[32,32,256]{2,1,0:T(8,128)} %param.6) | copy-start | bytes 3145732
  5.4 34.0 %copy-start.11 = (f32[32,32,256]{2,1,0:T(8,128)S(1)}, f32[32,32,256]{2,1,0:T(8,128)}, u32[]{:S(2)}) copy-start(f32[32,32,256]{2,1,0:T(8,128)} %refs_0_.3) | copy-start | bytes 3145732
  8.5 30.8 %collective-permute-start = (f32[6,4,32,256]{3,2,1,0:T(8,128)S(1)}, f32[6,4,32,256]{3,2,1,0:T(8,128)S(1)}, u32[]{:S(2)}, u32[]{:S(2)}) collective-permute-start(f32[6,4,32,256]{3,2,1,0:T(8,128)S(1)} %get-tuple-element.50), channel_id=1, source_target_pairs={{0,2},{2,4},{4,6},{1,3},{3,5},{5,7},{8,10},{10,12},{12,14},{9,11},... | collective-permute-start | bytes 2359304 | tf_op jit(solution)/shard_map/ppermute | solution.py:101
  11.0 28.4 %collective-permute-start.1 = (f32[6,4,32,256]{3,2,1,0:T(8,128)S(1)}, f32[6,4,32,256]{3,2,1,0:T(8,128)S(1)}, u32[]{:S(2)}, u32[]{:S(2)}) collective-permute-start(f32[6,4,32,256]{3,2,1,0:T(8,128)S(1)} %get-tuple-element.51), channel_id=1, source_target_pairs={{2,0},{4,2},{6,4},{3,1},{5,3},{7,5},{10,8},{12,10},{14,12},{11,9},... | collective-permute-start | bytes 2359304 | tf_op jit(solution)/shard_map/ppermute | solution.py:102
  12.3 27.1 %collective-permute-start.2 = (f32[6,16,8,256]{3,2,1,0:T(8,128)S(1)}, f32[6,16,8,256]{3,2,1,0:T(8,128)S(1)}, u32[]{:S(2)}, u32[]{:S(2)}) collective-permute-start(f32[6,16,8,256]{3,2,1,0:T(8,128)S(1)} %get-tuple-element.52), channel_id=1, source_target_pairs={{0,1},{1,0},{2,3},{3,2},{4,5},{5,4},{6,7},{7,6},{8,9},{9,8},{10,11... | collective-permute-start | bytes 2359304 | tf_op jit(solution)/shard_map/ppermute | solution.py:99
  14.7 49.4 %collective-permute-start.10 = (f32[2,32,32,256]{3,2,1,0:T(8,128)S(1)}, f32[2,32,32,256]{3,2,1,0:T(8,128)S(1)}, u32[]{:S(2)}, u32[]{:S(2)}) collective-permute-start(f32[2,32,32,256]{3,2,1,0:T(8,128)S(1)} %copy-done.2), channel_id=1, source_target_pairs={{0,8},{8,16},{16,24},{1,9},{9,17},{17,25},{2,10},{10,18},{18,26},{... | collective-permute-start | bytes 6291464 | tf_op jit(solution)/shard_map/ppermute | solution.py:475
  18.3 15.0 %collective-permute-start.3 = (f32[6,2,8,256]{3,2,1,0:T(8,128)S(1)}, f32[6,2,8,256]{3,2,1,0:T(8,128)S(1)}, u32[]{:S(2)}, u32[]{:S(2)}) collective-permute-start(f32[6,2,8,256]{3,2,1,0:T(8,128)S(1)} %get-tuple-element.53), channel_id=1, source_target_pairs={{0,3},{1,2},{2,5},{3,4},{4,7},{5,6},{8,11},{9,10},{10,13},{11,12},... | collective-permute-start | bytes 294920 | tf_op jit(solution)/shard_map/ppermute | solution.py:99
  33.3 6.1 %collective-permute-start.4 = (f32[6,2,8,256]{3,2,1,0:T(8,128)S(1)}, f32[6,2,8,256]{3,2,1,0:T(8,128)S(1)}, u32[]{:S(2)}, u32[]{:S(2)}) collective-permute-start(f32[6,2,8,256]{3,2,1,0:T(8,128)S(1)} %get-tuple-element.54), channel_id=1, source_target_pairs={{2,1},{3,0},{4,3},{5,2},{6,5},{7,4},{10,9},{11,8},{12,11},{13,10},... | collective-permute-start | bytes 294920 | tf_op jit(solution)/shard_map/ppermute | solution.py:99
  53.7 18.8 %collective-permute-start.5 = (f32[2,4,32,256]{3,2,1,0:T(8,128)S(1)}, f32[2,4,32,256]{3,2,1,0:T(8,128)S(1)}, u32[]{:S(2)}, u32[]{:S(2)}) collective-permute-start(f32[2,4,32,256]{3,2,1,0:T(8,128)S(1)} %get-tuple-element.57), channel_id=1, source_target_pairs={{0,2},{2,4},{4,6},{1,3},{3,5},{5,7},{8,10},{10,12},{12,14},{9,11},... | collective-permute-start | bytes 786440 | tf_op jit(solution)/shard_map/ppermute | solution.py:101
  57.1 16.1 %collective-permute-start.6 = (f32[2,4,32,256]{3,2,1,0:T(8,128)S(1)}, f32[2,4,32,256]{3,2,1,0:T(8,128)S(1)}, u32[]{:S(2)}, u32[]{:S(2)}) collective-permute-start(f32[2,4,32,256]{3,2,1,0:T(8,128)S(1)} %get-tuple-element.58), channel_id=1, source_target_pairs={{2,0},{4,2},{6,4},{3,1},{5,3},{7,5},{10,8},{12,10},{14,12},{11,9},... | collective-permute-start | bytes 786440 | tf_op jit(solution)/shard_map/ppermute | solution.py:102
  58.4 19.8 %collective-permute-start.7 = (f32[2,16,8,256]{3,2,1,0:T(8,128)S(1)}, f32[2,16,8,256]{3,2,1,0:T(8,128)S(1)}, u32[]{:S(2)}, u32[]{:S(2)}) collective-permute-start(f32[2,16,8,256]{3,2,1,0:T(8,128)S(1)} %get-tuple-element.59), channel_id=1, source_target_pairs={{0,1},{1,0},{2,3},{3,2},{4,5},{5,4},{6,7},{7,6},{8,9},{9,8},{10,11... | collective-permute-start | bytes 786440 | tf_op jit(solution)/shard_map/ppermute | solution.py:99
  60.1 7.1 %collective-permute-start.8 = (f32[2,2,8,256]{3,2,1,0:T(8,128)S(1)}, f32[2,2,8,256]{3,2,1,0:T(8,128)S(1)}, u32[]{:S(2)}, u32[]{:S(2)}) collective-permute-start(f32[2,2,8,256]{3,2,1,0:T(8,128)S(1)} %get-tuple-element.60), channel_id=1, source_target_pairs={{0,3},{1,2},{2,5},{3,4},{4,7},{5,6},{8,11},{9,10},{10,13},{11,12},... | collective-permute-start | bytes 98312 | tf_op jit(solution)/shard_map/ppermute | solution.py:99
  64.1 7.1 %collective-permute-start.9 = (f32[2,2,8,256]{3,2,1,0:T(8,128)S(1)}, f32[2,2,8,256]{3,2,1,0:T(8,128)S(1)}, u32[]{:S(2)}, u32[]{:S(2)}) collective-permute-start(f32[2,2,8,256]{3,2,1,0:T(8,128)S(1)} %get-tuple-element.61), channel_id=1, source_target_pairs={{2,1},{3,0},{4,3},{5,2},{6,5},{7,4},{10,9},{11,8},{12,11},{13,10},... | collective-permute-start | bytes 98312 | tf_op jit(solution)/shard_map/ppermute | solution.py:99
  67.1 30.8 %collective-permute-start.11 = (f32[2,4,32,256]{3,2,1,0:T(8,128)S(1)}, f32[2,4,32,256]{3,2,1,0:T(8,128)S(1)}, u32[]{:S(2)}, u32[]{:S(2)}) collective-permute-start(f32[2,4,32,256]{3,2,1,0:T(8,128)S(1)} %get-tuple-element.68), channel_id=1, source_target_pairs={{0,2},{2,4},{4,6},{1,3},{3,5},{5,7},{8,10},{10,12},{12,14},{9,11},... | collective-permute-start | bytes 786440 | tf_op jit(solution)/shard_map/ppermute | solution.py:101
  71.3 26.7 %collective-permute-start.12 = (f32[2,4,32,256]{3,2,1,0:T(8,128)S(1)}, f32[2,4,32,256]{3,2,1,0:T(8,128)S(1)}, u32[]{:S(2)}, u32[]{:S(2)}) collective-permute-start(f32[2,4,32,256]{3,2,1,0:T(8,128)S(1)} %get-tuple-element.69), channel_id=1, source_target_pairs={{2,0},{4,2},{6,4},{3,1},{5,3},{7,5},{10,8},{12,10},{14,12},{11,9},... | collective-permute-start | bytes 786440 | tf_op jit(solution)/shard_map/ppermute | solution.py:102
  72.6 25.4 %collective-permute-start.13 = (f32[2,16,8,256]{3,2,1,0:T(8,128)S(1)}, f32[2,16,8,256]{3,2,1,0:T(8,128)S(1)}, u32[]{:S(2)}, u32[]{:S(2)}) collective-permute-start(f32[2,16,8,256]{3,2,1,0:T(8,128)S(1)} %get-tuple-element.70), channel_id=1, source_target_pairs={{0,1},{1,0},{2,3},{3,2},{4,5},{5,4},{6,7},{7,6},{8,9},{9,8},{10,11... | collective-permute-start | bytes 786440 | tf_op jit(solution)/shard_map/ppermute | solution.py:99
  73.1 19.1 %collective-permute-start.14 = (f32[2,2,8,256]{3,2,1,0:T(8,128)S(1)}, f32[2,2,8,256]{3,2,1,0:T(8,128)S(1)}, u32[]{:S(2)}, u32[]{:S(2)}) collective-permute-start(f32[2,2,8,256]{3,2,1,0:T(8,128)S(1)} %get-tuple-element.71), channel_id=1, source_target_pairs={{0,3},{1,2},{2,5},{3,4},{4,7},{5,6},{8,11},{9,10},{10,13},{11,12},... | collective-permute-start | bytes 98312 | tf_op jit(solution)/shard_map/ppermute | solution.py:99
  78.2 19.7 %collective-permute-start.15 = (f32[2,2,8,256]{3,2,1,0:T(8,128)S(1)}, f32[2,2,8,256]{3,2,1,0:T(8,128)S(1)}, u32[]{:S(2)}, u32[]{:S(2)}) collective-permute-start(f32[2,2,8,256]{3,2,1,0:T(8,128)S(1)} %get-tuple-element.72), channel_id=1, source_target_pairs={{2,1},{3,0},{4,3},{5,2},{6,5},{7,4},{10,9},{11,8},{12,11},{13,10},... | collective-permute-start | bytes 98312 | tf_op jit(solution)/shard_map/ppermute | solution.py:99
  92.3 64.0 %collective-permute-start.31 = (f32[2,32,32,256]{3,2,1,0:T(8,128)S(1)}, f32[2,32,32,256]{3,2,1,0:T(8,128)S(1)}, u32[]{:S(2)}, u32[]{:S(2)}) collective-permute-start(f32[2,32,32,256]{3,2,1,0:T(8,128)S(1)} %get-tuple-element.62.tile.refs_0_), channel_id=1, source_target_pairs={{0,24},{1,25},{2,26},{3,27},{4,28},{5,29},{6,30},{7,31}} | collective-permute-start | bytes 6291464 | tf_op jit(solution)/shard_map/ppermute | solution.py:475
  110.4 30.0 %collective-permute-start.21 = (f32[2,4,32,256]{3,2,1,0:T(8,128)S(1)}, f32[2,4,32,256]{3,2,1,0:T(8,128)S(1)}, u32[]{:S(2)}, u32[]{:S(2)}) collective-permute-start(f32[2,4,32,256]{3,2,1,0:T(8,128)S(1)} %get-tuple-element.80), channel_id=1, source_target_pairs={{0,2},{2,4},{4,6},{1,3},{3,5},{5,7},{8,10},{10,12},{12,14},{9,11},... | collective-permute-start | bytes 786440 | tf_op jit(solution)/shard_map/ppermute | solution.py:101
  114.5 27.2 %collective-permute-start.22 = (f32[2,4,32,256]{3,2,1,0:T(8,128)S(1)}, f32[2,4,32,256]{3,2,1,0:T(8,128)S(1)}, u32[]{:S(2)}, u32[]{:S(2)}) collective-permute-start(f32[2,4,32,256]{3,2,1,0:T(8,128)S(1)} %get-tuple-element.81), channel_id=1, source_target_pairs={{2,0},{4,2},{6,4},{3,1},{5,3},{7,5},{10,8},{12,10},{14,12},{11,9},... | collective-permute-start | bytes 786440 | tf_op jit(solution)/shard_map/ppermute | solution.py:102
  115.8 26.5 %collective-permute-start.23 = (f32[2,16,8,256]{3,2,1,0:T(8,128)S(1)}, f32[2,16,8,256]{3,2,1,0:T(8,128)S(1)}, u32[]{:S(2)}, u32[]{:S(2)}) collective-permute-start(f32[2,16,8,256]{3,2,1,0:T(8,128)S(1)} %get-tuple-element.82), channel_id=1, source_target_pairs={{0,1},{1,0},{2,3},{3,2},{4,5},{5,4},{6,7},{7,6},{8,9},{9,8},{10,11... | collective-permute-start | bytes 786440 | tf_op jit(solution)/shard_map/ppermute | solution.py:99
  117.4 7.1 %collective-permute-start.19 = (f32[2,2,8,256]{3,2,1,0:T(8,128)S(1)}, f32[2,2,8,256]{3,2,1,0:T(8,128)S(1)}, u32[]{:S(2)}, u32[]{:S(2)}) collective-permute-start(f32[2,2,8,256]{3,2,1,0:T(8,128)S(1)} %get-tuple-element.77), channel_id=1, source_target_pairs={{0,3},{1,2},{2,5},{3,4},{4,7},{5,6},{8,11},{9,10},{10,13},{11,12},... | collective-permute-start | bytes 98312 | tf_op jit(solution)/shard_map/ppermute | solution.py:99
  124.5 5.4 %collective-permute-start.24 = (f32[2,2,8,256]{3,2,1,0:T(8,128)S(1)}, f32[2,2,8,256]{3,2,1,0:T(8,128)S(1)}, u32[]{:S(2)}, u32[]{:S(2)}) collective-permute-start(f32[2,2,8,256]{3,2,1,0:T(8,128)S(1)} %get-tuple-element.83), channel_id=1, source_target_pairs={{0,3},{1,2},{2,5},{3,4},{4,7},{5,6},{8,11},{9,10},{10,13},{11,12},... | collective-permute-start | bytes 98312 | tf_op jit(solution)/shard_map/ppermute | solution.py:99
  129.9 5.6 %collective-permute-start.25 = (f32[2,2,8,256]{3,2,1,0:T(8,128)S(1)}, f32[2,2,8,256]{3,2,1,0:T(8,128)S(1)}, u32[]{:S(2)}, u32[]{:S(2)}) collective-permute-start(f32[2,2,8,256]{3,2,1,0:T(8,128)S(1)} %get-tuple-element.84), channel_id=1, source_target_pairs={{2,1},{3,0},{4,3},{5,2},{6,5},{7,4},{10,9},{11,8},{12,11},{13,10},... | collective-permute-start | bytes 98312 | tf_op jit(solution)/shard_map/ppermute | solution.py:99
  135.4 20.9 %collective-permute-start.16 = (f32[2,4,32,256]{3,2,1,0:T(8,128)S(1)}, f32[2,4,32,256]{3,2,1,0:T(8,128)S(1)}, u32[]{:S(2)}, u32[]{:S(2)}) collective-permute-start(f32[2,4,32,256]{3,2,1,0:T(8,128)S(1)} %get-tuple-element.74), channel_id=1, source_target_pairs={{0,2},{2,4},{4,6},{1,3},{3,5},{5,7},{8,10},{10,12},{12,14},{9,11},... | collective-permute-start | bytes 786440 | tf_op jit(solution)/shard_map/ppermute | solution.py:101
  140.4 15.9 %collective-permute-start.17 = (f32[2,4,32,256]{3,2,1,0:T(8,128)S(1)}, f32[2,4,32,256]{3,2,1,0:T(8,128)S(1)}, u32[]{:S(2)}, u32[]{:S(2)}) collective-permute-start(f32[2,4,32,256]{3,2,1,0:T(8,128)S(1)} %get-tuple-element.75), channel_id=1, source_target_pairs={{2,0},{4,2},{6,4},{3,1},{5,3},{7,5},{10,8},{12,10},{14,12},{11,9},... | collective-permute-start | bytes 786440 | tf_op jit(solution)/shard_map/ppermute | solution.py:102
  141.7 14.6 %collective-permute-start.18 = (f32[2,16,8,256]{3,2,1,0:T(8,128)S(1)}, f32[2,16,8,256]{3,2,1,0:T(8,128)S(1)}, u32[]{:S(2)}, u32[]{:S(2)}) collective-permute-start(f32[2,16,8,256]{3,2,1,0:T(8,128)S(1)} %get-tuple-element.76), channel_id=1, source_target_pairs={{0,1},{1,0},{2,3},{3,2},{4,5},{5,4},{6,7},{7,6},{8,9},{9,8},{10,11... | collective-permute-start | bytes 786440 | tf_op jit(solution)/shard_map/ppermute | solution.py:99
  142.4 13.9 %collective-permute-start.20 = (f32[2,2,8,256]{3,2,1,0:T(8,128)S(1)}, f32[2,2,8,256]{3,2,1,0:T(8,128)S(1)}, u32[]{:S(2)}, u32[]{:S(2)}) collective-permute-start(f32[2,2,8,256]{3,2,1,0:T(8,128)S(1)} %get-tuple-element.78), channel_id=1, source_target_pairs={{2,1},{3,0},{4,3},{5,2},{6,5},{7,4},{10,9},{11,8},{12,11},{13,10},... | collective-permute-start | bytes 98312 | tf_op jit(solution)/shard_map/ppermute | solution.py:99
  156.3 45.6 %copy-start.5 = (f32[2,32,32,256]{3,2,1,0:T(8,128)}, f32[2,32,32,256]{3,2,1,0:T(8,128)S(1)}, u32[]{:S(2)}) copy-start(f32[2,32,32,256]{3,2,1,0:T(8,128)S(1)} %shard_map.64.refs_1_) | copy-start | bytes 6291460
  156.3 45.5 %copy-start.3 = (f32[2,32,32,256]{3,2,1,0:T(8,128)}, f32[2,32,32,256]{3,2,1,0:T(8,128)S(1)}, u32[]{:S(2)}) copy-start(f32[2,32,32,256]{3,2,1,0:T(8,128)S(1)} %collective-permute-done.31.refs_3_) | copy-start | bytes 6291460
  156.3 45.5 %collective-permute-start.32 = (f32[2,32,32,256]{3,2,1,0:T(8,128)S(1)}, f32[2,32,32,256]{3,2,1,0:T(8,128)S(1)}, u32[]{:S(2)}, u32[]{:S(2)}) collective-permute-start(f32[2,32,32,256]{3,2,1,0:T(8,128)S(1)} %shard_map.64.refs_1_), channel_id=1, source_target_pairs={{0,8},{8,16},{16,24},{1,9},{9,17},{17,25},{2,10},{10,18},{18,26},{... | collective-permute-start | bytes 6291464 | tf_op jit(solution)/shard_map/ppermute | solution.py:475
  170.2 19.0 %collective-permute-start.26 = (f32[2,4,32,256]{3,2,1,0:T(8,128)S(1)}, f32[2,4,32,256]{3,2,1,0:T(8,128)S(1)}, u32[]{:S(2)}, u32[]{:S(2)}) collective-permute-start(f32[2,4,32,256]{3,2,1,0:T(8,128)S(1)} %get-tuple-element.91), channel_id=1, source_target_pairs={{0,2},{2,4},{4,6},{1,3},{3,5},{5,7},{8,10},{10,12},{12,14},{9,11},... | collective-permute-start | bytes 786440 | tf_op jit(solution)/shard_map/ppermute | solution.py:101
  174.8 14.4 %collective-permute-start.27 = (f32[2,4,32,256]{3,2,1,0:T(8,128)S(1)}, f32[2,4,32,256]{3,2,1,0:T(8,128)S(1)}, u32[]{:S(2)}, u32[]{:S(2)}) collective-permute-start(f32[2,4,32,256]{3,2,1,0:T(8,128)S(1)} %get-tuple-element.92), channel_id=1, source_target_pairs={{2,0},{4,2},{6,4},{3,1},{5,3},{7,5},{10,8},{12,10},{14,12},{11,9},... | collective-permute-start | bytes 786440 | tf_op jit(solution)/shard_map/ppermute | solution.py:102
  176.1 13.1 %collective-permute-start.28 = (f32[2,16,8,256]{3,2,1,0:T(8,128)S(1)}, f32[2,16,8,256]{3,2,1,0:T(8,128)S(1)}, u32[]{:S(2)}, u32[]{:S(2)}) collective-permute-start(f32[2,16,8,256]{3,2,1,0:T(8,128)S(1)} %get-tuple-element.93), channel_id=1, source_target_pairs={{0,1},{1,0},{2,3},{3,2},{4,5},{5,4},{6,7},{7,6},{8,9},{9,8},{10,11... | collective-permute-start | bytes 786440 | tf_op jit(solution)/shard_map/ppermute | solution.py:99
  176.8 7.1 %collective-permute-start.29 = (f32[2,2,8,256]{3,2,1,0:T(8,128)S(1)}, f32[2,2,8,256]{3,2,1,0:T(8,128)S(1)}, u32[]{:S(2)}, u32[]{:S(2)}) collective-permute-start(f32[2,2,8,256]{3,2,1,0:T(8,128)S(1)} %get-tuple-element.94), channel_id=1, source_target_pairs={{0,3},{1,2},{2,5},{3,4},{4,7},{5,6},{8,11},{9,10},{10,13},{11,12},... | collective-permute-start | bytes 98312 | tf_op jit(solution)/shard_map/ppermute | solution.py:99
  183.8 5.4 %collective-permute-start.30 = (f32[2,2,8,256]{3,2,1,0:T(8,128)S(1)}, f32[2,2,8,256]{3,2,1,0:T(8,128)S(1)}, u32[]{:S(2)}, u32[]{:S(2)}) collective-permute-start(f32[2,2,8,256]{3,2,1,0:T(8,128)S(1)} %get-tuple-element.95), channel_id=1, source_target_pairs={{2,1},{3,0},{4,3},{5,2},{6,5},{7,4},{10,9},{11,8},{12,11},{13,10},... | collective-permute-start | bytes 98312 | tf_op jit(solution)/shard_map/ppermute | solution.py:99
  205.9 1.3 copy-start.7
  207.3 8.8 %collective-permute-start.34 = (f32[8,128]{0,1:T(8,128)S(1)}, f32[8,128]{0,1:T(8,128)S(1)}, u32[]{:S(2)}, u32[]{:S(2)}) collective-permute-start(f32[8,128]{0,1:T(8,128)S(1)} %copy.18), channel_id=1, source_target_pairs={{0,4},{2,6},{4,0},{6,2},{1,5},{3,7},{5,1},{7,3},{8,12},{10,14},{12... | collective-permute-start | bytes 12296 | tf_op jit(solution)/shard_map/ppermute | solution.py:426
  213.7 4.4 %collective-permute-start.35 = (f32[8,128]{0,1:T(8,128)S(1)}, f32[8,128]{0,1:T(8,128)S(1)}, u32[]{:S(2)}, u32[]{:S(2)}) collective-permute-start(f32[8,128]{0,1:T(8,128)S(1)} %copy.18), channel_id=1, source_target_pairs={{0,6},{2,4},{4,2},{6,0},{1,7},{3,5},{5,3},{7,1},{8,14},{10,12},{12... | collective-permute-start | bytes 12296 | tf_op jit(solution)/shard_map/ppermute | solution.py:426
  213.7 4.4 %collective-permute-start.33 = (f32[8,128]{0,1:T(8,128)S(1)}, f32[8,128]{0,1:T(8,128)S(1)}, u32[]{:S(2)}, u32[]{:S(2)}) collective-permute-start(f32[8,128]{0,1:T(8,128)S(1)} %copy.18), channel_id=1, source_target_pairs={{0,2},{2,0},{4,6},{6,4},{1,3},{3,1},{5,7},{7,5},{8,10},{10,8},{12,... | collective-permute-start | bytes 12296 | tf_op jit(solution)/shard_map/ppermute | solution.py:426
  218.1 4.3 %collective-permute-start.36 = (f32[8,128]{0,1:T(8,128)S(1)}, f32[8,128]{0,1:T(8,128)S(1)}, u32[]{:S(2)}, u32[]{:S(2)}) collective-permute-start(f32[8,128]{0,1:T(8,128)S(1)} %add_add_fusion), channel_id=1, source_target_pairs={{0,1},{1,0},{2,3},{3,2},{4,5},{5,4},{6,7},{7,6},{8,9},{9,8},{10,11... | collective-permute-start | bytes 12296 | tf_op jit(solution)/shard_map/ppermute | solution.py:426
  222.5 5.0 %collective-permute-start.37 = (f32[8,128]{0,1:T(8,128)S(1)}, f32[8,128]{0,1:T(8,128)S(1)}, u32[]{:S(2)}, u32[]{:S(2)}) collective-permute-start(f32[8,128]{0,1:T(8,128)S(1)} %add.79), channel_id=1, source_target_pairs={{0,8},{8,0},{16,24},{24,16},{1,9},{9,1},{17,25},{25,17},{2,10},{10... | collective-permute-start | bytes 12296 | tf_op jit(solution)/shard_map/ppermute | solution.py:426
  225.0 6.8 %collective-permute-start.38 = (f32[8,128]{0,1:T(8,128)S(1)}, f32[8,128]{0,1:T(8,128)S(1)}, u32[]{:S(2)}, u32[]{:S(2)}) collective-permute-start(f32[8,128]{0,1:T(8,128)S(1)} %add.79), channel_id=1, source_target_pairs={{0,16},{8,24},{16,0},{24,8},{1,17},{9,25},{17,1},{25,9},{2,18},{10... | collective-permute-start | bytes 12296 | tf_op jit(solution)/shard_map/ppermute | solution.py:426
  225.0 6.8 %collective-permute-start.39 = (f32[8,128]{0,1:T(8,128)S(1)}, f32[8,128]{0,1:T(8,128)S(1)}, u32[]{:S(2)}, u32[]{:S(2)}) collective-permute-start(f32[8,128]{0,1:T(8,128)S(1)} %add.79), channel_id=1, source_target_pairs={{0,24},{8,16},{16,8},{24,0},{1,25},{9,17},{17,9},{25,1},{2,26},{10... | collective-permute-start | bytes 12296 | tf_op jit(solution)/shard_map/ppermute | solution.py:426
  236.3 1.6 copy-start.4
  237.9 1.6 copy-start.6
  239.5 1.6 copy-start.8

commit v4 on v3

--- a/solution.py
+++ b/solution.py
@@ -11,16 +11,16 @@
 SUB = 8
 LANES = 128
 ROWS = 2
-BLOCK = 4
 MIB = 1024 * 1024
 FLOPS_PER_MICRO = 1.15e9
 BYTES_PER_MICRO = 3.6e6
 
 
-def kernel_call(body, outs, scratch, ins, micros, mib, anywhere=(), outs_anywhere=()):
-    spec = lambda n, names: pl.BlockSpec(memory_space=pl.ANY if n in names else pltpu.VMEM)
+def kernel_call(body, outs, scratch, ins, micros, mib, anywhere=(), outs_anywhere=(), space=pl.ANY, scalars=True):
+    spec = lambda n, names: pl.BlockSpec(memory_space=space if n in names else pltpu.VMEM)
     specs = [spec(n, anywhere) for n in range(len(ins))]
-    specs[0] = pl.BlockSpec(memory_space=pltpu.SMEM)
+    if scalars:
+        specs[0] = pl.BlockSpec(memory_space=pltpu.SMEM)
     return pl.pallas_call(
         body,
         out_shape=outs,
@@ -40,8 +40,8 @@
     return jax.ShapeDtypeStruct(shape, jnp.float32)
 
 
-def strip_shapes(fields, x, y, z, both):
-    packs = [f32(fields, x // 2, SUB, z), f32(fields, 2, SUB, z), f32(fields, 2, SUB, z)]
+def strip_shapes(fields, x, y, z, both, joined=False):
+    packs = [f32(fields, x // 2, SUB, z)] + [f32(fields, 2, SUB, z)] * (0 if joined else 2)
     return [f32(fields, STEPS, y, z)] * 2 + packs * (2 if both else 1)
 
 
@@ -60,7 +60,7 @@
 
 
 def write_packs(field, n, rows, last, outs):
-    pack, corner_lo, corner_hi = outs[2 + 3 * n : 5 + 3 * n]
+    pack, *corners = outs[2 + 3 * n : 5 + 3 * n]
     half, z = pack.shape[1], pack.shape[3]
     row = lax.broadcasted_iota(jnp.int32, (SUB, z), 0)
 
@@ -69,9 +69,9 @@
         return carry
 
     lax.fori_loop(0, half, step, None, unroll=4)
-    for i in range(2):
-        corner_lo[field, i] = pack[field, i]
-        corner_hi[field, i] = pack[field, half - 2 + i]
+    for corner, start in zip(corners, (0, half - 2)):
+        for i in range(2):
+            corner[field, i] = pack[field, start + i]
 
 
 def write_strips(tile, outs, side):
@@ -80,8 +80,26 @@
         for i in range(STEPS):
             outs[0][p, i] = tile[p, i]
             outs[1][p, i] = tile[p, x - STEPS + i]
-        for n, (start, last) in enumerate(pack_starts((len(outs) - 2) // 3, y, side)):
+        for n, (start, last) in enumerate(pack_starts(max((len(outs) - 2) // 3, 1), y, side)):
             write_packs(p, n, lambda i: tile[p, i, pl.ds(start, SUB)], last, outs)
+
+
+def join_kernel(xlo, xhi, pack, lo, hi):
+    fields, steps, y, _ = xlo.shape
+    chunks, half = y // SUB, pack.shape[1]
+    for f in range(fields):
+        for strip, out, start in ((xlo, lo, 0), (xhi, hi, half - 2)):
+            for i in range(steps):
+                for c in range(chunks):
+                    out[f, i * chunks + c] = strip[f, i, SUB * c : SUB * (c + 1)]
+            for i in range(2):
+                out[f, steps * chunks + i] = pack[f, start + i]
+
+
+def join(xlo, xhi, pack):
+    fields, steps, y, z = xlo.shape
+    out = f32(fields, steps * y // SUB + 2, SUB, z)
+    return kernel_call(join_kernel, [out, out], [], [xlo, xhi, pack], 1.0, 8, scalars=False)
 
 
 def exchange(strips):
@@ -98,6 +116,10 @@
                         pairs.append((i * ny + j, (i + dx) * ny + j + dy))
         return lax.ppermute(value, ("sx", "sy"), pairs)
 
+    if len(strips) == 3:
+        pack = moved(strips[2], 0, lambda j: (1 - 2 * j,))
+        lo, hi = join(strips[0], strips[1], pack)
+        return [lax.ppermute(hi, "sx", up), lax.ppermute(lo, "sx", down), pack]
     below = lax.ppermute(strips[1], "sx", up)
     above = lax.ppermute(strips[0], "sx", down)
     received = [below, above]
@@ -133,6 +155,8 @@
 def start_widening(copies, dst, tile, field, received):
     x, y = tile.shape[0], tile.shape[1]
     copies.start(tile, dst.at[pl.ds(0, x), pl.ds(0, y)])
+    if len(received) == 3:
+        return
     copies.start(received[1].at[field], dst.at[pl.ds(x, STEPS), pl.ds(0, y)])
     copies.start(received[0].at[field], dst.at[pl.ds(x + STEPS, STEPS), pl.ds(0, y)])
 
@@ -153,6 +177,15 @@
         dst[at + 1, y : y + SUB] = jnp.where(row < STEPS, pltpu.roll(hi, STEPS, 0), lo)
 
     groups = [received[2:5]] + ([received[5:8]] if both else [])
+    first = 0
+    if len(received) == 3:
+        below, above, pack = received
+        groups = [[pack, below, above]]
+        first = STEPS * y // SUB
+        for strip, at in ((above, x), (below, x + STEPS)):
+            for i in range(STEPS):
+                for c in range(y // SUB):
+                    dst[at + i, SUB * c : SUB * (c + 1)] = strip[field, i * (y // SUB) + c]
 
     def main(i, carry):
         put(2 * i, [g[0][field, i] for g in groups])
@@ -160,8 +193,8 @@
 
     lax.fori_loop(0, half, main, None, unroll=4)
     for i in range(2):
-        put(x + 2 * i, [g[2][field, i] for g in groups])
-        put(x + STEPS + 2 * i, [g[1][field, i] for g in groups])
+        put(x + 2 * i, [g[2][field, first + i] for g in groups])
+        put(x + STEPS + 2 * i, [g[1][field, first + i] for g in groups])
 
 
 def coefficient_rows(coef):
@@ -274,7 +307,7 @@
     side = scalars[0]
     tiles = [ref.at[n] for ref in sources for n in range(ref.shape[0])]
     x, y, _ = tiles[0].shape
-    starts = pack_starts((len(outs) - 2) // 3, y, side)
+    starts = pack_starts(max((len(outs) - 2) // 3, 1), y, side)
     copies = Copies(sems)
     for f, tile in enumerate(tiles):
         for n, (start, _) in enumerate(starts):
@@ -328,40 +361,15 @@
         write_strips(out, strips, side)
 
 
-def blocked_call(body, out_shape, out_block, scratch, scalars, ins, micros):
-    group, x, y, z = ins[0].shape
-    block = pl.BlockSpec((group, BLOCK, y, z), lambda i: (0, i, 0, 0))
-    out = block if out_block else pl.BlockSpec(out_shape.shape, lambda i: (0, 0))
-    return pl.pallas_call(
-        body,
-        grid=(x // BLOCK,),
-        out_shape=out_shape,
-        in_specs=[pl.BlockSpec(memory_space=pltpu.SMEM)] + [block] * len(ins),
-        out_specs=out,
-        scratch_shapes=scratch,
-        compiler_params=pltpu.CompilerParams(vmem_limit_bytes=12 * MIB),
-        cost_estimate=pl.CostEstimate(
-            flops=int(micros * FLOPS_PER_MICRO),
-            bytes_accessed=int(micros * BYTES_PER_MICRO),
-            transcendentals=0,
-        ),
-    )(scalars, *ins)
-
-
 def dots_pairs(group, slots):
     return [(s, a, b) for s in range(slots) for a in range(group) for b in range(group) if s or b <= a]
 
 
 def dots_kernel(scalars, second, *refs):
-    passed, (out, held) = refs[:-2], refs[-2:]
+    passed, out = refs[:-1], refs[-1]
     group, rows, y, z = second.shape
     chunks, cols = y // SUB, z // LANES
     pairs = dots_pairs(group, len(passed))
-    at_step = pl.program_id(0)
-
-    @pl.when(at_step == 0)
-    def _():
-        held[...] = jnp.zeros(held.shape, jnp.float32)
 
     def body(i, sums):
         sums = list(sums)
@@ -377,30 +385,48 @@
                     sums[2 * n + 1] = sums[2 * n + 1] + then[a] * value
         return tuple(sums)
 
-    sums = lax.fori_loop(0, rows, body, tuple(held[n] for n in range(2 * len(pairs))))
-    for n, value in enumerate(sums):
-        held[n] = value
-
-    @pl.when(at_step == pl.num_programs(0) - 1)
-    def _():
-        me = scalars[1]
-        count = out.shape[0]
-        row = lax.broadcasted_iota(jnp.int32, out.shape, 0)
-        lane = lax.broadcasted_iota(jnp.int32, out.shape, 1)
-        total = jnp.zeros(out.shape, jnp.float32)
-        for n, (s, a, b) in enumerate(pairs):
-            for k in range(2):
-                value = jnp.sum(jnp.sum(sums[2 * n + k], axis=0, keepdims=True), axis=1, keepdims=True)
-                column = (me - s) * group + b + k * count
-                here = (row == me * group + a) & (lane == column) & (me >= s)
-                total = total + jnp.where(here, value, 0.0)
-        out[...] = total
-
-
-def basis_kernel(inverse, *refs):
-    images, out = refs[:-1], refs[-1]
-    group, rows, y, z = out.shape
-    factors = [[inverse[a, n] for n in range(group * len(images))] for a in range(group)]
+    zero = jnp.zeros((SUB, LANES), jnp.float32)
+    sums = lax.fori_loop(0, rows, body, (zero,) * (2 * len(pairs)))
+    me = scalars[1]
+    count = out.shape[0]
+    row = lax.broadcasted_iota(jnp.int32, out.shape, 0)
+    lane = lax.broadcasted_iota(jnp.int32, out.shape, 1)
+    total = jnp.zeros(out.shape, jnp.float32)
+    for n, (s, a, b) in enumerate(pairs):
+        for k in range(2):
+            value = jnp.sum(jnp.sum(sums[2 * n + k], axis=0, keepdims=True), axis=1, keepdims=True)
+            i, j = me * group + a, (me - s) * group + b
+            here = (row == i) & (lane == j + k * count) | (row == j) & (lane == i + k * count)
+            total = total + jnp.where(here & (me >= s), value, 0.0)
+    out[...] = total
+
+
+def finish_kernel(scale, scalars, inner, *refs):
+    images, (basis, projected, held, sems) = refs[:-4], refs[-4:]
+    group, x, y, z = held.shape
+    count = inner.shape[0]
+    me = scalars[1]
+    row = lax.broadcasted_iota(jnp.int32, inner.shape, 0)
+    lane = lax.broadcasted_iota(jnp.int32, inner.shape, 1)
+    base = 2 * count
+    work = jnp.where(lane == row + base, 1.0, inner[...] * scale)
+    for k in range(count):
+        column = jnp.broadcast_to(work[:, k : k + 1], inner.shape)
+        pivot = jnp.broadcast_to(column[k : k + 1], inner.shape)
+        line = jnp.broadcast_to(work[k : k + 1], inner.shape)
+        work = work - jnp.where(row > k, column / pivot, 0.0) * line
+    pivots = jnp.sum(jnp.where(lane == row, work, 0.0), axis=1, keepdims=True)
+    work = work * (1.0 / jnp.sqrt(pivots))
+
+    factors = []
+    for a in range(group):
+        factors.append([])
+        for s in range(len(images)):
+            for b in range(group):
+                here = (row == me * group + a) & (lane == base + (me - s) * group + b) & (me >= s)
+                value = jnp.sum(jnp.where(here, work, 0.0), axis=0, keepdims=True)
+                value = jnp.sum(value, axis=1, keepdims=True)
+                factors[a].append(jnp.broadcast_to(value, (SUB, LANES)))
 
     def body(i, carry):
         for c in range(y // SUB):
@@ -411,10 +437,25 @@
                     terms = [factor * value for factor, value in zip(factors[a], values)]
                     while len(terms) > 1:
                         terms = [sum(terms[n : n + 2][1:], terms[n]) for n in range(0, len(terms), 2)]
-                    out[a, i, *at] = terms[0]
+                    held[a, i, *at] = terms[0]
         return carry
 
-    lax.fori_loop(0, rows, body, None)
+    copies = Copies(sems)
+    for start in range(0, x, SUB):
+        lax.fori_loop(start, start + SUB, body, None)
+        for a in range(group):
+            copies.start(held.at[a, pl.ds(start, SUB)], basis.at[a, pl.ds(start, SUB)])
+
+    left = jnp.where((lane >= count) & (lane < base), work, 0.0)
+    right = jnp.where((lane >= count) & (lane < base), pltpu.roll(work, LANES - count, 1), 0.0)
+    projected[...] = lax.dot_general(
+        left,
+        right,
+        (((1,), (1,)), ((), ())),
+        precision=lax.Precision.HIGHEST,
+        preferred_element_type=jnp.float32,
+    )
+    copies.wait()
 
 
 def all_sum(value):
@@ -446,7 +487,7 @@
     where = jnp.stack([side, mine]).astype(jnp.int32)
     wide = (x + 2 * STEPS, y + 2 * STEPS, z)
     tile = f32(group, x, y, z)
-    strips2 = strip_shapes(group, x, y, z, both)
+    strips2 = strip_shapes(group, x, y, z, both, not both)
     fields = [diffusivity[None], velocity, probes]
     total = 4 + group
 
@@ -461,14 +502,16 @@
 
     def pack(sources):
         number = sum(a.shape[0] for a in sources)
+        joined = number == group and not both
         return kernel_call(
             functools.partial(pack_kernel, len(sources)),
-            strip_shapes(number, x, y, z, both),
+            strip_shapes(number, x, y, z, both, joined),
             [pltpu.VMEM((packs, number, x, SUB, z), jnp.float32), pltpu.SemaphoreType.DMA((number * (packs + 2),))],
             [where] + sources,
             3.0,
             12,
             anywhere=range(1, len(sources) + 1),
+            space=pl.ANY if joined else pltpu.HBM,
         )
 
     def right(value, hops):
@@ -496,7 +539,7 @@
             ins + received,
             12.0,
             14,
-            anywhere=(2, len(ins), len(ins) + 1),
+            anywhere=(2, len(ins), len(ins) + 1) if both else (2,),
         )
 
     images, *strips = model(halfway, exchange(strips), True)
@@ -512,32 +555,23 @@
     halfway, *strips = model(images, received, False)
     (second,) = model(halfway, exchange(strips), True, True)
 
-    slots = len(passed)
-    partial = blocked_call(
+    (partial,) = kernel_call(
         dots_kernel,
-        f32(count, LANES),
-        False,
-        [pltpu.VMEM((2 * len(dots_pairs(group, slots)), SUB, LANES), jnp.float32)],
-        where,
-        [second] + passed,
+        [f32(count, LANES)],
+        [],
+        [where, second] + passed,
+        4.0,
+        14,
+    )
+    basis, projected = kernel_call(
+        functools.partial(finish_kernel, 1.0 / ncells),
+        [tile, f32(count, count)],
+        [pltpu.VMEM((group, x, y, z), jnp.float32), pltpu.SemaphoreType.DMA((group * (x // SUB),))],
+        [where, all_sum(partial)] + passed,
         5.0,
+        14,
+        outs_anywhere=(0,),
     )
-    inner = all_sum(partial) / ncells
-    strict = jnp.tril(jnp.ones((count, count), jnp.float32), -1)
-    gram, ritz = inner[:, :count], inner[:, count : 2 * count]
-    gram = gram + (gram * strict).T
-    ritz = ritz + (ritz * strict).T
-    lower = jnp.linalg.cholesky(gram)
-    inverse = jax.scipy.linalg.solve_triangular(lower, jnp.eye(count, dtype=jnp.float32), lower=True)
-    highest = lax.Precision.HIGHEST
-    projected = jnp.dot(jnp.dot(inverse, ritz, precision=highest), inverse.T, precision=highest)
-
-    rows = lax.dynamic_slice_in_dim(inverse, mine * group, group, 0)
-    parts = []
-    for n in range(groups):
-        part = lax.dynamic_slice_in_dim(rows, jnp.maximum(mine - n, 0) * group, group, 1)
-        parts.append(jnp.where(mine >= n, part, 0.0))
-    basis = blocked_call(basis_kernel, tile, True, [], jnp.concatenate(parts, 1), passed, 4.0)
     return (basis, projected)
 
 

time: 247 us -> 216 us (0.87)
  starting transfers between devices: 96.8 us -> 52.8 us
  waiting for transfers between devices: 41.9 us -> 68 us
  local copies, waits for them, and re-layouts: 11.3 us -> 4.72 us
  other arithmetic: 3.05 us -> 0.09 us
    ppermute x18 -> x8, starting transfers between devices: 42.5 us -> 10.3 us  [moved(): return lax.ppermute(value, ('sx', 'sy'), pairs)]
    ppermute x6 -> x1, starting transfers between devices: 23.5 us -> 2.41 us  [exchange(): below = lax.ppermute(strips[1], 'sx', up)]
    ppermute x3, waiting for transfers between devices: 0.01 us -> 17.8 us  [right(): lax.ppermute(value, 'probe', [(i, i + hops) for i in range(groups - hops)])]
    ppermute x0 -> x10, starting transfers between devices: none -> 17.8 us  [exchange(): return [lax.ppermute(hi, 'sx', up), lax.ppermute(lo, 'sx', down), pack]]
    ppermute x18 -> x8, waiting for transfers between devices: 29.7 us -> 38.6 us  [moved(): return lax.ppermute(value, ('sx', 'sy'), pairs)]
    pallas_call x2 -> x0, Pallas kernels: 8.56 us -> none  [blocked_call(): pl.pallas_call(body, grid=(x // BLOCK,), out_shape=out_shape, in_specs=[p...]
    pallas_call x8 -> x15, Pallas kernels: 81.7 us -> 88.4 us  [kernel_call(): pl.pallas_call(body, out_shape=outs, in_specs=specs, out_specs=[spec(n, o...]
    ppermute x6 -> x1, starting transfers between devices: 7.75 us -> 1.29 us  [exchange(): above = lax.ppermute(strips[0], 'sx', down)]
  transfers between devices with their start and end apart: 40 -> 30, of which waited for: 12 -> 15; matrix products, arithmetic and copies ran while one was open for 0% -> 0% of each run, Pallas kernels for 32% -> 36%
where the time goes in v4:
time: 216 us; the launch traced here: 215 us
  Pallas kernels  88.4 us (41%)
  waiting for transfers between devices  68 us (31%)
  starting transfers between devices  52.8 us (24%)
  local copies, waits for them, and re-layouts  4.72 us (2%)
    pallas_call x15, Pallas kernels, kernel_call(): pl.pallas_call(body, out_shape=outs, in_specs=specs, out_specs=[spec(n, o...  88.4 us
    ppermute x8, waiting for transfers between devices, moved(): return lax.ppermute(value, ('sx', 'sy'), pairs)  38.6 us
    ppermute x3, waiting for transfers between devices, right(): lax.ppermute(value, 'probe', [(i, i + hops) for i in range(groups - hops)])  17.8 us
    ppermute x10, starting transfers between devices, exchange(): return [lax.ppermute(hi, 'sx', up), lax.ppermute(lo, 'sx', down), pack]  17.8 us
    ppermute x3, starting transfers between devices, right(): lax.ppermute(value, 'probe', [(i, i + hops) for i in range(groups - hops)])  11.8 us
    ppermute x8, starting transfers between devices, moved(): return lax.ppermute(value, ('sx', 'sy'), pairs)  10.3 us
    ppermute x7, waiting for transfers between devices, all_sum(): lax.ppermute(value, axis, [(i, i ^ bits) for i in range(devices)])  9.3 us
    ppermute x7, starting transfers between devices, all_sum(): lax.ppermute(value, axis, [(i, i ^ bits) for i in range(devices)])  9.22 us
  transfers between devices with their start and end apart: 30, of which 15 were waited for; matrix products, arithmetic and copies ran while one was open for 0% of the time, Pallas kernels for 36%

profile of v4, /device:TPU:0, one launch (start us, length us, event | category | flops | bytes accessed | tf_op | source)
XLA Modules:
  0.0 214.9 jit_solution(5033267217338881643)
XLA Ops:
  0.6 0.1 pad_add_fusion.scalars
  0.7 1.9 copy-done
  2.6 1.6 copy-done.2
  4.2 1.2 copy-done.3
  5.4 3.1 %shard_map.59 = (f32[6,4,32,256]{3,2,1,0:T(8,128)S(1)}, f32[6,4,32,256]{3,2,1,0:T(8,128)S(1)}, f32[6,16,8,256]{3,2,1,0:T(8,128)S(1)}, f32[6,2,8,256]{3,2,1,0:T(8,128)S(1)}, f32[6,2,8,256]{3,2,1,0:T(8,128)S(1)}) custom-call(s32[2]{0:T(128)S(1)} %pad_add_fusion.scalars, f32[1,32,32,256]{3,2,1,0:T(8,128)S(1)} %bitcast.3, f32[3,32,32,256]{3,2,1,0:T(8,128)S(1)} %copy-done, ...), custom_call_target="tpu_custom_call" | custom-call | flops 3449999872 | bytes 10800000 | tf_op jit(solution)/shard_map/pallas_call | solution.py:24
  8.5 2.4 %collective-permute-start = (f32[6,4,32,256]{3,2,1,0:T(8,128)S(1)}, f32[6,4,32,256]{3,2,1,0:T(8,128)S(1)}, u32[]{:S(2)}, u32[]{:S(2)}) collective-permute-start(f32[6,4,32,256]{3,2,1,0:T(8,128)S(1)} %get-tuple-element.46), channel_id=1, source_target_pairs={{0,2},{2,4},{4,6},{1,3},{3,5},{5,7},{8,10},{10,12},{12,14},{9,11},... | collective-permute-start | bytes 2359304 | tf_op jit(solution)/shard_map/ppermute | solution.py:123
  11.0 1.3 collective-permute-start.1
  12.3 2.4 %collective-permute-start.2 = (f32[6,16,8,256]{3,2,1,0:T(8,128)S(1)}, f32[6,16,8,256]{3,2,1,0:T(8,128)S(1)}, u32[]{:S(2)}, u32[]{:S(2)}) collective-permute-start(f32[6,16,8,256]{3,2,1,0:T(8,128)S(1)} %get-tuple-element.48), channel_id=1, source_target_pairs={{0,1},{1,0},{2,3},{3,2},{4,5},{5,4},{6,7},{7,6},{8,9},{9,8},{10,11... | collective-permute-start | bytes 2359304 | tf_op jit(solution)/shard_map/ppermute | solution.py:117
  14.7 3.6 %collective-permute-start.8 = (f32[2,32,32,256]{3,2,1,0:T(8,128)S(1)}, f32[2,32,32,256]{3,2,1,0:T(8,128)S(1)}, u32[]{:S(2)}, u32[]{:S(2)}) collective-permute-start(f32[2,32,32,256]{3,2,1,0:T(8,128)S(1)} %copy-done.2), channel_id=1, source_target_pairs={{0,8},{8,16},{16,24},{1,9},{9,17},{17,25},{2,10},{10,18},{18,26},{... | collective-permute-start | bytes 6291464 | tf_op jit(solution)/shard_map/ppermute | solution.py:518
  18.3 3.8 %collective-permute-start.3 = (f32[6,2,8,256]{3,2,1,0:T(8,128)S(1)}, f32[6,2,8,256]{3,2,1,0:T(8,128)S(1)}, u32[]{:S(2)}, u32[]{:S(2)}) collective-permute-start(f32[6,2,8,256]{3,2,1,0:T(8,128)S(1)} %get-tuple-element.49), channel_id=1, source_target_pairs={{0,3},{1,2},{2,5},{3,4},{4,7},{5,6},{8,11},{9,10},{10,13},{11,12},... | collective-permute-start | bytes 294920 | tf_op jit(solution)/shard_map/ppermute | solution.py:117
  22.1 11.2 %collective-permute-done.3.refs_3_ = f32[6,2,8,256]{3,2,1,0:T(8,128)S(1)} collective-permute-done((f32[6,2,8,256]{3,2,1,0:T(8,128)S(1)}, f32[6,2,8,256]{3,2,1,0:T(8,128)S(1)}, u32[]{:S(2)}, u32[]{:S(2)}) %collective-permute-start.3) | collective-permute-done | bytes 98336 | tf_op jit(solution)/shard_map/ppermute | solution.py:117
  33.3 1.3 collective-permute-start.4
  34.6 4.8 %collective-permute-done.4.refs_4_ = f32[6,2,8,256]{3,2,1,0:T(8,128)S(1)} collective-permute-done((f32[6,2,8,256]{3,2,1,0:T(8,128)S(1)}, f32[6,2,8,256]{3,2,1,0:T(8,128)S(1)}, u32[]{:S(2)}, u32[]{:S(2)}) %collective-permute-start.4) | collective-permute-done | bytes 98336 | tf_op jit(solution)/shard_map/ppermute | solution.py:117
  39.4 0.0 collective-permute-done.refs_0_
  39.4 0.0 collective-permute-done.1.refs_1_
  39.4 0.0 collective-permute-done.2.refs_2_
  39.4 14.3 %shard_map.60 = (f32[7,40,40,256]{3,2,1,0:T(8,128)S(1)}, f32[2,32,32,256]{3,2,1,0:T(8,128)S(1)}, f32[2,4,32,256]{3,2,1,0:T(8,128)S(1)}, f32[2,4,32,256]{3,2,1,0:T(8,128)S(1)}, f32[2,16,8,256]{3,2,1,0:T(8,128)S(1)}) custom-call(s32[2]{0:T(128)S(1)} %pad_add_fusion.scalars, f32[1,32,32,256]{3,2,1,0:T(8,128)S(1)} %bitcast.4, f32[3,32,32,256]{3,2,1,0:T(8,128)S(1)} %copy-done.1, ...), custom_call_target="tpu_custom_call" | custom-call | flops 16099999744 | bytes 50400000 | tf_op jit(solution)/shard_map/pallas_call | solution.py:24
  53.7 0.1 collective-permute-start.5
  53.8 9.2 %collective-permute-done.8.refs_0_.tile = f32[2,32,32,256]{3,2,1,0:T(8,128)S(1)} collective-permute-done((f32[2,32,32,256]{3,2,1,0:T(8,128)S(1)}, f32[2,32,32,256]{3,2,1,0:T(8,128)S(1)}, u32[]{:S(2)}, u32[]{:S(2)}) %collective-permute-start.8) | collective-permute-done | bytes 2097184 | tf_op jit(solution)/shard_map/ppermute | solution.py:518
  63.0 1.4 shard_map.63
  64.4 0.6 collective-permute-start.9
  65.1 2.9 %collective-permute-start.6 = (f32[2,18,8,256]{3,2,1,0:T(8,128)S(1)}, f32[2,18,8,256]{3,2,1,0:T(8,128)S(1)}, u32[]{:S(2)}, u32[]{:S(2)}) collective-permute-start(f32[2,18,8,256]{3,2,1,0:T(8,128)S(1)} %get-tuple-element.56), channel_id=1, source_target_pairs={{0,2},{2,4},{4,6},{1,3},{3,5},{5,7},{8,10},{10,12},{12,14},{9,11},... | collective-permute-start | bytes 884744 | tf_op jit(solution)/shard_map/ppermute | solution.py:122
  67.9 1.3 collective-permute-start.7
  69.2 4.2 %collective-permute-done.9.pack.refs_3_ = f32[2,16,8,256]{3,2,1,0:T(8,128)S(1)} collective-permute-done((f32[2,16,8,256]{3,2,1,0:T(8,128)S(1)}, f32[2,16,8,256]{3,2,1,0:T(8,128)S(1)}, u32[]{:S(2)}, u32[]{:S(2)}) %collective-permute-start.9) | collective-permute-done | bytes 262176 | tf_op jit(solution)/shard_map/ppermute | solution.py:117
  73.5 2.0 collective-permute-start.10
  75.5 1.3 collective-permute-start.11
  76.8 0.0 collective-permute-done.6.refs_0_
  76.8 0.0 collective-permute-done.7.refs_1_
  76.8 12.6 %shard_map.62 = (f32[2,32,32,256]{3,2,1,0:T(8,128)S(1)}, f32[2,4,32,256]{3,2,1,0:T(8,128)S(1)}, f32[2,4,32,256]{3,2,1,0:T(8,128)S(1)}, f32[2,16,8,256]{3,2,1,0:T(8,128)S(1)}) custom-call(s32[2]{0:T(128)S(1)} %pad_add_fusion.scalars, f32[7,40,40,256]{3,2,1,0:T(8,128)S(1)} %get-tuple-element.51.coef, f32[2,32,32,256]{3,2,1,0:T(8,128)S(1)} %get-tuple-element.52.tile, ...), custom_call_target="tpu_custom_call" | custom-call | flops 13799999488 | bytes 43200000 | tf_op jit(solution)/shard_map/pallas_call | solution.py:24
  89.5 6.8 %collective-permute-start.21 = (f32[2,32,32,256]{3,2,1,0:T(8,128)S(1)}, f32[2,32,32,256]{3,2,1,0:T(8,128)S(1)}, u32[]{:S(2)}, u32[]{:S(2)}) collective-permute-start(f32[2,32,32,256]{3,2,1,0:T(8,128)S(1)} %get-tuple-element.58.tile.refs_0_), channel_id=1, source_target_pairs={{0,24},{1,25},{2,26},{3,27},{4,28},{5,29},{6,30},{7,31}} | collective-permute-start | bytes 6291464 | tf_op jit(solution)/shard_map/ppermute | solution.py:518
  96.2 0.0 collective-permute-done.11.refs_2_
  96.2 12.3 %shard_map.65 = (f32[2,32,32,256]{3,2,1,0:T(8,128)S(1)}, f32[2,4,32,256]{3,2,1,0:T(8,128)S(1)}, f32[2,4,32,256]{3,2,1,0:T(8,128)S(1)}, f32[2,16,8,256]{3,2,1,0:T(8,128)S(1)}) custom-call(s32[2]{0:T(128)S(1)} %pad_add_fusion.scalars, f32[7,40,40,256]{3,2,1,0:T(8,128)S(1)} %get-tuple-element.51.coef, ...), custom_call_target="tpu_custom_call" | custom-call | flops 13799999488 | bytes 43200000 | tf_op jit(solution)/shard_map/pallas_call | solution.py:24
  108.6 0.6 collective-permute-start.15
  109.1 1.5 collective-permute-start.12
  110.7 7.2 %collective-permute-done.15.pack.refs_2_ = f32[2,16,8,256]{3,2,1,0:T(8,128)S(1)} collective-permute-done((f32[2,16,8,256]{3,2,1,0:T(8,128)S(1)}, f32[2,16,8,256]{3,2,1,0:T(8,128)S(1)}, u32[]{:S(2)}, u32[]{:S(2)}) %collective-permute-start.15) | collective-permute-done | bytes 262176 | tf_op jit(solution)/shard_map/ppermute | solution.py:117
  117.9 1.8 collective-permute-start.16
  119.7 1.3 collective-permute-start.17
  121.0 2.4 %collective-permute-done.12.pack.refs_3_ = f32[2,16,8,256]{3,2,1,0:T(8,128)S(1)} collective-permute-done((f32[2,16,8,256]{3,2,1,0:T(8,128)S(1)}, f32[2,16,8,256]{3,2,1,0:T(8,128)S(1)}, u32[]{:S(2)}, u32[]{:S(2)}) %collective-permute-start.12) | collective-permute-done | bytes 262176 | tf_op jit(solution)/shard_map/ppermute | solution.py:117
  123.4 2.8 %collective-permute-start.13 = (f32[2,18,8,256]{3,2,1,0:T(8,128)S(1)}, f32[2,18,8,256]{3,2,1,0:T(8,128)S(1)}, u32[]{:S(2)}, u32[]{:S(2)}) collective-permute-start(f32[2,18,8,256]{3,2,1,0:T(8,128)S(1)} %get-tuple-element.71), channel_id=1, source_target_pairs={{0,2},{2,4},{4,6},{1,3},{3,5},{5,7},{8,10},{10,12},{12,14},{9,11},... | collective-permute-start | bytes 884744 | tf_op jit(solution)/shard_map/ppermute | solution.py:122
  126.1 1.3 collective-permute-start.14
  127.4 0.0 collective-permute-done.17.refs_1_
  127.4 12.5 %shard_map.68.refs_1_ = f32[2,32,32,256]{3,2,1,0:T(8,128)S(1)} custom-call(s32[2]{0:T(128)S(1)} %pad_add_fusion.scalars, f32[7,40,40,256]{3,2,1,0:T(8,128)S(1)} %get-tuple-element.51.coef, f32[2,32,32,256]{3,2,1,0:T(8,128)S(1)} %get-tuple-element.73.tile, f32[2,18,8,256]{3,2,1,0:T(8,128)S(1)} %collective-permute-done.16.refs_0_, ...), custom_call_target="tpu_custom_call" | custom-call | flops 13799999488 | bytes 43200000 | tf_op jit(solution)/shard_map/pallas_call | solution.py:24
  139.9 2.1 collective-permute-done.21.refs_3_
  142.0 1.4 collective-permute-start.22
  143.4 12.3 %shard_map.69 = (f32[2,32,32,256]{3,2,1,0:T(8,128)S(1)}, f32[2,4,32,256]{3,2,1,0:T(8,128)S(1)}, f32[2,4,32,256]{3,2,1,0:T(8,128)S(1)}, f32[2,16,8,256]{3,2,1,0:T(8,128)S(1)}) custom-call(s32[2]{0:T(128)S(1)} %pad_add_fusion.scalars, f32[7,40,40,256]{3,2,1,0:T(8,128)S(1)} %get-tuple-element.51.coef, f32[2,32,32,256]{3,2,1,0:T(8,128)S(1)} %get-tuple-element.58.tile.refs_0_, ...), custom_call_target="tpu_custom_call" | custom-call | flops 13799999488 | bytes 43200000 | tf_op jit(solution)/shard_map/pallas_call | solution.py:24
  155.7 0.1 collective-permute-start.18
  155.8 9.0 %collective-permute-done.18.pack.refs_2_ = f32[2,16,8,256]{3,2,1,0:T(8,128)S(1)} collective-permute-done((f32[2,16,8,256]{3,2,1,0:T(8,128)S(1)}, f32[2,16,8,256]{3,2,1,0:T(8,128)S(1)}, u32[]{:S(2)}, u32[]{:S(2)}) %collective-permute-start.18) | collective-permute-done | bytes 262176 | tf_op jit(solution)/shard_map/ppermute | solution.py:117
  164.8 1.8 collective-permute-start.19
  166.7 1.3 collective-permute-start.20
  168.0 2.2 %collective-permute-done.20.refs_1_ = f32[2,18,8,256]{3,2,1,0:T(8,128)S(1)} collective-permute-done((f32[2,18,8,256]{3,2,1,0:T(8,128)S(1)}, f32[2,18,8,256]{3,2,1,0:T(8,128)S(1)}, u32[]{:S(2)}, u32[]{:S(2)}) %collective-permute-start.20) | collective-permute-done | bytes 294944 | tf_op jit(solution)/shard_map/ppermute | solution.py:122
  170.1 12.5 %shard_map.71.second = f32[2,32,32,256]{3,2,1,0:T(8,128)S(1)} custom-call(s32[2]{0:T(128)S(1)} %pad_add_fusion.scalars, f32[7,40,40,256]{3,2,1,0:T(8,128)S(1)} %get-tuple-element.51.coef, f32[2,32,32,256]{3,2,1,0:T(8,128)S(1)} %get-tuple-element.82.tile, f32[2,18,8,256]{3,2,1,0:T(8,128)S(1)} %collective-permute-done.19.refs_0_, ...), custom_call_target="tpu_custom_call" | custom-call | flops 13799999488 | bytes 43200000 | tf_op jit(solution)/shard_map/pallas_call | solution.py:24
  182.6 6.6 %collective-permute-done.22.refs_2_ = f32[2,32,32,256]{3,2,1,0:T(8,128)S(1)} collective-permute-done((f32[2,32,32,256]{3,2,1,0:T(8,128)S(1)}, f32[2,32,32,256]{3,2,1,0:T(8,128)S(1)}, u32[]{:S(2)}, u32[]{:S(2)}) %collective-permute-start.22) | collective-permute-done | bytes 2097184 | tf_op jit(solution)/shard_map/ppermute | solution.py:518
  189.2 3.0 %shard_map.72 = f32[8,128]{1,0:T(8,128)S(1)} custom-call(s32[2]{0:T(128)S(1)} %pad_add_fusion.scalars, f32[2,32,32,256]{3,2,1,0:T(8,128)S(1)} %shard_map.71.second, f32[2,32,32,256]{3,2,1,0:T(8,128)S(1)} %get-tuple-element.58.tile.refs_0_, f32[2,32,32,256]{3,2,1,0:T(8,128)S(1)} %shard_map.68.refs_1_, f32[2,32,32,256]{3,2,1,0:T(8,128)S(1)} %collective-permute-done.22.refs_2_, ...), custom_call_target="tpu_custom_call" | custom-call | flops 4600000000 | bytes 14400000 | tf_op jit(solution)/shard_map/pallas_call | solution.py:24
  192.2 0.1 collective-permute-start.25
  192.3 1.9 collective-permute-start.24
  194.2 1.1 collective-permute-done.25
  195.3 0.6 collective-permute-done.24
  196.0 0.1 collective-permute-start.26
  196.0 3.6 %collective-permute-done.26 = f32[8,128]{1,0:T(8,128)S(1)} collective-permute-done((f32[8,128]{1,0:T(8,128)S(1)}, f32[8,128]{1,0:T(8,128)S(1)}, u32[]{:S(2)}, u32[]{:S(2)}) %collective-permute-start.26) | collective-permute-done | bytes 4128 | tf_op jit(solution)/shard_map/ppermute | solution.py:467
  199.6 6.6 %collective-permute-start.29 = (f32[8,128]{1,0:T(8,128)S(1)}, f32[8,128]{1,0:T(8,128)S(1)}, u32[]{:S(2)}, u32[]{:S(2)}) collective-permute-start(f32[8,128]{1,0:T(8,128)S(1)} %add.24), channel_id=1, source_target_pairs={{0,24},{8,16},{16,8},{24,0},{1,25},{9,17},{17,9},{25,1},{2,26},{10... | collective-permute-start | bytes 12296 | tf_op jit(solution)/shard_map/ppermute | solution.py:467
  206.3 0.6 collective-permute-start.27
  206.8 1.0 collective-permute-done.29
  207.9 2.9 %collective-permute-done.28 = f32[8,128]{1,0:T(8,128)S(1)} collective-permute-done((f32[8,128]{1,0:T(8,128)S(1)}, f32[8,128]{1,0:T(8,128)S(1)}, u32[]{:S(2)}, u32[]{:S(2)}) %collective-permute-start.28) | collective-permute-done | bytes 4128 | tf_op jit(solution)/shard_map/ppermute | solution.py:467
  210.8 4.1 %shard_map.73 = (f32[2,32,32,256]{3,2,1,0:T(8,128)}, f32[8,8]{1,0:T(8,128)}) custom-call(s32[2]{0:T(128)S(1)} %pad_add_fusion.scalars, f32[8,128]{1,0:T(8,128)S(1)} %add_add_fusion.inner, f32[2,32,32,256]{3,2,1,0:T(8,128)S(1)} %get-tuple-element.58.tile.refs_0_, f32[2,32,32,256]{3,2,1,0:T(8,128)S(1)} %shard_map.68.refs_1_, ...), custom_call_target="tpu_custom_call" | custom-call | flops 5750000128 | bytes 18000000 | tf_op jit(solution)/shard_map/pallas_call | solution.py:24
  (27 shorter events, 0.3 us)
Async XLA Ops:
  0.7 1.9 copy-start
  2.6 1.6 copy-start.2
  4.2 1.2 copy-start.3
  5.4 34.0 %copy-start.1 = (f32[3,32,32,256]{3,2,1,0:T(8,128)S(1)}, f32[3,32,32,256]{3,2,1,0:T(8,128)}, u32[]{:S(2)}) copy-start(f32[3,32,32,256]{3,2,1,0:T(8,128)} %velocity.1) | copy-start | bytes 9437188
  5.4 34.0 %copy-start.4 = (f32[32,32,256]{2,1,0:T(8,128)S(1)}, f32[32,32,256]{2,1,0:T(8,128)}, u32[]{:S(2)}) copy-start(f32[32,32,256]{2,1,0:T(8,128)} %param.6) | copy-start | bytes 3145732
  5.4 34.0 %copy-start.5 = (f32[32,32,256]{2,1,0:T(8,128)S(1)}, f32[32,32,256]{2,1,0:T(8,128)}, u32[]{:S(2)}) copy-start(f32[32,32,256]{2,1,0:T(8,128)} %refs_0_.3) | copy-start | bytes 3145732
  8.5 30.8 %collective-permute-start = (f32[6,4,32,256]{3,2,1,0:T(8,128)S(1)}, f32[6,4,32,256]{3,2,1,0:T(8,128)S(1)}, u32[]{:S(2)}, u32[]{:S(2)}) collective-permute-start(f32[6,4,32,256]{3,2,1,0:T(8,128)S(1)} %get-tuple-element.46), channel_id=1, source_target_pairs={{0,2},{2,4},{4,6},{1,3},{3,5},{5,7},{8,10},{10,12},{12,14},{9,11},... | collective-permute-start | bytes 2359304 | tf_op jit(solution)/shard_map/ppermute | solution.py:123
  11.0 28.4 %collective-permute-start.1 = (f32[6,4,32,256]{3,2,1,0:T(8,128)S(1)}, f32[6,4,32,256]{3,2,1,0:T(8,128)S(1)}, u32[]{:S(2)}, u32[]{:S(2)}) collective-permute-start(f32[6,4,32,256]{3,2,1,0:T(8,128)S(1)} %get-tuple-element.47), channel_id=1, source_target_pairs={{2,0},{4,2},{6,4},{3,1},{5,3},{7,5},{10,8},{12,10},{14,12},{11,9},... | collective-permute-start | bytes 2359304 | tf_op jit(solution)/shard_map/ppermute | solution.py:124
  12.3 27.1 %collective-permute-start.2 = (f32[6,16,8,256]{3,2,1,0:T(8,128)S(1)}, f32[6,16,8,256]{3,2,1,0:T(8,128)S(1)}, u32[]{:S(2)}, u32[]{:S(2)}) collective-permute-start(f32[6,16,8,256]{3,2,1,0:T(8,128)S(1)} %get-tuple-element.48), channel_id=1, source_target_pairs={{0,1},{1,0},{2,3},{3,2},{4,5},{5,4},{6,7},{7,6},{8,9},{9,8},{10,11... | collective-permute-start | bytes 2359304 | tf_op jit(solution)/shard_map/ppermute | solution.py:117
  14.7 48.4 %collective-permute-start.8 = (f32[2,32,32,256]{3,2,1,0:T(8,128)S(1)}, f32[2,32,32,256]{3,2,1,0:T(8,128)S(1)}, u32[]{:S(2)}, u32[]{:S(2)}) collective-permute-start(f32[2,32,32,256]{3,2,1,0:T(8,128)S(1)} %copy-done.2), channel_id=1, source_target_pairs={{0,8},{8,16},{16,24},{1,9},{9,17},{17,25},{2,10},{10,18},{18,26},{... | collective-permute-start | bytes 6291464 | tf_op jit(solution)/shard_map/ppermute | solution.py:518
  18.3 15.0 %collective-permute-start.3 = (f32[6,2,8,256]{3,2,1,0:T(8,128)S(1)}, f32[6,2,8,256]{3,2,1,0:T(8,128)S(1)}, u32[]{:S(2)}, u32[]{:S(2)}) collective-permute-start(f32[6,2,8,256]{3,2,1,0:T(8,128)S(1)} %get-tuple-element.49), channel_id=1, source_target_pairs={{0,3},{1,2},{2,5},{3,4},{4,7},{5,6},{8,11},{9,10},{10,13},{11,12},... | collective-permute-start | bytes 294920 | tf_op jit(solution)/shard_map/ppermute | solution.py:117
  33.3 6.1 %collective-permute-start.4 = (f32[6,2,8,256]{3,2,1,0:T(8,128)S(1)}, f32[6,2,8,256]{3,2,1,0:T(8,128)S(1)}, u32[]{:S(2)}, u32[]{:S(2)}) collective-permute-start(f32[6,2,8,256]{3,2,1,0:T(8,128)S(1)} %get-tuple-element.50), channel_id=1, source_target_pairs={{2,1},{3,0},{4,3},{5,2},{6,5},{7,4},{10,9},{11,8},{12,11},{13,10},... | collective-permute-start | bytes 294920 | tf_op jit(solution)/shard_map/ppermute | solution.py:117
  53.7 11.3 %collective-permute-start.5 = (f32[2,16,8,256]{3,2,1,0:T(8,128)S(1)}, f32[2,16,8,256]{3,2,1,0:T(8,128)S(1)}, u32[]{:S(2)}, u32[]{:S(2)}) collective-permute-start(f32[2,16,8,256]{3,2,1,0:T(8,128)S(1)} %get-tuple-element.55), channel_id=1, source_target_pairs={{0,1},{1,0},{2,3},{3,2},{4,5},{5,4},{6,7},{7,6},{8,9},{9,8},{10,11... | collective-permute-start | bytes 786440 | tf_op jit(solution)/shard_map/ppermute | solution.py:117
  64.4 9.0 %collective-permute-start.9 = (f32[2,16,8,256]{3,2,1,0:T(8,128)S(1)}, f32[2,16,8,256]{3,2,1,0:T(8,128)S(1)}, u32[]{:S(2)}, u32[]{:S(2)}) collective-permute-start(f32[2,16,8,256]{3,2,1,0:T(8,128)S(1)} %get-tuple-element.64), channel_id=1, source_target_pairs={{0,1},{1,0},{2,3},{3,2},{4,5},{5,4},{6,7},{7,6},{8,9},{9,8},{10,11... | collective-permute-start | bytes 786440 | tf_op jit(solution)/shard_map/ppermute | solution.py:117
  65.1 11.8 %collective-permute-start.6 = (f32[2,18,8,256]{3,2,1,0:T(8,128)S(1)}, f32[2,18,8,256]{3,2,1,0:T(8,128)S(1)}, u32[]{:S(2)}, u32[]{:S(2)}) collective-permute-start(f32[2,18,8,256]{3,2,1,0:T(8,128)S(1)} %get-tuple-element.56), channel_id=1, source_target_pairs={{0,2},{2,4},{4,6},{1,3},{3,5},{5,7},{8,10},{10,12},{12,14},{9,11},... | collective-permute-start | bytes 884744 | tf_op jit(solution)/shard_map/ppermute | solution.py:122
  67.9 8.9 %collective-permute-start.7 = (f32[2,18,8,256]{3,2,1,0:T(8,128)S(1)}, f32[2,18,8,256]{3,2,1,0:T(8,128)S(1)}, u32[]{:S(2)}, u32[]{:S(2)}) collective-permute-start(f32[2,18,8,256]{3,2,1,0:T(8,128)S(1)} %get-tuple-element.57), channel_id=1, source_target_pairs={{2,0},{4,2},{6,4},{3,1},{5,3},{7,5},{10,8},{12,10},{14,12},{11,9},... | collective-permute-start | bytes 884744 | tf_op jit(solution)/shard_map/ppermute | solution.py:122
  73.5 22.8 %collective-permute-start.10 = (f32[2,18,8,256]{3,2,1,0:T(8,128)S(1)}, f32[2,18,8,256]{3,2,1,0:T(8,128)S(1)}, u32[]{:S(2)}, u32[]{:S(2)}) collective-permute-start(f32[2,18,8,256]{3,2,1,0:T(8,128)S(1)} %get-tuple-element.65), channel_id=1, source_target_pairs={{0,2},{2,4},{4,6},{1,3},{3,5},{5,7},{8,10},{10,12},{12,14},{9,11},... | collective-permute-start | bytes 884744 | tf_op jit(solution)/shard_map/ppermute | solution.py:122
  75.5 20.7 %collective-permute-start.11 = (f32[2,18,8,256]{3,2,1,0:T(8,128)S(1)}, f32[2,18,8,256]{3,2,1,0:T(8,128)S(1)}, u32[]{:S(2)}, u32[]{:S(2)}) collective-permute-start(f32[2,18,8,256]{3,2,1,0:T(8,128)S(1)} %get-tuple-element.66), channel_id=1, source_target_pairs={{2,0},{4,2},{6,4},{3,1},{5,3},{7,5},{10,8},{12,10},{14,12},{11,9},... | collective-permute-start | bytes 884744 | tf_op jit(solution)/shard_map/ppermute | solution.py:122
  89.5 52.5 %collective-permute-start.21 = (f32[2,32,32,256]{3,2,1,0:T(8,128)S(1)}, f32[2,32,32,256]{3,2,1,0:T(8,128)S(1)}, u32[]{:S(2)}, u32[]{:S(2)}) collective-permute-start(f32[2,32,32,256]{3,2,1,0:T(8,128)S(1)} %get-tuple-element.58.tile.refs_0_), channel_id=1, source_target_pairs={{0,24},{1,25},{2,26},{3,27},{4,28},{5,29},{6,30},{7,31}} | collective-permute-start | bytes 6291464 | tf_op jit(solution)/shard_map/ppermute | solution.py:518
  108.6 9.2 %collective-permute-start.15 = (f32[2,16,8,256]{3,2,1,0:T(8,128)S(1)}, f32[2,16,8,256]{3,2,1,0:T(8,128)S(1)}, u32[]{:S(2)}, u32[]{:S(2)}) collective-permute-start(f32[2,16,8,256]{3,2,1,0:T(8,128)S(1)} %get-tuple-element.76), channel_id=1, source_target_pairs={{0,1},{1,0},{2,3},{3,2},{4,5},{5,4},{6,7},{7,6},{8,9},{9,8},{10,11... | collective-permute-start | bytes 786440 | tf_op jit(solution)/shard_map/ppermute | solution.py:117
  109.1 14.2 %collective-permute-start.12 = (f32[2,16,8,256]{3,2,1,0:T(8,128)S(1)}, f32[2,16,8,256]{3,2,1,0:T(8,128)S(1)}, u32[]{:S(2)}, u32[]{:S(2)}) collective-permute-start(f32[2,16,8,256]{3,2,1,0:T(8,128)S(1)} %get-tuple-element.70), channel_id=1, source_target_pairs={{0,1},{1,0},{2,3},{3,2},{4,5},{5,4},{6,7},{7,6},{8,9},{9,8},{10,11... | collective-permute-start | bytes 786440 | tf_op jit(solution)/shard_map/ppermute | solution.py:117
  117.9 9.6 %collective-permute-start.16 = (f32[2,18,8,256]{3,2,1,0:T(8,128)S(1)}, f32[2,18,8,256]{3,2,1,0:T(8,128)S(1)}, u32[]{:S(2)}, u32[]{:S(2)}) collective-permute-start(f32[2,18,8,256]{3,2,1,0:T(8,128)S(1)} %get-tuple-element.77), channel_id=1, source_target_pairs={{0,2},{2,4},{4,6},{1,3},{3,5},{5,7},{8,10},{10,12},{12,14},{9,11},... | collective-permute-start | bytes 884744 | tf_op jit(solution)/shard_map/ppermute | solution.py:122
  119.7 7.8 %collective-permute-start.17 = (f32[2,18,8,256]{3,2,1,0:T(8,128)S(1)}, f32[2,18,8,256]{3,2,1,0:T(8,128)S(1)}, u32[]{:S(2)}, u32[]{:S(2)}) collective-permute-start(f32[2,18,8,256]{3,2,1,0:T(8,128)S(1)} %get-tuple-element.78), channel_id=1, source_target_pairs={{2,0},{4,2},{6,4},{3,1},{5,3},{7,5},{10,8},{12,10},{14,12},{11,9},... | collective-permute-start | bytes 884744 | tf_op jit(solution)/shard_map/ppermute | solution.py:122
  123.4 16.6 %collective-permute-start.13 = (f32[2,18,8,256]{3,2,1,0:T(8,128)S(1)}, f32[2,18,8,256]{3,2,1,0:T(8,128)S(1)}, u32[]{:S(2)}, u32[]{:S(2)}) collective-permute-start(f32[2,18,8,256]{3,2,1,0:T(8,128)S(1)} %get-tuple-element.71), channel_id=1, source_target_pairs={{0,2},{2,4},{4,6},{1,3},{3,5},{5,7},{8,10},{10,12},{12,14},{9,11},... | collective-permute-start | bytes 884744 | tf_op jit(solution)/shard_map/ppermute | solution.py:122
  126.1 13.8 %collective-permute-start.14 = (f32[2,18,8,256]{3,2,1,0:T(8,128)S(1)}, f32[2,18,8,256]{3,2,1,0:T(8,128)S(1)}, u32[]{:S(2)}, u32[]{:S(2)}) collective-permute-start(f32[2,18,8,256]{3,2,1,0:T(8,128)S(1)} %get-tuple-element.72), channel_id=1, source_target_pairs={{2,0},{4,2},{6,4},{3,1},{5,3},{7,5},{10,8},{12,10},{14,12},{11,9},... | collective-permute-start | bytes 884744 | tf_op jit(solution)/shard_map/ppermute | solution.py:122
  142.0 47.2 %collective-permute-start.22 = (f32[2,32,32,256]{3,2,1,0:T(8,128)S(1)}, f32[2,32,32,256]{3,2,1,0:T(8,128)S(1)}, u32[]{:S(2)}, u32[]{:S(2)}) collective-permute-start(f32[2,32,32,256]{3,2,1,0:T(8,128)S(1)} %shard_map.68.refs_1_), channel_id=1, source_target_pairs={{0,8},{8,16},{16,24},{1,9},{9,17},{17,25},{2,10},{10,18},{18,26},{... | collective-permute-start | bytes 6291464 | tf_op jit(solution)/shard_map/ppermute | solution.py:518
  155.7 9.0 %collective-permute-start.18 = (f32[2,16,8,256]{3,2,1,0:T(8,128)S(1)}, f32[2,16,8,256]{3,2,1,0:T(8,128)S(1)}, u32[]{:S(2)}, u32[]{:S(2)}) collective-permute-start(f32[2,16,8,256]{3,2,1,0:T(8,128)S(1)} %get-tuple-element.85), channel_id=1, source_target_pairs={{0,1},{1,0},{2,3},{3,2},{4,5},{5,4},{6,7},{7,6},{8,9},{9,8},{10,11... | collective-permute-start | bytes 786440 | tf_op jit(solution)/shard_map/ppermute | solution.py:117
  164.8 3.2 %collective-permute-start.19 = (f32[2,18,8,256]{3,2,1,0:T(8,128)S(1)}, f32[2,18,8,256]{3,2,1,0:T(8,128)S(1)}, u32[]{:S(2)}, u32[]{:S(2)}) collective-permute-start(f32[2,18,8,256]{3,2,1,0:T(8,128)S(1)} %get-tuple-element.86), channel_id=1, source_target_pairs={{0,2},{2,4},{4,6},{1,3},{3,5},{5,7},{8,10},{10,12},{12,14},{9,11},... | collective-permute-start | bytes 884744 | tf_op jit(solution)/shard_map/ppermute | solution.py:122
  166.7 3.5 %collective-permute-start.20 = (f32[2,18,8,256]{3,2,1,0:T(8,128)S(1)}, f32[2,18,8,256]{3,2,1,0:T(8,128)S(1)}, u32[]{:S(2)}, u32[]{:S(2)}) collective-permute-start(f32[2,18,8,256]{3,2,1,0:T(8,128)S(1)} %get-tuple-element.87), channel_id=1, source_target_pairs={{2,0},{4,2},{6,4},{3,1},{5,3},{7,5},{10,8},{12,10},{14,12},{11,9},... | collective-permute-start | bytes 884744 | tf_op jit(solution)/shard_map/ppermute | solution.py:122
  192.2 3.1 %collective-permute-start.25 = (f32[8,128]{1,0:T(8,128)S(1)}, f32[8,128]{1,0:T(8,128)S(1)}, u32[]{:S(2)}, u32[]{:S(2)}) collective-permute-start(f32[8,128]{1,0:T(8,128)S(1)} %shard_map.72), channel_id=1, source_target_pairs={{0,6},{2,4},{4,2},{6,0},{1,7},{3,5},{5,3},{7,1},{8,14},{10,12},{12... | collective-permute-start | bytes 12296 | tf_op jit(solution)/shard_map/ppermute | solution.py:467
  192.3 3.7 %collective-permute-start.24 = (f32[8,128]{1,0:T(8,128)S(1)}, f32[8,128]{1,0:T(8,128)S(1)}, u32[]{:S(2)}, u32[]{:S(2)}) collective-permute-start(f32[8,128]{1,0:T(8,128)S(1)} %shard_map.72), channel_id=1, source_target_pairs={{0,4},{2,6},{4,0},{6,2},{1,5},{3,7},{5,1},{7,3},{8,12},{10,14},{12... | collective-permute-start | bytes 12296 | tf_op jit(solution)/shard_map/ppermute | solution.py:467
  194.2 1.8 collective-permute-start.23
  196.0 3.7 %collective-permute-start.26 = (f32[8,128]{1,0:T(8,128)S(1)}, f32[8,128]{1,0:T(8,128)S(1)}, u32[]{:S(2)}, u32[]{:S(2)}) collective-permute-start(f32[8,128]{1,0:T(8,128)S(1)} %add_add_fusion.1), channel_id=1, source_target_pairs={{0,1},{1,0},{2,3},{3,2},{4,5},{5,4},{6,7},{7,6},{8,9},{9,8},{10,11... | collective-permute-start | bytes 12296 | tf_op jit(solution)/shard_map/ppermute | solution.py:467
  199.6 8.2 %collective-permute-start.29 = (f32[8,128]{1,0:T(8,128)S(1)}, f32[8,128]{1,0:T(8,128)S(1)}, u32[]{:S(2)}, u32[]{:S(2)}) collective-permute-start(f32[8,128]{1,0:T(8,128)S(1)} %add.24), channel_id=1, source_target_pairs={{0,24},{8,16},{16,8},{24,0},{1,25},{9,17},{17,9},{25,1},{2,26},{10... | collective-permute-start | bytes 12296 | tf_op jit(solution)/shard_map/ppermute | solution.py:467
  206.3 4.5 %collective-permute-start.28 = (f32[8,128]{1,0:T(8,128)S(1)}, f32[8,128]{1,0:T(8,128)S(1)}, u32[]{:S(2)}, u32[]{:S(2)}) collective-permute-start(f32[8,128]{1,0:T(8,128)S(1)} %add.24), channel_id=1, source_target_pairs={{0,16},{8,24},{16,0},{24,8},{1,17},{9,25},{17,1},{25,9},{2,18},{10... | collective-permute-start | bytes 12296 | tf_op jit(solution)/shard_map/ppermute | solution.py:467
  206.3 4.5 %collective-permute-start.27 = (f32[8,128]{1,0:T(8,128)S(1)}, f32[8,128]{1,0:T(8,128)S(1)}, u32[]{:S(2)}, u32[]{:S(2)}) collective-permute-start(f32[8,128]{1,0:T(8,128)S(1)} %add.24), channel_id=1, source_target_pairs={{0,8},{8,0},{16,24},{24,16},{1,9},{9,1},{17,25},{25,17},{2,10},{10... | collective-permute-start | bytes 12296 | tf_op jit(solution)/shard_map/ppermute | solution.py:467

commit v5 on v4

--- a/solution.py
+++ b/solution.py
@@ -16,8 +16,8 @@
 BYTES_PER_MICRO = 3.6e6
 
 
-def kernel_call(body, outs, scratch, ins, micros, mib, anywhere=(), outs_anywhere=(), space=pl.ANY, scalars=True):
-    spec = lambda n, names: pl.BlockSpec(memory_space=space if n in names else pltpu.VMEM)
+def kernel_call(body, outs, scratch, ins, micros, mib, anywhere=(), outs_anywhere=(), scalars=True):
+    spec = lambda n, names: pl.BlockSpec(memory_space=pl.ANY if n in names else pltpu.VMEM)
     specs = [spec(n, anywhere) for n in range(len(ins))]
     if scalars:
         specs[0] = pl.BlockSpec(memory_space=pltpu.SMEM)
@@ -102,7 +102,7 @@
     return kernel_call(join_kernel, [out, out], [], [xlo, xhi, pack], 1.0, 8, scalars=False)
 
 
-def exchange(strips):
+def exchange(strips, after=None):
     nx, ny = lax.axis_size("sx"), lax.axis_size("sy")
     up = [(i, i + 1) for i in range(nx - 1)]
     down = [(j, i) for i, j in up]
@@ -118,6 +118,8 @@
 
     if len(strips) == 3:
         pack = moved(strips[2], 0, lambda j: (1 - 2 * j,))
+        if after is not None:
+            strips, pack, _ = lax.optimization_barrier((strips, pack, after))
         lo, hi = join(strips[0], strips[1], pack)
         return [lax.ppermute(hi, "sx", up), lax.ppermute(lo, "sx", down), pack]
     below = lax.ppermute(strips[1], "sx", up)
@@ -302,24 +304,30 @@
         sweep(coef, src, -reach, x + reach, adjoint, done, write)
 
 
-def pack_kernel(fields_in, scalars, *refs):
+def flat_tiles(sources):
+    return [ref.at[n] for ref in sources for n in range(ref.shape[0])]
+
+
+def pack_y_kernel(fields_in, packs, scalars, *refs):
     sources, outs, (buffers, sems) = refs[:fields_in], refs[fields_in:-2], refs[-2:]
-    side = scalars[0]
-    tiles = [ref.at[n] for ref in sources for n in range(ref.shape[0])]
-    x, y, _ = tiles[0].shape
-    starts = pack_starts(max((len(outs) - 2) // 3, 1), y, side)
+    tiles = flat_tiles(sources)
+    starts = pack_starts(packs, tiles[0].shape[1], scalars[0])
     copies = Copies(sems)
     for f, tile in enumerate(tiles):
         for n, (start, _) in enumerate(starts):
             copies.start(tile.at[:, pl.ds(start, SUB)], buffers.at[n, f])
-    loads, copies.open = copies.open, []
-    for f, tile in enumerate(tiles):
-        copies.start(tile.at[pl.ds(0, STEPS)], outs[0].at[f])
-        copies.start(tile.at[pl.ds(x - STEPS, STEPS)], outs[1].at[f])
     for f in range(len(tiles)):
         for n, (_, last) in enumerate(starts):
-            loads[f * len(starts) + n].wait()
-            write_packs(f, n, lambda i: buffers[n, f, i], last, outs)
+            copies.open[f * len(starts) + n].wait()
+            write_packs(f, n, lambda i: buffers[n, f, i], last, (None, None) + outs)
+
+
+def pack_x_kernel(fields_in, *refs):
+    sources, (low, high, sems) = refs[:fields_in], refs[fields_in:]
+    copies = Copies(sems)
+    for f, tile in enumerate(flat_tiles(sources)):
+        copies.start(tile.at[pl.ds(0, STEPS)], low.at[f])
+        copies.start(tile.at[pl.ds(tile.shape[0] - STEPS, STEPS)], high.at[f])
     copies.wait()
 
 
@@ -500,32 +508,42 @@
 
     packs = 2 if both else 1
 
-    def pack(sources):
+    def pack(sources, joined, mib):
         number = sum(a.shape[0] for a in sources)
-        joined = number == group and not both
-        return kernel_call(
-            functools.partial(pack_kernel, len(sources)),
-            strip_shapes(number, x, y, z, both, joined),
-            [pltpu.VMEM((packs, number, x, SUB, z), jnp.float32), pltpu.SemaphoreType.DMA((number * (packs + 2),))],
+        outs = strip_shapes(number, x, y, z, both, joined)
+        in_y = kernel_call(
+            functools.partial(pack_y_kernel, len(sources), packs),
+            outs[2:],
+            [pltpu.VMEM((packs, number, x, SUB, z), jnp.float32), pltpu.SemaphoreType.DMA((number * packs,))],
             [where] + sources,
-            3.0,
-            12,
+            2.0,
+            mib,
             anywhere=range(1, len(sources) + 1),
-            space=pl.ANY if joined else pltpu.HBM,
         )
+        in_x = kernel_call(
+            functools.partial(pack_x_kernel, len(sources)),
+            outs[:2],
+            [pltpu.SemaphoreType.DMA((2 * number,))],
+            sources,
+            2.0,
+            mib,
+            anywhere=range(len(sources)),
+            scalars=False,
+        )
+        return list(in_x) + list(in_y)
 
     def right(value, hops):
         return lax.ppermute(value, "probe", [(i, i + hops) for i in range(groups - hops)])
 
     next_probes = right(probes, 1)
-    strips = pack(fields)
+    strips = pack(fields, False, 56)
     received = exchange(strips)
     coef, halfway, *strips = kernel_call(
         functools.partial(first_kernel, len(received)),
         [f32(7, *wide), tile] + strips2,
         scratch(3 * total),
         [where] + fields + [obs_weight] + received,
-        14.0,
+        4.0,
         14,
         anywhere=(1, 2, 3, 5, 6),
     )
@@ -545,13 +563,13 @@
     images, *strips = model(halfway, exchange(strips), True)
     far = [right(images, hops) for hops in range(3, groups)]
 
-    half_next, *strips_next = model(next_probes, exchange(pack([next_probes])), False)
+    half_next, *strips_next = model(next_probes, exchange(pack([next_probes], not both, 8)), False)
     strips, half_next = lax.optimization_barrier((strips, half_next))
     (images_next,) = model(half_next, exchange(strips_next), True, True)
-    ready, (shifting, far) = images_next, lax.optimization_barrier((images_next, far))
+    shifting, far = lax.optimization_barrier((images_next, far))
     passed = [images, images_next, right(shifting, 1)] + far
 
-    received, _ = lax.optimization_barrier((exchange(strips), ready))
+    received = exchange(strips, after=images_next)
     halfway, *strips = model(images, received, False)
     (second,) = model(halfway, exchange(strips), True, True)
 

time: 216 us -> 235 us (1.088)
  waiting for transfers between devices: 68 us -> 77.9 us
  starting transfers between devices: 52.8 us -> 62.6 us
  local copies, waits for them, and re-layouts: 4.72 us -> 0.03 us
  Pallas kernels: 88.4 us -> 92.6 us
    ppermute x3, waiting for transfers between devices: 17.8 us -> 52.1 us  [right(): lax.ppermute(value, 'probe', [(i, i + hops) for i in range(groups - hops)])]
    ppermute x8, waiting for transfers between devices: 38.6 us -> 13.7 us  [moved(): return lax.ppermute(value, ('sx', 'sy'), pairs)]
    ppermute x8, starting transfers between devices: 10.3 us -> 15.3 us  [moved(): return lax.ppermute(value, ('sx', 'sy'), pairs)]
    unnamed x12 -> x14, local copies, waits for them, and re-layouts: 4.72 us -> 0.03 us
    pallas_call x15 -> x17, Pallas kernels: 88.4 us -> 92.6 us  [kernel_call(): pl.pallas_call(body, out_shape=outs, in_specs=specs, out_specs=[spec(n, o...]
    ppermute x10, starting transfers between devices: 17.8 us -> 21 us  [exchange(): return [lax.ppermute(hi, 'sx', up), lax.ppermute(lo, 'sx', down), pack]]
  transfers between devices with their start and end apart: 30 -> 30, of which waited for: 15 -> 13; matrix products, arithmetic and copies ran while one was open for 0% -> 0% of each run, Pallas kernels for 36% -> 36%
where the time goes in v5:
time: 235 us
  Pallas kernels  92.6 us (39%)
  waiting for transfers between devices  77.9 us (33%)
  starting transfers between devices  62.6 us (27%)
    pallas_call x17, Pallas kernels, kernel_call(): pl.pallas_call(body, out_shape=outs, in_specs=specs, out_specs=[spec(n, o...  92.6 us
    ppermute x3, waiting for transfers between devices, right(): lax.ppermute(value, 'probe', [(i, i + hops) for i in range(groups - hops)])  52.1 us
    ppermute x10, starting transfers between devices, exchange(): return [lax.ppermute(hi, 'sx', up), lax.ppermute(lo, 'sx', down), pack]  21 us
    ppermute x8, starting transfers between devices, moved(): return lax.ppermute(value, ('sx', 'sy'), pairs)  15.3 us
    ppermute x8, waiting for transfers between devices, moved(): return lax.ppermute(value, ('sx', 'sy'), pairs)  13.7 us
    ppermute x3, starting transfers between devices, right(): lax.ppermute(value, 'probe', [(i, i + hops) for i in range(groups - hops)])  12.9 us
    ppermute x7, starting transfers between devices, all_sum(): lax.ppermute(value, axis, [(i, i ^ bits) for i in range(devices)])  10.8 us
    ppermute x7, waiting for transfers between devices, all_sum(): lax.ppermute(value, axis, [(i, i ^ bits) for i in range(devices)])  7.93 us
  transfers between devices with their start and end apart: 30, of which 13 were waited for; matrix products, arithmetic and copies ran while one was open for 0% of the time, Pallas kernels for 36%

profile of v5, /device:TPU:0, one launch (start us, length us, event | category | flops | bytes accessed | tf_op | source)
XLA Modules:
  0.0 234.8 jit_solution(9558295952286495457)
XLA Ops:
  0.6 5.1 %collective-permute-start.8 = (f32[2,32,32,256]{3,2,1,0:T(8,128)}, f32[2,32,32,256]{3,2,1,0:T(8,128)S(1)}, u32[]{:S(2)}, u32[]{:S(2)}) collective-permute-start(f32[2,32,32,256]{3,2,1,0:T(8,128)} %probes.1), channel_id=1, source_target_pairs={{0,8},{8,16},{16,24},{1,9},{9,17},{17,25},{2,10},{10,18},{18,26},{... | collective-permute-start | bytes 6291464 | tf_op jit(solution)/shard_map/ppermute | solution.py:536
  5.7 0.6 pad_add_fusion.scalars
  6.3 3.1 %shard_map.60 = (f32[6,16,8,256]{3,2,1,0:T(8,128)}, f32[6,2,8,256]{3,2,1,0:T(8,128)}, f32[6,2,8,256]{3,2,1,0:T(8,128)}) custom-call(s32[2]{0:T(128)} %pad_add_fusion.scalars, f32[1,32,32,256]{3,2,1,0:T(8,128)} %bitcast.3, f32[3,32,32,256]{3,2,1,0:T(8,128)} %velocity.1, f32[2,32,32,256]{3,2,1,0:T(8,128)} %probes.1), custom_call_target="tpu_custom_call" | custom-call | flops 2300000000 | bytes 7200000 | tf_op jit(solution)/shard_map/pallas_call | solution.py:24
  9.4 1.6 collective-permute-start.2
  11.0 2.7 %shard_map.59 = (f32[6,4,32,256]{3,2,1,0:T(8,128)}, f32[6,4,32,256]{3,2,1,0:T(8,128)}) custom-call(f32[1,32,32,256]{3,2,1,0:T(8,128)} %bitcast.4, f32[3,32,32,256]{3,2,1,0:T(8,128)} %velocity.1, f32[2,32,32,256]{3,2,1,0:T(8,128)} %probes.1), custom_call_target="tpu_custom_call" | custom-call | flops 2300000000 | bytes 7200000 | tf_op jit(solution)/shard_map/pallas_call | solution.py:24
  13.7 1.3 collective-permute-start
  15.0 1.3 collective-permute-start.1
  16.3 4.8 %collective-permute-start.3 = (f32[6,2,8,256]{3,2,1,0:T(8,128)S(1)}, f32[6,2,8,256]{3,2,1,0:T(8,128)S(1)}, u32[]{:S(2)}, u32[]{:S(2)}) collective-permute-start(f32[6,2,8,256]{3,2,1,0:T(8,128)S(1)} %copy-done.6), channel_id=1, source_target_pairs={{0,3},{1,2},{2,5},{3,4},{4,7},{5,6},{8,11},{9,10},{10,13},{11,12},... | collective-permute-start | bytes 294920 | tf_op jit(solution)/shard_map/ppermute | solution.py:117
  21.2 29.6 %collective-permute-done.8.refs_0_.tile = f32[2,32,32,256]{3,2,1,0:T(8,128)S(1)} collective-permute-done((f32[2,32,32,256]{3,2,1,0:T(8,128)}, f32[2,32,32,256]{3,2,1,0:T(8,128)S(1)}, u32[]{:S(2)}, u32[]{:S(2)}) %collective-permute-start.8) | collective-permute-done | bytes 2097184 | tf_op jit(solution)/shard_map/ppermute | solution.py:536
  50.8 0.0 copy-start.3
  50.8 1.6 collective-permute-start.4
  52.3 0.7 shard_map.65
  53.0 0.0 collective-permute-done.3.refs_3_
  53.0 1.6 collective-permute-start.9
  54.6 3.7 %collective-permute-done.4.refs_4_ = f32[6,2,8,256]{3,2,1,0:T(8,128)S(1)} collective-permute-done((f32[6,2,8,256]{3,2,1,0:T(8,128)S(1)}, f32[6,2,8,256]{3,2,1,0:T(8,128)S(1)}, u32[]{:S(2)}, u32[]{:S(2)}) %collective-permute-start.4) | collective-permute-done | bytes 98336 | tf_op jit(solution)/shard_map/ppermute | solution.py:117
  58.4 0.0 collective-permute-done.refs_0_
  58.4 0.0 collective-permute-done.1.refs_1_
  58.4 14.6 %shard_map.61 = (f32[7,40,40,256]{3,2,1,0:T(8,128)S(1)}, f32[2,32,32,256]{3,2,1,0:T(8,128)S(1)}, f32[2,4,32,256]{3,2,1,0:T(8,128)S(1)}, f32[2,4,32,256]{3,2,1,0:T(8,128)S(1)}, f32[2,16,8,256]{3,2,1,0:T(8,128)S(1)}) custom-call(s32[2]{0:T(128)S(1)} %copy-done.4, f32[1,32,32,256]{3,2,1,0:T(8,128)S(1)} %bitcast.5, f32[3,32,32,256]{3,2,1,0:T(8,128)S(1)} %copy-done, ...), custom_call_target="tpu_custom_call" | custom-call | flops 4600000000 | bytes 14400000 | tf_op jit(solution)/shard_map/pallas_call | solution.py:24
  73.0 2.0 collective-permute-start.5
  75.0 0.7 shard_map.64
  75.7 0.0 collective-permute-done.9.pack.refs_3_
  75.8 1.3 collective-permute-start.10
  77.1 1.3 collective-permute-start.11
  78.4 2.6 %collective-permute-done.5.pack.refs_2_ = f32[2,16,8,256]{3,2,1,0:T(8,128)S(1)} collective-permute-done((f32[2,16,8,256]{3,2,1,0:T(8,128)S(1)}, f32[2,16,8,256]{3,2,1,0:T(8,128)S(1)}, u32[]{:S(2)}, u32[]{:S(2)}) %collective-permute-start.5) | collective-permute-done | bytes 262176 | tf_op jit(solution)/shard_map/ppermute | solution.py:117
  81.0 1.3 collective-permute-start.6
  82.3 1.3 collective-permute-start.7
  83.6 0.0 collective-permute-done.11.refs_2_
  83.6 12.6 %shard_map.67 = (f32[2,32,32,256]{3,2,1,0:T(8,128)S(1)}, f32[2,4,32,256]{3,2,1,0:T(8,128)S(1)}, f32[2,4,32,256]{3,2,1,0:T(8,128)S(1)}, f32[2,16,8,256]{3,2,1,0:T(8,128)S(1)}) custom-call(s32[2]{0:T(128)S(1)} %copy-done.4, f32[7,40,40,256]{3,2,1,0:T(8,128)S(1)} %get-tuple-element.50.coef, f32[2,32,32,256]{3,2,1,0:T(8,128)S(1)} %collective-permute-done.8.refs_0_.tile, ...), custom_call_target="tpu_custom_call" | custom-call | flops 13799999488 | bytes 43200000 | tf_op jit(solution)/shard_map/pallas_call | solution.py:24
  96.2 0.6 collective-permute-start.13
  96.8 0.0 collective-permute-done.7.refs_1_
  96.8 12.9 %shard_map.63 = (f32[2,32,32,256]{3,2,1,0:T(8,128)S(1)}, f32[2,4,32,256]{3,2,1,0:T(8,128)S(1)}, f32[2,4,32,256]{3,2,1,0:T(8,128)S(1)}, f32[2,16,8,256]{3,2,1,0:T(8,128)S(1)}) custom-call(s32[2]{0:T(128)S(1)} %copy-done.4, f32[7,40,40,256]{3,2,1,0:T(8,128)S(1)} %get-tuple-element.50.coef, f32[2,32,32,256]{3,2,1,0:T(8,128)S(1)} %get-tuple-element.51.tile, ...), custom_call_target="tpu_custom_call" | custom-call | flops 13799999488 | bytes 43200000 | tf_op jit(solution)/shard_map/pallas_call | solution.py:24
  109.7 6.4 %collective-permute-start.21 = (f32[2,32,32,256]{3,2,1,0:T(8,128)S(1)}, f32[2,32,32,256]{3,2,1,0:T(8,128)S(1)}, u32[]{:S(2)}, u32[]{:S(2)}) collective-permute-start(f32[2,32,32,256]{3,2,1,0:T(8,128)S(1)} %get-tuple-element.57.tile.refs_0_), channel_id=1, source_target_pairs={{0,24},{1,25},{2,26},{3,27},{4,28},{5,29},{6,30},{7,31}} | collective-permute-start | bytes 6291464 | tf_op jit(solution)/shard_map/ppermute | solution.py:536
  116.2 0.0 collective-permute-done.13.pack.refs_2_
  116.3 3.2 %collective-permute-start.14 = (f32[2,18,8,256]{3,2,1,0:T(8,128)S(1)}, f32[2,18,8,256]{3,2,1,0:T(8,128)S(1)}, u32[]{:S(2)}, u32[]{:S(2)}) collective-permute-start(f32[2,18,8,256]{3,2,1,0:T(8,128)S(1)} %get-tuple-element.73), channel_id=1, source_target_pairs={{0,2},{2,4},{4,6},{1,3},{3,5},{5,7},{8,10},{10,12},{12,14},{9,11},... | collective-permute-start | bytes 884744 | tf_op jit(solution)/shard_map/ppermute | solution.py:124
  119.5 1.3 collective-permute-start.15
  120.8 1.6 collective-permute-start.12
  122.3 1.9 collective-permute-done.15.refs_1_
  124.3 12.8 %shard_map.69.refs_1_ = f32[2,32,32,256]{3,2,1,0:T(8,128)S(1)} custom-call(s32[2]{0:T(128)S(1)} %copy-done.4, f32[7,40,40,256]{3,2,1,0:T(8,128)S(1)} %get-tuple-element.50.coef, f32[2,32,32,256]{3,2,1,0:T(8,128)S(1)} %get-tuple-element.69.tile, f32[2,18,8,256]{3,2,1,0:T(8,128)S(1)} %collective-permute-done.14.refs_0_, ...), custom_call_target="tpu_custom_call" | custom-call | flops 13799999488 | bytes 43200000 | tf_op jit(solution)/shard_map/pallas_call | solution.py:24
  137.0 0.0 collective-permute-done.12.pack.refs_3_
  137.1 7.0 %collective-permute-start.16 = (f32[2,18,8,256]{3,2,1,0:T(8,128)S(1)}, f32[2,18,8,256]{3,2,1,0:T(8,128)S(1)}, u32[]{:S(2)}, u32[]{:S(2)}) collective-permute-start(f32[2,18,8,256]{3,2,1,0:T(8,128)S(1)} %get-tuple-element.78), channel_id=1, source_target_pairs={{0,2},{2,4},{4,6},{1,3},{3,5},{5,7},{8,10},{10,12},{12,14},{9,11},... | collective-permute-start | bytes 884744 | tf_op jit(solution)/shard_map/ppermute | solution.py:124
  144.1 1.3 collective-permute-start.17
  145.4 16.2 %collective-permute-done.21.refs_3_ = f32[2,32,32,256]{3,2,1,0:T(8,128)S(1)} collective-permute-done((f32[2,32,32,256]{3,2,1,0:T(8,128)S(1)}, f32[2,32,32,256]{3,2,1,0:T(8,128)S(1)}, u32[]{:S(2)}, u32[]{:S(2)}) %collective-permute-start.21) | collective-permute-done | bytes 2097184 | tf_op jit(solution)/shard_map/ppermute | solution.py:536
  161.6 1.4 collective-permute-start.22
  163.0 12.6 %shard_map.71 = (f32[2,32,32,256]{3,2,1,0:T(8,128)S(1)}, f32[2,4,32,256]{3,2,1,0:T(8,128)S(1)}, f32[2,4,32,256]{3,2,1,0:T(8,128)S(1)}, f32[2,16,8,256]{3,2,1,0:T(8,128)S(1)}) custom-call(s32[2]{0:T(128)S(1)} %copy-done.4, f32[7,40,40,256]{3,2,1,0:T(8,128)S(1)} %get-tuple-element.50.coef, f32[2,32,32,256]{3,2,1,0:T(8,128)S(1)} %get-tuple-element.57.tile.refs_0_, ...), custom_call_target="tpu_custom_call" | custom-call | flops 13799999488 | bytes 43200000 | tf_op jit(solution)/shard_map/pallas_call | solution.py:24
  175.6 1.5 collective-permute-start.18
  177.1 7.4 %collective-permute-done.18.pack.refs_2_ = f32[2,16,8,256]{3,2,1,0:T(8,128)S(1)} collective-permute-done((f32[2,16,8,256]{3,2,1,0:T(8,128)S(1)}, f32[2,16,8,256]{3,2,1,0:T(8,128)S(1)}, u32[]{:S(2)}, u32[]{:S(2)}) %collective-permute-start.18) | collective-permute-done | bytes 262176 | tf_op jit(solution)/shard_map/ppermute | solution.py:117
  184.6 1.7 collective-permute-start.19
  186.3 1.3 collective-permute-start.20
  187.6 2.2 collective-permute-done.20.refs_1_
  189.7 12.8 %shard_map.73.second = f32[2,32,32,256]{3,2,1,0:T(8,128)S(1)} custom-call(s32[2]{0:T(128)S(1)} %copy-done.4, f32[7,40,40,256]{3,2,1,0:T(8,128)S(1)} %get-tuple-element.50.coef, f32[2,32,32,256]{3,2,1,0:T(8,128)S(1)} %get-tuple-element.80.tile, f32[2,18,8,256]{3,2,1,0:T(8,128)S(1)} %collective-permute-done.19.refs_0_, ...), custom_call_target="tpu_custom_call" | custom-call | flops 13799999488 | bytes 43200000 | tf_op jit(solution)/shard_map/pallas_call | solution.py:24
  202.5 6.4 %collective-permute-done.22.refs_2_ = f32[2,32,32,256]{3,2,1,0:T(8,128)S(1)} collective-permute-done((f32[2,32,32,256]{3,2,1,0:T(8,128)S(1)}, f32[2,32,32,256]{3,2,1,0:T(8,128)S(1)}, u32[]{:S(2)}, u32[]{:S(2)}) %collective-permute-start.22) | collective-permute-done | bytes 2097184 | tf_op jit(solution)/shard_map/ppermute | solution.py:536
  208.9 3.0 %shard_map.74 = f32[8,128]{1,0:T(8,128)S(1)} custom-call(s32[2]{0:T(128)S(1)} %copy-done.4, f32[2,32,32,256]{3,2,1,0:T(8,128)S(1)} %shard_map.73.second, f32[2,32,32,256]{3,2,1,0:T(8,128)S(1)} %get-tuple-element.57.tile.refs_0_, f32[2,32,32,256]{3,2,1,0:T(8,128)S(1)} %shard_map.69.refs_1_, f32[2,32,32,256]{3,2,1,0:T(8,128)S(1)} %collective-permute-done.22.refs_2_, ...), custom_call_target="tpu_custom_call" | custom-call | flops 4600000000 | bytes 14400000 | tf_op jit(solution)/shard_map/pallas_call | solution.py:24
  211.9 0.1 collective-permute-start.25
  212.0 1.6 collective-permute-start.24
  213.6 0.2 collective-permute-start.23
  213.8 1.2 collective-permute-done.25
  215.0 0.7 collective-permute-done.24
  215.7 1.5 collective-permute-start.26
  217.2 2.2 collective-permute-done.26
  219.3 6.8 %collective-permute-start.29 = (f32[8,128]{1,0:T(8,128)S(1)}, f32[8,128]{1,0:T(8,128)S(1)}, u32[]{:S(2)}, u32[]{:S(2)}) collective-permute-start(f32[8,128]{1,0:T(8,128)S(1)} %add.24), channel_id=1, source_target_pairs={{0,24},{8,16},{16,8},{24,0},{1,25},{9,17},{17,9},{25,1},{2,26},{10... | collective-permute-start | bytes 12296 | tf_op jit(solution)/shard_map/ppermute | solution.py:475
  226.2 0.6 collective-permute-start.27
  226.7 1.0 collective-permute-done.29
  227.8 2.9 %collective-permute-done.28 = f32[8,128]{1,0:T(8,128)S(1)} collective-permute-done((f32[8,128]{1,0:T(8,128)S(1)}, f32[8,128]{1,0:T(8,128)S(1)}, u32[]{:S(2)}, u32[]{:S(2)}) %collective-permute-start.28) | collective-permute-done | bytes 4128 | tf_op jit(solution)/shard_map/ppermute | solution.py:475
  230.7 4.1 %shard_map.75 = (f32[2,32,32,256]{3,2,1,0:T(8,128)}, f32[8,8]{1,0:T(8,128)}) custom-call(s32[2]{0:T(128)S(1)} %copy-done.4, f32[8,128]{1,0:T(8,128)S(1)} %add_add_fusion.inner, f32[2,32,32,256]{3,2,1,0:T(8,128)S(1)} %get-tuple-element.57.tile.refs_0_, f32[2,32,32,256]{3,2,1,0:T(8,128)S(1)} %shard_map.69.refs_1_, ...), custom_call_target="tpu_custom_call" | custom-call | flops 5750000128 | bytes 18000000 | tf_op jit(solution)/shard_map/pallas_call | solution.py:24
  (31 shorter events, 0.3 us)
Async XLA Ops:
  0.6 50.1 %collective-permute-start.8 = (f32[2,32,32,256]{3,2,1,0:T(8,128)}, f32[2,32,32,256]{3,2,1,0:T(8,128)S(1)}, u32[]{:S(2)}, u32[]{:S(2)}) collective-permute-start(f32[2,32,32,256]{3,2,1,0:T(8,128)} %probes.1), channel_id=1, source_target_pairs={{0,8},{8,16},{16,24},{1,9},{9,17},{17,25},{2,10},{10,18},{18,26},{... | collective-permute-start | bytes 6291464 | tf_op jit(solution)/shard_map/ppermute | solution.py:536
  9.4 7.0 %copy-start.6 = (f32[6,2,8,256]{3,2,1,0:T(8,128)S(1)}, f32[6,2,8,256]{3,2,1,0:T(8,128)}, u32[]{:S(2)}) copy-start(f32[6,2,8,256]{3,2,1,0:T(8,128)} %get-tuple-element.48) | copy-start | bytes 294916
  9.4 41.4 %copy-start.5 = (f32[6,2,8,256]{3,2,1,0:T(8,128)S(1)}, f32[6,2,8,256]{3,2,1,0:T(8,128)}, u32[]{:S(2)}) copy-start(f32[6,2,8,256]{3,2,1,0:T(8,128)} %get-tuple-element.49) | copy-start | bytes 294916
  9.4 43.0 %copy-start.4 = (s32[2]{0:T(128)S(1)}, s32[2]{0:T(128)}, u32[]{:S(2)}) copy-start(s32[2]{0:T(128)} %pad_add_fusion.scalars) | copy-start | bytes 28
  9.4 49.0 %collective-permute-start.2 = (f32[6,16,8,256]{3,2,1,0:T(8,128)}, f32[6,16,8,256]{3,2,1,0:T(8,128)S(1)}, u32[]{:S(2)}, u32[]{:S(2)}) collective-permute-start(f32[6,16,8,256]{3,2,1,0:T(8,128)} %get-tuple-element.47), channel_id=1, source_target_pairs={{0,1},{1,0},{2,3},{3,2},{4,5},{5,4},{6,7},{7,6},{8,9},{9,8},{10,11... | collective-permute-start | bytes 2359304 | tf_op jit(solution)/shard_map/ppermute | solution.py:117
  13.7 44.7 %collective-permute-start = (f32[6,4,32,256]{3,2,1,0:T(8,128)}, f32[6,4,32,256]{3,2,1,0:T(8,128)S(1)}, u32[]{:S(2)}, u32[]{:S(2)}) collective-permute-start(f32[6,4,32,256]{3,2,1,0:T(8,128)} %get-tuple-element.45), channel_id=1, source_target_pairs={{0,2},{2,4},{4,6},{1,3},{3,5},{5,7},{8,10},{10,12},{12,14},{9,11},... | collective-permute-start | bytes 2359304 | tf_op jit(solution)/shard_map/ppermute | solution.py:125
  15.0 43.3 %collective-permute-start.1 = (f32[6,4,32,256]{3,2,1,0:T(8,128)}, f32[6,4,32,256]{3,2,1,0:T(8,128)S(1)}, u32[]{:S(2)}, u32[]{:S(2)}) collective-permute-start(f32[6,4,32,256]{3,2,1,0:T(8,128)} %get-tuple-element.46), channel_id=1, source_target_pairs={{2,0},{4,2},{6,4},{3,1},{5,3},{7,5},{10,8},{12,10},{14,12},{11,9},... | collective-permute-start | bytes 2359304 | tf_op jit(solution)/shard_map/ppermute | solution.py:126
  16.3 36.7 %collective-permute-start.3 = (f32[6,2,8,256]{3,2,1,0:T(8,128)S(1)}, f32[6,2,8,256]{3,2,1,0:T(8,128)S(1)}, u32[]{:S(2)}, u32[]{:S(2)}) collective-permute-start(f32[6,2,8,256]{3,2,1,0:T(8,128)S(1)} %copy-done.6), channel_id=1, source_target_pairs={{0,3},{1,2},{2,5},{3,4},{4,7},{5,6},{8,11},{9,10},{10,13},{11,12},... | collective-permute-start | bytes 294920 | tf_op jit(solution)/shard_map/ppermute | solution.py:117
  50.8 7.6 %copy-start = (f32[3,32,32,256]{3,2,1,0:T(8,128)S(1)}, f32[3,32,32,256]{3,2,1,0:T(8,128)}, u32[]{:S(2)}) copy-start(f32[3,32,32,256]{3,2,1,0:T(8,128)} %velocity.1) | copy-start | bytes 9437188
  50.8 7.6 %copy-start.1 = (f32[2,32,32,256]{3,2,1,0:T(8,128)S(1)}, f32[2,32,32,256]{3,2,1,0:T(8,128)}, u32[]{:S(2)}) copy-start(f32[2,32,32,256]{3,2,1,0:T(8,128)} %probes.1) | copy-start | bytes 6291460
  50.8 7.6 %copy-start.2 = (f32[32,32,256]{2,1,0:T(8,128)S(1)}, f32[32,32,256]{2,1,0:T(8,128)}, u32[]{:S(2)}) copy-start(f32[32,32,256]{2,1,0:T(8,128)} %param.6) | copy-start | bytes 3145732
  50.8 7.6 %copy-start.3 = (f32[32,32,256]{2,1,0:T(8,128)S(1)}, f32[32,32,256]{2,1,0:T(8,128)}, u32[]{:S(2)}) copy-start(f32[32,32,256]{2,1,0:T(8,128)} %refs_0_.3) | copy-start | bytes 3145732
  50.8 7.6 %collective-permute-start.4 = (f32[6,2,8,256]{3,2,1,0:T(8,128)S(1)}, f32[6,2,8,256]{3,2,1,0:T(8,128)S(1)}, u32[]{:S(2)}, u32[]{:S(2)}) collective-permute-start(f32[6,2,8,256]{3,2,1,0:T(8,128)S(1)} %copy-done.5), channel_id=1, source_target_pairs={{2,1},{3,0},{4,3},{5,2},{6,5},{7,4},{10,9},{11,8},{12,11},{13,10},... | collective-permute-start | bytes 294920 | tf_op jit(solution)/shard_map/ppermute | solution.py:117
  53.0 22.7 %collective-permute-start.9 = (f32[2,16,8,256]{3,2,1,0:T(8,128)S(1)}, f32[2,16,8,256]{3,2,1,0:T(8,128)S(1)}, u32[]{:S(2)}, u32[]{:S(2)}) collective-permute-start(f32[2,16,8,256]{3,2,1,0:T(8,128)S(1)} %shard_map.65), channel_id=1, source_target_pairs={{0,1},{1,0},{2,3},{3,2},{4,5},{5,4},{6,7},{7,6},{8,9},{9,8},{10,11... | collective-permute-start | bytes 786440 | tf_op jit(solution)/shard_map/ppermute | solution.py:117
  73.0 8.0 %collective-permute-start.5 = (f32[2,16,8,256]{3,2,1,0:T(8,128)S(1)}, f32[2,16,8,256]{3,2,1,0:T(8,128)S(1)}, u32[]{:S(2)}, u32[]{:S(2)}) collective-permute-start(f32[2,16,8,256]{3,2,1,0:T(8,128)S(1)} %get-tuple-element.54), channel_id=1, source_target_pairs={{0,1},{1,0},{2,3},{3,2},{4,5},{5,4},{6,7},{7,6},{8,9},{9,8},{10,11... | collective-permute-start | bytes 786440 | tf_op jit(solution)/shard_map/ppermute | solution.py:117
  75.8 7.8 %collective-permute-start.10 = (f32[2,18,8,256]{3,2,1,0:T(8,128)S(1)}, f32[2,18,8,256]{3,2,1,0:T(8,128)S(1)}, u32[]{:S(2)}, u32[]{:S(2)}) collective-permute-start(f32[2,18,8,256]{3,2,1,0:T(8,128)S(1)} %get-tuple-element.63), channel_id=1, source_target_pairs={{0,2},{2,4},{4,6},{1,3},{3,5},{5,7},{8,10},{10,12},{12,14},{9,11},... | collective-permute-start | bytes 884744 | tf_op jit(solution)/shard_map/ppermute | solution.py:124
  77.1 6.5 %collective-permute-start.11 = (f32[2,18,8,256]{3,2,1,0:T(8,128)S(1)}, f32[2,18,8,256]{3,2,1,0:T(8,128)S(1)}, u32[]{:S(2)}, u32[]{:S(2)}) collective-permute-start(f32[2,18,8,256]{3,2,1,0:T(8,128)S(1)} %get-tuple-element.64), channel_id=1, source_target_pairs={{2,0},{4,2},{6,4},{3,1},{5,3},{7,5},{10,8},{12,10},{14,12},{11,9},... | collective-permute-start | bytes 884744 | tf_op jit(solution)/shard_map/ppermute | solution.py:124
  81.0 15.8 %collective-permute-start.6 = (f32[2,18,8,256]{3,2,1,0:T(8,128)S(1)}, f32[2,18,8,256]{3,2,1,0:T(8,128)S(1)}, u32[]{:S(2)}, u32[]{:S(2)}) collective-permute-start(f32[2,18,8,256]{3,2,1,0:T(8,128)S(1)} %get-tuple-element.55), channel_id=1, source_target_pairs={{0,2},{2,4},{4,6},{1,3},{3,5},{5,7},{8,10},{10,12},{12,14},{9,11},... | collective-permute-start | bytes 884744 | tf_op jit(solution)/shard_map/ppermute | solution.py:124
  82.3 14.5 %collective-permute-start.7 = (f32[2,18,8,256]{3,2,1,0:T(8,128)S(1)}, f32[2,18,8,256]{3,2,1,0:T(8,128)S(1)}, u32[]{:S(2)}, u32[]{:S(2)}) collective-permute-start(f32[2,18,8,256]{3,2,1,0:T(8,128)S(1)} %get-tuple-element.56), channel_id=1, source_target_pairs={{2,0},{4,2},{6,4},{3,1},{5,3},{7,5},{10,8},{12,10},{14,12},{11,9},... | collective-permute-start | bytes 884744 | tf_op jit(solution)/shard_map/ppermute | solution.py:124
  96.2 20.0 %collective-permute-start.13 = (f32[2,16,8,256]{3,2,1,0:T(8,128)S(1)}, f32[2,16,8,256]{3,2,1,0:T(8,128)S(1)}, u32[]{:S(2)}, u32[]{:S(2)}) collective-permute-start(f32[2,16,8,256]{3,2,1,0:T(8,128)S(1)} %get-tuple-element.72), channel_id=1, source_target_pairs={{0,1},{1,0},{2,3},{3,2},{4,5},{5,4},{6,7},{7,6},{8,9},{9,8},{10,11... | collective-permute-start | bytes 786440 | tf_op jit(solution)/shard_map/ppermute | solution.py:117
  109.7 51.8 %collective-permute-start.21 = (f32[2,32,32,256]{3,2,1,0:T(8,128)S(1)}, f32[2,32,32,256]{3,2,1,0:T(8,128)S(1)}, u32[]{:S(2)}, u32[]{:S(2)}) collective-permute-start(f32[2,32,32,256]{3,2,1,0:T(8,128)S(1)} %get-tuple-element.57.tile.refs_0_), channel_id=1, source_target_pairs={{0,24},{1,25},{2,26},{3,27},{4,28},{5,29},{6,30},{7,31}} | collective-permute-start | bytes 6291464 | tf_op jit(solution)/shard_map/ppermute | solution.py:536
  116.3 6.1 %collective-permute-start.14 = (f32[2,18,8,256]{3,2,1,0:T(8,128)S(1)}, f32[2,18,8,256]{3,2,1,0:T(8,128)S(1)}, u32[]{:S(2)}, u32[]{:S(2)}) collective-permute-start(f32[2,18,8,256]{3,2,1,0:T(8,128)S(1)} %get-tuple-element.73), channel_id=1, source_target_pairs={{0,2},{2,4},{4,6},{1,3},{3,5},{5,7},{8,10},{10,12},{12,14},{9,11},... | collective-permute-start | bytes 884744 | tf_op jit(solution)/shard_map/ppermute | solution.py:124
  119.5 4.8 %collective-permute-start.15 = (f32[2,18,8,256]{3,2,1,0:T(8,128)S(1)}, f32[2,18,8,256]{3,2,1,0:T(8,128)S(1)}, u32[]{:S(2)}, u32[]{:S(2)}) collective-permute-start(f32[2,18,8,256]{3,2,1,0:T(8,128)S(1)} %get-tuple-element.74), channel_id=1, source_target_pairs={{2,0},{4,2},{6,4},{3,1},{5,3},{7,5},{10,8},{12,10},{14,12},{11,9},... | collective-permute-start | bytes 884744 | tf_op jit(solution)/shard_map/ppermute | solution.py:124
  120.8 16.3 %collective-permute-start.12 = (f32[2,16,8,256]{3,2,1,0:T(8,128)S(1)}, f32[2,16,8,256]{3,2,1,0:T(8,128)S(1)}, u32[]{:S(2)}, u32[]{:S(2)}) collective-permute-start(f32[2,16,8,256]{3,2,1,0:T(8,128)S(1)} %get-tuple-element.68), channel_id=1, source_target_pairs={{0,1},{1,0},{2,3},{3,2},{4,5},{5,4},{6,7},{7,6},{8,9},{9,8},{10,11... | collective-permute-start | bytes 786440 | tf_op jit(solution)/shard_map/ppermute | solution.py:117
  137.1 25.9 %collective-permute-start.16 = (f32[2,18,8,256]{3,2,1,0:T(8,128)S(1)}, f32[2,18,8,256]{3,2,1,0:T(8,128)S(1)}, u32[]{:S(2)}, u32[]{:S(2)}) collective-permute-start(f32[2,18,8,256]{3,2,1,0:T(8,128)S(1)} %get-tuple-element.78), channel_id=1, source_target_pairs={{0,2},{2,4},{4,6},{1,3},{3,5},{5,7},{8,10},{10,12},{12,14},{9,11},... | collective-permute-start | bytes 884744 | tf_op jit(solution)/shard_map/ppermute | solution.py:124
  144.1 18.9 %collective-permute-start.17 = (f32[2,18,8,256]{3,2,1,0:T(8,128)S(1)}, f32[2,18,8,256]{3,2,1,0:T(8,128)S(1)}, u32[]{:S(2)}, u32[]{:S(2)}) collective-permute-start(f32[2,18,8,256]{3,2,1,0:T(8,128)S(1)} %get-tuple-element.79), channel_id=1, source_target_pairs={{2,0},{4,2},{6,4},{3,1},{5,3},{7,5},{10,8},{12,10},{14,12},{11,9},... | collective-permute-start | bytes 884744 | tf_op jit(solution)/shard_map/ppermute | solution.py:124
  161.6 47.3 %collective-permute-start.22 = (f32[2,32,32,256]{3,2,1,0:T(8,128)S(1)}, f32[2,32,32,256]{3,2,1,0:T(8,128)S(1)}, u32[]{:S(2)}, u32[]{:S(2)}) collective-permute-start(f32[2,32,32,256]{3,2,1,0:T(8,128)S(1)} %shard_map.69.refs_1_), channel_id=1, source_target_pairs={{0,8},{8,16},{16,24},{1,9},{9,17},{17,25},{2,10},{10,18},{18,26},{... | collective-permute-start | bytes 6291464 | tf_op jit(solution)/shard_map/ppermute | solution.py:536
  175.6 8.9 %collective-permute-start.18 = (f32[2,16,8,256]{3,2,1,0:T(8,128)S(1)}, f32[2,16,8,256]{3,2,1,0:T(8,128)S(1)}, u32[]{:S(2)}, u32[]{:S(2)}) collective-permute-start(f32[2,16,8,256]{3,2,1,0:T(8,128)S(1)} %get-tuple-element.83), channel_id=1, source_target_pairs={{0,1},{1,0},{2,3},{3,2},{4,5},{5,4},{6,7},{7,6},{8,9},{9,8},{10,11... | collective-permute-start | bytes 786440 | tf_op jit(solution)/shard_map/ppermute | solution.py:117
  184.6 3.0 %collective-permute-start.19 = (f32[2,18,8,256]{3,2,1,0:T(8,128)S(1)}, f32[2,18,8,256]{3,2,1,0:T(8,128)S(1)}, u32[]{:S(2)}, u32[]{:S(2)}) collective-permute-start(f32[2,18,8,256]{3,2,1,0:T(8,128)S(1)} %get-tuple-element.84), channel_id=1, source_target_pairs={{0,2},{2,4},{4,6},{1,3},{3,5},{5,7},{8,10},{10,12},{12,14},{9,11},... | collective-permute-start | bytes 884744 | tf_op jit(solution)/shard_map/ppermute | solution.py:124
  186.3 3.5 %collective-permute-start.20 = (f32[2,18,8,256]{3,2,1,0:T(8,128)S(1)}, f32[2,18,8,256]{3,2,1,0:T(8,128)S(1)}, u32[]{:S(2)}, u32[]{:S(2)}) collective-permute-start(f32[2,18,8,256]{3,2,1,0:T(8,128)S(1)} %get-tuple-element.85), channel_id=1, source_target_pairs={{2,0},{4,2},{6,4},{3,1},{5,3},{7,5},{10,8},{12,10},{14,12},{11,9},... | collective-permute-start | bytes 884744 | tf_op jit(solution)/shard_map/ppermute | solution.py:124
  211.9 3.1 %collective-permute-start.25 = (f32[8,128]{1,0:T(8,128)S(1)}, f32[8,128]{1,0:T(8,128)S(1)}, u32[]{:S(2)}, u32[]{:S(2)}) collective-permute-start(f32[8,128]{1,0:T(8,128)S(1)} %shard_map.74), channel_id=1, source_target_pairs={{0,6},{2,4},{4,2},{6,0},{1,7},{3,5},{5,3},{7,1},{8,14},{10,12},{12... | collective-permute-start | bytes 12296 | tf_op jit(solution)/shard_map/ppermute | solution.py:475
  212.0 3.7 %collective-permute-start.24 = (f32[8,128]{1,0:T(8,128)S(1)}, f32[8,128]{1,0:T(8,128)S(1)}, u32[]{:S(2)}, u32[]{:S(2)}) collective-permute-start(f32[8,128]{1,0:T(8,128)S(1)} %shard_map.74), channel_id=1, source_target_pairs={{0,4},{2,6},{4,0},{6,2},{1,5},{3,7},{5,1},{7,3},{8,12},{10,14},{12... | collective-permute-start | bytes 12296 | tf_op jit(solution)/shard_map/ppermute | solution.py:475
  213.6 2.0 collective-permute-start.23
  215.7 3.7 %collective-permute-start.26 = (f32[8,128]{1,0:T(8,128)S(1)}, f32[8,128]{1,0:T(8,128)S(1)}, u32[]{:S(2)}, u32[]{:S(2)}) collective-permute-start(f32[8,128]{1,0:T(8,128)S(1)} %add_add_fusion.1), channel_id=1, source_target_pairs={{0,1},{1,0},{2,3},{3,2},{4,5},{5,4},{6,7},{7,6},{8,9},{9,8},{10,11... | collective-permute-start | bytes 12296 | tf_op jit(solution)/shard_map/ppermute | solution.py:475
  219.3 8.4 %collective-permute-start.29 = (f32[8,128]{1,0:T(8,128)S(1)}, f32[8,128]{1,0:T(8,128)S(1)}, u32[]{:S(2)}, u32[]{:S(2)}) collective-permute-start(f32[8,128]{1,0:T(8,128)S(1)} %add.24), channel_id=1, source_target_pairs={{0,24},{8,16},{16,8},{24,0},{1,25},{9,17},{17,9},{25,1},{2,26},{10... | collective-permute-start | bytes 12296 | tf_op jit(solution)/shard_map/ppermute | solution.py:475
  226.2 4.5 %collective-permute-start.28 = (f32[8,128]{1,0:T(8,128)S(1)}, f32[8,128]{1,0:T(8,128)S(1)}, u32[]{:S(2)}, u32[]{:S(2)}) collective-permute-start(f32[8,128]{1,0:T(8,128)S(1)} %add.24), channel_id=1, source_target_pairs={{0,16},{8,24},{16,0},{24,8},{1,17},{9,25},{17,1},{25,9},{2,18},{10... | collective-permute-start | bytes 12296 | tf_op jit(solution)/shard_map/ppermute | solution.py:475
  226.2 4.5 %collective-permute-start.27 = (f32[8,128]{1,0:T(8,128)S(1)}, f32[8,128]{1,0:T(8,128)S(1)}, u32[]{:S(2)}, u32[]{:S(2)}) collective-permute-start(f32[8,128]{1,0:T(8,128)S(1)} %add.24), channel_id=1, source_target_pairs={{0,8},{8,0},{16,24},{24,16},{1,9},{9,1},{17,25},{25,17},{2,10},{10... | collective-permute-start | bytes 12296 | tf_op jit(solution)/shard_map/ppermute | solution.py:475

commit v6 on v5

--- a/solution.py
+++ b/solution.py
@@ -555,15 +555,18 @@
             [tile] + ([] if last else strips2),
             scratch(3 * group),
             ins + received,
-            12.0,
+            5.0,
             14,
             anywhere=(2, len(ins), len(ins) + 1) if both else (2,),
         )
 
+    next_probes, halfway = lax.optimization_barrier((next_probes, halfway))
+    strips_next = pack([next_probes], not both, 8)
     images, *strips = model(halfway, exchange(strips), True)
     far = [right(images, hops) for hops in range(3, groups)]
 
-    half_next, *strips_next = model(next_probes, exchange(pack([next_probes], not both, 8)), False)
+    received, _ = lax.optimization_barrier((exchange(strips_next), images))
+    half_next, *strips_next = model(next_probes, received, False)
     strips, half_next = lax.optimization_barrier((strips, half_next))
     (images_next,) = model(half_next, exchange(strips_next), True, True)
     shifting, far = lax.optimization_barrier((images_next, far))

time: 235 us -> 215 us (0.915)
  waiting for transfers between devices: 77.9 us -> 45.4 us
  starting transfers between devices: 62.6 us -> 71.8 us
  local copies, waits for them, and re-layouts: 0.03 us -> 2.47 us
    ppermute x3, waiting for transfers between devices: 52.1 us -> 0.01 us  [right(): lax.ppermute(value, 'probe', [(i, i + hops) for i in range(groups - hops)])]
    ppermute x8, waiting for transfers between devices: 13.7 us -> 30.6 us  [moved(): return lax.ppermute(value, ('sx', 'sy'), pairs)]
    ppermute x10, starting transfers between devices: 21 us -> 33.3 us  [exchange(): return [lax.ppermute(hi, 'sx', up), lax.ppermute(lo, 'sx', down), pack]]
    ppermute x10, waiting for transfers between devices: 4.11 us -> 9.24 us  [exchange(): return [lax.ppermute(hi, 'sx', up), lax.ppermute(lo, 'sx', down), pack]]
    ppermute x3, starting transfers between devices: 12.9 us -> 10.4 us  [right(): lax.ppermute(value, 'probe', [(i, i + hops) for i in range(groups - hops)])]
    unnamed x14, local copies, waits for them, and re-layouts: 0.03 us -> 2.47 us
    ppermute x8, starting transfers between devices: 15.3 us -> 12.9 us  [moved(): return lax.ppermute(value, ('sx', 'sy'), pairs)]
    ppermute x7, waiting for transfers between devices: 7.93 us -> 5.58 us  [all_sum(): lax.ppermute(value, axis, [(i, i ^ bits) for i in range(devices)])]
  transfers between devices with their start and end apart: 30 -> 30, of which waited for: 13 -> 14; matrix products, arithmetic and copies ran while one was open for 0% -> 0% of each run, Pallas kernels for 36% -> 40%
where the time goes in v6:
time: 215 us; the launch traced here: 214 us
  Pallas kernels  92.6 us (43%)
  starting transfers between devices  71.8 us (33%)
  waiting for transfers between devices  45.4 us (21%)
  local copies, waits for them, and re-layouts  2.47 us (1%)
    pallas_call x17, Pallas kernels, kernel_call(): pl.pallas_call(body, out_shape=outs, in_specs=specs, out_specs=[spec(n, o...  92.6 us
    ppermute x10, starting transfers between devices, exchange(): return [lax.ppermute(hi, 'sx', up), lax.ppermute(lo, 'sx', down), pack]  33.3 us
    ppermute x8, waiting for transfers between devices, moved(): return lax.ppermute(value, ('sx', 'sy'), pairs)  30.6 us
    ppermute x8, starting transfers between devices, moved(): return lax.ppermute(value, ('sx', 'sy'), pairs)  12.9 us
    ppermute x7, starting transfers between devices, all_sum(): lax.ppermute(value, axis, [(i, i ^ bits) for i in range(devices)])  12.4 us
    ppermute x3, starting transfers between devices, right(): lax.ppermute(value, 'probe', [(i, i + hops) for i in range(groups - hops)])  10.4 us
    ppermute x10, waiting for transfers between devices, exchange(): return [lax.ppermute(hi, 'sx', up), lax.ppermute(lo, 'sx', down), pack]  9.24 us
    ppermute x7, waiting for transfers between devices, all_sum(): lax.ppermute(value, axis, [(i, i ^ bits) for i in range(devices)])  5.58 us
  transfers between devices with their start and end apart: 30, of which 14 were waited for; matrix products, arithmetic and copies ran while one was open for 0% of the time, Pallas kernels for 40%

profile of v6, /device:TPU:0, one launch (start us, length us, event | category | flops | bytes accessed | tf_op | source)
XLA Modules:
  0.0 213.9 jit_solution(13355706853504446710)
XLA Ops:
  0.6 5.1 %collective-permute-start.5 = (f32[2,32,32,256]{3,2,1,0:T(8,128)}, f32[2,32,32,256]{3,2,1,0:T(8,128)S(1)}, u32[]{:S(2)}, u32[]{:S(2)}) collective-permute-start(f32[2,32,32,256]{3,2,1,0:T(8,128)} %probes.1), channel_id=1, source_target_pairs={{0,8},{8,16},{16,24},{1,9},{9,17},{17,25},{2,10},{10,18},{18,26},{... | collective-permute-start | bytes 6291464 | tf_op jit(solution)/shard_map/ppermute | solution.py:536
  5.7 0.6 pad_add_fusion.scalars
  6.3 3.1 %shard_map.60 = (f32[6,16,8,256]{3,2,1,0:T(8,128)}, f32[6,2,8,256]{3,2,1,0:T(8,128)}, f32[6,2,8,256]{3,2,1,0:T(8,128)}) custom-call(s32[2]{0:T(128)} %pad_add_fusion.scalars, f32[1,32,32,256]{3,2,1,0:T(8,128)} %bitcast.3, f32[3,32,32,256]{3,2,1,0:T(8,128)} %velocity.1, f32[2,32,32,256]{3,2,1,0:T(8,128)} %probes.1), custom_call_target="tpu_custom_call" | custom-call | flops 2300000000 | bytes 7200000 | tf_op jit(solution)/shard_map/pallas_call | solution.py:24
  9.4 0.0 copy-start
  9.4 0.0 copy-start.1
  9.4 1.6 collective-permute-start.2
  11.0 2.7 %shard_map.59 = (f32[6,4,32,256]{3,2,1,0:T(8,128)}, f32[6,4,32,256]{3,2,1,0:T(8,128)}) custom-call(f32[1,32,32,256]{3,2,1,0:T(8,128)} %bitcast.4, f32[3,32,32,256]{3,2,1,0:T(8,128)} %velocity.1, f32[2,32,32,256]{3,2,1,0:T(8,128)} %probes.1), custom_call_target="tpu_custom_call" | custom-call | flops 2300000000 | bytes 7200000 | tf_op jit(solution)/shard_map/pallas_call | solution.py:24
  13.7 1.5 collective-permute-start
  15.2 1.3 collective-permute-start.1
  16.5 5.0 %collective-permute-start.3 = (f32[6,2,8,256]{3,2,1,0:T(8,128)}, f32[6,2,8,256]{3,2,1,0:T(8,128)S(1)}, u32[]{:S(2)}, u32[]{:S(2)}) collective-permute-start(f32[6,2,8,256]{3,2,1,0:T(8,128)} %get-tuple-element.53), channel_id=1, source_target_pairs={{0,3},{1,2},{2,5},{3,4},{4,7},{5,6},{8,11},{9,10},{10,13},{11,12},... | collective-permute-start | bytes 294920 | tf_op jit(solution)/shard_map/ppermute | solution.py:117
  21.5 7.4 %collective-permute-done.3.refs_3_ = f32[6,2,8,256]{3,2,1,0:T(8,128)S(1)} collective-permute-done((f32[6,2,8,256]{3,2,1,0:T(8,128)}, f32[6,2,8,256]{3,2,1,0:T(8,128)S(1)}, u32[]{:S(2)}, u32[]{:S(2)}) %collective-permute-start.3) | collective-permute-done | bytes 98336 | tf_op jit(solution)/shard_map/ppermute | solution.py:117
  28.9 1.3 collective-permute-start.4
  30.2 4.7 %collective-permute-done.4.refs_4_ = f32[6,2,8,256]{3,2,1,0:T(8,128)S(1)} collective-permute-done((f32[6,2,8,256]{3,2,1,0:T(8,128)S(1)}, f32[6,2,8,256]{3,2,1,0:T(8,128)S(1)}, u32[]{:S(2)}, u32[]{:S(2)}) %collective-permute-start.4) | collective-permute-done | bytes 98336 | tf_op jit(solution)/shard_map/ppermute | solution.py:117
  34.9 0.0 collective-permute-done.2.refs_2_
  34.9 0.0 collective-permute-done.refs_0_
  34.9 0.0 collective-permute-done.1.refs_1_
  34.9 0.0 copy-start.2
  34.9 1.2 copy-done.2
  36.1 1.2 copy-done.3
  37.4 14.6 %shard_map.61 = (f32[7,40,40,256]{3,2,1,0:T(8,128)S(1)}, f32[2,32,32,256]{3,2,1,0:T(8,128)S(1)}, f32[2,4,32,256]{3,2,1,0:T(8,128)S(1)}, f32[2,4,32,256]{3,2,1,0:T(8,128)S(1)}, f32[2,16,8,256]{3,2,1,0:T(8,128)S(1)}) custom-call(s32[2]{0:T(128)S(1)} %copy-done.5, f32[1,32,32,256]{3,2,1,0:T(8,128)S(1)} %bitcast.5, f32[3,32,32,256]{3,2,1,0:T(8,128)S(1)} %copy-done, ...), custom_call_target="tpu_custom_call" | custom-call | flops 4600000000 | bytes 14400000 | tf_op jit(solution)/shard_map/pallas_call | solution.py:24
  51.9 0.6 collective-permute-start.6
  52.5 8.2 %collective-permute-done.6.pack.refs_2_ = f32[2,16,8,256]{3,2,1,0:T(8,128)S(1)} collective-permute-done((f32[2,16,8,256]{3,2,1,0:T(8,128)S(1)}, f32[2,16,8,256]{3,2,1,0:T(8,128)S(1)}, u32[]{:S(2)}, u32[]{:S(2)}) %collective-permute-start.6) | collective-permute-done | bytes 262176 | tf_op jit(solution)/shard_map/ppermute | solution.py:117
  60.7 2.2 %collective-permute-start.7 = (f32[2,18,8,256]{3,2,1,0:T(8,128)S(1)}, f32[2,18,8,256]{3,2,1,0:T(8,128)S(1)}, u32[]{:S(2)}, u32[]{:S(2)}) collective-permute-start(f32[2,18,8,256]{3,2,1,0:T(8,128)S(1)} %get-tuple-element.61), channel_id=1, source_target_pairs={{0,2},{2,4},{4,6},{1,3},{3,5},{5,7},{8,10},{10,12},{12,14},{9,11},... | collective-permute-start | bytes 884744 | tf_op jit(solution)/shard_map/ppermute | solution.py:124
  63.0 1.3 collective-permute-start.8
  64.3 0.7 shard_map.65
  65.0 0.6 collective-permute-start.9
  65.5 0.9 collective-permute-done.8.refs_1_
  66.4 12.9 %shard_map.63 = (f32[2,32,32,256]{3,2,1,0:T(8,128)S(1)}, f32[2,4,32,256]{3,2,1,0:T(8,128)S(1)}, f32[2,4,32,256]{3,2,1,0:T(8,128)S(1)}, f32[2,16,8,256]{3,2,1,0:T(8,128)S(1)}) custom-call(s32[2]{0:T(128)S(1)} %copy-done.5, f32[7,40,40,256]{3,2,1,0:T(8,128)S(1)} %get-tuple-element.55.coef, f32[2,32,32,256]{3,2,1,0:T(8,128)S(1)} %get-tuple-element.57.tile, ...), custom_call_target="tpu_custom_call" | custom-call | flops 5750000128 | bytes 18000000 | tf_op jit(solution)/shard_map/pallas_call | solution.py:24
  79.4 3.9 %collective-permute-start.21 = (f32[2,32,32,256]{3,2,1,0:T(8,128)S(1)}, f32[2,32,32,256]{3,2,1,0:T(8,128)S(1)}, u32[]{:S(2)}, u32[]{:S(2)}) collective-permute-start(f32[2,32,32,256]{3,2,1,0:T(8,128)S(1)} %get-tuple-element.63.tile.refs_0_), channel_id=1, source_target_pairs={{0,24},{1,25},{2,26},{3,27},{4,28},{5,29},{6,30},{7,31}} | collective-permute-start | bytes 6291464 | tf_op jit(solution)/shard_map/ppermute | solution.py:536
  83.3 0.7 shard_map.64
  84.0 0.0 copy-start.4
  84.1 6.6 %collective-permute-start.10 = (f32[2,18,8,256]{3,2,1,0:T(8,128)S(1)}, f32[2,18,8,256]{3,2,1,0:T(8,128)S(1)}, u32[]{:S(2)}, u32[]{:S(2)}) collective-permute-start(f32[2,18,8,256]{3,2,1,0:T(8,128)S(1)} %get-tuple-element.70), channel_id=1, source_target_pairs={{0,2},{2,4},{4,6},{1,3},{3,5},{5,7},{8,10},{10,12},{12,14},{9,11},... | collective-permute-start | bytes 884744 | tf_op jit(solution)/shard_map/ppermute | solution.py:124
  90.7 1.3 collective-permute-start.11
  92.0 2.2 %collective-permute-done.11.refs_2_ = f32[2,18,8,256]{3,2,1,0:T(8,128)S(1)} collective-permute-done((f32[2,18,8,256]{3,2,1,0:T(8,128)S(1)}, f32[2,18,8,256]{3,2,1,0:T(8,128)S(1)}, u32[]{:S(2)}, u32[]{:S(2)}) %collective-permute-start.11) | collective-permute-done | bytes 294944 | tf_op jit(solution)/shard_map/ppermute | solution.py:124
  94.2 12.6 %shard_map.67 = (f32[2,32,32,256]{3,2,1,0:T(8,128)S(1)}, f32[2,4,32,256]{3,2,1,0:T(8,128)S(1)}, f32[2,4,32,256]{3,2,1,0:T(8,128)S(1)}, f32[2,16,8,256]{3,2,1,0:T(8,128)S(1)}) custom-call(s32[2]{0:T(128)S(1)} %copy-done.5, f32[7,40,40,256]{3,2,1,0:T(8,128)S(1)} %get-tuple-element.55.coef, f32[2,32,32,256]{3,2,1,0:T(8,128)S(1)} %collective-permute-done.5.refs_0_.tile, ...), custom_call_target="tpu_custom_call" | custom-call | flops 5750000128 | bytes 18000000 | tf_op jit(solution)/shard_map/pallas_call | solution.py:24
  106.8 1.3 collective-permute-start.13
  108.1 5.1 %collective-permute-done.13.pack.refs_2_ = f32[2,16,8,256]{3,2,1,0:T(8,128)S(1)} collective-permute-done((f32[2,16,8,256]{3,2,1,0:T(8,128)S(1)}, f32[2,16,8,256]{3,2,1,0:T(8,128)S(1)}, u32[]{:S(2)}, u32[]{:S(2)}) %collective-permute-start.13) | collective-permute-done | bytes 262176 | tf_op jit(solution)/shard_map/ppermute | solution.py:117
  113.2 5.3 %collective-permute-start.14 = (f32[2,18,8,256]{3,2,1,0:T(8,128)S(1)}, f32[2,18,8,256]{3,2,1,0:T(8,128)S(1)}, u32[]{:S(2)}, u32[]{:S(2)}) collective-permute-start(f32[2,18,8,256]{3,2,1,0:T(8,128)S(1)} %get-tuple-element.83), channel_id=1, source_target_pairs={{0,2},{2,4},{4,6},{1,3},{3,5},{5,7},{8,10},{10,12},{12,14},{9,11},... | collective-permute-start | bytes 884744 | tf_op jit(solution)/shard_map/ppermute | solution.py:124
  118.6 1.3 collective-permute-start.15
  119.9 1.3 collective-permute-start.12
  121.2 1.4 collective-permute-done.15.refs_1_
  122.5 12.8 %shard_map.69.refs_1_ = f32[2,32,32,256]{3,2,1,0:T(8,128)S(1)} custom-call(s32[2]{0:T(128)S(1)} %copy-done.5, f32[7,40,40,256]{3,2,1,0:T(8,128)S(1)} %get-tuple-element.55.coef, f32[2,32,32,256]{3,2,1,0:T(8,128)S(1)} %get-tuple-element.79.tile, f32[2,18,8,256]{3,2,1,0:T(8,128)S(1)} %collective-permute-done.14.refs_0_, ...), custom_call_target="tpu_custom_call" | custom-call | flops 5750000128 | bytes 18000000 | tf_op jit(solution)/shard_map/pallas_call | solution.py:24
  135.3 1.4 collective-permute-start.22
  136.8 7.3 %collective-permute-start.16 = (f32[2,18,8,256]{3,2,1,0:T(8,128)S(1)}, f32[2,18,8,256]{3,2,1,0:T(8,128)S(1)}, u32[]{:S(2)}, u32[]{:S(2)}) collective-permute-start(f32[2,18,8,256]{3,2,1,0:T(8,128)S(1)} %get-tuple-element.88), channel_id=1, source_target_pairs={{0,2},{2,4},{4,6},{1,3},{3,5},{5,7},{8,10},{10,12},{12,14},{9,11},... | collective-permute-start | bytes 884744 | tf_op jit(solution)/shard_map/ppermute | solution.py:124
  144.1 1.3 collective-permute-start.17
  145.4 2.2 %collective-permute-done.17.refs_2_ = f32[2,18,8,256]{3,2,1,0:T(8,128)S(1)} collective-permute-done((f32[2,18,8,256]{3,2,1,0:T(8,128)S(1)}, f32[2,18,8,256]{3,2,1,0:T(8,128)S(1)}, u32[]{:S(2)}, u32[]{:S(2)}) %collective-permute-start.17) | collective-permute-done | bytes 294944 | tf_op jit(solution)/shard_map/ppermute | solution.py:124
  147.6 12.6 %shard_map.71 = (f32[2,32,32,256]{3,2,1,0:T(8,128)S(1)}, f32[2,4,32,256]{3,2,1,0:T(8,128)S(1)}, f32[2,4,32,256]{3,2,1,0:T(8,128)S(1)}, f32[2,16,8,256]{3,2,1,0:T(8,128)S(1)}) custom-call(s32[2]{0:T(128)S(1)} %copy-done.5, f32[7,40,40,256]{3,2,1,0:T(8,128)S(1)} %get-tuple-element.55.coef, f32[2,32,32,256]{3,2,1,0:T(8,128)S(1)} %get-tuple-element.63.tile.refs_0_, ...), custom_call_target="tpu_custom_call" | custom-call | flops 5750000128 | bytes 18000000 | tf_op jit(solution)/shard_map/pallas_call | solution.py:24
  160.1 1.3 collective-permute-start.18
  161.4 5.1 %collective-permute-done.18.pack.refs_2_ = f32[2,16,8,256]{3,2,1,0:T(8,128)S(1)} collective-permute-done((f32[2,16,8,256]{3,2,1,0:T(8,128)S(1)}, f32[2,16,8,256]{3,2,1,0:T(8,128)S(1)}, u32[]{:S(2)}, u32[]{:S(2)}) %collective-permute-start.18) | collective-permute-done | bytes 262176 | tf_op jit(solution)/shard_map/ppermute | solution.py:117
  166.6 5.3 %collective-permute-start.19 = (f32[2,18,8,256]{3,2,1,0:T(8,128)S(1)}, f32[2,18,8,256]{3,2,1,0:T(8,128)S(1)}, u32[]{:S(2)}, u32[]{:S(2)}) collective-permute-start(f32[2,18,8,256]{3,2,1,0:T(8,128)S(1)} %get-tuple-element.94), channel_id=1, source_target_pairs={{0,2},{2,4},{4,6},{1,3},{3,5},{5,7},{8,10},{10,12},{12,14},{9,11},... | collective-permute-start | bytes 884744 | tf_op jit(solution)/shard_map/ppermute | solution.py:124
  172.0 1.3 collective-permute-start.20
  173.3 2.6 %collective-permute-done.20.refs_1_ = f32[2,18,8,256]{3,2,1,0:T(8,128)S(1)} collective-permute-done((f32[2,18,8,256]{3,2,1,0:T(8,128)S(1)}, f32[2,18,8,256]{3,2,1,0:T(8,128)S(1)}, u32[]{:S(2)}, u32[]{:S(2)}) %collective-permute-start.20) | collective-permute-done | bytes 294944 | tf_op jit(solution)/shard_map/ppermute | solution.py:124
  175.9 12.8 %shard_map.73.second = f32[2,32,32,256]{3,2,1,0:T(8,128)S(1)} custom-call(s32[2]{0:T(128)S(1)} %copy-done.5, f32[7,40,40,256]{3,2,1,0:T(8,128)S(1)} %get-tuple-element.55.coef, f32[2,32,32,256]{3,2,1,0:T(8,128)S(1)} %get-tuple-element.90.tile, f32[2,18,8,256]{3,2,1,0:T(8,128)S(1)} %collective-permute-done.19.refs_0_, ...), custom_call_target="tpu_custom_call" | custom-call | flops 5750000128 | bytes 18000000 | tf_op jit(solution)/shard_map/pallas_call | solution.py:24
  188.7 3.0 %shard_map.74 = f32[8,128]{1,0:T(8,128)S(1)} custom-call(s32[2]{0:T(128)S(1)} %copy-done.5, f32[2,32,32,256]{3,2,1,0:T(8,128)S(1)} %shard_map.73.second, f32[2,32,32,256]{3,2,1,0:T(8,128)S(1)} %get-tuple-element.63.tile.refs_0_, f32[2,32,32,256]{3,2,1,0:T(8,128)S(1)} %shard_map.69.refs_1_, f32[2,32,32,256]{3,2,1,0:T(8,128)S(1)} %collective-permute-done.22.refs_2_, ...), custom_call_target="tpu_custom_call" | custom-call | flops 4600000000 | bytes 14400000 | tf_op jit(solution)/shard_map/pallas_call | solution.py:24
  191.7 0.2 collective-permute-start.25
  191.9 6.6 %collective-permute-start.24 = (f32[8,128]{1,0:T(8,128)S(1)}, f32[8,128]{1,0:T(8,128)S(1)}, u32[]{:S(2)}, u32[]{:S(2)}) collective-permute-start(f32[8,128]{1,0:T(8,128)S(1)} %shard_map.74), channel_id=1, source_target_pairs={{0,4},{2,6},{4,0},{6,2},{1,5},{3,7},{5,1},{7,3},{8,12},{10,14},{12... | collective-permute-start | bytes 12296 | tf_op jit(solution)/shard_map/ppermute | solution.py:475
  198.5 1.6 collective-permute-done.24
  200.1 1.3 collective-permute-start.26
  201.4 2.4 %collective-permute-done.26 = f32[8,128]{1,0:T(8,128)S(1)} collective-permute-done((f32[8,128]{1,0:T(8,128)S(1)}, f32[8,128]{1,0:T(8,128)S(1)}, u32[]{:S(2)}, u32[]{:S(2)}) %collective-permute-start.26) | collective-permute-done | bytes 4128 | tf_op jit(solution)/shard_map/ppermute | solution.py:475
  203.8 2.2 %collective-permute-start.28 = (f32[8,128]{1,0:T(8,128)S(1)}, f32[8,128]{1,0:T(8,128)S(1)}, u32[]{:S(2)}, u32[]{:S(2)}) collective-permute-start(f32[8,128]{1,0:T(8,128)S(1)} %add.24), channel_id=1, source_target_pairs={{0,16},{8,24},{16,0},{24,8},{1,17},{9,25},{17,1},{25,9},{2,18},{10... | collective-permute-start | bytes 12296 | tf_op jit(solution)/shard_map/ppermute | solution.py:475
  206.0 2.2 %collective-permute-start.27 = (f32[8,128]{1,0:T(8,128)S(1)}, f32[8,128]{1,0:T(8,128)S(1)}, u32[]{:S(2)}, u32[]{:S(2)}) collective-permute-start(f32[8,128]{1,0:T(8,128)S(1)} %add.24), channel_id=1, source_target_pairs={{0,8},{8,0},{16,24},{24,16},{1,9},{9,1},{17,25},{25,17},{2,10},{10... | collective-permute-start | bytes 12296 | tf_op jit(solution)/shard_map/ppermute | solution.py:475
  208.2 1.0 collective-permute-done.29
  209.2 0.6 collective-permute-done.27
  209.8 4.1 %shard_map.75 = (f32[2,32,32,256]{3,2,1,0:T(8,128)}, f32[8,8]{1,0:T(8,128)}) custom-call(s32[2]{0:T(128)S(1)} %copy-done.5, f32[8,128]{1,0:T(8,128)S(1)} %add_add_fusion.inner, f32[2,32,32,256]{3,2,1,0:T(8,128)S(1)} %get-tuple-element.63.tile.refs_0_, f32[2,32,32,256]{3,2,1,0:T(8,128)S(1)} %shard_map.69.refs_1_, ...), custom_call_target="tpu_custom_call" | custom-call | flops 5750000128 | bytes 18000000 | tf_op jit(solution)/shard_map/pallas_call | solution.py:24
  (31 shorter events, 0.3 us)
Async XLA Ops:
  0.6 63.6 %collective-permute-start.5 = (f32[2,32,32,256]{3,2,1,0:T(8,128)}, f32[2,32,32,256]{3,2,1,0:T(8,128)S(1)}, u32[]{:S(2)}, u32[]{:S(2)}) collective-permute-start(f32[2,32,32,256]{3,2,1,0:T(8,128)} %probes.1), channel_id=1, source_target_pairs={{0,8},{8,16},{16,24},{1,9},{9,17},{17,25},{2,10},{10,18},{18,26},{... | collective-permute-start | bytes 6291464 | tf_op jit(solution)/shard_map/ppermute | solution.py:536
  9.4 19.5 %copy-start.6 = (f32[6,2,8,256]{3,2,1,0:T(8,128)S(1)}, f32[6,2,8,256]{3,2,1,0:T(8,128)}, u32[]{:S(2)}) copy-start(f32[6,2,8,256]{3,2,1,0:T(8,128)} %get-tuple-element.54) | copy-start | bytes 294916
  9.4 25.5 %copy-start = (f32[3,32,32,256]{3,2,1,0:T(8,128)S(1)}, f32[3,32,32,256]{3,2,1,0:T(8,128)}, u32[]{:S(2)}) copy-start(f32[3,32,32,256]{3,2,1,0:T(8,128)} %velocity.1) | copy-start | bytes 9437188
  9.4 25.5 %copy-start.1 = (f32[2,32,32,256]{3,2,1,0:T(8,128)S(1)}, f32[2,32,32,256]{3,2,1,0:T(8,128)}, u32[]{:S(2)}) copy-start(f32[2,32,32,256]{3,2,1,0:T(8,128)} %probes.1) | copy-start | bytes 6291460
  9.4 25.5 %copy-start.5 = (s32[2]{0:T(128)S(1)}, s32[2]{0:T(128)}, u32[]{:S(2)}) copy-start(s32[2]{0:T(128)} %pad_add_fusion.scalars) | copy-start | bytes 28
  9.4 25.5 %collective-permute-start.2 = (f32[6,16,8,256]{3,2,1,0:T(8,128)}, f32[6,16,8,256]{3,2,1,0:T(8,128)S(1)}, u32[]{:S(2)}, u32[]{:S(2)}) collective-permute-start(f32[6,16,8,256]{3,2,1,0:T(8,128)} %get-tuple-element.52), channel_id=1, source_target_pairs={{0,1},{1,0},{2,3},{3,2},{4,5},{5,4},{6,7},{7,6},{8,9},{9,8},{10,11... | collective-permute-start | bytes 2359304 | tf_op jit(solution)/shard_map/ppermute | solution.py:117
  13.7 21.2 %collective-permute-start = (f32[6,4,32,256]{3,2,1,0:T(8,128)}, f32[6,4,32,256]{3,2,1,0:T(8,128)S(1)}, u32[]{:S(2)}, u32[]{:S(2)}) collective-permute-start(f32[6,4,32,256]{3,2,1,0:T(8,128)} %get-tuple-element.50), channel_id=1, source_target_pairs={{0,2},{2,4},{4,6},{1,3},{3,5},{5,7},{8,10},{10,12},{12,14},{9,11},... | collective-permute-start | bytes 2359304 | tf_op jit(solution)/shard_map/ppermute | solution.py:125
  15.2 19.7 %collective-permute-start.1 = (f32[6,4,32,256]{3,2,1,0:T(8,128)}, f32[6,4,32,256]{3,2,1,0:T(8,128)S(1)}, u32[]{:S(2)}, u32[]{:S(2)}) collective-permute-start(f32[6,4,32,256]{3,2,1,0:T(8,128)} %get-tuple-element.51), channel_id=1, source_target_pairs={{2,0},{4,2},{6,4},{3,1},{5,3},{7,5},{10,8},{12,10},{14,12},{11,9},... | collective-permute-start | bytes 2359304 | tf_op jit(solution)/shard_map/ppermute | solution.py:126
  16.5 12.4 %collective-permute-start.3 = (f32[6,2,8,256]{3,2,1,0:T(8,128)}, f32[6,2,8,256]{3,2,1,0:T(8,128)S(1)}, u32[]{:S(2)}, u32[]{:S(2)}) collective-permute-start(f32[6,2,8,256]{3,2,1,0:T(8,128)} %get-tuple-element.53), channel_id=1, source_target_pairs={{0,3},{1,2},{2,5},{3,4},{4,7},{5,6},{8,11},{9,10},{10,13},{11,12},... | collective-permute-start | bytes 294920 | tf_op jit(solution)/shard_map/ppermute | solution.py:117
  28.9 6.0 %collective-permute-start.4 = (f32[6,2,8,256]{3,2,1,0:T(8,128)S(1)}, f32[6,2,8,256]{3,2,1,0:T(8,128)S(1)}, u32[]{:S(2)}, u32[]{:S(2)}) collective-permute-start(f32[6,2,8,256]{3,2,1,0:T(8,128)S(1)} %copy-done.6), channel_id=1, source_target_pairs={{2,1},{3,0},{4,3},{5,2},{6,5},{7,4},{10,9},{11,8},{12,11},{13,10},... | collective-permute-start | bytes 294920 | tf_op jit(solution)/shard_map/ppermute | solution.py:117
  34.9 1.2 copy-start.2
  36.1 1.2 copy-start.3
  51.9 8.8 %collective-permute-start.6 = (f32[2,16,8,256]{3,2,1,0:T(8,128)S(1)}, f32[2,16,8,256]{3,2,1,0:T(8,128)S(1)}, u32[]{:S(2)}, u32[]{:S(2)}) collective-permute-start(f32[2,16,8,256]{3,2,1,0:T(8,128)S(1)} %get-tuple-element.60), channel_id=1, source_target_pairs={{0,1},{1,0},{2,3},{3,2},{4,5},{5,4},{6,7},{7,6},{8,9},{9,8},{10,11... | collective-permute-start | bytes 786440 | tf_op jit(solution)/shard_map/ppermute | solution.py:117
  60.7 4.8 %collective-permute-start.7 = (f32[2,18,8,256]{3,2,1,0:T(8,128)S(1)}, f32[2,18,8,256]{3,2,1,0:T(8,128)S(1)}, u32[]{:S(2)}, u32[]{:S(2)}) collective-permute-start(f32[2,18,8,256]{3,2,1,0:T(8,128)S(1)} %get-tuple-element.61), channel_id=1, source_target_pairs={{0,2},{2,4},{4,6},{1,3},{3,5},{5,7},{8,10},{10,12},{12,14},{9,11},... | collective-permute-start | bytes 884744 | tf_op jit(solution)/shard_map/ppermute | solution.py:124
  63.0 3.5 %collective-permute-start.8 = (f32[2,18,8,256]{3,2,1,0:T(8,128)S(1)}, f32[2,18,8,256]{3,2,1,0:T(8,128)S(1)}, u32[]{:S(2)}, u32[]{:S(2)}) collective-permute-start(f32[2,18,8,256]{3,2,1,0:T(8,128)S(1)} %get-tuple-element.62), channel_id=1, source_target_pairs={{2,0},{4,2},{6,4},{3,1},{5,3},{7,5},{10,8},{12,10},{14,12},{11,9},... | collective-permute-start | bytes 884744 | tf_op jit(solution)/shard_map/ppermute | solution.py:124
  65.0 19.0 %collective-permute-start.9 = (f32[2,16,8,256]{3,2,1,0:T(8,128)S(1)}, f32[2,16,8,256]{3,2,1,0:T(8,128)S(1)}, u32[]{:S(2)}, u32[]{:S(2)}) collective-permute-start(f32[2,16,8,256]{3,2,1,0:T(8,128)S(1)} %shard_map.65), channel_id=1, source_target_pairs={{0,1},{1,0},{2,3},{3,2},{4,5},{5,4},{6,7},{7,6},{8,9},{9,8},{10,11... | collective-permute-start | bytes 786440 | tf_op jit(solution)/shard_map/ppermute | solution.py:117
  79.4 55.9 %collective-permute-start.21 = (f32[2,32,32,256]{3,2,1,0:T(8,128)S(1)}, f32[2,32,32,256]{3,2,1,0:T(8,128)S(1)}, u32[]{:S(2)}, u32[]{:S(2)}) collective-permute-start(f32[2,32,32,256]{3,2,1,0:T(8,128)S(1)} %get-tuple-element.63.tile.refs_0_), channel_id=1, source_target_pairs={{0,24},{1,25},{2,26},{3,27},{4,28},{5,29},{6,30},{7,31}} | collective-permute-start | bytes 6291464 | tf_op jit(solution)/shard_map/ppermute | solution.py:536
  84.0 10.2 %copy-start.4 = (f32[32,32,256]{2,1,0:T(8,128)S(1)}, f32[32,32,256]{2,1,0:T(8,128)}, u32[]{:S(2)}) copy-start(f32[32,32,256]{2,1,0:T(8,128)} %refs_0_.3) | copy-start | bytes 3145732
  84.1 7.9 %collective-permute-start.10 = (f32[2,18,8,256]{3,2,1,0:T(8,128)S(1)}, f32[2,18,8,256]{3,2,1,0:T(8,128)S(1)}, u32[]{:S(2)}, u32[]{:S(2)}) collective-permute-start(f32[2,18,8,256]{3,2,1,0:T(8,128)S(1)} %get-tuple-element.70), channel_id=1, source_target_pairs={{0,2},{2,4},{4,6},{1,3},{3,5},{5,7},{8,10},{10,12},{12,14},{9,11},... | collective-permute-start | bytes 884744 | tf_op jit(solution)/shard_map/ppermute | solution.py:124
  90.7 3.5 %collective-permute-start.11 = (f32[2,18,8,256]{3,2,1,0:T(8,128)S(1)}, f32[2,18,8,256]{3,2,1,0:T(8,128)S(1)}, u32[]{:S(2)}, u32[]{:S(2)}) collective-permute-start(f32[2,18,8,256]{3,2,1,0:T(8,128)S(1)} %get-tuple-element.71), channel_id=1, source_target_pairs={{2,0},{4,2},{6,4},{3,1},{5,3},{7,5},{10,8},{12,10},{14,12},{11,9},... | collective-permute-start | bytes 884744 | tf_op jit(solution)/shard_map/ppermute | solution.py:124
  106.8 6.4 %collective-permute-start.13 = (f32[2,16,8,256]{3,2,1,0:T(8,128)S(1)}, f32[2,16,8,256]{3,2,1,0:T(8,128)S(1)}, u32[]{:S(2)}, u32[]{:S(2)}) collective-permute-start(f32[2,16,8,256]{3,2,1,0:T(8,128)S(1)} %get-tuple-element.82), channel_id=1, source_target_pairs={{0,1},{1,0},{2,3},{3,2},{4,5},{5,4},{6,7},{7,6},{8,9},{9,8},{10,11... | collective-permute-start | bytes 786440 | tf_op jit(solution)/shard_map/ppermute | solution.py:117
  113.2 7.9 %collective-permute-start.14 = (f32[2,18,8,256]{3,2,1,0:T(8,128)S(1)}, f32[2,18,8,256]{3,2,1,0:T(8,128)S(1)}, u32[]{:S(2)}, u32[]{:S(2)}) collective-permute-start(f32[2,18,8,256]{3,2,1,0:T(8,128)S(1)} %get-tuple-element.83), channel_id=1, source_target_pairs={{0,2},{2,4},{4,6},{1,3},{3,5},{5,7},{8,10},{10,12},{12,14},{9,11},... | collective-permute-start | bytes 884744 | tf_op jit(solution)/shard_map/ppermute | solution.py:124
  118.6 4.0 %collective-permute-start.15 = (f32[2,18,8,256]{3,2,1,0:T(8,128)S(1)}, f32[2,18,8,256]{3,2,1,0:T(8,128)S(1)}, u32[]{:S(2)}, u32[]{:S(2)}) collective-permute-start(f32[2,18,8,256]{3,2,1,0:T(8,128)S(1)} %get-tuple-element.84), channel_id=1, source_target_pairs={{2,0},{4,2},{6,4},{3,1},{5,3},{7,5},{10,8},{12,10},{14,12},{11,9},... | collective-permute-start | bytes 884744 | tf_op jit(solution)/shard_map/ppermute | solution.py:124
  119.9 15.4 %collective-permute-start.12 = (f32[2,16,8,256]{3,2,1,0:T(8,128)S(1)}, f32[2,16,8,256]{3,2,1,0:T(8,128)S(1)}, u32[]{:S(2)}, u32[]{:S(2)}) collective-permute-start(f32[2,16,8,256]{3,2,1,0:T(8,128)S(1)} %get-tuple-element.78), channel_id=1, source_target_pairs={{0,1},{1,0},{2,3},{3,2},{4,5},{5,4},{6,7},{7,6},{8,9},{9,8},{10,11... | collective-permute-start | bytes 786440 | tf_op jit(solution)/shard_map/ppermute | solution.py:117
  135.3 53.4 %collective-permute-start.22 = (f32[2,32,32,256]{3,2,1,0:T(8,128)S(1)}, f32[2,32,32,256]{3,2,1,0:T(8,128)S(1)}, u32[]{:S(2)}, u32[]{:S(2)}) collective-permute-start(f32[2,32,32,256]{3,2,1,0:T(8,128)S(1)} %shard_map.69.refs_1_), channel_id=1, source_target_pairs={{0,8},{8,16},{16,24},{1,9},{9,17},{17,25},{2,10},{10,18},{18,26},{... | collective-permute-start | bytes 6291464 | tf_op jit(solution)/shard_map/ppermute | solution.py:536
  136.8 8.6 %collective-permute-start.16 = (f32[2,18,8,256]{3,2,1,0:T(8,128)S(1)}, f32[2,18,8,256]{3,2,1,0:T(8,128)S(1)}, u32[]{:S(2)}, u32[]{:S(2)}) collective-permute-start(f32[2,18,8,256]{3,2,1,0:T(8,128)S(1)} %get-tuple-element.88), channel_id=1, source_target_pairs={{0,2},{2,4},{4,6},{1,3},{3,5},{5,7},{8,10},{10,12},{12,14},{9,11},... | collective-permute-start | bytes 884744 | tf_op jit(solution)/shard_map/ppermute | solution.py:124
  144.1 3.5 %collective-permute-start.17 = (f32[2,18,8,256]{3,2,1,0:T(8,128)S(1)}, f32[2,18,8,256]{3,2,1,0:T(8,128)S(1)}, u32[]{:S(2)}, u32[]{:S(2)}) collective-permute-start(f32[2,18,8,256]{3,2,1,0:T(8,128)S(1)} %get-tuple-element.89), channel_id=1, source_target_pairs={{2,0},{4,2},{6,4},{3,1},{5,3},{7,5},{10,8},{12,10},{14,12},{11,9},... | collective-permute-start | bytes 884744 | tf_op jit(solution)/shard_map/ppermute | solution.py:124
  160.1 6.4 %collective-permute-start.18 = (f32[2,16,8,256]{3,2,1,0:T(8,128)S(1)}, f32[2,16,8,256]{3,2,1,0:T(8,128)S(1)}, u32[]{:S(2)}, u32[]{:S(2)}) collective-permute-start(f32[2,16,8,256]{3,2,1,0:T(8,128)S(1)} %get-tuple-element.93), channel_id=1, source_target_pairs={{0,1},{1,0},{2,3},{3,2},{4,5},{5,4},{6,7},{7,6},{8,9},{9,8},{10,11... | collective-permute-start | bytes 786440 | tf_op jit(solution)/shard_map/ppermute | solution.py:117
  166.6 6.6 %collective-permute-start.19 = (f32[2,18,8,256]{3,2,1,0:T(8,128)S(1)}, f32[2,18,8,256]{3,2,1,0:T(8,128)S(1)}, u32[]{:S(2)}, u32[]{:S(2)}) collective-permute-start(f32[2,18,8,256]{3,2,1,0:T(8,128)S(1)} %get-tuple-element.94), channel_id=1, source_target_pairs={{0,2},{2,4},{4,6},{1,3},{3,5},{5,7},{8,10},{10,12},{12,14},{9,11},... | collective-permute-start | bytes 884744 | tf_op jit(solution)/shard_map/ppermute | solution.py:124
  172.0 4.0 %collective-permute-start.20 = (f32[2,18,8,256]{3,2,1,0:T(8,128)S(1)}, f32[2,18,8,256]{3,2,1,0:T(8,128)S(1)}, u32[]{:S(2)}, u32[]{:S(2)}) collective-permute-start(f32[2,18,8,256]{3,2,1,0:T(8,128)S(1)} %get-tuple-element.95), channel_id=1, source_target_pairs={{2,0},{4,2},{6,4},{3,1},{5,3},{7,5},{10,8},{12,10},{14,12},{11,9},... | collective-permute-start | bytes 884744 | tf_op jit(solution)/shard_map/ppermute | solution.py:124
  191.7 6.8 %collective-permute-start.25 = (f32[8,128]{1,0:T(8,128)S(1)}, f32[8,128]{1,0:T(8,128)S(1)}, u32[]{:S(2)}, u32[]{:S(2)}) collective-permute-start(f32[8,128]{1,0:T(8,128)S(1)} %shard_map.74), channel_id=1, source_target_pairs={{0,6},{2,4},{4,2},{6,0},{1,7},{3,5},{5,3},{7,1},{8,14},{10,12},{12... | collective-permute-start | bytes 12296 | tf_op jit(solution)/shard_map/ppermute | solution.py:475
  191.9 8.2 %collective-permute-start.24 = (f32[8,128]{1,0:T(8,128)S(1)}, f32[8,128]{1,0:T(8,128)S(1)}, u32[]{:S(2)}, u32[]{:S(2)}) collective-permute-start(f32[8,128]{1,0:T(8,128)S(1)} %shard_map.74), channel_id=1, source_target_pairs={{0,4},{2,6},{4,0},{6,2},{1,5},{3,7},{5,1},{7,3},{8,12},{10,14},{12... | collective-permute-start | bytes 12296 | tf_op jit(solution)/shard_map/ppermute | solution.py:475
  198.5 1.6 collective-permute-start.23
  200.1 3.7 %collective-permute-start.26 = (f32[8,128]{1,0:T(8,128)S(1)}, f32[8,128]{1,0:T(8,128)S(1)}, u32[]{:S(2)}, u32[]{:S(2)}) collective-permute-start(f32[8,128]{1,0:T(8,128)S(1)} %add_add_fusion.1), channel_id=1, source_target_pairs={{0,1},{1,0},{2,3},{3,2},{4,5},{5,4},{6,7},{7,6},{8,9},{9,8},{10,11... | collective-permute-start | bytes 12296 | tf_op jit(solution)/shard_map/ppermute | solution.py:475
  203.8 5.4 %collective-permute-start.29 = (f32[8,128]{1,0:T(8,128)S(1)}, f32[8,128]{1,0:T(8,128)S(1)}, u32[]{:S(2)}, u32[]{:S(2)}) collective-permute-start(f32[8,128]{1,0:T(8,128)S(1)} %add.24), channel_id=1, source_target_pairs={{0,24},{8,16},{16,8},{24,0},{1,25},{9,17},{17,9},{25,1},{2,26},{10... | collective-permute-start | bytes 12296 | tf_op jit(solution)/shard_map/ppermute | solution.py:475
  203.8 5.4 %collective-permute-start.28 = (f32[8,128]{1,0:T(8,128)S(1)}, f32[8,128]{1,0:T(8,128)S(1)}, u32[]{:S(2)}, u32[]{:S(2)}) collective-permute-start(f32[8,128]{1,0:T(8,128)S(1)} %add.24), channel_id=1, source_target_pairs={{0,16},{8,24},{16,0},{24,8},{1,17},{9,25},{17,1},{25,9},{2,18},{10... | collective-permute-start | bytes 12296 | tf_op jit(solution)/shard_map/ppermute | solution.py:475
  206.0 3.8 %collective-permute-start.27 = (f32[8,128]{1,0:T(8,128)S(1)}, f32[8,128]{1,0:T(8,128)S(1)}, u32[]{:S(2)}, u32[]{:S(2)}) collective-permute-start(f32[8,128]{1,0:T(8,128)S(1)} %add.24), channel_id=1, source_target_pairs={{0,8},{8,0},{16,24},{24,16},{1,9},{9,1},{17,25},{25,17},{2,10},{10... | collective-permute-start | bytes 12296 | tf_op jit(solution)/shard_map/ppermute | solution.py:475

commit v7 on v6

--- a/solution.py
+++ b/solution.py
@@ -535,8 +535,9 @@
     def right(value, hops):
         return lax.ppermute(value, "probe", [(i, i + hops) for i in range(groups - hops)])
 
-    next_probes = right(probes, 1)
     strips = pack(fields, False, 56)
+    strips[2], leaving = lax.optimization_barrier((strips[2], probes))
+    next_probes = right(leaving, 1)
     received = exchange(strips)
     coef, halfway, *strips = kernel_call(
         functools.partial(first_kernel, len(received)),
@@ -555,7 +556,7 @@
             [tile] + ([] if last else strips2),
             scratch(3 * group),
             ins + received,
-            5.0,
+            8.0,
             14,
             anywhere=(2, len(ins), len(ins) + 1) if both else (2,),
         )

time: 215 us -> 209 us (0.972)
  starting transfers between devices: 71.8 us -> 61.4 us
  Pallas kernels: 92.6 us -> 95.4 us
    ppermute x7, starting transfers between devices: 12.4 us -> 8.19 us  [all_sum(): lax.ppermute(value, axis, [(i, i ^ bits) for i in range(devices)])]
    ppermute x3, waiting for transfers between devices: 0.01 us -> 4.18 us  [right(): lax.ppermute(value, 'probe', [(i, i + hops) for i in range(groups - hops)])]
    ppermute x10, starting transfers between devices: 33.3 us -> 29.3 us  [exchange(): return [lax.ppermute(hi, 'sx', up), lax.ppermute(lo, 'sx', down), pack]]
    ppermute x10, waiting for transfers between devices: 9.24 us -> 6.42 us  [exchange(): return [lax.ppermute(hi, 'sx', up), lax.ppermute(lo, 'sx', down), pack]]
    pallas_call x17, Pallas kernels: 92.6 us -> 95.4 us  [kernel_call(): pl.pallas_call(body, out_shape=outs, in_specs=specs, out_specs=[spec(n, o...]
  transfers between devices with their start and end apart: 30 -> 30, of which waited for: 14 -> 16; matrix products, arithmetic and copies ran while one was open for 0% -> 0% of each run, Pallas kernels for 40% -> 41%
where the time goes in v7:
time: 209 us; the launch traced here: 208 us
  Pallas kernels  95.4 us (46%)
  starting transfers between devices  61.4 us (29%)
  waiting for transfers between devices  47.2 us (23%)
  local copies, waits for them, and re-layouts  2.48 us (1%)
    pallas_call x17, Pallas kernels, kernel_call(): pl.pallas_call(body, out_shape=outs, in_specs=specs, out_specs=[spec(n, o...  95.4 us
    ppermute x8, waiting for transfers between devices, moved(): return lax.ppermute(value, ('sx', 'sy'), pairs)  29.9 us
    ppermute x10, starting transfers between devices, exchange(): return [lax.ppermute(hi, 'sx', up), lax.ppermute(lo, 'sx', down), pack]  29.3 us
    ppermute x8, starting transfers between devices, moved(): return lax.ppermute(value, ('sx', 'sy'), pairs)  11.9 us
    ppermute x3, starting transfers between devices, right(): lax.ppermute(value, 'probe', [(i, i + hops) for i in range(groups - hops)])  9.38 us
    ppermute x7, starting transfers between devices, all_sum(): lax.ppermute(value, axis, [(i, i ^ bits) for i in range(devices)])  8.19 us
    ppermute x7, waiting for transfers between devices, all_sum(): lax.ppermute(value, axis, [(i, i ^ bits) for i in range(devices)])  6.78 us
    ppermute x10, waiting for transfers between devices, exchange(): return [lax.ppermute(hi, 'sx', up), lax.ppermute(lo, 'sx', down), pack]  6.42 us
  transfers between devices with their start and end apart: 30, of which 16 were waited for; matrix products, arithmetic and copies ran while one was open for 0% of the time, Pallas kernels for 41%

profile of v7, /device:TPU:0, one launch (start us, length us, event | category | flops | bytes accessed | tf_op | source)
XLA Modules:
  0.0 208.2 jit_solution(15632813191239532620)
XLA Ops:
  0.6 0.7 pad_add_fusion.scalars
  1.3 3.2 %shard_map.60 = (f32[6,16,8,256]{3,2,1,0:T(8,128)}, f32[6,2,8,256]{3,2,1,0:T(8,128)}, f32[6,2,8,256]{3,2,1,0:T(8,128)}) custom-call(s32[2]{0:T(128)} %pad_add_fusion.scalars, f32[1,32,32,256]{3,2,1,0:T(8,128)} %bitcast.3, f32[3,32,32,256]{3,2,1,0:T(8,128)} %velocity.1, f32[2,32,32,256]{3,2,1,0:T(8,128)} %probes.1), custom_call_target="tpu_custom_call" | custom-call | flops 2300000000 | bytes 7200000 | tf_op jit(solution)/shard_map/pallas_call | solution.py:24
  4.5 0.0 copy-start
  4.5 0.0 copy-start.2
  4.6 6.5 %collective-permute-start.5 = (f32[2,32,32,256]{3,2,1,0:T(8,128)S(1)}, f32[2,32,32,256]{3,2,1,0:T(8,128)}, u32[]{:S(2)}, u32[]{:S(2)}) collective-permute-start(f32[2,32,32,256]{3,2,1,0:T(8,128)S(1)} %copy-done.1), channel_id=1, source_target_pairs={{0,8},{8,16},{16,24},{1,9},{9,17},{17,25},{2,10},{10,18},{18,26},{... | collective-permute-start | bytes 6291464 | tf_op jit(solution)/shard_map/ppermute | solution.py:536
  11.1 1.5 collective-permute-start.2
  12.6 2.7 %shard_map.59 = (f32[6,4,32,256]{3,2,1,0:T(8,128)}, f32[6,4,32,256]{3,2,1,0:T(8,128)}) custom-call(f32[1,32,32,256]{3,2,1,0:T(8,128)} %bitcast.4, f32[3,32,32,256]{3,2,1,0:T(8,128)} %velocity.1, f32[2,32,32,256]{3,2,1,0:T(8,128)} %probes.1), custom_call_target="tpu_custom_call" | custom-call | flops 2300000000 | bytes 7200000 | tf_op jit(solution)/shard_map/pallas_call | solution.py:24
  15.3 1.3 collective-permute-start
  16.7 1.3 collective-permute-start.1
  18.0 4.8 %collective-permute-start.3 = (f32[6,2,8,256]{3,2,1,0:T(8,128)}, f32[6,2,8,256]{3,2,1,0:T(8,128)S(1)}, u32[]{:S(2)}, u32[]{:S(2)}) collective-permute-start(f32[6,2,8,256]{3,2,1,0:T(8,128)} %get-tuple-element.56), channel_id=1, source_target_pairs={{0,3},{1,2},{2,5},{3,4},{4,7},{5,6},{8,11},{9,10},{10,13},{11,12},... | collective-permute-start | bytes 294920 | tf_op jit(solution)/shard_map/ppermute | solution.py:117
  22.8 7.7 %collective-permute-done.3.refs_3_ = f32[6,2,8,256]{3,2,1,0:T(8,128)S(1)} collective-permute-done((f32[6,2,8,256]{3,2,1,0:T(8,128)}, f32[6,2,8,256]{3,2,1,0:T(8,128)S(1)}, u32[]{:S(2)}, u32[]{:S(2)}) %collective-permute-start.3) | collective-permute-done | bytes 98336 | tf_op jit(solution)/shard_map/ppermute | solution.py:117
  30.5 1.3 collective-permute-start.4
  31.8 4.7 %collective-permute-done.4.refs_4_ = f32[6,2,8,256]{3,2,1,0:T(8,128)S(1)} collective-permute-done((f32[6,2,8,256]{3,2,1,0:T(8,128)S(1)}, f32[6,2,8,256]{3,2,1,0:T(8,128)S(1)}, u32[]{:S(2)}, u32[]{:S(2)}) %collective-permute-start.4) | collective-permute-done | bytes 98336 | tf_op jit(solution)/shard_map/ppermute | solution.py:117
  36.5 0.0 copy-start.3
  36.6 1.2 copy-done.3
  37.8 1.2 copy-done.4
  39.0 14.6 %shard_map.61 = (f32[7,40,40,256]{3,2,1,0:T(8,128)S(1)}, f32[2,32,32,256]{3,2,1,0:T(8,128)S(1)}, f32[2,4,32,256]{3,2,1,0:T(8,128)S(1)}, f32[2,4,32,256]{3,2,1,0:T(8,128)S(1)}, f32[2,16,8,256]{3,2,1,0:T(8,128)S(1)}) custom-call(s32[2]{0:T(128)S(1)} %copy-done.6, f32[1,32,32,256]{3,2,1,0:T(8,128)S(1)} %bitcast.5, f32[3,32,32,256]{3,2,1,0:T(8,128)S(1)} %copy-done, ...), custom_call_target="tpu_custom_call" | custom-call | flops 4600000000 | bytes 14400000 | tf_op jit(solution)/shard_map/pallas_call | solution.py:24
  53.6 0.6 collective-permute-start.6
  54.1 0.5 collective-permute-done.5.refs_0_.tile
  54.6 1.6 shard_map.65
  56.3 1.6 collective-permute-start.9
  57.8 4.5 %collective-permute-done.6.pack.refs_2_ = f32[2,16,8,256]{3,2,1,0:T(8,128)S(1)} collective-permute-done((f32[2,16,8,256]{3,2,1,0:T(8,128)S(1)}, f32[2,16,8,256]{3,2,1,0:T(8,128)S(1)}, u32[]{:S(2)}, u32[]{:S(2)}) %collective-permute-start.6) | collective-permute-done | bytes 262176 | tf_op jit(solution)/shard_map/ppermute | solution.py:117
  62.4 3.0 %collective-permute-start.7 = (f32[2,18,8,256]{3,2,1,0:T(8,128)S(1)}, f32[2,18,8,256]{3,2,1,0:T(8,128)S(1)}, u32[]{:S(2)}, u32[]{:S(2)}) collective-permute-start(f32[2,18,8,256]{3,2,1,0:T(8,128)S(1)} %get-tuple-element.65), channel_id=1, source_target_pairs={{0,2},{2,4},{4,6},{1,3},{3,5},{5,7},{8,10},{10,12},{12,14},{9,11},... | collective-permute-start | bytes 884744 | tf_op jit(solution)/shard_map/ppermute | solution.py:124
  65.4 1.3 collective-permute-start.8
  66.7 1.1 shard_map.64
  67.8 0.1 collective-permute-done.9.pack.refs_3_
  68.0 4.4 %collective-permute-start.10 = (f32[2,18,8,256]{3,2,1,0:T(8,128)S(1)}, f32[2,18,8,256]{3,2,1,0:T(8,128)S(1)}, u32[]{:S(2)}, u32[]{:S(2)}) collective-permute-start(f32[2,18,8,256]{3,2,1,0:T(8,128)S(1)} %get-tuple-element.74), channel_id=1, source_target_pairs={{0,2},{2,4},{4,6},{1,3},{3,5},{5,7},{8,10},{10,12},{12,14},{9,11},... | collective-permute-start | bytes 884744 | tf_op jit(solution)/shard_map/ppermute | solution.py:124
  72.3 1.3 collective-permute-start.11
  73.7 0.0 copy-start.5
  73.7 12.9 %shard_map.63 = (f32[2,32,32,256]{3,2,1,0:T(8,128)S(1)}, f32[2,4,32,256]{3,2,1,0:T(8,128)S(1)}, f32[2,4,32,256]{3,2,1,0:T(8,128)S(1)}, f32[2,16,8,256]{3,2,1,0:T(8,128)S(1)}) custom-call(s32[2]{0:T(128)S(1)} %copy-done.6, f32[7,40,40,256]{3,2,1,0:T(8,128)S(1)} %get-tuple-element.58.coef, f32[2,32,32,256]{3,2,1,0:T(8,128)S(1)} %get-tuple-element.61.tile, ...), custom_call_target="tpu_custom_call" | custom-call | flops 9200000000 | bytes 28800000 | tf_op jit(solution)/shard_map/pallas_call | solution.py:24
  86.6 1.4 collective-permute-start.21
  88.1 13.8 %shard_map.67 = (f32[2,32,32,256]{3,2,1,0:T(8,128)S(1)}, f32[2,4,32,256]{3,2,1,0:T(8,128)S(1)}, f32[2,4,32,256]{3,2,1,0:T(8,128)S(1)}, f32[2,16,8,256]{3,2,1,0:T(8,128)S(1)}) custom-call(s32[2]{0:T(128)S(1)} %copy-done.6, f32[7,40,40,256]{3,2,1,0:T(8,128)S(1)} %get-tuple-element.58.coef, f32[2,32,32,256]{3,2,1,0:T(8,128)} %collective-permute-done.5.refs_0_.tile, ...), custom_call_target="tpu_custom_call" | custom-call | flops 9200000000 | bytes 28800000 | tf_op jit(solution)/shard_map/pallas_call | solution.py:24
  101.9 0.7 collective-permute-start.13
  102.6 7.1 %collective-permute-done.13.pack.refs_2_ = f32[2,16,8,256]{3,2,1,0:T(8,128)S(1)} collective-permute-done((f32[2,16,8,256]{3,2,1,0:T(8,128)S(1)}, f32[2,16,8,256]{3,2,1,0:T(8,128)S(1)}, u32[]{:S(2)}, u32[]{:S(2)}) %collective-permute-start.13) | collective-permute-done | bytes 262176 | tf_op jit(solution)/shard_map/ppermute | solution.py:117
  109.7 3.2 %collective-permute-start.14 = (f32[2,18,8,256]{3,2,1,0:T(8,128)S(1)}, f32[2,18,8,256]{3,2,1,0:T(8,128)S(1)}, u32[]{:S(2)}, u32[]{:S(2)}) collective-permute-start(f32[2,18,8,256]{3,2,1,0:T(8,128)S(1)} %get-tuple-element.87), channel_id=1, source_target_pairs={{0,2},{2,4},{4,6},{1,3},{3,5},{5,7},{8,10},{10,12},{12,14},{9,11},... | collective-permute-start | bytes 884744 | tf_op jit(solution)/shard_map/ppermute | solution.py:124
  112.9 1.3 collective-permute-start.15
  114.2 0.7 collective-permute-start.12
  114.9 3.0 %collective-permute-done.15.refs_1_ = f32[2,18,8,256]{3,2,1,0:T(8,128)S(1)} collective-permute-done((f32[2,18,8,256]{3,2,1,0:T(8,128)S(1)}, f32[2,18,8,256]{3,2,1,0:T(8,128)S(1)}, u32[]{:S(2)}, u32[]{:S(2)}) %collective-permute-start.15) | collective-permute-done | bytes 294944 | tf_op jit(solution)/shard_map/ppermute | solution.py:124
  118.0 12.8 %shard_map.69.refs_1_ = f32[2,32,32,256]{3,2,1,0:T(8,128)S(1)} custom-call(s32[2]{0:T(128)S(1)} %copy-done.6, f32[7,40,40,256]{3,2,1,0:T(8,128)S(1)} %get-tuple-element.58.coef, f32[2,32,32,256]{3,2,1,0:T(8,128)S(1)} %get-tuple-element.83.tile, f32[2,18,8,256]{3,2,1,0:T(8,128)S(1)} %collective-permute-done.14.refs_0_, ...), custom_call_target="tpu_custom_call" | custom-call | flops 9200000000 | bytes 28800000 | tf_op jit(solution)/shard_map/pallas_call | solution.py:24
  130.8 7.0 %collective-permute-start.16 = (f32[2,18,8,256]{3,2,1,0:T(8,128)S(1)}, f32[2,18,8,256]{3,2,1,0:T(8,128)S(1)}, u32[]{:S(2)}, u32[]{:S(2)}) collective-permute-start(f32[2,18,8,256]{3,2,1,0:T(8,128)S(1)} %get-tuple-element.92), channel_id=1, source_target_pairs={{0,2},{2,4},{4,6},{1,3},{3,5},{5,7},{8,10},{10,12},{12,14},{9,11},... | collective-permute-start | bytes 884744 | tf_op jit(solution)/shard_map/ppermute | solution.py:124
  137.8 1.3 collective-permute-start.17
  139.1 1.4 collective-permute-start.22
  140.5 0.7 collective-permute-done.17.refs_2_
  141.3 12.6 %shard_map.71 = (f32[2,32,32,256]{3,2,1,0:T(8,128)S(1)}, f32[2,4,32,256]{3,2,1,0:T(8,128)S(1)}, f32[2,4,32,256]{3,2,1,0:T(8,128)S(1)}, f32[2,16,8,256]{3,2,1,0:T(8,128)S(1)}) custom-call(s32[2]{0:T(128)S(1)} %copy-done.6, f32[7,40,40,256]{3,2,1,0:T(8,128)S(1)} %get-tuple-element.58.coef, f32[2,32,32,256]{3,2,1,0:T(8,128)S(1)} %get-tuple-element.67.tile.refs_0_, ...), custom_call_target="tpu_custom_call" | custom-call | flops 9200000000 | bytes 28800000 | tf_op jit(solution)/shard_map/pallas_call | solution.py:24
  153.8 0.7 collective-permute-start.18
  154.5 5.7 %collective-permute-done.18.pack.refs_2_ = f32[2,16,8,256]{3,2,1,0:T(8,128)S(1)} collective-permute-done((f32[2,16,8,256]{3,2,1,0:T(8,128)S(1)}, f32[2,16,8,256]{3,2,1,0:T(8,128)S(1)}, u32[]{:S(2)}, u32[]{:S(2)}) %collective-permute-start.18) | collective-permute-done | bytes 262176 | tf_op jit(solution)/shard_map/ppermute | solution.py:117
  160.3 5.3 %collective-permute-start.19 = (f32[2,18,8,256]{3,2,1,0:T(8,128)S(1)}, f32[2,18,8,256]{3,2,1,0:T(8,128)S(1)}, u32[]{:S(2)}, u32[]{:S(2)}) collective-permute-start(f32[2,18,8,256]{3,2,1,0:T(8,128)S(1)} %get-tuple-element.98), channel_id=1, source_target_pairs={{0,2},{2,4},{4,6},{1,3},{3,5},{5,7},{8,10},{10,12},{12,14},{9,11},... | collective-permute-start | bytes 884744 | tf_op jit(solution)/shard_map/ppermute | solution.py:124
  165.7 1.3 collective-permute-start.20
  167.0 2.6 %collective-permute-done.20.refs_1_ = f32[2,18,8,256]{3,2,1,0:T(8,128)S(1)} collective-permute-done((f32[2,18,8,256]{3,2,1,0:T(8,128)S(1)}, f32[2,18,8,256]{3,2,1,0:T(8,128)S(1)}, u32[]{:S(2)}, u32[]{:S(2)}) %collective-permute-start.20) | collective-permute-done | bytes 294944 | tf_op jit(solution)/shard_map/ppermute | solution.py:124
  169.6 12.8 %shard_map.73.second = f32[2,32,32,256]{3,2,1,0:T(8,128)S(1)} custom-call(s32[2]{0:T(128)S(1)} %copy-done.6, f32[7,40,40,256]{3,2,1,0:T(8,128)S(1)} %get-tuple-element.58.coef, f32[2,32,32,256]{3,2,1,0:T(8,128)S(1)} %get-tuple-element.94.tile, f32[2,18,8,256]{3,2,1,0:T(8,128)S(1)} %collective-permute-done.19.refs_0_, ...), custom_call_target="tpu_custom_call" | custom-call | flops 9200000000 | bytes 28800000 | tf_op jit(solution)/shard_map/pallas_call | solution.py:24
  182.4 3.7 %collective-permute-done.22.refs_2_ = f32[2,32,32,256]{3,2,1,0:T(8,128)S(1)} collective-permute-done((f32[2,32,32,256]{3,2,1,0:T(8,128)S(1)}, f32[2,32,32,256]{3,2,1,0:T(8,128)S(1)}, u32[]{:S(2)}, u32[]{:S(2)}) %collective-permute-start.22) | collective-permute-done | bytes 2097184 | tf_op jit(solution)/shard_map/ppermute | solution.py:536
  186.1 3.0 %shard_map.74 = f32[8,128]{1,0:T(8,128)S(1)} custom-call(s32[2]{0:T(128)S(1)} %copy-done.6, f32[2,32,32,256]{3,2,1,0:T(8,128)S(1)} %shard_map.73.second, f32[2,32,32,256]{3,2,1,0:T(8,128)S(1)} %get-tuple-element.67.tile.refs_0_, f32[2,32,32,256]{3,2,1,0:T(8,128)S(1)} %shard_map.69.refs_1_, f32[2,32,32,256]{3,2,1,0:T(8,128)S(1)} %collective-permute-done.22.refs_2_, ...), custom_call_target="tpu_custom_call" | custom-call | flops 4600000000 | bytes 14400000 | tf_op jit(solution)/shard_map/pallas_call | solution.py:24
  189.1 0.1 collective-permute-start.25
  189.2 3.0 %collective-permute-start.24 = (f32[8,128]{1,0:T(8,128)S(1)}, f32[8,128]{1,0:T(8,128)S(1)}, u32[]{:S(2)}, u32[]{:S(2)}) collective-permute-start(f32[8,128]{1,0:T(8,128)S(1)} %shard_map.74), channel_id=1, source_target_pairs={{0,4},{2,6},{4,0},{6,2},{1,5},{3,7},{5,1},{7,3},{8,12},{10,14},{12... | collective-permute-start | bytes 12296 | tf_op jit(solution)/shard_map/ppermute | solution.py:475
  192.2 1.6 collective-permute-done.24
  193.8 0.7 collective-permute-start.26
  194.5 3.0 %collective-permute-done.26 = f32[8,128]{1,0:T(8,128)S(1)} collective-permute-done((f32[8,128]{1,0:T(8,128)S(1)}, f32[8,128]{1,0:T(8,128)S(1)}, u32[]{:S(2)}, u32[]{:S(2)}) %collective-permute-start.26) | collective-permute-done | bytes 4128 | tf_op jit(solution)/shard_map/ppermute | solution.py:475
  197.5 1.2 collective-permute-start.29
  198.7 1.7 collective-permute-start.28
  200.5 1.4 collective-permute-start.27
  201.9 1.0 collective-permute-done.29
  202.9 0.3 collective-permute-done.28
  203.2 0.8 collective-permute-done.27
  204.1 4.1 %shard_map.75 = (f32[2,32,32,256]{3,2,1,0:T(8,128)}, f32[8,8]{1,0:T(8,128)}) custom-call(s32[2]{0:T(128)S(1)} %copy-done.6, f32[8,128]{1,0:T(8,128)S(1)} %add_add_fusion.inner, f32[2,32,32,256]{3,2,1,0:T(8,128)S(1)} %get-tuple-element.67.tile.refs_0_, f32[2,32,32,256]{3,2,1,0:T(8,128)S(1)} %shard_map.69.refs_1_, ...), custom_call_target="tpu_custom_call" | custom-call | flops 5750000128 | bytes 18000000 | tf_op jit(solution)/shard_map/pallas_call | solution.py:24
  (33 shorter events, 0.3 us)
Async XLA Ops:
  1.3 3.2 %copy-start.1 = (f32[2,32,32,256]{3,2,1,0:T(8,128)S(1)}, f32[2,32,32,256]{3,2,1,0:T(8,128)}, u32[]{:S(2)}) copy-start(f32[2,32,32,256]{3,2,1,0:T(8,128)} %probes.1) | copy-start | bytes 6291460
  4.5 26.0 %copy-start.7 = (f32[6,2,8,256]{3,2,1,0:T(8,128)S(1)}, f32[6,2,8,256]{3,2,1,0:T(8,128)}, u32[]{:S(2)}) copy-start(f32[6,2,8,256]{3,2,1,0:T(8,128)} %get-tuple-element.57) | copy-start | bytes 294916
  4.5 32.0 %copy-start = (f32[3,32,32,256]{3,2,1,0:T(8,128)S(1)}, f32[3,32,32,256]{3,2,1,0:T(8,128)}, u32[]{:S(2)}) copy-start(f32[3,32,32,256]{3,2,1,0:T(8,128)} %velocity.1) | copy-start | bytes 9437188
  4.5 32.0 %copy-start.2 = (f32[2,32,32,256]{3,2,1,0:T(8,128)S(1)}, f32[2,32,32,256]{3,2,1,0:T(8,128)}, u32[]{:S(2)}) copy-start(f32[2,32,32,256]{3,2,1,0:T(8,128)} %probes.1) | copy-start | bytes 6291460
  4.6 32.0 %copy-start.6 = (s32[2]{0:T(128)S(1)}, s32[2]{0:T(128)}, u32[]{:S(2)}) copy-start(s32[2]{0:T(128)} %pad_add_fusion.scalars) | copy-start | bytes 28
  4.6 50.1 %collective-permute-start.5 = (f32[2,32,32,256]{3,2,1,0:T(8,128)S(1)}, f32[2,32,32,256]{3,2,1,0:T(8,128)}, u32[]{:S(2)}, u32[]{:S(2)}) collective-permute-start(f32[2,32,32,256]{3,2,1,0:T(8,128)S(1)} %copy-done.1), channel_id=1, source_target_pairs={{0,8},{8,16},{16,24},{1,9},{9,17},{17,25},{2,10},{10,18},{18,26},{... | collective-permute-start | bytes 6291464 | tf_op jit(solution)/shard_map/ppermute | solution.py:536
  11.1 25.4 %collective-permute-start.2 = (f32[6,16,8,256]{3,2,1,0:T(8,128)}, f32[6,16,8,256]{3,2,1,0:T(8,128)S(1)}, u32[]{:S(2)}, u32[]{:S(2)}) collective-permute-start(f32[6,16,8,256]{3,2,1,0:T(8,128)} %get-tuple-element.55), channel_id=1, source_target_pairs={{0,1},{1,0},{2,3},{3,2},{4,5},{5,4},{6,7},{7,6},{8,9},{9,8},{10,11... | collective-permute-start | bytes 2359304 | tf_op jit(solution)/shard_map/ppermute | solution.py:117
  15.3 21.2 %collective-permute-start = (f32[6,4,32,256]{3,2,1,0:T(8,128)}, f32[6,4,32,256]{3,2,1,0:T(8,128)S(1)}, u32[]{:S(2)}, u32[]{:S(2)}) collective-permute-start(f32[6,4,32,256]{3,2,1,0:T(8,128)} %get-tuple-element.52), channel_id=1, source_target_pairs={{0,2},{2,4},{4,6},{1,3},{3,5},{5,7},{8,10},{10,12},{12,14},{9,11},... | collective-permute-start | bytes 2359304 | tf_op jit(solution)/shard_map/ppermute | solution.py:125
  16.7 19.9 %collective-permute-start.1 = (f32[6,4,32,256]{3,2,1,0:T(8,128)}, f32[6,4,32,256]{3,2,1,0:T(8,128)S(1)}, u32[]{:S(2)}, u32[]{:S(2)}) collective-permute-start(f32[6,4,32,256]{3,2,1,0:T(8,128)} %get-tuple-element.53), channel_id=1, source_target_pairs={{2,0},{4,2},{6,4},{3,1},{5,3},{7,5},{10,8},{12,10},{14,12},{11,9},... | collective-permute-start | bytes 2359304 | tf_op jit(solution)/shard_map/ppermute | solution.py:126
  18.0 12.5 %collective-permute-start.3 = (f32[6,2,8,256]{3,2,1,0:T(8,128)}, f32[6,2,8,256]{3,2,1,0:T(8,128)S(1)}, u32[]{:S(2)}, u32[]{:S(2)}) collective-permute-start(f32[6,2,8,256]{3,2,1,0:T(8,128)} %get-tuple-element.56), channel_id=1, source_target_pairs={{0,3},{1,2},{2,5},{3,4},{4,7},{5,6},{8,11},{9,10},{10,13},{11,12},... | collective-permute-start | bytes 294920 | tf_op jit(solution)/shard_map/ppermute | solution.py:117
  30.5 6.0 %collective-permute-start.4 = (f32[6,2,8,256]{3,2,1,0:T(8,128)S(1)}, f32[6,2,8,256]{3,2,1,0:T(8,128)S(1)}, u32[]{:S(2)}, u32[]{:S(2)}) collective-permute-start(f32[6,2,8,256]{3,2,1,0:T(8,128)S(1)} %copy-done.7), channel_id=1, source_target_pairs={{2,1},{3,0},{4,3},{5,2},{6,5},{7,4},{10,9},{11,8},{12,11},{13,10},... | collective-permute-start | bytes 294920 | tf_op jit(solution)/shard_map/ppermute | solution.py:117
  36.5 1.2 copy-start.3
  37.8 1.2 copy-start.4
  53.6 8.8 %collective-permute-start.6 = (f32[2,16,8,256]{3,2,1,0:T(8,128)S(1)}, f32[2,16,8,256]{3,2,1,0:T(8,128)S(1)}, u32[]{:S(2)}, u32[]{:S(2)}) collective-permute-start(f32[2,16,8,256]{3,2,1,0:T(8,128)S(1)} %get-tuple-element.64), channel_id=1, source_target_pairs={{0,1},{1,0},{2,3},{3,2},{4,5},{5,4},{6,7},{7,6},{8,9},{9,8},{10,11... | collective-permute-start | bytes 786440 | tf_op jit(solution)/shard_map/ppermute | solution.py:117
  56.3 11.7 %collective-permute-start.9 = (f32[2,16,8,256]{3,2,1,0:T(8,128)S(1)}, f32[2,16,8,256]{3,2,1,0:T(8,128)S(1)}, u32[]{:S(2)}, u32[]{:S(2)}) collective-permute-start(f32[2,16,8,256]{3,2,1,0:T(8,128)S(1)} %shard_map.65), channel_id=1, source_target_pairs={{0,1},{1,0},{2,3},{3,2},{4,5},{5,4},{6,7},{7,6},{8,9},{9,8},{10,11... | collective-permute-start | bytes 786440 | tf_op jit(solution)/shard_map/ppermute | solution.py:117
  62.4 11.3 %collective-permute-start.7 = (f32[2,18,8,256]{3,2,1,0:T(8,128)S(1)}, f32[2,18,8,256]{3,2,1,0:T(8,128)S(1)}, u32[]{:S(2)}, u32[]{:S(2)}) collective-permute-start(f32[2,18,8,256]{3,2,1,0:T(8,128)S(1)} %get-tuple-element.65), channel_id=1, source_target_pairs={{0,2},{2,4},{4,6},{1,3},{3,5},{5,7},{8,10},{10,12},{12,14},{9,11},... | collective-permute-start | bytes 884744 | tf_op jit(solution)/shard_map/ppermute | solution.py:124
  65.4 8.3 %collective-permute-start.8 = (f32[2,18,8,256]{3,2,1,0:T(8,128)S(1)}, f32[2,18,8,256]{3,2,1,0:T(8,128)S(1)}, u32[]{:S(2)}, u32[]{:S(2)}) collective-permute-start(f32[2,18,8,256]{3,2,1,0:T(8,128)S(1)} %get-tuple-element.66), channel_id=1, source_target_pairs={{2,0},{4,2},{6,4},{3,1},{5,3},{7,5},{10,8},{12,10},{14,12},{11,9},... | collective-permute-start | bytes 884744 | tf_op jit(solution)/shard_map/ppermute | solution.py:124
  68.0 20.1 %collective-permute-start.10 = (f32[2,18,8,256]{3,2,1,0:T(8,128)S(1)}, f32[2,18,8,256]{3,2,1,0:T(8,128)S(1)}, u32[]{:S(2)}, u32[]{:S(2)}) collective-permute-start(f32[2,18,8,256]{3,2,1,0:T(8,128)S(1)} %get-tuple-element.74), channel_id=1, source_target_pairs={{0,2},{2,4},{4,6},{1,3},{3,5},{5,7},{8,10},{10,12},{12,14},{9,11},... | collective-permute-start | bytes 884744 | tf_op jit(solution)/shard_map/ppermute | solution.py:124
  72.3 15.7 %collective-permute-start.11 = (f32[2,18,8,256]{3,2,1,0:T(8,128)S(1)}, f32[2,18,8,256]{3,2,1,0:T(8,128)S(1)}, u32[]{:S(2)}, u32[]{:S(2)}) collective-permute-start(f32[2,18,8,256]{3,2,1,0:T(8,128)S(1)} %get-tuple-element.75), channel_id=1, source_target_pairs={{2,0},{4,2},{6,4},{3,1},{5,3},{7,5},{10,8},{12,10},{14,12},{11,9},... | collective-permute-start | bytes 884744 | tf_op jit(solution)/shard_map/ppermute | solution.py:124
  73.7 14.4 %copy-start.5 = (f32[32,32,256]{2,1,0:T(8,128)S(1)}, f32[32,32,256]{2,1,0:T(8,128)}, u32[]{:S(2)}) copy-start(f32[32,32,256]{2,1,0:T(8,128)} %refs_0_.3) | copy-start | bytes 3145732
  86.6 52.5 %collective-permute-start.21 = (f32[2,32,32,256]{3,2,1,0:T(8,128)S(1)}, f32[2,32,32,256]{3,2,1,0:T(8,128)S(1)}, u32[]{:S(2)}, u32[]{:S(2)}) collective-permute-start(f32[2,32,32,256]{3,2,1,0:T(8,128)S(1)} %get-tuple-element.67.tile.refs_0_), channel_id=1, source_target_pairs={{0,24},{1,25},{2,26},{3,27},{4,28},{5,29},{6,30},{7,31}} | collective-permute-start | bytes 6291464 | tf_op jit(solution)/shard_map/ppermute | solution.py:536
  101.9 7.8 %collective-permute-start.13 = (f32[2,16,8,256]{3,2,1,0:T(8,128)S(1)}, f32[2,16,8,256]{3,2,1,0:T(8,128)S(1)}, u32[]{:S(2)}, u32[]{:S(2)}) collective-permute-start(f32[2,16,8,256]{3,2,1,0:T(8,128)S(1)} %get-tuple-element.86), channel_id=1, source_target_pairs={{0,1},{1,0},{2,3},{3,2},{4,5},{5,4},{6,7},{7,6},{8,9},{9,8},{10,11... | collective-permute-start | bytes 786440 | tf_op jit(solution)/shard_map/ppermute | solution.py:117
  109.7 5.2 %collective-permute-start.14 = (f32[2,18,8,256]{3,2,1,0:T(8,128)S(1)}, f32[2,18,8,256]{3,2,1,0:T(8,128)S(1)}, u32[]{:S(2)}, u32[]{:S(2)}) collective-permute-start(f32[2,18,8,256]{3,2,1,0:T(8,128)S(1)} %get-tuple-element.87), channel_id=1, source_target_pairs={{0,2},{2,4},{4,6},{1,3},{3,5},{5,7},{8,10},{10,12},{12,14},{9,11},... | collective-permute-start | bytes 884744 | tf_op jit(solution)/shard_map/ppermute | solution.py:124
  112.9 5.0 %collective-permute-start.15 = (f32[2,18,8,256]{3,2,1,0:T(8,128)S(1)}, f32[2,18,8,256]{3,2,1,0:T(8,128)S(1)}, u32[]{:S(2)}, u32[]{:S(2)}) collective-permute-start(f32[2,18,8,256]{3,2,1,0:T(8,128)S(1)} %get-tuple-element.88), channel_id=1, source_target_pairs={{2,0},{4,2},{6,4},{3,1},{5,3},{7,5},{10,8},{12,10},{14,12},{11,9},... | collective-permute-start | bytes 884744 | tf_op jit(solution)/shard_map/ppermute | solution.py:124
  114.2 16.5 %collective-permute-start.12 = (f32[2,16,8,256]{3,2,1,0:T(8,128)S(1)}, f32[2,16,8,256]{3,2,1,0:T(8,128)S(1)}, u32[]{:S(2)}, u32[]{:S(2)}) collective-permute-start(f32[2,16,8,256]{3,2,1,0:T(8,128)S(1)} %get-tuple-element.82), channel_id=1, source_target_pairs={{0,1},{1,0},{2,3},{3,2},{4,5},{5,4},{6,7},{7,6},{8,9},{9,8},{10,11... | collective-permute-start | bytes 786440 | tf_op jit(solution)/shard_map/ppermute | solution.py:117
  130.8 9.7 %collective-permute-start.16 = (f32[2,18,8,256]{3,2,1,0:T(8,128)S(1)}, f32[2,18,8,256]{3,2,1,0:T(8,128)S(1)}, u32[]{:S(2)}, u32[]{:S(2)}) collective-permute-start(f32[2,18,8,256]{3,2,1,0:T(8,128)S(1)} %get-tuple-element.92), channel_id=1, source_target_pairs={{0,2},{2,4},{4,6},{1,3},{3,5},{5,7},{8,10},{10,12},{12,14},{9,11},... | collective-permute-start | bytes 884744 | tf_op jit(solution)/shard_map/ppermute | solution.py:124
  137.8 3.5 %collective-permute-start.17 = (f32[2,18,8,256]{3,2,1,0:T(8,128)S(1)}, f32[2,18,8,256]{3,2,1,0:T(8,128)S(1)}, u32[]{:S(2)}, u32[]{:S(2)}) collective-permute-start(f32[2,18,8,256]{3,2,1,0:T(8,128)S(1)} %get-tuple-element.93), channel_id=1, source_target_pairs={{2,0},{4,2},{6,4},{3,1},{5,3},{7,5},{10,8},{12,10},{14,12},{11,9},... | collective-permute-start | bytes 884744 | tf_op jit(solution)/shard_map/ppermute | solution.py:124
  139.1 46.9 %collective-permute-start.22 = (f32[2,32,32,256]{3,2,1,0:T(8,128)S(1)}, f32[2,32,32,256]{3,2,1,0:T(8,128)S(1)}, u32[]{:S(2)}, u32[]{:S(2)}) collective-permute-start(f32[2,32,32,256]{3,2,1,0:T(8,128)S(1)} %shard_map.69.refs_1_), channel_id=1, source_target_pairs={{0,8},{8,16},{16,24},{1,9},{9,17},{17,25},{2,10},{10,18},{18,26},{... | collective-permute-start | bytes 6291464 | tf_op jit(solution)/shard_map/ppermute | solution.py:536
  153.8 6.4 %collective-permute-start.18 = (f32[2,16,8,256]{3,2,1,0:T(8,128)S(1)}, f32[2,16,8,256]{3,2,1,0:T(8,128)S(1)}, u32[]{:S(2)}, u32[]{:S(2)}) collective-permute-start(f32[2,16,8,256]{3,2,1,0:T(8,128)S(1)} %get-tuple-element.97), channel_id=1, source_target_pairs={{0,1},{1,0},{2,3},{3,2},{4,5},{5,4},{6,7},{7,6},{8,9},{9,8},{10,11... | collective-permute-start | bytes 786440 | tf_op jit(solution)/shard_map/ppermute | solution.py:117
  160.3 6.6 %collective-permute-start.19 = (f32[2,18,8,256]{3,2,1,0:T(8,128)S(1)}, f32[2,18,8,256]{3,2,1,0:T(8,128)S(1)}, u32[]{:S(2)}, u32[]{:S(2)}) collective-permute-start(f32[2,18,8,256]{3,2,1,0:T(8,128)S(1)} %get-tuple-element.98), channel_id=1, source_target_pairs={{0,2},{2,4},{4,6},{1,3},{3,5},{5,7},{8,10},{10,12},{12,14},{9,11},... | collective-permute-start | bytes 884744 | tf_op jit(solution)/shard_map/ppermute | solution.py:124
  165.7 4.0 %collective-permute-start.20 = (f32[2,18,8,256]{3,2,1,0:T(8,128)S(1)}, f32[2,18,8,256]{3,2,1,0:T(8,128)S(1)}, u32[]{:S(2)}, u32[]{:S(2)}) collective-permute-start(f32[2,18,8,256]{3,2,1,0:T(8,128)S(1)} %get-tuple-element.99), channel_id=1, source_target_pairs={{2,0},{4,2},{6,4},{3,1},{5,3},{7,5},{10,8},{12,10},{14,12},{11,9},... | collective-permute-start | bytes 884744 | tf_op jit(solution)/shard_map/ppermute | solution.py:124
  189.1 3.1 %collective-permute-start.25 = (f32[8,128]{1,0:T(8,128)S(1)}, f32[8,128]{1,0:T(8,128)S(1)}, u32[]{:S(2)}, u32[]{:S(2)}) collective-permute-start(f32[8,128]{1,0:T(8,128)S(1)} %shard_map.74), channel_id=1, source_target_pairs={{0,6},{2,4},{4,2},{6,0},{1,7},{3,5},{5,3},{7,1},{8,14},{10,12},{12... | collective-permute-start | bytes 12296 | tf_op jit(solution)/shard_map/ppermute | solution.py:475
  189.2 4.6 %collective-permute-start.24 = (f32[8,128]{1,0:T(8,128)S(1)}, f32[8,128]{1,0:T(8,128)S(1)}, u32[]{:S(2)}, u32[]{:S(2)}) collective-permute-start(f32[8,128]{1,0:T(8,128)S(1)} %shard_map.74), channel_id=1, source_target_pairs={{0,4},{2,6},{4,0},{6,2},{1,5},{3,7},{5,1},{7,3},{8,12},{10,14},{12... | collective-permute-start | bytes 12296 | tf_op jit(solution)/shard_map/ppermute | solution.py:475
  192.2 1.6 collective-permute-start.23
  193.8 3.7 %collective-permute-start.26 = (f32[8,128]{1,0:T(8,128)S(1)}, f32[8,128]{1,0:T(8,128)S(1)}, u32[]{:S(2)}, u32[]{:S(2)}) collective-permute-start(f32[8,128]{1,0:T(8,128)S(1)} %add_add_fusion.1), channel_id=1, source_target_pairs={{0,1},{1,0},{2,3},{3,2},{4,5},{5,4},{6,7},{7,6},{8,9},{9,8},{10,11... | collective-permute-start | bytes 12296 | tf_op jit(solution)/shard_map/ppermute | solution.py:475
  197.5 5.4 %collective-permute-start.29 = (f32[8,128]{1,0:T(8,128)S(1)}, f32[8,128]{1,0:T(8,128)S(1)}, u32[]{:S(2)}, u32[]{:S(2)}) collective-permute-start(f32[8,128]{1,0:T(8,128)S(1)} %add.24), channel_id=1, source_target_pairs={{0,24},{8,16},{16,8},{24,0},{1,25},{9,17},{17,9},{25,1},{2,26},{10... | collective-permute-start | bytes 12296 | tf_op jit(solution)/shard_map/ppermute | solution.py:475
  198.7 4.5 %collective-permute-start.28 = (f32[8,128]{1,0:T(8,128)S(1)}, f32[8,128]{1,0:T(8,128)S(1)}, u32[]{:S(2)}, u32[]{:S(2)}) collective-permute-start(f32[8,128]{1,0:T(8,128)S(1)} %add.24), channel_id=1, source_target_pairs={{0,16},{8,24},{16,0},{24,8},{1,17},{9,25},{17,1},{25,9},{2,18},{10... | collective-permute-start | bytes 12296 | tf_op jit(solution)/shard_map/ppermute | solution.py:475
  200.5 3.6 %collective-permute-start.27 = (f32[8,128]{1,0:T(8,128)S(1)}, f32[8,128]{1,0:T(8,128)S(1)}, u32[]{:S(2)}, u32[]{:S(2)}) collective-permute-start(f32[8,128]{1,0:T(8,128)S(1)} %add.24), channel_id=1, source_target_pairs={{0,8},{8,0},{16,24},{24,16},{1,9},{9,1},{17,25},{25,17},{2,10},{10... | collective-permute-start | bytes 12296 | tf_op jit(solution)/shard_map/ppermute | solution.py:475

commit v8 on v7

--- a/solution.py
+++ b/solution.py
@@ -526,7 +526,7 @@
             [pltpu.SemaphoreType.DMA((2 * number,))],
             sources,
             2.0,
-            mib,
+            min(mib, 12),
             anywhere=range(len(sources)),
             scalars=False,
         )
@@ -549,14 +549,14 @@
         anywhere=(1, 2, 3, 5, 6),
     )
 
-    def model(field, received, adjoint, last=False):
+    def model(field, received, adjoint, last=False, micros=8.0):
         ins = [where, coef, field] + ([] if adjoint else [obs_weight])
         return kernel_call(
             functools.partial(next_kernel, len(received), adjoint),
             [tile] + ([] if last else strips2),
             scratch(3 * group),
             ins + received,
-            8.0,
+            micros,
             14,
             anywhere=(2, len(ins), len(ins) + 1) if both else (2,),
         )
@@ -574,8 +574,8 @@
     passed = [images, images_next, right(shifting, 1)] + far
 
     received = exchange(strips, after=images_next)
-    halfway, *strips = model(images, received, False)
-    (second,) = model(halfway, exchange(strips), True, True)
+    halfway, *strips = model(images, received, False, micros=5.0)
+    (second,) = model(halfway, exchange(strips), True, True, micros=5.0)
 
     (partial,) = kernel_call(
         dots_kernel,

time: 209 us -> 210 us (level)
  waiting for transfers between devices: 47.2 us -> 54.5 us
  Pallas kernels: 95.4 us -> 90.9 us
  local copies, waits for them, and re-layouts: 2.48 us -> 0.03 us
    ppermute x10, starting transfers between devices: 29.3 us -> 22.8 us  [exchange(): return [lax.ppermute(hi, 'sx', up), lax.ppermute(lo, 'sx', down), pack]]
    ppermute x7, starting transfers between devices: 8.19 us -> 13.8 us  [all_sum(): lax.ppermute(value, axis, [(i, i ^ bits) for i in range(devices)])]
    pallas_call x17, Pallas kernels: 95.4 us -> 90.9 us  [kernel_call(): pl.pallas_call(body, out_shape=outs, in_specs=specs, out_specs=[spec(n, o...]
    ppermute x3, waiting for transfers between devices: 4.18 us -> 8.2 us  [right(): lax.ppermute(value, 'probe', [(i, i + hops) for i in range(groups - hops)])]
    ppermute x10, waiting for transfers between devices: 6.42 us -> 9.4 us  [exchange(): return [lax.ppermute(hi, 'sx', up), lax.ppermute(lo, 'sx', down), pack]]
    unnamed x16 -> x14, local copies, waits for them, and re-layouts: 2.48 us -> 0.03 us
    ppermute x3, starting transfers between devices: 9.38 us -> 11.6 us  [right(): lax.ppermute(value, 'probe', [(i, i + hops) for i in range(groups - hops)])]
  transfers between devices with their start and end apart: 30 -> 30, of which waited for: 16 -> 15; matrix products, arithmetic and copies ran while one was open for 0% -> 0% of each run, Pallas kernels for 41% -> 38%
where the time goes in v8:
time: 210 us
  Pallas kernels  90.9 us (43%)
  starting transfers between devices  62.8 us (30%)
  waiting for transfers between devices  54.5 us (26%)
    pallas_call x17, Pallas kernels, kernel_call(): pl.pallas_call(body, out_shape=outs, in_specs=specs, out_specs=[spec(n, o...  90.9 us
    ppermute x8, waiting for transfers between devices, moved(): return lax.ppermute(value, ('sx', 'sy'), pairs)  29.5 us
    ppermute x10, starting transfers between devices, exchange(): return [lax.ppermute(hi, 'sx', up), lax.ppermute(lo, 'sx', down), pack]  22.8 us
    ppermute x7, starting transfers between devices, all_sum(): lax.ppermute(value, axis, [(i, i ^ bits) for i in range(devices)])  13.8 us
    ppermute x8, starting transfers between devices, moved(): return lax.ppermute(value, ('sx', 'sy'), pairs)  11.9 us
    ppermute x3, starting transfers between devices, right(): lax.ppermute(value, 'probe', [(i, i + hops) for i in range(groups - hops)])  11.6 us
    ppermute x10, waiting for transfers between devices, exchange(): return [lax.ppermute(hi, 'sx', up), lax.ppermute(lo, 'sx', down), pack]  9.4 us
    ppermute x3, waiting for transfers between devices, right(): lax.ppermute(value, 'probe', [(i, i + hops) for i in range(groups - hops)])  8.2 us
  transfers between devices with their start and end apart: 30, of which 15 were waited for; matrix products, arithmetic and copies ran while one was open for 0% of the time, Pallas kernels for 38%

profile of v8, /device:TPU:0, one launch (start us, length us, event | category | flops | bytes accessed | tf_op | source)
XLA Modules:
  0.0 209.9 jit_solution(9387048002216088094)
XLA Ops:
  0.6 0.6 pad_add_fusion.scalars
  1.2 3.5 %shard_map.60 = (f32[6,16,8,256]{3,2,1,0:T(8,128)}, f32[6,2,8,256]{3,2,1,0:T(8,128)}, f32[6,2,8,256]{3,2,1,0:T(8,128)}) custom-call(s32[2]{0:T(128)} %pad_add_fusion.scalars, f32[1,32,32,256]{3,2,1,0:T(8,128)} %bitcast.3, f32[3,32,32,256]{3,2,1,0:T(8,128)} %velocity.1, f32[2,32,32,256]{3,2,1,0:T(8,128)} %probes.1), custom_call_target="tpu_custom_call" | custom-call | flops 2300000000 | bytes 7200000 | tf_op jit(solution)/shard_map/pallas_call | solution.py:24
  4.8 0.0 copy-start.3
  4.8 5.2 %collective-permute-start.5 = (f32[2,32,32,256]{3,2,1,0:T(8,128)S(1)}, f32[2,32,32,256]{3,2,1,0:T(8,128)S(1)}, u32[]{:S(2)}, u32[]{:S(2)}) collective-permute-start(f32[2,32,32,256]{3,2,1,0:T(8,128)S(1)} %copy-done.1), channel_id=1, source_target_pairs={{0,8},{8,16},{16,24},{1,9},{9,17},{17,25},{2,10},{10,18},{18,26},{... | collective-permute-start | bytes 6291464 | tf_op jit(solution)/shard_map/ppermute | solution.py:536
  10.0 1.6 collective-permute-start.2
  11.6 2.1 %shard_map.59 = (f32[6,4,32,256]{3,2,1,0:T(8,128)S(1)}, f32[6,4,32,256]{3,2,1,0:T(8,128)S(1)}) custom-call(f32[1,32,32,256]{3,2,1,0:T(8,128)S(1)} %bitcast.4, f32[3,32,32,256]{3,2,1,0:T(8,128)S(1)} %copy-done, f32[2,32,32,256]{3,2,1,0:T(8,128)S(1)} %copy-done.1), custom_call_target="tpu_custom_call" | custom-call | flops 2300000000 | bytes 7200000 | tf_op jit(solution)/shard_map/pallas_call | solution.py:24
  13.7 1.3 collective-permute-start
  15.1 1.3 collective-permute-start.1
  16.4 4.8 %collective-permute-start.3 = (f32[6,2,8,256]{3,2,1,0:T(8,128)S(1)}, f32[6,2,8,256]{3,2,1,0:T(8,128)S(1)}, u32[]{:S(2)}, u32[]{:S(2)}) collective-permute-start(f32[6,2,8,256]{3,2,1,0:T(8,128)S(1)} %copy-done.6), channel_id=1, source_target_pairs={{0,3},{1,2},{2,5},{3,4},{4,7},{5,6},{8,11},{9,10},{10,13},{11,12},... | collective-permute-start | bytes 294920 | tf_op jit(solution)/shard_map/ppermute | solution.py:117
  21.2 8.1 %collective-permute-done.3.refs_3_ = f32[6,2,8,256]{3,2,1,0:T(8,128)S(1)} collective-permute-done((f32[6,2,8,256]{3,2,1,0:T(8,128)S(1)}, f32[6,2,8,256]{3,2,1,0:T(8,128)S(1)}, u32[]{:S(2)}, u32[]{:S(2)}) %collective-permute-start.3) | collective-permute-done | bytes 98336 | tf_op jit(solution)/shard_map/ppermute | solution.py:117
  29.4 1.3 collective-permute-start.4
  30.7 4.8 %collective-permute-done.4.refs_4_ = f32[6,2,8,256]{3,2,1,0:T(8,128)S(1)} collective-permute-done((f32[6,2,8,256]{3,2,1,0:T(8,128)S(1)}, f32[6,2,8,256]{3,2,1,0:T(8,128)S(1)}, u32[]{:S(2)}, u32[]{:S(2)}) %collective-permute-start.4) | collective-permute-done | bytes 98336 | tf_op jit(solution)/shard_map/ppermute | solution.py:117
  35.5 0.0 collective-permute-done.1.refs_1_
  35.5 14.3 %shard_map.61 = (f32[7,40,40,256]{3,2,1,0:T(8,128)S(1)}, f32[2,32,32,256]{3,2,1,0:T(8,128)S(1)}, f32[2,4,32,256]{3,2,1,0:T(8,128)S(1)}, f32[2,4,32,256]{3,2,1,0:T(8,128)S(1)}, f32[2,16,8,256]{3,2,1,0:T(8,128)S(1)}) custom-call(s32[2]{0:T(128)S(1)} %copy-done.4, f32[1,32,32,256]{3,2,1,0:T(8,128)S(1)} %bitcast.5, f32[3,32,32,256]{3,2,1,0:T(8,128)S(1)} %copy-done, ...), custom_call_target="tpu_custom_call" | custom-call | flops 4600000000 | bytes 14400000 | tf_op jit(solution)/shard_map/pallas_call | solution.py:24
  49.8 0.6 collective-permute-start.6
  50.4 4.3 %collective-permute-done.5.refs_0_.tile = f32[2,32,32,256]{3,2,1,0:T(8,128)S(1)} collective-permute-done((f32[2,32,32,256]{3,2,1,0:T(8,128)S(1)}, f32[2,32,32,256]{3,2,1,0:T(8,128)S(1)}, u32[]{:S(2)}, u32[]{:S(2)}) %collective-permute-start.5) | collective-permute-done | bytes 2097184 | tf_op jit(solution)/shard_map/ppermute | solution.py:536
  54.7 0.7 shard_map.65
  55.4 1.6 collective-permute-start.9
  57.0 1.6 collective-permute-done.6.pack.refs_2_
  58.6 2.2 %collective-permute-start.7 = (f32[2,18,8,256]{3,2,1,0:T(8,128)S(1)}, f32[2,18,8,256]{3,2,1,0:T(8,128)S(1)}, u32[]{:S(2)}, u32[]{:S(2)}) collective-permute-start(f32[2,18,8,256]{3,2,1,0:T(8,128)S(1)} %get-tuple-element.65), channel_id=1, source_target_pairs={{0,2},{2,4},{4,6},{1,3},{3,5},{5,7},{8,10},{10,12},{12,14},{9,11},... | collective-permute-start | bytes 884744 | tf_op jit(solution)/shard_map/ppermute | solution.py:124
  60.9 1.3 collective-permute-start.8
  62.2 0.7 shard_map.64
  62.9 1.8 collective-permute-done.9.pack.refs_3_
  64.7 2.0 collective-permute-start.10
  66.7 1.3 collective-permute-start.11
  68.0 0.0 collective-permute-done.8.refs_1_
  68.1 12.6 %shard_map.63 = (f32[2,32,32,256]{3,2,1,0:T(8,128)S(1)}, f32[2,4,32,256]{3,2,1,0:T(8,128)S(1)}, f32[2,4,32,256]{3,2,1,0:T(8,128)S(1)}, f32[2,16,8,256]{3,2,1,0:T(8,128)S(1)}) custom-call(s32[2]{0:T(128)S(1)} %copy-done.4, f32[7,40,40,256]{3,2,1,0:T(8,128)S(1)} %get-tuple-element.58.coef, f32[2,32,32,256]{3,2,1,0:T(8,128)S(1)} %get-tuple-element.61.tile, ...), custom_call_target="tpu_custom_call" | custom-call | flops 9200000000 | bytes 28800000 | tf_op jit(solution)/shard_map/pallas_call | solution.py:24
  80.7 5.0 %collective-permute-start.21 = (f32[2,32,32,256]{3,2,1,0:T(8,128)S(1)}, f32[2,32,32,256]{3,2,1,0:T(8,128)S(1)}, u32[]{:S(2)}, u32[]{:S(2)}) collective-permute-start(f32[2,32,32,256]{3,2,1,0:T(8,128)S(1)} %get-tuple-element.67.tile.refs_0_), channel_id=1, source_target_pairs={{0,24},{1,25},{2,26},{3,27},{4,28},{5,29},{6,30},{7,31}} | collective-permute-start | bytes 6291464 | tf_op jit(solution)/shard_map/ppermute | solution.py:536
  85.7 0.0 collective-permute-done.11.refs_2_
  85.8 12.3 %shard_map.67 = (f32[2,32,32,256]{3,2,1,0:T(8,128)S(1)}, f32[2,4,32,256]{3,2,1,0:T(8,128)S(1)}, f32[2,4,32,256]{3,2,1,0:T(8,128)S(1)}, f32[2,16,8,256]{3,2,1,0:T(8,128)S(1)}) custom-call(s32[2]{0:T(128)S(1)} %copy-done.4, f32[7,40,40,256]{3,2,1,0:T(8,128)S(1)} %get-tuple-element.58.coef, f32[2,32,32,256]{3,2,1,0:T(8,128)S(1)} %collective-permute-done.5.refs_0_.tile, ...), custom_call_target="tpu_custom_call" | custom-call | flops 9200000000 | bytes 28800000 | tf_op jit(solution)/shard_map/pallas_call | solution.py:24
  98.1 0.6 collective-permute-start.13
  98.7 7.6 %collective-permute-done.13.pack.refs_2_ = f32[2,16,8,256]{3,2,1,0:T(8,128)S(1)} collective-permute-done((f32[2,16,8,256]{3,2,1,0:T(8,128)S(1)}, f32[2,16,8,256]{3,2,1,0:T(8,128)S(1)}, u32[]{:S(2)}, u32[]{:S(2)}) %collective-permute-start.13) | collective-permute-done | bytes 262176 | tf_op jit(solution)/shard_map/ppermute | solution.py:117
  106.3 2.9 %collective-permute-start.14 = (f32[2,18,8,256]{3,2,1,0:T(8,128)S(1)}, f32[2,18,8,256]{3,2,1,0:T(8,128)S(1)}, u32[]{:S(2)}, u32[]{:S(2)}) collective-permute-start(f32[2,18,8,256]{3,2,1,0:T(8,128)S(1)} %get-tuple-element.87), channel_id=1, source_target_pairs={{0,2},{2,4},{4,6},{1,3},{3,5},{5,7},{8,10},{10,12},{12,14},{9,11},... | collective-permute-start | bytes 884744 | tf_op jit(solution)/shard_map/ppermute | solution.py:124
  109.1 1.3 collective-permute-start.15
  110.4 0.6 collective-permute-start.12
  111.0 2.9 %collective-permute-done.15.refs_1_ = f32[2,18,8,256]{3,2,1,0:T(8,128)S(1)} collective-permute-done((f32[2,18,8,256]{3,2,1,0:T(8,128)S(1)}, f32[2,18,8,256]{3,2,1,0:T(8,128)S(1)}, u32[]{:S(2)}, u32[]{:S(2)}) %collective-permute-start.15) | collective-permute-done | bytes 294944 | tf_op jit(solution)/shard_map/ppermute | solution.py:124
  113.9 12.5 %shard_map.69.refs_1_ = f32[2,32,32,256]{3,2,1,0:T(8,128)S(1)} custom-call(s32[2]{0:T(128)S(1)} %copy-done.4, f32[7,40,40,256]{3,2,1,0:T(8,128)S(1)} %get-tuple-element.58.coef, f32[2,32,32,256]{3,2,1,0:T(8,128)S(1)} %get-tuple-element.83.tile, f32[2,18,8,256]{3,2,1,0:T(8,128)S(1)} %collective-permute-done.14.refs_0_, ...), custom_call_target="tpu_custom_call" | custom-call | flops 9200000000 | bytes 28800000 | tf_op jit(solution)/shard_map/pallas_call | solution.py:24
  126.4 3.8 %collective-permute-done.21.refs_3_ = f32[2,32,32,256]{3,2,1,0:T(8,128)S(1)} collective-permute-done((f32[2,32,32,256]{3,2,1,0:T(8,128)S(1)}, f32[2,32,32,256]{3,2,1,0:T(8,128)S(1)}, u32[]{:S(2)}, u32[]{:S(2)}) %collective-permute-start.21) | collective-permute-done | bytes 2097184 | tf_op jit(solution)/shard_map/ppermute | solution.py:536
  130.2 1.4 collective-permute-start.22
  131.7 3.5 %collective-permute-start.16 = (f32[2,18,8,256]{3,2,1,0:T(8,128)S(1)}, f32[2,18,8,256]{3,2,1,0:T(8,128)S(1)}, u32[]{:S(2)}, u32[]{:S(2)}) collective-permute-start(f32[2,18,8,256]{3,2,1,0:T(8,128)S(1)} %get-tuple-element.92), channel_id=1, source_target_pairs={{0,2},{2,4},{4,6},{1,3},{3,5},{5,7},{8,10},{10,12},{12,14},{9,11},... | collective-permute-start | bytes 884744 | tf_op jit(solution)/shard_map/ppermute | solution.py:124
  135.2 1.3 collective-permute-start.17
  136.5 3.8 %collective-permute-done.17.refs_2_ = f32[2,18,8,256]{3,2,1,0:T(8,128)S(1)} collective-permute-done((f32[2,18,8,256]{3,2,1,0:T(8,128)S(1)}, f32[2,18,8,256]{3,2,1,0:T(8,128)S(1)}, u32[]{:S(2)}, u32[]{:S(2)}) %collective-permute-start.17) | collective-permute-done | bytes 294944 | tf_op jit(solution)/shard_map/ppermute | solution.py:124
  140.3 12.3 %shard_map.71 = (f32[2,32,32,256]{3,2,1,0:T(8,128)S(1)}, f32[2,4,32,256]{3,2,1,0:T(8,128)S(1)}, f32[2,4,32,256]{3,2,1,0:T(8,128)S(1)}, f32[2,16,8,256]{3,2,1,0:T(8,128)S(1)}) custom-call(s32[2]{0:T(128)S(1)} %copy-done.4, f32[7,40,40,256]{3,2,1,0:T(8,128)S(1)} %get-tuple-element.58.coef, f32[2,32,32,256]{3,2,1,0:T(8,128)S(1)} %get-tuple-element.67.tile.refs_0_, ...), custom_call_target="tpu_custom_call" | custom-call | flops 5750000128 | bytes 18000000 | tf_op jit(solution)/shard_map/pallas_call | solution.py:24
  152.6 0.9 collective-permute-start.18
  153.5 5.6 %collective-permute-done.18.pack.refs_2_ = f32[2,16,8,256]{3,2,1,0:T(8,128)S(1)} collective-permute-done((f32[2,16,8,256]{3,2,1,0:T(8,128)S(1)}, f32[2,16,8,256]{3,2,1,0:T(8,128)S(1)}, u32[]{:S(2)}, u32[]{:S(2)}) %collective-permute-start.18) | collective-permute-done | bytes 262176 | tf_op jit(solution)/shard_map/ppermute | solution.py:117
  159.1 5.8 %collective-permute-start.19 = (f32[2,18,8,256]{3,2,1,0:T(8,128)S(1)}, f32[2,18,8,256]{3,2,1,0:T(8,128)S(1)}, u32[]{:S(2)}, u32[]{:S(2)}) collective-permute-start(f32[2,18,8,256]{3,2,1,0:T(8,128)S(1)} %get-tuple-element.98), channel_id=1, source_target_pairs={{0,2},{2,4},{4,6},{1,3},{3,5},{5,7},{8,10},{10,12},{12,14},{9,11},... | collective-permute-start | bytes 884744 | tf_op jit(solution)/shard_map/ppermute | solution.py:124
  165.0 1.3 collective-permute-start.20
  166.3 2.6 %collective-permute-done.20.refs_1_ = f32[2,18,8,256]{3,2,1,0:T(8,128)S(1)} collective-permute-done((f32[2,18,8,256]{3,2,1,0:T(8,128)S(1)}, f32[2,18,8,256]{3,2,1,0:T(8,128)S(1)}, u32[]{:S(2)}, u32[]{:S(2)}) %collective-permute-start.20) | collective-permute-done | bytes 294944 | tf_op jit(solution)/shard_map/ppermute | solution.py:124
  168.9 12.5 %shard_map.73.second = f32[2,32,32,256]{3,2,1,0:T(8,128)S(1)} custom-call(s32[2]{0:T(128)S(1)} %copy-done.4, f32[7,40,40,256]{3,2,1,0:T(8,128)S(1)} %get-tuple-element.58.coef, f32[2,32,32,256]{3,2,1,0:T(8,128)S(1)} %get-tuple-element.94.tile, f32[2,18,8,256]{3,2,1,0:T(8,128)S(1)} %collective-permute-done.19.refs_0_, ...), custom_call_target="tpu_custom_call" | custom-call | flops 5750000128 | bytes 18000000 | tf_op jit(solution)/shard_map/pallas_call | solution.py:24
  181.4 0.0 collective-permute-done.22.refs_2_
  181.4 3.0 %shard_map.74 = f32[8,128]{1,0:T(8,128)S(1)} custom-call(s32[2]{0:T(128)S(1)} %copy-done.4, f32[2,32,32,256]{3,2,1,0:T(8,128)S(1)} %shard_map.73.second, f32[2,32,32,256]{3,2,1,0:T(8,128)S(1)} %get-tuple-element.67.tile.refs_0_, f32[2,32,32,256]{3,2,1,0:T(8,128)S(1)} %shard_map.69.refs_1_, f32[2,32,32,256]{3,2,1,0:T(8,128)S(1)} %collective-permute-done.22.refs_2_, ...), custom_call_target="tpu_custom_call" | custom-call | flops 4600000000 | bytes 14400000 | tf_op jit(solution)/shard_map/pallas_call | solution.py:24
  184.4 0.2 collective-permute-start.25
  184.6 6.6 %collective-permute-start.24 = (f32[8,128]{1,0:T(8,128)S(1)}, f32[8,128]{1,0:T(8,128)S(1)}, u32[]{:S(2)}, u32[]{:S(2)}) collective-permute-start(f32[8,128]{1,0:T(8,128)S(1)} %shard_map.74), channel_id=1, source_target_pairs={{0,4},{2,6},{4,0},{6,2},{1,5},{3,7},{5,1},{7,3},{8,12},{10,14},{12... | collective-permute-start | bytes 12296 | tf_op jit(solution)/shard_map/ppermute | solution.py:475
  191.2 0.0 collective-permute-start.23
  191.2 0.0 collective-permute-done.25
  191.2 1.6 collective-permute-done.24
  192.8 0.9 collective-permute-start.26
  193.7 2.8 %collective-permute-done.26 = f32[8,128]{1,0:T(8,128)S(1)} collective-permute-done((f32[8,128]{1,0:T(8,128)S(1)}, f32[8,128]{1,0:T(8,128)S(1)}, u32[]{:S(2)}, u32[]{:S(2)}) %collective-permute-start.26) | collective-permute-done | bytes 4128 | tf_op jit(solution)/shard_map/ppermute | solution.py:475
  196.5 4.4 %collective-permute-start.29 = (f32[8,128]{1,0:T(8,128)S(1)}, f32[8,128]{1,0:T(8,128)S(1)}, u32[]{:S(2)}, u32[]{:S(2)}) collective-permute-start(f32[8,128]{1,0:T(8,128)S(1)} %add.24), channel_id=1, source_target_pairs={{0,24},{8,16},{16,8},{24,0},{1,25},{9,17},{17,9},{25,1},{2,26},{10... | collective-permute-start | bytes 12296 | tf_op jit(solution)/shard_map/ppermute | solution.py:475
  201.0 1.2 collective-permute-start.28
  202.1 0.6 collective-permute-start.27
  202.7 2.8 %collective-permute-done.28 = f32[8,128]{1,0:T(8,128)S(1)} collective-permute-done((f32[8,128]{1,0:T(8,128)S(1)}, f32[8,128]{1,0:T(8,128)S(1)}, u32[]{:S(2)}, u32[]{:S(2)}) %collective-permute-start.28) | collective-permute-done | bytes 4128 | tf_op jit(solution)/shard_map/ppermute | solution.py:475
  205.5 0.3 collective-permute-done.27
  205.7 4.1 %shard_map.75 = (f32[2,32,32,256]{3,2,1,0:T(8,128)}, f32[8,8]{1,0:T(8,128)}) custom-call(s32[2]{0:T(128)S(1)} %copy-done.4, f32[8,128]{1,0:T(8,128)S(1)} %add_add_fusion.inner, f32[2,32,32,256]{3,2,1,0:T(8,128)S(1)} %get-tuple-element.67.tile.refs_0_, f32[2,32,32,256]{3,2,1,0:T(8,128)S(1)} %shard_map.69.refs_1_, ...), custom_call_target="tpu_custom_call" | custom-call | flops 5750000128 | bytes 18000000 | tf_op jit(solution)/shard_map/pallas_call | solution.py:24
  (31 shorter events, 0.3 us)
Async XLA Ops:
  1.2 3.6 %copy-start.1 = (f32[2,32,32,256]{3,2,1,0:T(8,128)S(1)}, f32[2,32,32,256]{3,2,1,0:T(8,128)}, u32[]{:S(2)}) copy-start(f32[2,32,32,256]{3,2,1,0:T(8,128)} %probes.1) | copy-start | bytes 6291460
  1.2 10.4 %copy-start = (f32[3,32,32,256]{3,2,1,0:T(8,128)S(1)}, f32[3,32,32,256]{3,2,1,0:T(8,128)}, u32[]{:S(2)}) copy-start(f32[3,32,32,256]{3,2,1,0:T(8,128)} %velocity.1) | copy-start | bytes 9437188
  1.2 10.4 %copy-start.2 = (f32[32,32,256]{2,1,0:T(8,128)S(1)}, f32[32,32,256]{2,1,0:T(8,128)}, u32[]{:S(2)}) copy-start(f32[32,32,256]{2,1,0:T(8,128)} %param.6) | copy-start | bytes 3145732
  4.8 11.6 %copy-start.6 = (f32[6,2,8,256]{3,2,1,0:T(8,128)S(1)}, f32[6,2,8,256]{3,2,1,0:T(8,128)}, u32[]{:S(2)}) copy-start(f32[6,2,8,256]{3,2,1,0:T(8,128)} %get-tuple-element.56) | copy-start | bytes 294916
  4.8 24.6 %copy-start.5 = (f32[6,2,8,256]{3,2,1,0:T(8,128)S(1)}, f32[6,2,8,256]{3,2,1,0:T(8,128)}, u32[]{:S(2)}) copy-start(f32[6,2,8,256]{3,2,1,0:T(8,128)} %get-tuple-element.57) | copy-start | bytes 294916
  4.8 30.7 %copy-start.3 = (f32[32,32,256]{2,1,0:T(8,128)S(1)}, f32[32,32,256]{2,1,0:T(8,128)}, u32[]{:S(2)}) copy-start(f32[32,32,256]{2,1,0:T(8,128)} %refs_0_.3) | copy-start | bytes 3145732
  4.8 30.7 %copy-start.4 = (s32[2]{0:T(128)S(1)}, s32[2]{0:T(128)}, u32[]{:S(2)}) copy-start(s32[2]{0:T(128)} %pad_add_fusion.scalars) | copy-start | bytes 28
  4.8 49.9 %collective-permute-start.5 = (f32[2,32,32,256]{3,2,1,0:T(8,128)S(1)}, f32[2,32,32,256]{3,2,1,0:T(8,128)S(1)}, u32[]{:S(2)}, u32[]{:S(2)}) collective-permute-start(f32[2,32,32,256]{3,2,1,0:T(8,128)S(1)} %copy-done.1), channel_id=1, source_target_pairs={{0,8},{8,16},{16,24},{1,9},{9,17},{17,25},{2,10},{10,18},{18,26},{... | collective-permute-start | bytes 6291464 | tf_op jit(solution)/shard_map/ppermute | solution.py:536
  10.0 25.5 %collective-permute-start.2 = (f32[6,16,8,256]{3,2,1,0:T(8,128)}, f32[6,16,8,256]{3,2,1,0:T(8,128)S(1)}, u32[]{:S(2)}, u32[]{:S(2)}) collective-permute-start(f32[6,16,8,256]{3,2,1,0:T(8,128)} %get-tuple-element.55), channel_id=1, source_target_pairs={{0,1},{1,0},{2,3},{3,2},{4,5},{5,4},{6,7},{7,6},{8,9},{9,8},{10,11... | collective-permute-start | bytes 2359304 | tf_op jit(solution)/shard_map/ppermute | solution.py:117
  13.7 21.7 %collective-permute-start = (f32[6,4,32,256]{3,2,1,0:T(8,128)S(1)}, f32[6,4,32,256]{3,2,1,0:T(8,128)S(1)}, u32[]{:S(2)}, u32[]{:S(2)}) collective-permute-start(f32[6,4,32,256]{3,2,1,0:T(8,128)S(1)} %get-tuple-element.52), channel_id=1, source_target_pairs={{0,2},{2,4},{4,6},{1,3},{3,5},{5,7},{8,10},{10,12},{12,14},{9,11},... | collective-permute-start | bytes 2359304 | tf_op jit(solution)/shard_map/ppermute | solution.py:125
  15.1 20.4 %collective-permute-start.1 = (f32[6,4,32,256]{3,2,1,0:T(8,128)S(1)}, f32[6,4,32,256]{3,2,1,0:T(8,128)S(1)}, u32[]{:S(2)}, u32[]{:S(2)}) collective-permute-start(f32[6,4,32,256]{3,2,1,0:T(8,128)S(1)} %get-tuple-element.53), channel_id=1, source_target_pairs={{2,0},{4,2},{6,4},{3,1},{5,3},{7,5},{10,8},{12,10},{14,12},{11,9},... | collective-permute-start | bytes 2359304 | tf_op jit(solution)/shard_map/ppermute | solution.py:126
  16.4 13.0 %collective-permute-start.3 = (f32[6,2,8,256]{3,2,1,0:T(8,128)S(1)}, f32[6,2,8,256]{3,2,1,0:T(8,128)S(1)}, u32[]{:S(2)}, u32[]{:S(2)}) collective-permute-start(f32[6,2,8,256]{3,2,1,0:T(8,128)S(1)} %copy-done.6), channel_id=1, source_target_pairs={{0,3},{1,2},{2,5},{3,4},{4,7},{5,6},{8,11},{9,10},{10,13},{11,12},... | collective-permute-start | bytes 294920 | tf_op jit(solution)/shard_map/ppermute | solution.py:117
  29.4 6.1 %collective-permute-start.4 = (f32[6,2,8,256]{3,2,1,0:T(8,128)S(1)}, f32[6,2,8,256]{3,2,1,0:T(8,128)S(1)}, u32[]{:S(2)}, u32[]{:S(2)}) collective-permute-start(f32[6,2,8,256]{3,2,1,0:T(8,128)S(1)} %copy-done.5), channel_id=1, source_target_pairs={{2,1},{3,0},{4,3},{5,2},{6,5},{7,4},{10,9},{11,8},{12,11},{13,10},... | collective-permute-start | bytes 294920 | tf_op jit(solution)/shard_map/ppermute | solution.py:117
  49.8 8.8 %collective-permute-start.6 = (f32[2,16,8,256]{3,2,1,0:T(8,128)S(1)}, f32[2,16,8,256]{3,2,1,0:T(8,128)S(1)}, u32[]{:S(2)}, u32[]{:S(2)}) collective-permute-start(f32[2,16,8,256]{3,2,1,0:T(8,128)S(1)} %get-tuple-element.64), channel_id=1, source_target_pairs={{0,1},{1,0},{2,3},{3,2},{4,5},{5,4},{6,7},{7,6},{8,9},{9,8},{10,11... | collective-permute-start | bytes 786440 | tf_op jit(solution)/shard_map/ppermute | solution.py:117
  55.4 9.3 %collective-permute-start.9 = (f32[2,16,8,256]{3,2,1,0:T(8,128)S(1)}, f32[2,16,8,256]{3,2,1,0:T(8,128)S(1)}, u32[]{:S(2)}, u32[]{:S(2)}) collective-permute-start(f32[2,16,8,256]{3,2,1,0:T(8,128)S(1)} %shard_map.65), channel_id=1, source_target_pairs={{0,1},{1,0},{2,3},{3,2},{4,5},{5,4},{6,7},{7,6},{8,9},{9,8},{10,11... | collective-permute-start | bytes 786440 | tf_op jit(solution)/shard_map/ppermute | solution.py:117
  58.6 9.4 %collective-permute-start.7 = (f32[2,18,8,256]{3,2,1,0:T(8,128)S(1)}, f32[2,18,8,256]{3,2,1,0:T(8,128)S(1)}, u32[]{:S(2)}, u32[]{:S(2)}) collective-permute-start(f32[2,18,8,256]{3,2,1,0:T(8,128)S(1)} %get-tuple-element.65), channel_id=1, source_target_pairs={{0,2},{2,4},{4,6},{1,3},{3,5},{5,7},{8,10},{10,12},{12,14},{9,11},... | collective-permute-start | bytes 884744 | tf_op jit(solution)/shard_map/ppermute | solution.py:124
  60.9 7.2 %collective-permute-start.8 = (f32[2,18,8,256]{3,2,1,0:T(8,128)S(1)}, f32[2,18,8,256]{3,2,1,0:T(8,128)S(1)}, u32[]{:S(2)}, u32[]{:S(2)}) collective-permute-start(f32[2,18,8,256]{3,2,1,0:T(8,128)S(1)} %get-tuple-element.66), channel_id=1, source_target_pairs={{2,0},{4,2},{6,4},{3,1},{5,3},{7,5},{10,8},{12,10},{14,12},{11,9},... | collective-permute-start | bytes 884744 | tf_op jit(solution)/shard_map/ppermute | solution.py:124
  64.7 21.0 %collective-permute-start.10 = (f32[2,18,8,256]{3,2,1,0:T(8,128)S(1)}, f32[2,18,8,256]{3,2,1,0:T(8,128)S(1)}, u32[]{:S(2)}, u32[]{:S(2)}) collective-permute-start(f32[2,18,8,256]{3,2,1,0:T(8,128)S(1)} %get-tuple-element.74), channel_id=1, source_target_pairs={{0,2},{2,4},{4,6},{1,3},{3,5},{5,7},{8,10},{10,12},{12,14},{9,11},... | collective-permute-start | bytes 884744 | tf_op jit(solution)/shard_map/ppermute | solution.py:124
  66.7 19.0 %collective-permute-start.11 = (f32[2,18,8,256]{3,2,1,0:T(8,128)S(1)}, f32[2,18,8,256]{3,2,1,0:T(8,128)S(1)}, u32[]{:S(2)}, u32[]{:S(2)}) collective-permute-start(f32[2,18,8,256]{3,2,1,0:T(8,128)S(1)} %get-tuple-element.75), channel_id=1, source_target_pairs={{2,0},{4,2},{6,4},{3,1},{5,3},{7,5},{10,8},{12,10},{14,12},{11,9},... | collective-permute-start | bytes 884744 | tf_op jit(solution)/shard_map/ppermute | solution.py:124
  80.7 49.5 %collective-permute-start.21 = (f32[2,32,32,256]{3,2,1,0:T(8,128)S(1)}, f32[2,32,32,256]{3,2,1,0:T(8,128)S(1)}, u32[]{:S(2)}, u32[]{:S(2)}) collective-permute-start(f32[2,32,32,256]{3,2,1,0:T(8,128)S(1)} %get-tuple-element.67.tile.refs_0_), channel_id=1, source_target_pairs={{0,24},{1,25},{2,26},{3,27},{4,28},{5,29},{6,30},{7,31}} | collective-permute-start | bytes 6291464 | tf_op jit(solution)/shard_map/ppermute | solution.py:536
  98.1 8.1 %collective-permute-start.13 = (f32[2,16,8,256]{3,2,1,0:T(8,128)S(1)}, f32[2,16,8,256]{3,2,1,0:T(8,128)S(1)}, u32[]{:S(2)}, u32[]{:S(2)}) collective-permute-start(f32[2,16,8,256]{3,2,1,0:T(8,128)S(1)} %get-tuple-element.86), channel_id=1, source_target_pairs={{0,1},{1,0},{2,3},{3,2},{4,5},{5,4},{6,7},{7,6},{8,9},{9,8},{10,11... | collective-permute-start | bytes 786440 | tf_op jit(solution)/shard_map/ppermute | solution.py:117
  106.3 4.7 %collective-permute-start.14 = (f32[2,18,8,256]{3,2,1,0:T(8,128)S(1)}, f32[2,18,8,256]{3,2,1,0:T(8,128)S(1)}, u32[]{:S(2)}, u32[]{:S(2)}) collective-permute-start(f32[2,18,8,256]{3,2,1,0:T(8,128)S(1)} %get-tuple-element.87), channel_id=1, source_target_pairs={{0,2},{2,4},{4,6},{1,3},{3,5},{5,7},{8,10},{10,12},{12,14},{9,11},... | collective-permute-start | bytes 884744 | tf_op jit(solution)/shard_map/ppermute | solution.py:124
  109.1 4.8 %collective-permute-start.15 = (f32[2,18,8,256]{3,2,1,0:T(8,128)S(1)}, f32[2,18,8,256]{3,2,1,0:T(8,128)S(1)}, u32[]{:S(2)}, u32[]{:S(2)}) collective-permute-start(f32[2,18,8,256]{3,2,1,0:T(8,128)S(1)} %get-tuple-element.88), channel_id=1, source_target_pairs={{2,0},{4,2},{6,4},{3,1},{5,3},{7,5},{10,8},{12,10},{14,12},{11,9},... | collective-permute-start | bytes 884744 | tf_op jit(solution)/shard_map/ppermute | solution.py:124
  110.4 15.9 %collective-permute-start.12 = (f32[2,16,8,256]{3,2,1,0:T(8,128)S(1)}, f32[2,16,8,256]{3,2,1,0:T(8,128)S(1)}, u32[]{:S(2)}, u32[]{:S(2)}) collective-permute-start(f32[2,16,8,256]{3,2,1,0:T(8,128)S(1)} %get-tuple-element.82), channel_id=1, source_target_pairs={{0,1},{1,0},{2,3},{3,2},{4,5},{5,4},{6,7},{7,6},{8,9},{9,8},{10,11... | collective-permute-start | bytes 786440 | tf_op jit(solution)/shard_map/ppermute | solution.py:117
  130.2 51.2 %collective-permute-start.22 = (f32[2,32,32,256]{3,2,1,0:T(8,128)S(1)}, f32[2,32,32,256]{3,2,1,0:T(8,128)S(1)}, u32[]{:S(2)}, u32[]{:S(2)}) collective-permute-start(f32[2,32,32,256]{3,2,1,0:T(8,128)S(1)} %shard_map.69.refs_1_), channel_id=1, source_target_pairs={{0,8},{8,16},{16,24},{1,9},{9,17},{17,25},{2,10},{10,18},{18,26},{... | collective-permute-start | bytes 6291464 | tf_op jit(solution)/shard_map/ppermute | solution.py:536
  131.7 4.8 %collective-permute-start.16 = (f32[2,18,8,256]{3,2,1,0:T(8,128)S(1)}, f32[2,18,8,256]{3,2,1,0:T(8,128)S(1)}, u32[]{:S(2)}, u32[]{:S(2)}) collective-permute-start(f32[2,18,8,256]{3,2,1,0:T(8,128)S(1)} %get-tuple-element.92), channel_id=1, source_target_pairs={{0,2},{2,4},{4,6},{1,3},{3,5},{5,7},{8,10},{10,12},{12,14},{9,11},... | collective-permute-start | bytes 884744 | tf_op jit(solution)/shard_map/ppermute | solution.py:124
  135.2 5.2 %collective-permute-start.17 = (f32[2,18,8,256]{3,2,1,0:T(8,128)S(1)}, f32[2,18,8,256]{3,2,1,0:T(8,128)S(1)}, u32[]{:S(2)}, u32[]{:S(2)}) collective-permute-start(f32[2,18,8,256]{3,2,1,0:T(8,128)S(1)} %get-tuple-element.93), channel_id=1, source_target_pairs={{2,0},{4,2},{6,4},{3,1},{5,3},{7,5},{10,8},{12,10},{14,12},{11,9},... | collective-permute-start | bytes 884744 | tf_op jit(solution)/shard_map/ppermute | solution.py:124
  152.6 6.4 %collective-permute-start.18 = (f32[2,16,8,256]{3,2,1,0:T(8,128)S(1)}, f32[2,16,8,256]{3,2,1,0:T(8,128)S(1)}, u32[]{:S(2)}, u32[]{:S(2)}) collective-permute-start(f32[2,16,8,256]{3,2,1,0:T(8,128)S(1)} %get-tuple-element.97), channel_id=1, source_target_pairs={{0,1},{1,0},{2,3},{3,2},{4,5},{5,4},{6,7},{7,6},{8,9},{9,8},{10,11... | collective-permute-start | bytes 786440 | tf_op jit(solution)/shard_map/ppermute | solution.py:117
  159.1 7.1 %collective-permute-start.19 = (f32[2,18,8,256]{3,2,1,0:T(8,128)S(1)}, f32[2,18,8,256]{3,2,1,0:T(8,128)S(1)}, u32[]{:S(2)}, u32[]{:S(2)}) collective-permute-start(f32[2,18,8,256]{3,2,1,0:T(8,128)S(1)} %get-tuple-element.98), channel_id=1, source_target_pairs={{0,2},{2,4},{4,6},{1,3},{3,5},{5,7},{8,10},{10,12},{12,14},{9,11},... | collective-permute-start | bytes 884744 | tf_op jit(solution)/shard_map/ppermute | solution.py:124
  165.0 4.0 %collective-permute-start.20 = (f32[2,18,8,256]{3,2,1,0:T(8,128)S(1)}, f32[2,18,8,256]{3,2,1,0:T(8,128)S(1)}, u32[]{:S(2)}, u32[]{:S(2)}) collective-permute-start(f32[2,18,8,256]{3,2,1,0:T(8,128)S(1)} %get-tuple-element.99), channel_id=1, source_target_pairs={{2,0},{4,2},{6,4},{3,1},{5,3},{7,5},{10,8},{12,10},{14,12},{11,9},... | collective-permute-start | bytes 884744 | tf_op jit(solution)/shard_map/ppermute | solution.py:124
  184.4 6.8 %collective-permute-start.25 = (f32[8,128]{1,0:T(8,128)S(1)}, f32[8,128]{1,0:T(8,128)S(1)}, u32[]{:S(2)}, u32[]{:S(2)}) collective-permute-start(f32[8,128]{1,0:T(8,128)S(1)} %shard_map.74), channel_id=1, source_target_pairs={{0,6},{2,4},{4,2},{6,0},{1,7},{3,5},{5,3},{7,1},{8,14},{10,12},{12... | collective-permute-start | bytes 12296 | tf_op jit(solution)/shard_map/ppermute | solution.py:475
  184.6 8.2 %collective-permute-start.24 = (f32[8,128]{1,0:T(8,128)S(1)}, f32[8,128]{1,0:T(8,128)S(1)}, u32[]{:S(2)}, u32[]{:S(2)}) collective-permute-start(f32[8,128]{1,0:T(8,128)S(1)} %shard_map.74), channel_id=1, source_target_pairs={{0,4},{2,6},{4,0},{6,2},{1,5},{3,7},{5,1},{7,3},{8,12},{10,14},{12... | collective-permute-start | bytes 12296 | tf_op jit(solution)/shard_map/ppermute | solution.py:475
  191.2 1.6 collective-permute-start.23
  192.8 3.7 %collective-permute-start.26 = (f32[8,128]{1,0:T(8,128)S(1)}, f32[8,128]{1,0:T(8,128)S(1)}, u32[]{:S(2)}, u32[]{:S(2)}) collective-permute-start(f32[8,128]{1,0:T(8,128)S(1)} %add_add_fusion.1), channel_id=1, source_target_pairs={{0,1},{1,0},{2,3},{3,2},{4,5},{5,4},{6,7},{7,6},{8,9},{9,8},{10,11... | collective-permute-start | bytes 12296 | tf_op jit(solution)/shard_map/ppermute | solution.py:475
  196.5 6.2 %collective-permute-start.29 = (f32[8,128]{1,0:T(8,128)S(1)}, f32[8,128]{1,0:T(8,128)S(1)}, u32[]{:S(2)}, u32[]{:S(2)}) collective-permute-start(f32[8,128]{1,0:T(8,128)S(1)} %add.24), channel_id=1, source_target_pairs={{0,24},{8,16},{16,8},{24,0},{1,25},{9,17},{17,9},{25,1},{2,26},{10... | collective-permute-start | bytes 12296 | tf_op jit(solution)/shard_map/ppermute | solution.py:475
  201.0 4.5 %collective-permute-start.28 = (f32[8,128]{1,0:T(8,128)S(1)}, f32[8,128]{1,0:T(8,128)S(1)}, u32[]{:S(2)}, u32[]{:S(2)}) collective-permute-start(f32[8,128]{1,0:T(8,128)S(1)} %add.24), channel_id=1, source_target_pairs={{0,16},{8,24},{16,0},{24,8},{1,17},{9,25},{17,1},{25,9},{2,18},{10... | collective-permute-start | bytes 12296 | tf_op jit(solution)/shard_map/ppermute | solution.py:475
  202.1 3.6 %collective-permute-start.27 = (f32[8,128]{1,0:T(8,128)S(1)}, f32[8,128]{1,0:T(8,128)S(1)}, u32[]{:S(2)}, u32[]{:S(2)}) collective-permute-start(f32[8,128]{1,0:T(8,128)S(1)} %add.24), channel_id=1, source_target_pairs={{0,8},{8,0},{16,24},{24,16},{1,9},{9,1},{17,25},{25,17},{2,10},{10... | collective-permute-start | bytes 12296 | tf_op jit(solution)/shard_map/ppermute | solution.py:475

commit v9 on v8

--- a/solution.py
+++ b/solution.py
@@ -574,8 +574,8 @@
     passed = [images, images_next, right(shifting, 1)] + far
 
     received = exchange(strips, after=images_next)
-    halfway, *strips = model(images, received, False, micros=5.0)
-    (second,) = model(halfway, exchange(strips), True, True, micros=5.0)
+    halfway, *strips = model(images, received, False, micros=8.0)
+    (second,) = model(halfway, exchange(strips), True, True, micros=8.0)
 
     (partial,) = kernel_call(
         dots_kernel,

time: 210 us -> 204 us (0.971)
  starting transfers between devices: 62.8 us -> 59.8 us
  waiting for transfers between devices: 54.5 us -> 51.5 us
    ppermute x7, starting transfers between devices: 13.8 us -> 7.82 us  [all_sum(): lax.ppermute(value, axis, [(i, i ^ bits) for i in range(devices)])]
    ppermute x10, waiting for transfers between devices: 9.4 us -> 6.28 us  [exchange(): return [lax.ppermute(hi, 'sx', up), lax.ppermute(lo, 'sx', down), pack]]
    ppermute x10, starting transfers between devices: 22.8 us -> 25.8 us  [exchange(): return [lax.ppermute(hi, 'sx', up), lax.ppermute(lo, 'sx', down), pack]]
  transfers between devices with their start and end apart: 30 -> 30, of which waited for: 15 -> 16; matrix products, arithmetic and copies ran while one was open for 0% -> 0% of each run, Pallas kernels for 38% -> 39%
where the time goes in v9:
time: 204 us
  Pallas kernels  90.9 us (45%)
  starting transfers between devices  59.8 us (29%)
  waiting for transfers between devices  51.5 us (25%)
    pallas_call x17, Pallas kernels, kernel_call(): pl.pallas_call(body, out_shape=outs, in_specs=specs, out_specs=[spec(n, o...  90.9 us
    ppermute x8, waiting for transfers between devices, moved(): return lax.ppermute(value, ('sx', 'sy'), pairs)  29.5 us
    ppermute x10, starting transfers between devices, exchange(): return [lax.ppermute(hi, 'sx', up), lax.ppermute(lo, 'sx', down), pack]  25.8 us
    ppermute x8, starting transfers between devices, moved(): return lax.ppermute(value, ('sx', 'sy'), pairs)  11.9 us
    ppermute x3, starting transfers between devices, right(): lax.ppermute(value, 'probe', [(i, i + hops) for i in range(groups - hops)])  11.7 us
    ppermute x3, waiting for transfers between devices, right(): lax.ppermute(value, 'probe', [(i, i + hops) for i in range(groups - hops)])  8.56 us
    ppermute x7, starting transfers between devices, all_sum(): lax.ppermute(value, axis, [(i, i ^ bits) for i in range(devices)])  7.82 us
    ppermute x7, waiting for transfers between devices, all_sum(): lax.ppermute(value, axis, [(i, i ^ bits) for i in range(devices)])  7.21 us
  transfers between devices with their start and end apart: 30, of which 16 were waited for; matrix products, arithmetic and copies ran while one was open for 0% of the time, Pallas kernels for 39%

profile of v9, /device:TPU:0, one launch (start us, length us, event | category | flops | bytes accessed | tf_op | source)
XLA Modules:
  0.0 203.9 jit_solution(5979215328372112159)
XLA Ops:
  0.6 0.6 pad_add_fusion.scalars
  1.2 3.5 %shard_map.60 = (f32[6,16,8,256]{3,2,1,0:T(8,128)}, f32[6,2,8,256]{3,2,1,0:T(8,128)}, f32[6,2,8,256]{3,2,1,0:T(8,128)}) custom-call(s32[2]{0:T(128)} %pad_add_fusion.scalars, f32[1,32,32,256]{3,2,1,0:T(8,128)} %bitcast.3, f32[3,32,32,256]{3,2,1,0:T(8,128)} %velocity.1, f32[2,32,32,256]{3,2,1,0:T(8,128)} %probes.1), custom_call_target="tpu_custom_call" | custom-call | flops 2300000000 | bytes 7200000 | tf_op jit(solution)/shard_map/pallas_call | solution.py:24
  4.8 0.0 copy-start.3
  4.8 5.2 %collective-permute-start.5 = (f32[2,32,32,256]{3,2,1,0:T(8,128)S(1)}, f32[2,32,32,256]{3,2,1,0:T(8,128)S(1)}, u32[]{:S(2)}, u32[]{:S(2)}) collective-permute-start(f32[2,32,32,256]{3,2,1,0:T(8,128)S(1)} %copy-done.1), channel_id=1, source_target_pairs={{0,8},{8,16},{16,24},{1,9},{9,17},{17,25},{2,10},{10,18},{18,26},{... | collective-permute-start | bytes 6291464 | tf_op jit(solution)/shard_map/ppermute | solution.py:536
  10.0 1.6 collective-permute-start.2
  11.6 2.1 %shard_map.59 = (f32[6,4,32,256]{3,2,1,0:T(8,128)S(1)}, f32[6,4,32,256]{3,2,1,0:T(8,128)S(1)}) custom-call(f32[1,32,32,256]{3,2,1,0:T(8,128)S(1)} %bitcast.4, f32[3,32,32,256]{3,2,1,0:T(8,128)S(1)} %copy-done, f32[2,32,32,256]{3,2,1,0:T(8,128)S(1)} %copy-done.1), custom_call_target="tpu_custom_call" | custom-call | flops 2300000000 | bytes 7200000 | tf_op jit(solution)/shard_map/pallas_call | solution.py:24
  13.7 1.3 collective-permute-start
  15.1 1.3 collective-permute-start.1
  16.4 4.8 %collective-permute-start.3 = (f32[6,2,8,256]{3,2,1,0:T(8,128)S(1)}, f32[6,2,8,256]{3,2,1,0:T(8,128)S(1)}, u32[]{:S(2)}, u32[]{:S(2)}) collective-permute-start(f32[6,2,8,256]{3,2,1,0:T(8,128)S(1)} %copy-done.6), channel_id=1, source_target_pairs={{0,3},{1,2},{2,5},{3,4},{4,7},{5,6},{8,11},{9,10},{10,13},{11,12},... | collective-permute-start | bytes 294920 | tf_op jit(solution)/shard_map/ppermute | solution.py:117
  21.2 8.1 %collective-permute-done.3.refs_3_ = f32[6,2,8,256]{3,2,1,0:T(8,128)S(1)} collective-permute-done((f32[6,2,8,256]{3,2,1,0:T(8,128)S(1)}, f32[6,2,8,256]{3,2,1,0:T(8,128)S(1)}, u32[]{:S(2)}, u32[]{:S(2)}) %collective-permute-start.3) | collective-permute-done | bytes 98336 | tf_op jit(solution)/shard_map/ppermute | solution.py:117
  29.4 1.3 collective-permute-start.4
  30.7 4.8 %collective-permute-done.4.refs_4_ = f32[6,2,8,256]{3,2,1,0:T(8,128)S(1)} collective-permute-done((f32[6,2,8,256]{3,2,1,0:T(8,128)S(1)}, f32[6,2,8,256]{3,2,1,0:T(8,128)S(1)}, u32[]{:S(2)}, u32[]{:S(2)}) %collective-permute-start.4) | collective-permute-done | bytes 98336 | tf_op jit(solution)/shard_map/ppermute | solution.py:117
  35.5 14.3 %shard_map.61 = (f32[7,40,40,256]{3,2,1,0:T(8,128)S(1)}, f32[2,32,32,256]{3,2,1,0:T(8,128)S(1)}, f32[2,4,32,256]{3,2,1,0:T(8,128)S(1)}, f32[2,4,32,256]{3,2,1,0:T(8,128)S(1)}, f32[2,16,8,256]{3,2,1,0:T(8,128)S(1)}) custom-call(s32[2]{0:T(128)S(1)} %copy-done.4, f32[1,32,32,256]{3,2,1,0:T(8,128)S(1)} %bitcast.5, f32[3,32,32,256]{3,2,1,0:T(8,128)S(1)} %copy-done, ...), custom_call_target="tpu_custom_call" | custom-call | flops 4600000000 | bytes 14400000 | tf_op jit(solution)/shard_map/pallas_call | solution.py:24
  49.8 0.6 collective-permute-start.6
  50.4 4.3 %collective-permute-done.5.refs_0_.tile = f32[2,32,32,256]{3,2,1,0:T(8,128)S(1)} collective-permute-done((f32[2,32,32,256]{3,2,1,0:T(8,128)S(1)}, f32[2,32,32,256]{3,2,1,0:T(8,128)S(1)}, u32[]{:S(2)}, u32[]{:S(2)}) %collective-permute-start.5) | collective-permute-done | bytes 2097184 | tf_op jit(solution)/shard_map/ppermute | solution.py:536
  54.7 0.7 shard_map.65
  55.4 1.6 collective-permute-start.9
  57.0 1.6 collective-permute-done.6.pack.refs_2_
  58.6 2.2 %collective-permute-start.7 = (f32[2,18,8,256]{3,2,1,0:T(8,128)S(1)}, f32[2,18,8,256]{3,2,1,0:T(8,128)S(1)}, u32[]{:S(2)}, u32[]{:S(2)}) collective-permute-start(f32[2,18,8,256]{3,2,1,0:T(8,128)S(1)} %get-tuple-element.65), channel_id=1, source_target_pairs={{0,2},{2,4},{4,6},{1,3},{3,5},{5,7},{8,10},{10,12},{12,14},{9,11},... | collective-permute-start | bytes 884744 | tf_op jit(solution)/shard_map/ppermute | solution.py:124
  60.9 1.3 collective-permute-start.8
  62.2 0.7 shard_map.64
  62.9 1.8 collective-permute-done.9.pack.refs_3_
  64.7 2.0 collective-permute-start.10
  66.7 1.3 collective-permute-start.11
  68.0 0.0 collective-permute-done.7.refs_0_
  68.0 0.0 collective-permute-done.8.refs_1_
  68.1 12.6 %shard_map.63 = (f32[2,32,32,256]{3,2,1,0:T(8,128)S(1)}, f32[2,4,32,256]{3,2,1,0:T(8,128)S(1)}, f32[2,4,32,256]{3,2,1,0:T(8,128)S(1)}, f32[2,16,8,256]{3,2,1,0:T(8,128)S(1)}) custom-call(s32[2]{0:T(128)S(1)} %copy-done.4, f32[7,40,40,256]{3,2,1,0:T(8,128)S(1)} %get-tuple-element.58.coef, f32[2,32,32,256]{3,2,1,0:T(8,128)S(1)} %get-tuple-element.61.tile, ...), custom_call_target="tpu_custom_call" | custom-call | flops 9200000000 | bytes 28800000 | tf_op jit(solution)/shard_map/pallas_call | solution.py:24
  80.7 5.0 %collective-permute-start.21 = (f32[2,32,32,256]{3,2,1,0:T(8,128)S(1)}, f32[2,32,32,256]{3,2,1,0:T(8,128)S(1)}, u32[]{:S(2)}, u32[]{:S(2)}) collective-permute-start(f32[2,32,32,256]{3,2,1,0:T(8,128)S(1)} %get-tuple-element.67.tile.refs_0_), channel_id=1, source_target_pairs={{0,24},{1,25},{2,26},{3,27},{4,28},{5,29},{6,30},{7,31}} | collective-permute-start | bytes 6291464 | tf_op jit(solution)/shard_map/ppermute | solution.py:536
  85.7 0.0 collective-permute-done.11.refs_2_
  85.8 12.3 %shard_map.67 = (f32[2,32,32,256]{3,2,1,0:T(8,128)S(1)}, f32[2,4,32,256]{3,2,1,0:T(8,128)S(1)}, f32[2,4,32,256]{3,2,1,0:T(8,128)S(1)}, f32[2,16,8,256]{3,2,1,0:T(8,128)S(1)}) custom-call(s32[2]{0:T(128)S(1)} %copy-done.4, f32[7,40,40,256]{3,2,1,0:T(8,128)S(1)} %get-tuple-element.58.coef, f32[2,32,32,256]{3,2,1,0:T(8,128)S(1)} %collective-permute-done.5.refs_0_.tile, ...), custom_call_target="tpu_custom_call" | custom-call | flops 9200000000 | bytes 28800000 | tf_op jit(solution)/shard_map/pallas_call | solution.py:24
  98.1 0.6 collective-permute-start.13
  98.7 7.6 %collective-permute-done.13.pack.refs_2_ = f32[2,16,8,256]{3,2,1,0:T(8,128)S(1)} collective-permute-done((f32[2,16,8,256]{3,2,1,0:T(8,128)S(1)}, f32[2,16,8,256]{3,2,1,0:T(8,128)S(1)}, u32[]{:S(2)}, u32[]{:S(2)}) %collective-permute-start.13) | collective-permute-done | bytes 262176 | tf_op jit(solution)/shard_map/ppermute | solution.py:117
  106.3 2.9 %collective-permute-start.14 = (f32[2,18,8,256]{3,2,1,0:T(8,128)S(1)}, f32[2,18,8,256]{3,2,1,0:T(8,128)S(1)}, u32[]{:S(2)}, u32[]{:S(2)}) collective-permute-start(f32[2,18,8,256]{3,2,1,0:T(8,128)S(1)} %get-tuple-element.87), channel_id=1, source_target_pairs={{0,2},{2,4},{4,6},{1,3},{3,5},{5,7},{8,10},{10,12},{12,14},{9,11},... | collective-permute-start | bytes 884744 | tf_op jit(solution)/shard_map/ppermute | solution.py:124
  109.1 1.3 collective-permute-start.15
  110.4 0.6 collective-permute-start.12
  111.0 2.9 %collective-permute-done.15.refs_1_ = f32[2,18,8,256]{3,2,1,0:T(8,128)S(1)} collective-permute-done((f32[2,18,8,256]{3,2,1,0:T(8,128)S(1)}, f32[2,18,8,256]{3,2,1,0:T(8,128)S(1)}, u32[]{:S(2)}, u32[]{:S(2)}) %collective-permute-start.15) | collective-permute-done | bytes 294944 | tf_op jit(solution)/shard_map/ppermute | solution.py:124
  113.9 12.5 %shard_map.69.refs_1_ = f32[2,32,32,256]{3,2,1,0:T(8,128)S(1)} custom-call(s32[2]{0:T(128)S(1)} %copy-done.4, f32[7,40,40,256]{3,2,1,0:T(8,128)S(1)} %get-tuple-element.58.coef, f32[2,32,32,256]{3,2,1,0:T(8,128)S(1)} %get-tuple-element.83.tile, f32[2,18,8,256]{3,2,1,0:T(8,128)S(1)} %collective-permute-done.14.refs_0_, ...), custom_call_target="tpu_custom_call" | custom-call | flops 9200000000 | bytes 28800000 | tf_op jit(solution)/shard_map/pallas_call | solution.py:24
  126.4 0.0 collective-permute-done.12.pack.refs_3_
  126.4 7.0 %collective-permute-start.16 = (f32[2,18,8,256]{3,2,1,0:T(8,128)S(1)}, f32[2,18,8,256]{3,2,1,0:T(8,128)S(1)}, u32[]{:S(2)}, u32[]{:S(2)}) collective-permute-start(f32[2,18,8,256]{3,2,1,0:T(8,128)S(1)} %get-tuple-element.92), channel_id=1, source_target_pairs={{0,2},{2,4},{4,6},{1,3},{3,5},{5,7},{8,10},{10,12},{12,14},{9,11},... | collective-permute-start | bytes 884744 | tf_op jit(solution)/shard_map/ppermute | solution.py:124
  133.4 1.3 collective-permute-start.17
  134.7 0.0 collective-permute-done.21.refs_3_
  134.7 1.4 collective-permute-start.22
  136.2 0.7 collective-permute-done.17.refs_2_
  136.9 12.3 %shard_map.71 = (f32[2,32,32,256]{3,2,1,0:T(8,128)S(1)}, f32[2,4,32,256]{3,2,1,0:T(8,128)S(1)}, f32[2,4,32,256]{3,2,1,0:T(8,128)S(1)}, f32[2,16,8,256]{3,2,1,0:T(8,128)S(1)}) custom-call(s32[2]{0:T(128)S(1)} %copy-done.4, f32[7,40,40,256]{3,2,1,0:T(8,128)S(1)} %get-tuple-element.58.coef, f32[2,32,32,256]{3,2,1,0:T(8,128)S(1)} %get-tuple-element.67.tile.refs_0_, ...), custom_call_target="tpu_custom_call" | custom-call | flops 9200000000 | bytes 28800000 | tf_op jit(solution)/shard_map/pallas_call | solution.py:24
  149.2 0.9 collective-permute-start.18
  150.1 5.6 %collective-permute-done.18.pack.refs_2_ = f32[2,16,8,256]{3,2,1,0:T(8,128)S(1)} collective-permute-done((f32[2,16,8,256]{3,2,1,0:T(8,128)S(1)}, f32[2,16,8,256]{3,2,1,0:T(8,128)S(1)}, u32[]{:S(2)}, u32[]{:S(2)}) %collective-permute-start.18) | collective-permute-done | bytes 262176 | tf_op jit(solution)/shard_map/ppermute | solution.py:117
  155.7 5.3 %collective-permute-start.19 = (f32[2,18,8,256]{3,2,1,0:T(8,128)S(1)}, f32[2,18,8,256]{3,2,1,0:T(8,128)S(1)}, u32[]{:S(2)}, u32[]{:S(2)}) collective-permute-start(f32[2,18,8,256]{3,2,1,0:T(8,128)S(1)} %get-tuple-element.98), channel_id=1, source_target_pairs={{0,2},{2,4},{4,6},{1,3},{3,5},{5,7},{8,10},{10,12},{12,14},{9,11},... | collective-permute-start | bytes 884744 | tf_op jit(solution)/shard_map/ppermute | solution.py:124
  161.0 1.3 collective-permute-start.20
  162.3 2.6 %collective-permute-done.20.refs_1_ = f32[2,18,8,256]{3,2,1,0:T(8,128)S(1)} collective-permute-done((f32[2,18,8,256]{3,2,1,0:T(8,128)S(1)}, f32[2,18,8,256]{3,2,1,0:T(8,128)S(1)}, u32[]{:S(2)}, u32[]{:S(2)}) %collective-permute-start.20) | collective-permute-done | bytes 294944 | tf_op jit(solution)/shard_map/ppermute | solution.py:124
  165.0 12.5 %shard_map.73.second = f32[2,32,32,256]{3,2,1,0:T(8,128)S(1)} custom-call(s32[2]{0:T(128)S(1)} %copy-done.4, f32[7,40,40,256]{3,2,1,0:T(8,128)S(1)} %get-tuple-element.58.coef, f32[2,32,32,256]{3,2,1,0:T(8,128)S(1)} %get-tuple-element.94.tile, f32[2,18,8,256]{3,2,1,0:T(8,128)S(1)} %collective-permute-done.19.refs_0_, ...), custom_call_target="tpu_custom_call" | custom-call | flops 9200000000 | bytes 28800000 | tf_op jit(solution)/shard_map/pallas_call | solution.py:24
  177.5 4.2 %collective-permute-done.22.refs_2_ = f32[2,32,32,256]{3,2,1,0:T(8,128)S(1)} collective-permute-done((f32[2,32,32,256]{3,2,1,0:T(8,128)S(1)}, f32[2,32,32,256]{3,2,1,0:T(8,128)S(1)}, u32[]{:S(2)}, u32[]{:S(2)}) %collective-permute-start.22) | collective-permute-done | bytes 2097184 | tf_op jit(solution)/shard_map/ppermute | solution.py:536
  181.7 3.0 %shard_map.74 = f32[8,128]{1,0:T(8,128)S(1)} custom-call(s32[2]{0:T(128)S(1)} %copy-done.4, f32[2,32,32,256]{3,2,1,0:T(8,128)S(1)} %shard_map.73.second, f32[2,32,32,256]{3,2,1,0:T(8,128)S(1)} %get-tuple-element.67.tile.refs_0_, f32[2,32,32,256]{3,2,1,0:T(8,128)S(1)} %shard_map.69.refs_1_, f32[2,32,32,256]{3,2,1,0:T(8,128)S(1)} %collective-permute-done.22.refs_2_, ...), custom_call_target="tpu_custom_call" | custom-call | flops 4600000000 | bytes 14400000 | tf_op jit(solution)/shard_map/pallas_call | solution.py:24
  184.7 0.1 collective-permute-start.25
  184.8 2.5 %collective-permute-start.24 = (f32[8,128]{1,0:T(8,128)S(1)}, f32[8,128]{1,0:T(8,128)S(1)}, u32[]{:S(2)}, u32[]{:S(2)}) collective-permute-start(f32[8,128]{1,0:T(8,128)S(1)} %shard_map.74), channel_id=1, source_target_pairs={{0,4},{2,6},{4,0},{6,2},{1,5},{3,7},{5,1},{7,3},{8,12},{10,14},{12... | collective-permute-start | bytes 12296 | tf_op jit(solution)/shard_map/ppermute | solution.py:475
  187.3 0.5 collective-permute-done.25
  187.8 1.1 collective-permute-done.24
  188.9 0.9 collective-permute-start.26
  189.8 2.8 %collective-permute-done.26 = f32[8,128]{1,0:T(8,128)S(1)} collective-permute-done((f32[8,128]{1,0:T(8,128)S(1)}, f32[8,128]{1,0:T(8,128)S(1)}, u32[]{:S(2)}, u32[]{:S(2)}) %collective-permute-start.26) | collective-permute-done | bytes 4128 | tf_op jit(solution)/shard_map/ppermute | solution.py:475
  192.6 2.7 %collective-permute-start.29 = (f32[8,128]{1,0:T(8,128)S(1)}, f32[8,128]{1,0:T(8,128)S(1)}, u32[]{:S(2)}, u32[]{:S(2)}) collective-permute-start(f32[8,128]{1,0:T(8,128)S(1)} %add.24), channel_id=1, source_target_pairs={{0,24},{8,16},{16,8},{24,0},{1,25},{9,17},{17,9},{25,1},{2,26},{10... | collective-permute-start | bytes 12296 | tf_op jit(solution)/shard_map/ppermute | solution.py:475
  195.2 0.8 collective-permute-start.28
  196.1 0.9 collective-permute-start.27
  197.0 1.0 collective-permute-done.29
  198.0 1.7 collective-permute-done.28
  199.8 4.1 %shard_map.75 = (f32[2,32,32,256]{3,2,1,0:T(8,128)}, f32[8,8]{1,0:T(8,128)}) custom-call(s32[2]{0:T(128)S(1)} %copy-done.4, f32[8,128]{1,0:T(8,128)S(1)} %add_add_fusion.inner, f32[2,32,32,256]{3,2,1,0:T(8,128)S(1)} %get-tuple-element.67.tile.refs_0_, f32[2,32,32,256]{3,2,1,0:T(8,128)S(1)} %shard_map.69.refs_1_, ...), custom_call_target="tpu_custom_call" | custom-call | flops 5750000128 | bytes 18000000 | tf_op jit(solution)/shard_map/pallas_call | solution.py:24
  (31 shorter events, 0.3 us)
Async XLA Ops:
  1.2 3.6 %copy-start.1 = (f32[2,32,32,256]{3,2,1,0:T(8,128)S(1)}, f32[2,32,32,256]{3,2,1,0:T(8,128)}, u32[]{:S(2)}) copy-start(f32[2,32,32,256]{3,2,1,0:T(8,128)} %probes.1) | copy-start | bytes 6291460
  1.2 10.4 %copy-start = (f32[3,32,32,256]{3,2,1,0:T(8,128)S(1)}, f32[3,32,32,256]{3,2,1,0:T(8,128)}, u32[]{:S(2)}) copy-start(f32[3,32,32,256]{3,2,1,0:T(8,128)} %velocity.1) | copy-start | bytes 9437188
  1.2 10.4 %copy-start.2 = (f32[32,32,256]{2,1,0:T(8,128)S(1)}, f32[32,32,256]{2,1,0:T(8,128)}, u32[]{:S(2)}) copy-start(f32[32,32,256]{2,1,0:T(8,128)} %param.6) | copy-start | bytes 3145732
  4.8 11.6 %copy-start.6 = (f32[6,2,8,256]{3,2,1,0:T(8,128)S(1)}, f32[6,2,8,256]{3,2,1,0:T(8,128)}, u32[]{:S(2)}) copy-start(f32[6,2,8,256]{3,2,1,0:T(8,128)} %get-tuple-element.56) | copy-start | bytes 294916
  4.8 24.6 %copy-start.5 = (f32[6,2,8,256]{3,2,1,0:T(8,128)S(1)}, f32[6,2,8,256]{3,2,1,0:T(8,128)}, u32[]{:S(2)}) copy-start(f32[6,2,8,256]{3,2,1,0:T(8,128)} %get-tuple-element.57) | copy-start | bytes 294916
  4.8 30.7 %copy-start.3 = (f32[32,32,256]{2,1,0:T(8,128)S(1)}, f32[32,32,256]{2,1,0:T(8,128)}, u32[]{:S(2)}) copy-start(f32[32,32,256]{2,1,0:T(8,128)} %refs_0_.3) | copy-start | bytes 3145732
  4.8 30.7 %copy-start.4 = (s32[2]{0:T(128)S(1)}, s32[2]{0:T(128)}, u32[]{:S(2)}) copy-start(s32[2]{0:T(128)} %pad_add_fusion.scalars) | copy-start | bytes 28
  4.8 49.9 %collective-permute-start.5 = (f32[2,32,32,256]{3,2,1,0:T(8,128)S(1)}, f32[2,32,32,256]{3,2,1,0:T(8,128)S(1)}, u32[]{:S(2)}, u32[]{:S(2)}) collective-permute-start(f32[2,32,32,256]{3,2,1,0:T(8,128)S(1)} %copy-done.1), channel_id=1, source_target_pairs={{0,8},{8,16},{16,24},{1,9},{9,17},{17,25},{2,10},{10,18},{18,26},{... | collective-permute-start | bytes 6291464 | tf_op jit(solution)/shard_map/ppermute | solution.py:536
  10.0 25.5 %collective-permute-start.2 = (f32[6,16,8,256]{3,2,1,0:T(8,128)}, f32[6,16,8,256]{3,2,1,0:T(8,128)S(1)}, u32[]{:S(2)}, u32[]{:S(2)}) collective-permute-start(f32[6,16,8,256]{3,2,1,0:T(8,128)} %get-tuple-element.55), channel_id=1, source_target_pairs={{0,1},{1,0},{2,3},{3,2},{4,5},{5,4},{6,7},{7,6},{8,9},{9,8},{10,11... | collective-permute-start | bytes 2359304 | tf_op jit(solution)/shard_map/ppermute | solution.py:117
  13.7 21.7 %collective-permute-start = (f32[6,4,32,256]{3,2,1,0:T(8,128)S(1)}, f32[6,4,32,256]{3,2,1,0:T(8,128)S(1)}, u32[]{:S(2)}, u32[]{:S(2)}) collective-permute-start(f32[6,4,32,256]{3,2,1,0:T(8,128)S(1)} %get-tuple-element.52), channel_id=1, source_target_pairs={{0,2},{2,4},{4,6},{1,3},{3,5},{5,7},{8,10},{10,12},{12,14},{9,11},... | collective-permute-start | bytes 2359304 | tf_op jit(solution)/shard_map/ppermute | solution.py:125
  15.1 20.4 %collective-permute-start.1 = (f32[6,4,32,256]{3,2,1,0:T(8,128)S(1)}, f32[6,4,32,256]{3,2,1,0:T(8,128)S(1)}, u32[]{:S(2)}, u32[]{:S(2)}) collective-permute-start(f32[6,4,32,256]{3,2,1,0:T(8,128)S(1)} %get-tuple-element.53), channel_id=1, source_target_pairs={{2,0},{4,2},{6,4},{3,1},{5,3},{7,5},{10,8},{12,10},{14,12},{11,9},... | collective-permute-start | bytes 2359304 | tf_op jit(solution)/shard_map/ppermute | solution.py:126
  16.4 13.0 %collective-permute-start.3 = (f32[6,2,8,256]{3,2,1,0:T(8,128)S(1)}, f32[6,2,8,256]{3,2,1,0:T(8,128)S(1)}, u32[]{:S(2)}, u32[]{:S(2)}) collective-permute-start(f32[6,2,8,256]{3,2,1,0:T(8,128)S(1)} %copy-done.6), channel_id=1, source_target_pairs={{0,3},{1,2},{2,5},{3,4},{4,7},{5,6},{8,11},{9,10},{10,13},{11,12},... | collective-permute-start | bytes 294920 | tf_op jit(solution)/shard_map/ppermute | solution.py:117
  29.4 6.1 %collective-permute-start.4 = (f32[6,2,8,256]{3,2,1,0:T(8,128)S(1)}, f32[6,2,8,256]{3,2,1,0:T(8,128)S(1)}, u32[]{:S(2)}, u32[]{:S(2)}) collective-permute-start(f32[6,2,8,256]{3,2,1,0:T(8,128)S(1)} %copy-done.5), channel_id=1, source_target_pairs={{2,1},{3,0},{4,3},{5,2},{6,5},{7,4},{10,9},{11,8},{12,11},{13,10},... | collective-permute-start | bytes 294920 | tf_op jit(solution)/shard_map/ppermute | solution.py:117
  49.8 8.8 %collective-permute-start.6 = (f32[2,16,8,256]{3,2,1,0:T(8,128)S(1)}, f32[2,16,8,256]{3,2,1,0:T(8,128)S(1)}, u32[]{:S(2)}, u32[]{:S(2)}) collective-permute-start(f32[2,16,8,256]{3,2,1,0:T(8,128)S(1)} %get-tuple-element.64), channel_id=1, source_target_pairs={{0,1},{1,0},{2,3},{3,2},{4,5},{5,4},{6,7},{7,6},{8,9},{9,8},{10,11... | collective-permute-start | bytes 786440 | tf_op jit(solution)/shard_map/ppermute | solution.py:117
  55.4 9.3 %collective-permute-start.9 = (f32[2,16,8,256]{3,2,1,0:T(8,128)S(1)}, f32[2,16,8,256]{3,2,1,0:T(8,128)S(1)}, u32[]{:S(2)}, u32[]{:S(2)}) collective-permute-start(f32[2,16,8,256]{3,2,1,0:T(8,128)S(1)} %shard_map.65), channel_id=1, source_target_pairs={{0,1},{1,0},{2,3},{3,2},{4,5},{5,4},{6,7},{7,6},{8,9},{9,8},{10,11... | collective-permute-start | bytes 786440 | tf_op jit(solution)/shard_map/ppermute | solution.py:117
  58.6 9.4 %collective-permute-start.7 = (f32[2,18,8,256]{3,2,1,0:T(8,128)S(1)}, f32[2,18,8,256]{3,2,1,0:T(8,128)S(1)}, u32[]{:S(2)}, u32[]{:S(2)}) collective-permute-start(f32[2,18,8,256]{3,2,1,0:T(8,128)S(1)} %get-tuple-element.65), channel_id=1, source_target_pairs={{0,2},{2,4},{4,6},{1,3},{3,5},{5,7},{8,10},{10,12},{12,14},{9,11},... | collective-permute-start | bytes 884744 | tf_op jit(solution)/shard_map/ppermute | solution.py:124
  60.9 7.2 %collective-permute-start.8 = (f32[2,18,8,256]{3,2,1,0:T(8,128)S(1)}, f32[2,18,8,256]{3,2,1,0:T(8,128)S(1)}, u32[]{:S(2)}, u32[]{:S(2)}) collective-permute-start(f32[2,18,8,256]{3,2,1,0:T(8,128)S(1)} %get-tuple-element.66), channel_id=1, source_target_pairs={{2,0},{4,2},{6,4},{3,1},{5,3},{7,5},{10,8},{12,10},{14,12},{11,9},... | collective-permute-start | bytes 884744 | tf_op jit(solution)/shard_map/ppermute | solution.py:124
  64.7 21.0 %collective-permute-start.10 = (f32[2,18,8,256]{3,2,1,0:T(8,128)S(1)}, f32[2,18,8,256]{3,2,1,0:T(8,128)S(1)}, u32[]{:S(2)}, u32[]{:S(2)}) collective-permute-start(f32[2,18,8,256]{3,2,1,0:T(8,128)S(1)} %get-tuple-element.74), channel_id=1, source_target_pairs={{0,2},{2,4},{4,6},{1,3},{3,5},{5,7},{8,10},{10,12},{12,14},{9,11},... | collective-permute-start | bytes 884744 | tf_op jit(solution)/shard_map/ppermute | solution.py:124
  66.7 19.0 %collective-permute-start.11 = (f32[2,18,8,256]{3,2,1,0:T(8,128)S(1)}, f32[2,18,8,256]{3,2,1,0:T(8,128)S(1)}, u32[]{:S(2)}, u32[]{:S(2)}) collective-permute-start(f32[2,18,8,256]{3,2,1,0:T(8,128)S(1)} %get-tuple-element.75), channel_id=1, source_target_pairs={{2,0},{4,2},{6,4},{3,1},{5,3},{7,5},{10,8},{12,10},{14,12},{11,9},... | collective-permute-start | bytes 884744 | tf_op jit(solution)/shard_map/ppermute | solution.py:124
  80.7 54.0 %collective-permute-start.21 = (f32[2,32,32,256]{3,2,1,0:T(8,128)S(1)}, f32[2,32,32,256]{3,2,1,0:T(8,128)S(1)}, u32[]{:S(2)}, u32[]{:S(2)}) collective-permute-start(f32[2,32,32,256]{3,2,1,0:T(8,128)S(1)} %get-tuple-element.67.tile.refs_0_), channel_id=1, source_target_pairs={{0,24},{1,25},{2,26},{3,27},{4,28},{5,29},{6,30},{7,31}} | collective-permute-start | bytes 6291464 | tf_op jit(solution)/shard_map/ppermute | solution.py:536
  98.1 8.1 %collective-permute-start.13 = (f32[2,16,8,256]{3,2,1,0:T(8,128)S(1)}, f32[2,16,8,256]{3,2,1,0:T(8,128)S(1)}, u32[]{:S(2)}, u32[]{:S(2)}) collective-permute-start(f32[2,16,8,256]{3,2,1,0:T(8,128)S(1)} %get-tuple-element.86), channel_id=1, source_target_pairs={{0,1},{1,0},{2,3},{3,2},{4,5},{5,4},{6,7},{7,6},{8,9},{9,8},{10,11... | collective-permute-start | bytes 786440 | tf_op jit(solution)/shard_map/ppermute | solution.py:117
  106.3 4.7 %collective-permute-start.14 = (f32[2,18,8,256]{3,2,1,0:T(8,128)S(1)}, f32[2,18,8,256]{3,2,1,0:T(8,128)S(1)}, u32[]{:S(2)}, u32[]{:S(2)}) collective-permute-start(f32[2,18,8,256]{3,2,1,0:T(8,128)S(1)} %get-tuple-element.87), channel_id=1, source_target_pairs={{0,2},{2,4},{4,6},{1,3},{3,5},{5,7},{8,10},{10,12},{12,14},{9,11},... | collective-permute-start | bytes 884744 | tf_op jit(solution)/shard_map/ppermute | solution.py:124
  109.1 4.8 %collective-permute-start.15 = (f32[2,18,8,256]{3,2,1,0:T(8,128)S(1)}, f32[2,18,8,256]{3,2,1,0:T(8,128)S(1)}, u32[]{:S(2)}, u32[]{:S(2)}) collective-permute-start(f32[2,18,8,256]{3,2,1,0:T(8,128)S(1)} %get-tuple-element.88), channel_id=1, source_target_pairs={{2,0},{4,2},{6,4},{3,1},{5,3},{7,5},{10,8},{12,10},{14,12},{11,9},... | collective-permute-start | bytes 884744 | tf_op jit(solution)/shard_map/ppermute | solution.py:124
  110.4 15.9 %collective-permute-start.12 = (f32[2,16,8,256]{3,2,1,0:T(8,128)S(1)}, f32[2,16,8,256]{3,2,1,0:T(8,128)S(1)}, u32[]{:S(2)}, u32[]{:S(2)}) collective-permute-start(f32[2,16,8,256]{3,2,1,0:T(8,128)S(1)} %get-tuple-element.82), channel_id=1, source_target_pairs={{0,1},{1,0},{2,3},{3,2},{4,5},{5,4},{6,7},{7,6},{8,9},{9,8},{10,11... | collective-permute-start | bytes 786440 | tf_op jit(solution)/shard_map/ppermute | solution.py:117
  126.4 9.7 %collective-permute-start.16 = (f32[2,18,8,256]{3,2,1,0:T(8,128)S(1)}, f32[2,18,8,256]{3,2,1,0:T(8,128)S(1)}, u32[]{:S(2)}, u32[]{:S(2)}) collective-permute-start(f32[2,18,8,256]{3,2,1,0:T(8,128)S(1)} %get-tuple-element.92), channel_id=1, source_target_pairs={{0,2},{2,4},{4,6},{1,3},{3,5},{5,7},{8,10},{10,12},{12,14},{9,11},... | collective-permute-start | bytes 884744 | tf_op jit(solution)/shard_map/ppermute | solution.py:124
  133.4 3.5 %collective-permute-start.17 = (f32[2,18,8,256]{3,2,1,0:T(8,128)S(1)}, f32[2,18,8,256]{3,2,1,0:T(8,128)S(1)}, u32[]{:S(2)}, u32[]{:S(2)}) collective-permute-start(f32[2,18,8,256]{3,2,1,0:T(8,128)S(1)} %get-tuple-element.93), channel_id=1, source_target_pairs={{2,0},{4,2},{6,4},{3,1},{5,3},{7,5},{10,8},{12,10},{14,12},{11,9},... | collective-permute-start | bytes 884744 | tf_op jit(solution)/shard_map/ppermute | solution.py:124
  134.7 46.9 %collective-permute-start.22 = (f32[2,32,32,256]{3,2,1,0:T(8,128)S(1)}, f32[2,32,32,256]{3,2,1,0:T(8,128)S(1)}, u32[]{:S(2)}, u32[]{:S(2)}) collective-permute-start(f32[2,32,32,256]{3,2,1,0:T(8,128)S(1)} %shard_map.69.refs_1_), channel_id=1, source_target_pairs={{0,8},{8,16},{16,24},{1,9},{9,17},{17,25},{2,10},{10,18},{18,26},{... | collective-permute-start | bytes 6291464 | tf_op jit(solution)/shard_map/ppermute | solution.py:536
  149.2 6.4 %collective-permute-start.18 = (f32[2,16,8,256]{3,2,1,0:T(8,128)S(1)}, f32[2,16,8,256]{3,2,1,0:T(8,128)S(1)}, u32[]{:S(2)}, u32[]{:S(2)}) collective-permute-start(f32[2,16,8,256]{3,2,1,0:T(8,128)S(1)} %get-tuple-element.97), channel_id=1, source_target_pairs={{0,1},{1,0},{2,3},{3,2},{4,5},{5,4},{6,7},{7,6},{8,9},{9,8},{10,11... | collective-permute-start | bytes 786440 | tf_op jit(solution)/shard_map/ppermute | solution.py:117
  155.7 6.6 %collective-permute-start.19 = (f32[2,18,8,256]{3,2,1,0:T(8,128)S(1)}, f32[2,18,8,256]{3,2,1,0:T(8,128)S(1)}, u32[]{:S(2)}, u32[]{:S(2)}) collective-permute-start(f32[2,18,8,256]{3,2,1,0:T(8,128)S(1)} %get-tuple-element.98), channel_id=1, source_target_pairs={{0,2},{2,4},{4,6},{1,3},{3,5},{5,7},{8,10},{10,12},{12,14},{9,11},... | collective-permute-start | bytes 884744 | tf_op jit(solution)/shard_map/ppermute | solution.py:124
  161.0 4.0 %collective-permute-start.20 = (f32[2,18,8,256]{3,2,1,0:T(8,128)S(1)}, f32[2,18,8,256]{3,2,1,0:T(8,128)S(1)}, u32[]{:S(2)}, u32[]{:S(2)}) collective-permute-start(f32[2,18,8,256]{3,2,1,0:T(8,128)S(1)} %get-tuple-element.99), channel_id=1, source_target_pairs={{2,0},{4,2},{6,4},{3,1},{5,3},{7,5},{10,8},{12,10},{14,12},{11,9},... | collective-permute-start | bytes 884744 | tf_op jit(solution)/shard_map/ppermute | solution.py:124
  184.7 3.1 %collective-permute-start.25 = (f32[8,128]{1,0:T(8,128)S(1)}, f32[8,128]{1,0:T(8,128)S(1)}, u32[]{:S(2)}, u32[]{:S(2)}) collective-permute-start(f32[8,128]{1,0:T(8,128)S(1)} %shard_map.74), channel_id=1, source_target_pairs={{0,6},{2,4},{4,2},{6,0},{1,7},{3,5},{5,3},{7,1},{8,14},{10,12},{12... | collective-permute-start | bytes 12296 | tf_op jit(solution)/shard_map/ppermute | solution.py:475
  184.8 4.1 %collective-permute-start.24 = (f32[8,128]{1,0:T(8,128)S(1)}, f32[8,128]{1,0:T(8,128)S(1)}, u32[]{:S(2)}, u32[]{:S(2)}) collective-permute-start(f32[8,128]{1,0:T(8,128)S(1)} %shard_map.74), channel_id=1, source_target_pairs={{0,4},{2,6},{4,0},{6,2},{1,5},{3,7},{5,1},{7,3},{8,12},{10,14},{12... | collective-permute-start | bytes 12296 | tf_op jit(solution)/shard_map/ppermute | solution.py:475
  187.3 1.6 collective-permute-start.23
  188.9 3.7 %collective-permute-start.26 = (f32[8,128]{1,0:T(8,128)S(1)}, f32[8,128]{1,0:T(8,128)S(1)}, u32[]{:S(2)}, u32[]{:S(2)}) collective-permute-start(f32[8,128]{1,0:T(8,128)S(1)} %add_add_fusion.1), channel_id=1, source_target_pairs={{0,1},{1,0},{2,3},{3,2},{4,5},{5,4},{6,7},{7,6},{8,9},{9,8},{10,11... | collective-permute-start | bytes 12296 | tf_op jit(solution)/shard_map/ppermute | solution.py:475
  192.6 5.4 %collective-permute-start.29 = (f32[8,128]{1,0:T(8,128)S(1)}, f32[8,128]{1,0:T(8,128)S(1)}, u32[]{:S(2)}, u32[]{:S(2)}) collective-permute-start(f32[8,128]{1,0:T(8,128)S(1)} %add.24), channel_id=1, source_target_pairs={{0,24},{8,16},{16,8},{24,0},{1,25},{9,17},{17,9},{25,1},{2,26},{10... | collective-permute-start | bytes 12296 | tf_op jit(solution)/shard_map/ppermute | solution.py:475
  195.2 4.5 %collective-permute-start.28 = (f32[8,128]{1,0:T(8,128)S(1)}, f32[8,128]{1,0:T(8,128)S(1)}, u32[]{:S(2)}, u32[]{:S(2)}) collective-permute-start(f32[8,128]{1,0:T(8,128)S(1)} %add.24), channel_id=1, source_target_pairs={{0,16},{8,24},{16,0},{24,8},{1,17},{9,25},{17,1},{25,9},{2,18},{10... | collective-permute-start | bytes 12296 | tf_op jit(solution)/shard_map/ppermute | solution.py:475
  196.1 3.7 %collective-permute-start.27 = (f32[8,128]{1,0:T(8,128)S(1)}, f32[8,128]{1,0:T(8,128)S(1)}, u32[]{:S(2)}, u32[]{:S(2)}) collective-permute-start(f32[8,128]{1,0:T(8,128)S(1)} %add.24), channel_id=1, source_target_pairs={{0,8},{8,0},{16,24},{24,16},{1,9},{9,1},{17,25},{25,17},{2,10},{10... | collective-permute-start | bytes 12296 | tf_op jit(solution)/shard_map/ppermute | solution.py:475
